TPU v7x, 128 devices: a whole 4x4x4 slice. The times are simulated.
128 devices in a mesh: row: 16 (over y_lo, x, core), col: 8 (over z, y_hi).
Axes of the slice: x: 4, y: 4 (y_hi: 2, y_lo: 2; y = y_hi * 2 + y_lo), z: 4, core: 2. Of those that a mesh axis runs over, the one named last changes fastest.
Arguments:
- features: bfloat16 [65536, 128], P(('row', 'col')), may hold values from -6 to 6
- degree: int32 [65536], P(('row', 'col')), may hold values from 32 to 512
- cotangent: bfloat16 [65536, 256], P(('row', 'col')), may hold values from -24 to 24
- weight: bfloat16 [128, 256], replicated, may hold values from -0.5 to 0.5
- layer_bias: float32 [256], replicated, may hold values from -3 to 3
- patterns: bfloat16 [64, 128, 128], replicated, may hold values from 0 to 1, as said below
- tile_row: int32 [16, 8, 512], P('row', 'col'), may hold values from 0 to 31
- tile_col: int32 [16, 8, 512], P('row', 'col'), may hold values from 0 to 63
- tile_pattern: int32 [16, 8, 512], P('row', 'col'), may hold values from 0 to 63
- tile_weight: int32 [16, 8, 512], P('row', 'col'), may hold values from 1 to 4
- tile_count: int32 [16, 8], P('row', 'col'), may hold values from 64 to 512, as said below
Outputs:
- activations: bfloat16 [65536, 256], P(('row', 'col'))
- grad_features: bfloat16 [65536, 128], P(('row', 'col'))
- grad_weight: float32 [128, 256], replicated
- grad_bias: float32 [256], replicated
Inputs may be any that keep to these rules, and one draw needn't show every extreme that they name: `tile_row`: slots may name the same tile position more than once; such tiles add. `tile_count`: 512 is reached at some grid position in every draw. `patterns`: entries are 0 or 1.
All inputs are finite; a program needn't handle non-finite values.
Results may differ from a plain program's by a relative error of at most 0.0058.
Values may be sent and summed in bfloat16 or wider, within the bound.
No kernel may reach another device: no remote copies, remote signals or barrier semaphores. Data moves between devices by JAX's collectives and lax.ppermute only.
A program may use at most 128 MiB of HBM per device.

v0:
```python
import functools
import math

import jax
import jax.numpy as jnp
from jax import lax
from jax.experimental import pallas as pl
from jax.experimental.pallas import tpu as pltpu
from jax.sharding import PartitionSpec as P

GROUP = 64
VMEM_LIMIT = 20 * 1024 * 1024
ROOT_2_PI = math.sqrt(2.0 / math.pi)
CUBIC = 0.044715
BIAS_ROWS = 16
ANY = pl.BlockSpec(memory_space=pl.ANY)
VMEM = pl.BlockSpec(memory_space=pltpu.VMEM)
SMEM = pl.BlockSpec(memory_space=pltpu.SMEM)
PARAMS = pltpu.CompilerParams(vmem_limit_bytes=VMEM_LIMIT)


def pack_slots(tile_row, tile_col, tile_pattern, tile_weight, live, per_shard, core):
    shard = tile_col // per_shard
    half = (shard % 2) ^ core
    place = (half * 8 + shard // 2) * per_shard + tile_col % per_shard
    slots = tile_col.shape[0]
    factor = jnp.where(jnp.arange(slots, dtype=jnp.int32) < live, tile_weight, 0)
    return place | (tile_row << 6) | (tile_pattern << 11) | (factor << 17)


def unpack_slot(word):
    return word & 63, (word >> 6) & 31, (word >> 11) & 63, (word >> 17).astype(jnp.float32)


def root_columns(degree):
    rows = lax.rsqrt(degree.astype(jnp.float32))
    rows = jnp.concatenate([rows, jnp.ones((8 - rows.shape[0], rows.shape[1]), jnp.float32)], 0)
    return rows.T


def scale_kernel(features_hbm, degree_hbm, out_ref, features_ref, degree_ref, sems):
    copies = (
        pltpu.make_async_copy(degree_hbm, degree_ref, sems.at[0]),
        pltpu.make_async_copy(features_hbm, features_ref, sems.at[1]),
    )
    for copy in copies:
        copy.start()
    copies[0].wait()
    roots = root_columns(degree_ref[...])
    copies[1].wait()
    edge = degree_ref.shape[1]
    for tile in range(degree_ref.shape[0]):
        rows = pl.ds(tile * edge, edge)
        scaled = features_ref[rows, :].astype(jnp.float32) * roots[:, tile : tile + 1]
        scaled = scaled.astype(jnp.bfloat16)
        for copy in range(out_ref.shape[0]):
            out_ref[copy, rows, :] = scaled


def forward_kernel(live_ref, slots_ref, patterns_ref, own_ref, other_ref, out_ref, panel, sums, sems):
    edge = patterns_ref.shape[1]
    half = own_ref.shape[0]
    copies = (
        pltpu.make_async_copy(own_ref, panel.at[pl.ds(0, half)], sems.at[0]),
        pltpu.make_async_copy(other_ref, panel.at[pl.ds(half, half)], sems.at[1]),
    )
    for copy in copies:
        copy.start()
    sums[...] = jnp.zeros_like(sums)
    for copy in copies:
        copy.wait()

    def one_group(group, carry):
        terms = []
        for member in range(GROUP):
            place, row, pattern, factor = unpack_slot(slots_ref[group * GROUP + member])
            block = panel[pl.ds(pl.multiple_of(place * edge, edge), edge), :]
            product = jnp.dot(patterns_ref[pattern], block, preferred_element_type=jnp.float32)
            terms.append((row, factor, product))
        for row, factor, product in terms:
            rows = pl.ds(pl.multiple_of(row * edge, edge), edge)
            sums[rows, :] += factor * product
        return carry

    lax.fori_loop(0, (live_ref[0, 0] + GROUP - 1) // GROUP, one_group, 0)
    out_ref[...] = sums[...].astype(jnp.bfloat16)


def backward_kernel(
    live_ref, slots_ref, patterns_ref, spread_ref, keep_ref, send_ref, grads_ref, sums
):
    edge = patterns_ref.shape[1]
    shards, rows_in_shard, _ = spread_ref.shape
    half = sums.shape[0] // 2
    own = rows_in_shard - grads_ref.shape[0]
    per_shard = own // edge
    sums[...] = jnp.zeros_like(sums)

    def one_group(group, carry):
        terms = []
        for member in range(GROUP):
            place, row, pattern, factor = unpack_slot(slots_ref[group * GROUP + member])
            start = pl.multiple_of((row % per_shard) * edge, edge)
            block = spread_ref[row // per_shard, pl.ds(start, edge), :]
            product = jnp.dot(block, patterns_ref[pattern], preferred_element_type=jnp.float32)
            terms.append((place, factor, product))
        for place, factor, product in terms:
            rows = pl.ds(pl.multiple_of(place * edge, edge), edge)
            sums[rows, :] += factor * product
        return carry

    lax.fori_loop(0, (live_ref[0, 0] + GROUP - 1) // GROUP, one_group, 0)
    keep_ref[...] = sums[:half, :]
    send_ref[...] = sums[half:, :].astype(jnp.bfloat16)
    grads = spread_ref[0, own:, :].astype(jnp.float32)
    for shard in range(1, shards):
        grads += spread_ref[shard, own:, :].astype(jnp.float32)
    grads_ref[...] = grads.astype(jnp.bfloat16)


def split_product(left, right, dims):
    high = left.astype(jnp.bfloat16)
    low = (left - high.astype(jnp.float32)).astype(jnp.bfloat16)
    return lax.dot_general(
        high, right, (dims, ((), ())), preferred_element_type=jnp.float32
    ) + lax.dot_general(low, right, (dims, ((), ())), preferred_element_type=jnp.float32)


def activate(pre_act):
    square = pre_act * pre_act
    bent = jnp.tanh(ROOT_2_PI * (pre_act + CUBIC * (pre_act * square)))
    return square, bent, 0.5 * (1.0 + bent)


def middle_kernel(
    core_ref,
    parts_ref,
    degree_ref,
    cotangent_ref,
    weight_ref,
    bias_ref,
    pre_ref,
    upstream_ref,
    keep_ref,
    send_ref,
):
    tiles, edge = degree_ref.shape
    shards = parts_ref.shape[0]
    weight = weight_ref[...]
    height = weight.shape[0]
    roots = root_columns(degree_ref[...])
    grads = jnp.zeros(weight.shape, jnp.float32)
    bias_row = jnp.zeros(bias_ref.shape, jnp.float32)
    for tile in range(tiles):
        rows = pl.ds(tile * edge, edge)
        sums = parts_ref[0, rows, :].astype(jnp.float32)
        for shard in range(1, shards):
            sums += parts_ref[shard, rows, :].astype(jnp.float32)
        inv_root = roots[:, tile : tile + 1]
        pre_act = inv_root * split_product(sums, weight, ((1,), (0,))) + bias_ref[...]
        pre_ref[rows, :] = pre_act
        square, bent, half = activate(pre_act)
        rise = 0.5 * pre_act * (1.0 - bent * bent) * (ROOT_2_PI * (1.0 + 3.0 * CUBIC * square))
        slope = cotangent_ref[rows, :].astype(jnp.float32) * (half + rise)
        upstream = (inv_root * slope).astype(jnp.bfloat16)
        upstream_ref[rows, :] = upstream
        grads += split_product(sums, upstream, ((0,), (0,)))
        bias_row += jnp.sum(slope, axis=0, keepdims=True)
    width = keep_ref.shape[1]
    bias_high = bias_row.astype(jnp.bfloat16).astype(jnp.float32)
    bias_low = bias_row - bias_high
    first = core_ref[0] == 0

    def put(target, left):
        pick = lambda whole: jnp.where(left, whole[:, :width], whole[:, width:])
        target[:height, :] = pick(grads).astype(target.dtype)
        row_ids = lax.broadcasted_iota(jnp.int32, (BIAS_ROWS, width), 0)
        block = jnp.where(row_ids == 0, pick(bias_high), 0.0)
        block = jnp.where(row_ids == 1, pick(bias_low), block)
        target[height:, :] = block.astype(target.dtype)

    put(keep_ref, first)
    put(send_ref, jnp.logical_not(first))


def activation_kernel(pre_ref, act_ref):
    pre_act = pre_ref[...]
    act_ref[...] = (pre_act * activate(pre_act)[2]).astype(jnp.bfloat16)


def spread_kernel(upstream_ref, weight_ref, out_ref):
    edge = out_ref.shape[2]
    for tile in range(upstream_ref.shape[0] // edge):
        rows = pl.ds(tile * edge, edge)
        spread = lax.dot_general(
            weight_ref[...],
            upstream_ref[rows, :],
            (((1,), (1,)), ((), ())),
            preferred_element_type=jnp.float32,
        ).astype(jnp.bfloat16)
        for shard in range(out_ref.shape[0]):
            out_ref[shard, rows, :] = spread


def append_kernel(keep_ref, got_ref, spread_ref, out_ref):
    terms = (keep_ref[...] + got_ref[...].astype(jnp.float32)).astype(jnp.bfloat16)
    rows = pl.ds(out_ref.shape[1] - terms.shape[0], terms.shape[0])
    for shard in range(out_ref.shape[0]):
        out_ref[shard, rows, :] = terms


def join_kernel(keep_ref, got_ref, grads_ref, out_ref):
    shards = out_ref.shape[0]
    own = keep_ref.shape[0] // shards
    for shard in range(shards):
        rows = pl.ds(shard * own, own)
        total = keep_ref[rows, :] + got_ref[rows, :].astype(jnp.float32)
        out_ref[shard, pl.ds(0, own), :] = total.astype(jnp.bfloat16)
        out_ref[shard, pl.ds(own, grads_ref.shape[0]), :] = grads_ref[...]


def total_kernel(scale_factor, parts_ref, half_ref):
    shards = parts_ref.shape[0]
    own = parts_ref.shape[1] - (half_ref.shape[0] - 8 + BIAS_ROWS)
    tail = parts_ref[0, own:, :].astype(jnp.float32)
    for shard in range(1, shards):
        tail += parts_ref[shard, own:, :].astype(jnp.float32)
    tail = tail * scale_factor
    height = half_ref.shape[0] - 8
    half_ref[:height, :] = tail[:height, :]
    bias_row = tail[height : height + 1, :] + tail[height + 1 : height + 2, :]
    half_ref[height:, :] = jnp.broadcast_to(bias_row, (8, bias_row.shape[1]))


def features_kernel(parts_ref, degree_ref, features_ref):
    tiles, edge = degree_ref.shape
    roots = lax.rsqrt(degree_ref[...].astype(jnp.float32))
    for tile in range(tiles):
        rows = pl.ds(tile * edge, edge)
        total = parts_ref[0, rows, :].astype(jnp.float32)
        for shard in range(1, parts_ref.shape[0]):
            total += parts_ref[shard, rows, :].astype(jnp.float32)
        features_ref[rows, :] = (total * roots[tile : tile + 1, :]).T.astype(jnp.bfloat16)


def lay_out_kernel(core_ref, mine_ref, other_ref, grads_ref, bias_ref):
    first = core_ref[0] == 0
    height = grads_ref.shape[0]
    width = mine_ref.shape[1]
    mine, other = mine_ref[...], other_ref[...]
    halves = (jnp.where(first, mine, other), jnp.where(first, other, mine))
    for index, half in enumerate(halves):
        lanes = pl.ds(index * width, width)
        grads_ref[:, lanes] = half[:height, :]
        bias_ref[:, lanes] = half[height : height + 1, :]


def per_device(
    features,
    degree,
    cotangent,
    weight,
    layer_bias,
    patterns,
    tile_row,
    tile_col,
    tile_pattern,
    tile_weight,
    tile_count,
):
    node_dev, feature_count = features.shape
    hidden = weight.shape[1]
    row_devices = lax.axis_size("row")
    col_devices = lax.axis_size("col")
    chips = row_devices // 2
    edge = patterns.shape[1]
    per_shard = node_dev // edge
    core = lax.axis_index("row") % 2
    same_core = [list(range(first, row_devices, 2)) for first in range(2)]
    swap = [(index, index ^ 1) for index in range(row_devices)]
    across_chips = functools.partial(
        lax.all_to_all,
        axis_name="row",
        split_axis=0,
        concat_axis=0,
        axis_index_groups=same_core,
    )
    across_cols = functools.partial(lax.all_to_all, axis_name="col", split_axis=0, concat_axis=0)
    extra = feature_count + BIAS_ROWS
    half = chips * node_dev
    bf16, f32 = jnp.bfloat16, jnp.float32
    shape = jax.ShapeDtypeStruct
    degree_tiles = degree.reshape(per_shard, edge)
    slots = pack_slots(
        tile_row[0, 0],
        tile_col[0, 0],
        tile_pattern[0, 0],
        tile_weight[0, 0],
        tile_count[0, 0],
        per_shard,
        core,
    )
    tile_cost = pl.CostEstimate(
        flops=2 * slots.shape[0] * edge * edge * feature_count,
        bytes_accessed=patterns.size * 2 + 4 * half * feature_count * 2,
        transcendentals=0,
    )

    scaled = pl.pallas_call(
        scale_kernel,
        out_shape=shape((chips, node_dev, feature_count), bf16),
        in_specs=[ANY] * 2,
        out_specs=VMEM,
        scratch_shapes=[
            pltpu.VMEM(features.shape, bf16),
            pltpu.VMEM(degree_tiles.shape, jnp.int32),
            pltpu.SemaphoreType.DMA((2,)),
        ],
        compiler_params=PARAMS,
    )(features, degree_tiles)
    own_panel = across_chips(scaled).reshape(half, feature_count)
    other_panel = lax.ppermute(own_panel, "row", swap)
    row_part = pl.pallas_call(
        forward_kernel,
        out_shape=shape((col_devices * node_dev, feature_count), bf16),
        in_specs=[SMEM] * 2 + [VMEM] + [ANY] * 2,
        out_specs=VMEM,
        scratch_shapes=[
            pltpu.VMEM((2 * half, feature_count), bf16),
            pltpu.VMEM((col_devices * node_dev, feature_count), f32),
            pltpu.SemaphoreType.DMA((2,)),
        ],
        compiler_params=PARAMS,
        cost_estimate=tile_cost,
    )(tile_count, slots, patterns, own_panel, other_panel)
    parts = across_cols(row_part.reshape(col_devices, node_dev, feature_count))
    core_word = core.astype(jnp.int32).reshape(1)
    pre_act, upstream, keep_terms, send_terms = pl.pallas_call(
        middle_kernel,
        out_shape=(
            shape((node_dev, hidden), f32),
            shape((node_dev, hidden), bf16),
            shape((extra, edge), f32),
            shape((extra, edge), bf16),
        ),
        in_specs=[SMEM] + [VMEM] * 5,
        out_specs=(VMEM,) * 4,
        compiler_params=PARAMS,
    )(core_word, parts, degree_tiles, cotangent, weight, layer_bias[None, :])
    got_terms = lax.ppermute(send_terms, "row", swap)
    spread = pl.pallas_call(
        spread_kernel,
        out_shape=shape((col_devices, node_dev + extra, edge), bf16),
        in_specs=[VMEM] * 2,
        out_specs=VMEM,
        compiler_params=PARAMS,
    )(upstream, weight)
    spread = pl.pallas_call(
        append_kernel,
        out_shape=shape(spread.shape, bf16),
        in_specs=[VMEM] * 3,
        out_specs=VMEM,
        input_output_aliases={2: 0},
        compiler_params=PARAMS,
    )(keep_terms, got_terms, spread)
    spread_all = across_cols(spread)
    keep, send, grads = pl.pallas_call(
        backward_kernel,
        out_shape=(
            shape((half, edge), f32),
            shape((half, edge), bf16),
            shape((extra, edge), bf16),
        ),
        in_specs=[SMEM] * 2 + [VMEM] * 2,
        out_specs=(VMEM,) * 3,
        scratch_shapes=[pltpu.VMEM((2 * half, edge), f32)],
        compiler_params=PARAMS,
        cost_estimate=tile_cost,
    )(tile_count, slots, patterns, spread_all)
    got = lax.ppermute(send, "row", swap)
    pre_act, keep = lax.optimization_barrier((pre_act, keep))
    activations = pl.pallas_call(
        activation_kernel,
        out_shape=shape((node_dev, hidden), bf16),
        in_specs=[VMEM],
        out_specs=VMEM,
        compiler_params=PARAMS,
    )(pre_act)
    got, activations = lax.optimization_barrier((got, activations))
    joined = pl.pallas_call(
        join_kernel,
        out_shape=shape((chips, node_dev + extra, edge), bf16),
        in_specs=[VMEM] * 3,
        out_specs=VMEM,
        compiler_params=PARAMS,
    )(keep, got, grads)
    back_parts = across_chips(joined)
    scale_factor = 1.0 / math.sqrt(node_dev * row_devices * col_devices)
    mine = pl.pallas_call(
        functools.partial(total_kernel, scale_factor),
        out_shape=shape((feature_count + 8, edge), f32),
        in_specs=[VMEM],
        out_specs=VMEM,
        compiler_params=PARAMS,
    )(back_parts)
    other = lax.ppermute(mine, "row", swap)
    grad_features = pl.pallas_call(
        features_kernel,
        out_shape=shape((node_dev, feature_count), bf16),
        in_specs=[VMEM] * 2,
        out_specs=VMEM,
        compiler_params=PARAMS,
    )(back_parts, degree_tiles)
    grad_weight, grad_bias = pl.pallas_call(
        lay_out_kernel,
        out_shape=(shape((feature_count, hidden), f32), shape((1, hidden), f32)),
        in_specs=[SMEM] + [VMEM] * 2,
        out_specs=(VMEM,) * 2,
        compiler_params=PARAMS,
    )(core_word, mine, other)
    return (activations, grad_features, grad_weight, grad_bias[0])


def solution(mesh):
    in_specs = (
        P(("row", "col"), None),
        P(("row", "col")),
        P(("row", "col"), None),
        P(),
        P(),
        P(),
        P("row", "col", None),
        P("row", "col", None),
        P("row", "col", None),
        P("row", "col", None),
        P("row", "col"),
    )
    out_specs = (P(("row", "col"), None), P(("row", "col"), None), P(), P())
    return jax.shard_map(
        per_device, mesh=mesh, in_specs=in_specs, out_specs=out_specs, check_vma=False
    )
```

profile of v0, /device:TPU:1, one launch (start us, length us, event | category | flops | bytes accessed | tf_op | source)
XLA Modules:
  0.0 115.4 jit_solution(14186540963730935908)
XLA Ops:
  0.6 0.9 copy-done.2
  1.5 0.7 copy-done.3
  2.2 0.4 shard_map.138
  2.6 0.0 copy-start.7
  2.6 0.0 copy-start.8
  2.7 0.0 copy-start.9
  2.7 0.0 copy-start.10
  2.7 0.0 copy-start.6
  2.7 20.6 %all_to_all.20 = bf16[8,512,128]{2,1,0:T(8,128)(2,1)S(1)} all-to-all(bf16[8,512,128]{2,1,0:T(8,128)(2,1)S(1)} %shard_map.138), channel_id=1, replica_groups={{0,16,32,48,64,80,96,112},{8,24,40,56,72,88,104,120},{1,17,33,49,65,81,..., dimensions={0} | all-to-all | bytes 2097152 | tf_op jit(solution)/shard_map/all_to_all | solution.py:321
  23.3 1.9 %collective-permute-start = (bf16[4096,128]{1,0:T(8,128)(2,1)S(1)}, bf16[4096,128]{1,0:T(8,128)(2,1)}, u32[]{:S(2)}, u32[]{:S(2)}) collective-permute-start(bf16[4096,128]{1,0:T(8,128)(2,1)S(1)} %bitcast.12), channel_id=1, source_target_pairs={{0,8},{8,0},{16,24},{24,16},{32,40},{40,32},{48,56},{56,48},{64,72... | collective-permute-start | bytes 3145736 | tf_op jit(solution)/shard_map/ppermute | solution.py:322
  25.9 1.7 %collective-permute-done.other_ref = bf16[4096,128]{1,0:T(8,128)(2,1)} collective-permute-done((bf16[4096,128]{1,0:T(8,128)(2,1)S(1)}, bf16[4096,128]{1,0:T(8,128)(2,1)}, u32[]{:S(2)}, u32[]{:S(2)}) %collective-permute-start) | collective-permute-done | bytes 1048608 | tf_op jit(solution)/shard_map/ppermute | solution.py:322
  27.6 3.6 %shard_map.139 = bf16[4096,128]{1,0:T(8,128)(2,1)S(1)} custom-call(s32[1,1]{1,0:T(1,128)} %copy.17.live_ref, s32[512]{0:T(512)S(1)} %fusion.7.slots_ref, bf16[64,128,128]{2,1,0:T(8,128)(2,1)S(1)} %copy-done.6, bf16[4096,128]{1,0:T(8,128)(2,1)S(1)} %bitcast.13, bf16[4096,128]{1,0:T(8,128)(2,1)} %collective-permute-done.other_ref), custom_call_target="tpu_custom_call" | custom-call | flops 2147483648 | bytes 6291456 | tf_op jit(solution)/shard_map/pallas_call | solution.py:323
  31.2 0.0 copy-start
  31.2 0.0 copy-start.1
  31.2 0.0 copy-start.4
  31.3 0.0 copy-start.5
  31.3 25.5 %all_to_all.21.parts_ref = bf16[8,512,128]{2,1,0:T(8,128)(2,1)S(1)} all-to-all(bf16[8,512,128]{2,1,0:T(8,128)(2,1)S(1)} %bitcast.14), channel_id=1, replica_groups=mesh['row'=16,'col'=8] {'col'}, dimensions={0} | all-to-all | bytes 2097152 | tf_op jit(solution)/shard_map/all_to_all | solution.py:336
  56.8 0.9 shard_map.140
  57.6 2.1 %collective-permute-start.1 = (bf16[144,128]{1,0:T(8,128)(2,1)S(1)}, bf16[144,128]{1,0:T(8,128)(2,1)S(1)}, u32[]{:S(2)}, u32[]{:S(2)}) collective-permute-start(bf16[144,128]{1,0:T(8,128)(2,1)S(1)} %get-tuple-element.18), channel_id=1, source_target_pairs={{0,8},{8,0},{16,24},{24,16},{32,40},{40,32},{48,56},{56,48},{64,72... | collective-permute-start | bytes 110600 | tf_op jit(solution)/shard_map/ppermute | solution.py:350
  59.8 0.2 shard_map.141.spread_ref
  60.0 0.6 collective-permute-done.1.got_ref
  60.7 22.5 %all_to_all.22.spread_ref = bf16[8,656,128]{2,1,0:T(8,128)(2,1)S(1)} all-to-all(bf16[8,656,128]{2,1,0:T(8,128)(2,1)S(1)} %shard_map.142), channel_id=1, replica_groups=mesh['row'=16,'col'=8] {'col'}, dimensions={0} | all-to-all | bytes 2686976 | tf_op jit(solution)/shard_map/all_to_all | solution.py:366
  83.2 2.7 %shard_map.143 = (f32[4096,128]{1,0:T(8,128)S(1)}, bf16[4096,128]{1,0:T(8,128)(2,1)S(1)}, bf16[144,128]{1,0:T(8,128)(2,1)S(1)}) custom-call(s32[1,1]{1,0:T(1,128)} %copy.17.live_ref, s32[512]{0:T(512)S(1)} %fusion.7.slots_ref, bf16[64,128,128]{2,1,0:T(8,128)(2,1)S(1)} %copy-done.6, bf16[8,656,128]{2,1,0:T(8,128)(2,1)S(1)} %all_to_all.22.spread_ref), custom_call_target="tpu_custom_call" | custom-call | flops 2147483648 | bytes 6291456 | tf_op jit(solution)/shard_map/pallas_call | solution.py:367
  85.9 2.3 %collective-permute-start.2 = (bf16[4096,128]{1,0:T(8,128)(2,1)S(1)}, bf16[4096,128]{1,0:T(8,128)(2,1)S(1)}, u32[]{:S(2)}, u32[]{:S(2)}) collective-permute-start(bf16[4096,128]{1,0:T(8,128)(2,1)S(1)} %get-tuple-element.20), channel_id=1, source_target_pairs={{0,8},{8,0},{16,24},{24,16},{32,40},{40,32},{48,56},{56,48},{64,72... | collective-permute-start | bytes 3145736 | tf_op jit(solution)/shard_map/ppermute | solution.py:380
  88.2 0.9 shard_map.144
  89.1 1.4 %collective-permute-done.2.got_ref = bf16[4096,128]{1,0:T(8,128)(2,1)S(1)} collective-permute-done((bf16[4096,128]{1,0:T(8,128)(2,1)S(1)}, bf16[4096,128]{1,0:T(8,128)(2,1)S(1)}, u32[]{:S(2)}, u32[]{:S(2)}) %collective-permute-start.2) | collective-permute-done | bytes 1048608 | tf_op jit(solution)/shard_map/ppermute | solution.py:380
  90.5 0.3 shard_map.145
  90.8 21.9 %all_to_all.23.parts_ref = bf16[8,656,128]{2,1,0:T(8,128)(2,1)S(1)} all-to-all(bf16[8,656,128]{2,1,0:T(8,128)(2,1)S(1)} %shard_map.145), channel_id=1, replica_groups={{0,16,32,48,64,80,96,112},{8,24,40,56,72,88,104,120},{1,17,33,49,65,81,..., dimensions={0} | all-to-all | bytes 2686976 | tf_op jit(solution)/shard_map/all_to_all | solution.py:397
  112.7 1.2 %collective-permute-start.3 = (f32[136,128]{1,0:T(8,128)S(1)}, f32[136,128]{1,0:T(8,128)S(1)}, u32[]{:S(2)}, u32[]{:S(2)}) collective-permute-start(f32[136,128]{1,0:T(8,128)S(1)} %shard_map.147.mine_ref), channel_id=1, source_target_pairs={{0,8},{8,0},{16,24},{24,16},{32,40},{40,32},{48,56},{56,48},{64,72... | collective-permute-start | bytes 208904 | tf_op jit(solution)/shard_map/ppermute | solution.py:406
  113.9 0.9 shard_map.146
  114.7 0.0 collective-permute-done.3.other_ref
  114.8 0.7 shard_map.148
  (16 shorter events, 0.1 us)
Async XLA Ops:
  0.6 0.9 copy-start.2
  1.5 0.7 copy-start.3
  2.6 23.2 %copy-start.7 = (s32[1,1,512]{2,1,0:T(1,128)S(1)}, s32[1,1,512]{2,1,0:T(1,128)}, u32[]{:S(2)}) copy-start(s32[1,1,512]{2,1,0:T(1,128)} %param.17) | copy-start | bytes 6148
  2.6 23.2 %copy-start.8 = (s32[1,1,512]{2,1,0:T(1,128)S(1)}, s32[1,1,512]{2,1,0:T(1,128)}, u32[]{:S(2)}) copy-start(s32[1,1,512]{2,1,0:T(1,128)} %param.19) | copy-start | bytes 6148
  2.7 23.2 %copy-start.9 = (s32[1,1,512]{2,1,0:T(1,128)S(1)}, s32[1,1,512]{2,1,0:T(1,128)}, u32[]{:S(2)}) copy-start(s32[1,1,512]{2,1,0:T(1,128)} %param.20) | copy-start | bytes 6148
  2.7 23.2 %copy-start.10 = (s32[1,1,512]{2,1,0:T(1,128)S(1)}, s32[1,1,512]{2,1,0:T(1,128)}, u32[]{:S(2)}) copy-start(s32[1,1,512]{2,1,0:T(1,128)} %param.18) | copy-start | bytes 6148
  2.7 24.9 %copy-start.6 = (bf16[64,128,128]{2,1,0:T(8,128)(2,1)S(1)}, bf16[64,128,128]{2,1,0:T(8,128)(2,1)}, u32[]{:S(2)}) copy-start(bf16[64,128,128]{2,1,0:T(8,128)(2,1)} %patterns_ref.3) | copy-start | bytes 6291460
  23.3 4.3 %collective-permute-start = (bf16[4096,128]{1,0:T(8,128)(2,1)S(1)}, bf16[4096,128]{1,0:T(8,128)(2,1)}, u32[]{:S(2)}, u32[]{:S(2)}) collective-permute-start(bf16[4096,128]{1,0:T(8,128)(2,1)S(1)} %bitcast.12), channel_id=1, source_target_pairs={{0,8},{8,0},{16,24},{24,16},{32,40},{40,32},{48,56},{56,48},{64,72... | collective-permute-start | bytes 3145736 | tf_op jit(solution)/shard_map/ppermute | solution.py:322
  31.2 25.5 %copy-start = (bf16[128,256]{1,0:T(8,128)(2,1)S(1)}, bf16[128,256]{1,0:T(8,128)(2,1)}, u32[]{:S(2)}) copy-start(bf16[128,256]{1,0:T(8,128)(2,1)} %weight_ref.3) | copy-start | bytes 196612
  31.2 25.5 %copy-start.1 = (bf16[512,256]{1,0:T(8,128)(2,1)S(1)}, bf16[512,256]{1,0:T(8,128)(2,1)}, u32[]{:S(2)}) copy-start(bf16[512,256]{1,0:T(8,128)(2,1)} %cotangent_ref.1) | copy-start | bytes 786436
  31.2 25.5 %copy-start.4 = (s32[512]{0:T(512)S(1)}, s32[512]{0:T(512)}, u32[]{:S(2)}) copy-start(s32[512]{0:T(512)} %param.12) | copy-start | bytes 6148
  31.3 25.5 %copy-start.5 = (f32[256]{0:T(256)S(1)}, f32[256]{0:T(256)}, u32[]{:S(2)}) copy-start(f32[256]{0:T(256)} %param.15) | copy-start | bytes 3076
  57.6 3.0 %collective-permute-start.1 = (bf16[144,128]{1,0:T(8,128)(2,1)S(1)}, bf16[144,128]{1,0:T(8,128)(2,1)S(1)}, u32[]{:S(2)}, u32[]{:S(2)}) collective-permute-start(bf16[144,128]{1,0:T(8,128)(2,1)S(1)} %get-tuple-element.18), channel_id=1, source_target_pairs={{0,8},{8,0},{16,24},{24,16},{32,40},{40,32},{48,56},{56,48},{64,72... | collective-permute-start | bytes 110600 | tf_op jit(solution)/shard_map/ppermute | solution.py:350
  85.9 4.6 %collective-permute-start.2 = (bf16[4096,128]{1,0:T(8,128)(2,1)S(1)}, bf16[4096,128]{1,0:T(8,128)(2,1)S(1)}, u32[]{:S(2)}, u32[]{:S(2)}) collective-permute-start(bf16[4096,128]{1,0:T(8,128)(2,1)S(1)} %get-tuple-element.20), channel_id=1, source_target_pairs={{0,8},{8,0},{16,24},{24,16},{32,40},{40,32},{48,56},{56,48},{64,72... | collective-permute-start | bytes 3145736 | tf_op jit(solution)/shard_map/ppermute | solution.py:380
  112.7 2.1 %collective-permute-start.3 = (f32[136,128]{1,0:T(8,128)S(1)}, f32[136,128]{1,0:T(8,128)S(1)}, u32[]{:S(2)}, u32[]{:S(2)}) collective-permute-start(f32[136,128]{1,0:T(8,128)S(1)} %shard_map.147.mine_ref), channel_id=1, source_target_pairs={{0,8},{8,0},{16,24},{24,16},{32,40},{40,32},{48,56},{56,48},{64,72... | collective-permute-start | bytes 208904 | tf_op jit(solution)/shard_map/ppermute | solution.py:406
where the time goes:
time: 117 us; the launch traced here: 115 us
  blocking collectives  90.4 us (77%)
  Pallas kernels  10.6 us (9%)
  starting transfers between devices  7.5 us (6%)
  waiting for transfers between devices  3.75 us (3%)
  local copies, waits for them, and re-layouts  1.64 us (1%)
  between operations  1.48 us (1%)
    all_to_all x1, blocking collectives, per_device(): parts = across_cols(row_part.reshape(col_devices, node_dev, feature_count))  25.5 us
    all_to_all x1, blocking collectives, per_device(): spread_all = across_cols(spread)  22.5 us
    all_to_all x1, blocking collectives, per_device(): back_parts = across_chips(joined)  21.9 us
    all_to_all x1, blocking collectives, per_device(): own_panel = across_chips(scaled).reshape(half, feature_count)  20.6 us
    pallas_call x1, Pallas kernels, per_device(): pl.pallas_call(forward_kernel, out_shape=shape((col_devices * node_dev, f...  3.65 us
    pallas_call x1, Pallas kernels, per_device(): pl.pallas_call(backward_kernel, out_shape=(shape((half, edge), f32), shap...  2.73 us
  transfers between devices with their start and end apart: 4, of which 3 were waited for; matrix products, arithmetic and copies ran while one was open for 0% of the time, Pallas kernels for 2%

commit v1 on v0

--- a/solution.py
+++ b/solution.py
@@ -13,23 +13,51 @@
 ROOT_2_PI = math.sqrt(2.0 / math.pi)
 CUBIC = 0.044715
 BIAS_ROWS = 16
+PAIRS = (((0, 1), (2, 3)), ((0, 3), (1, 2)))
 ANY = pl.BlockSpec(memory_space=pl.ANY)
 VMEM = pl.BlockSpec(memory_space=pltpu.VMEM)
 SMEM = pl.BlockSpec(memory_space=pltpu.SMEM)
 PARAMS = pltpu.CompilerParams(vmem_limit_bytes=VMEM_LIMIT)
 
 
-def pack_slots(tile_row, tile_col, tile_pattern, tile_weight, live, per_shard, core):
+def pair_of(place, core):
+    return jnp.where(core == 0, place >> 1, (place ^ (place >> 1)) & 1)
+
+
+def pair_index(place, core):
+    return jnp.where(core == 0, place & 1, place >> 1)
+
+
+def far_neighbour(place, core):
+    return place ^ 3 if core == 0 else place ^ 1
+
+
+def pack_slots(tile_row, tile_col, tile_pattern, tile_weight, live, per_shard, row, col):
+    core = row % 2
     shard = tile_col // per_shard
-    half = (shard % 2) ^ core
-    place = (half * 8 + shard // 2) * per_shard + tile_col % per_shard
+    parity = shard % 2
+    chip = shard // 2
+    tile = tile_col % per_shard
+    half = parity ^ core
+    forward = (half * 8 + chip) * per_shard + tile
+    ring = chip % 4
+    far = (pair_of(ring, parity) != pair_of((row // 2) % 4, parity)).astype(jnp.int32)
+    rank = pair_index(ring, parity) * 2 + chip // 4
+    target = ((half * 2 + far) * 4 + rank) * per_shard + tile
+    peer = tile_row // per_shard
+    far = (pair_of(peer // 2, core) != pair_of(col // 2, core)).astype(jnp.int32)
+    rank = pair_index(peer // 2, core) * 2 + peer % 2
+    source = (far * 4 + rank) * per_shard + tile_row % per_shard
     slots = tile_col.shape[0]
     factor = jnp.where(jnp.arange(slots, dtype=jnp.int32) < live, tile_weight, 0)
-    return place | (tile_row << 6) | (tile_pattern << 11) | (factor << 17)
-
-
-def unpack_slot(word):
-    return word & 63, (word >> 6) & 31, (word >> 11) & 63, (word >> 17).astype(jnp.float32)
+    return (
+        forward
+        | (tile_row << 6)
+        | (tile_pattern << 11)
+        | (factor << 17)
+        | (target << 20)
+        | (source << 26)
+    )
 
 
 def root_columns(degree):
@@ -57,23 +85,19 @@
             out_ref[copy, rows, :] = scaled
 
 
-def forward_kernel(live_ref, slots_ref, patterns_ref, own_ref, other_ref, out_ref, panel, sums, sems):
+def forward_kernel(live_ref, slots_ref, patterns_ref, own_ref, other_ref, out_ref, panel, sums):
     edge = patterns_ref.shape[1]
     half = own_ref.shape[0]
-    copies = (
-        pltpu.make_async_copy(own_ref, panel.at[pl.ds(0, half)], sems.at[0]),
-        pltpu.make_async_copy(other_ref, panel.at[pl.ds(half, half)], sems.at[1]),
-    )
-    for copy in copies:
-        copy.start()
+    panel[:half, :] = own_ref[...]
+    panel[half:, :] = other_ref[...]
     sums[...] = jnp.zeros_like(sums)
-    for copy in copies:
-        copy.wait()
 
     def one_group(group, carry):
         terms = []
         for member in range(GROUP):
-            place, row, pattern, factor = unpack_slot(slots_ref[group * GROUP + member])
+            word = slots_ref[group * GROUP + member]
+            place, row, pattern = word & 63, (word >> 6) & 31, (word >> 11) & 63
+            factor = ((word >> 17) & 7).astype(jnp.float32)
             block = panel[pl.ds(pl.multiple_of(place * edge, edge), edge), :]
             product = jnp.dot(patterns_ref[pattern], block, preferred_element_type=jnp.float32)
             terms.append((row, factor, product))
@@ -87,34 +111,42 @@
 
 
 def backward_kernel(
-    live_ref, slots_ref, patterns_ref, spread_ref, keep_ref, send_ref, grads_ref, sums
+    live_ref,
+    slots_ref,
+    patterns_ref,
+    near_ref,
+    far_ref,
+    keep_ref,
+    send_ref,
+    grads_ref,
+    panel,
+    sums,
 ):
     edge = patterns_ref.shape[1]
-    shards, rows_in_shard, _ = spread_ref.shape
-    half = sums.shape[0] // 2
-    own = rows_in_shard - grads_ref.shape[0]
-    per_shard = own // edge
+    half = keep_ref.shape[0]
+    part = panel.shape[0] // 2
+    panel[:part, :] = near_ref[:part, :]
+    panel[part:, :] = far_ref[:part, :]
     sums[...] = jnp.zeros_like(sums)
 
     def one_group(group, carry):
         terms = []
         for member in range(GROUP):
-            place, row, pattern, factor = unpack_slot(slots_ref[group * GROUP + member])
-            start = pl.multiple_of((row % per_shard) * edge, edge)
-            block = spread_ref[row // per_shard, pl.ds(start, edge), :]
+            word = slots_ref[group * GROUP + member]
+            pattern, target, source = (word >> 11) & 63, (word >> 20) & 63, (word >> 26) & 31
+            factor = ((word >> 17) & 7).astype(jnp.float32)
+            block = panel[pl.ds(pl.multiple_of(source * edge, edge), edge), :]
             product = jnp.dot(block, patterns_ref[pattern], preferred_element_type=jnp.float32)
-            terms.append((place, factor, product))
-        for place, factor, product in terms:
-            rows = pl.ds(pl.multiple_of(place * edge, edge), edge)
+            terms.append((target, factor, product))
+        for target, factor, product in terms:
+            rows = pl.ds(pl.multiple_of(target * edge, edge), edge)
             sums[rows, :] += factor * product
         return carry
 
     lax.fori_loop(0, (live_ref[0, 0] + GROUP - 1) // GROUP, one_group, 0)
     keep_ref[...] = sums[:half, :]
     send_ref[...] = sums[half:, :].astype(jnp.bfloat16)
-    grads = spread_ref[0, own:, :].astype(jnp.float32)
-    for shard in range(1, shards):
-        grads += spread_ref[shard, own:, :].astype(jnp.float32)
+    grads = near_ref[part:, :].astype(jnp.float32) + far_ref[part:, :].astype(jnp.float32)
     grads_ref[...] = grads.astype(jnp.bfloat16)
 
 
@@ -209,22 +241,44 @@
         out_ref[shard, rows, :] = terms
 
 
-def join_kernel(keep_ref, got_ref, grads_ref, out_ref):
+def sum_of_four(parts_ref, rows):
+    part = lambda index: parts_ref[index, rows, :].astype(jnp.float32)
+    return (part(0) + part(2)) + (part(1) + part(3))
+
+
+def gather_kernel(parts_ref, out_ref):
+    shards, rows_in_shard, _ = parts_ref.shape
+    extra = (shards * rows_in_shard - out_ref.shape[0]) // (shards - 1)
+    own = rows_in_shard - extra
+    for shard in range(shards):
+        out_ref[pl.ds(shard * own, own), :] = parts_ref[shard, :own, :]
+    out_ref[shards * own :, :] = sum_of_four(parts_ref, pl.ds(own, extra)).astype(jnp.bfloat16)
+
+
+def split_kernel(keep_ref, got_ref, grads_ref, near_ref, far_ref):
+    half = near_ref.shape[0]
+    near_ref[...] = keep_ref[:half, :] + got_ref[:half, :].astype(jnp.float32)
+    far = keep_ref[half:, :] + got_ref[half:, :].astype(jnp.float32)
+    far_ref[:half, :] = far.astype(jnp.bfloat16)
+    far_ref[half:, :] = grads_ref[...]
+
+
+def join_kernel(near_ref, got_ref, grads_ref, out_ref):
     shards = out_ref.shape[0]
-    own = keep_ref.shape[0] // shards
+    half = near_ref.shape[0]
+    own = half // shards
+    grads = grads_ref[...].astype(jnp.float32) + got_ref[half:, :].astype(jnp.float32)
+    grads = grads.astype(jnp.bfloat16)
     for shard in range(shards):
         rows = pl.ds(shard * own, own)
-        total = keep_ref[rows, :] + got_ref[rows, :].astype(jnp.float32)
+        total = near_ref[rows, :] + got_ref[rows, :].astype(jnp.float32)
         out_ref[shard, pl.ds(0, own), :] = total.astype(jnp.bfloat16)
-        out_ref[shard, pl.ds(own, grads_ref.shape[0]), :] = grads_ref[...]
+        out_ref[shard, pl.ds(own, grads.shape[0]), :] = grads
 
 
 def total_kernel(scale_factor, parts_ref, half_ref):
-    shards = parts_ref.shape[0]
-    own = parts_ref.shape[1] - (half_ref.shape[0] - 8 + BIAS_ROWS)
-    tail = parts_ref[0, own:, :].astype(jnp.float32)
-    for shard in range(1, shards):
-        tail += parts_ref[shard, own:, :].astype(jnp.float32)
+    extra = half_ref.shape[0] - 8 + BIAS_ROWS
+    tail = sum_of_four(parts_ref, pl.ds(parts_ref.shape[1] - extra, extra))
     tail = tail * scale_factor
     height = half_ref.shape[0] - 8
     half_ref[:height, :] = tail[:height, :]
@@ -237,9 +291,7 @@
     roots = lax.rsqrt(degree_ref[...].astype(jnp.float32))
     for tile in range(tiles):
         rows = pl.ds(tile * edge, edge)
-        total = parts_ref[0, rows, :].astype(jnp.float32)
-        for shard in range(1, parts_ref.shape[0]):
-            total += parts_ref[shard, rows, :].astype(jnp.float32)
+        total = sum_of_four(parts_ref, rows)
         features_ref[rows, :] = (total * roots[tile : tile + 1, :]).T.astype(jnp.bfloat16)
 
 
@@ -275,17 +327,34 @@
     chips = row_devices // 2
     edge = patterns.shape[1]
     per_shard = node_dev // edge
-    core = lax.axis_index("row") % 2
+    row, col = lax.axis_index("row"), lax.axis_index("col")
+    core = row % 2
     same_core = [list(range(first, row_devices, 2)) for first in range(2)]
     swap = [(index, index ^ 1) for index in range(row_devices)]
-    across_chips = functools.partial(
-        lax.all_to_all,
-        axis_name="row",
-        split_axis=0,
-        concat_axis=0,
-        axis_index_groups=same_core,
-    )
-    across_cols = functools.partial(lax.all_to_all, axis_name="col", split_axis=0, concat_axis=0)
+    row_near = [
+        [(low * 4 + ring) * 2 + core_index for ring in pair for low in range(2)]
+        for core_index in range(2)
+        for pair in PAIRS[core_index]
+    ]
+    row_far = [
+        (index, (index // 8 * 4 + far_neighbour(index // 2 % 4, index % 2)) * 2 + index % 2)
+        for index in range(row_devices)
+    ]
+    col_near = [
+        [index * col_devices + ring * 2 + high for ring in pair for high in range(2)]
+        for index in range(row_devices)
+        for pair in PAIRS[index % 2]
+    ]
+    col_far = [
+        (
+            index * col_devices + place,
+            index * col_devices + far_neighbour(place // 2, index % 2) * 2 + place % 2,
+        )
+        for index in range(row_devices)
+        for place in range(col_devices)
+    ]
+    exchange = functools.partial(lax.all_to_all, split_axis=0, concat_axis=0)
+    both = ("row", "col")
     extra = feature_count + BIAS_ROWS
     half = chips * node_dev
     bf16, f32 = jnp.bfloat16, jnp.float32
@@ -298,7 +367,8 @@
         tile_weight[0, 0],
         tile_count[0, 0],
         per_shard,
-        core,
+        row,
+        col,
     )
     tile_cost = pl.CostEstimate(
         flops=2 * slots.shape[0] * edge * edge * feature_count,
@@ -318,22 +388,21 @@
         ],
         compiler_params=PARAMS,
     )(features, degree_tiles)
-    own_panel = across_chips(scaled).reshape(half, feature_count)
+    own_panel = exchange(scaled, "row", axis_index_groups=same_core).reshape(half, feature_count)
     other_panel = lax.ppermute(own_panel, "row", swap)
     row_part = pl.pallas_call(
         forward_kernel,
         out_shape=shape((col_devices * node_dev, feature_count), bf16),
-        in_specs=[SMEM] * 2 + [VMEM] + [ANY] * 2,
+        in_specs=[SMEM] * 2 + [VMEM] * 3,
         out_specs=VMEM,
         scratch_shapes=[
             pltpu.VMEM((2 * half, feature_count), bf16),
             pltpu.VMEM((col_devices * node_dev, feature_count), f32),
-            pltpu.SemaphoreType.DMA((2,)),
         ],
         compiler_params=PARAMS,
         cost_estimate=tile_cost,
     )(tile_count, slots, patterns, own_panel, other_panel)
-    parts = across_cols(row_part.reshape(col_devices, node_dev, feature_count))
+    parts = exchange(row_part.reshape(col_devices, node_dev, feature_count), "col")
     core_word = core.astype(jnp.int32).reshape(1)
     pre_act, upstream, keep_terms, send_terms = pl.pallas_call(
         middle_kernel,
@@ -350,7 +419,7 @@
     got_terms = lax.ppermute(send_terms, "row", swap)
     spread = pl.pallas_call(
         spread_kernel,
-        out_shape=shape((col_devices, node_dev + extra, edge), bf16),
+        out_shape=shape((4, node_dev + extra, edge), bf16),
         in_specs=[VMEM] * 2,
         out_specs=VMEM,
         compiler_params=PARAMS,
@@ -363,7 +432,23 @@
         input_output_aliases={2: 0},
         compiler_params=PARAMS,
     )(keep_terms, got_terms, spread)
-    spread_all = across_cols(spread)
+    near = pl.pallas_call(
+        gather_kernel,
+        out_shape=shape((4 * node_dev + extra, edge), bf16),
+        in_specs=[VMEM],
+        out_specs=VMEM,
+        compiler_params=PARAMS,
+    )(exchange(spread, both, axis_index_groups=col_near))
+    pre_act, near = lax.optimization_barrier((pre_act, near))
+    far = lax.ppermute(near, both, col_far)
+    activations = pl.pallas_call(
+        activation_kernel,
+        out_shape=shape((node_dev, hidden), bf16),
+        in_specs=[VMEM],
+        out_specs=VMEM,
+        compiler_params=PARAMS,
+    )(pre_act)
+    far, activations = lax.optimization_barrier((far, activations))
     keep, send, grads = pl.pallas_call(
         backward_kernel,
         out_shape=(
@@ -371,30 +456,31 @@
             shape((half, edge), bf16),
             shape((extra, edge), bf16),
         ),
-        in_specs=[SMEM] * 2 + [VMEM] * 2,
+        in_specs=[SMEM] * 2 + [VMEM] * 3,
         out_specs=(VMEM,) * 3,
-        scratch_shapes=[pltpu.VMEM((2 * half, edge), f32)],
+        scratch_shapes=[
+            pltpu.VMEM((col_devices * node_dev, edge), bf16),
+            pltpu.VMEM((2 * half, edge), f32),
+        ],
         compiler_params=PARAMS,
         cost_estimate=tile_cost,
-    )(tile_count, slots, patterns, spread_all)
+    )(tile_count, slots, patterns, near, far)
     got = lax.ppermute(send, "row", swap)
-    pre_act, keep = lax.optimization_barrier((pre_act, keep))
-    activations = pl.pallas_call(
-        activation_kernel,
-        out_shape=shape((node_dev, hidden), bf16),
-        in_specs=[VMEM],
-        out_specs=VMEM,
-        compiler_params=PARAMS,
-    )(pre_act)
-    got, activations = lax.optimization_barrier((got, activations))
+    near_sums, far_sums = pl.pallas_call(
+        split_kernel,
+        out_shape=(shape((half // 2, edge), f32), shape((half // 2 + extra, edge), bf16)),
+        in_specs=[VMEM] * 3,
+        out_specs=(VMEM,) * 2,
+        compiler_params=PARAMS,
+    )(keep, got, grads)
     joined = pl.pallas_call(
         join_kernel,
-        out_shape=shape((chips, node_dev + extra, edge), bf16),
+        out_shape=shape((4, node_dev + extra, edge), bf16),
         in_specs=[VMEM] * 3,
         out_specs=VMEM,
         compiler_params=PARAMS,
-    )(keep, got, grads)
-    back_parts = across_chips(joined)
+    )(near_sums, lax.ppermute(far_sums, "row", row_far), grads)
+    back_parts = exchange(joined, "row", axis_index_groups=row_near)
     scale_factor = 1.0 / math.sqrt(node_dev * row_devices * col_devices)
     mine = pl.pallas_call(
         functools.partial(total_kernel, scale_factor),

time: 117 us -> 118 us (level)
  waiting for transfers between devices: 3.75 us -> 21.2 us
  blocking collectives: 90.4 us -> 74.9 us
    ppermute x0 -> x2, waiting for transfers between devices: none -> 16.5 us  [the longest x1 8.71 us: per_device(): lax.ppermute(far_sums, 'row', row_far)]
    all_to_all x4, blocking collectives: 90.4 us -> 74.9 us  [the longest x1 26.1 us: per_device(): exchange(row_part.reshape(col_devices, node_dev, feature_count), 'col')]
    ppermute x1, starting transfers between devices: 2.31 us -> 1 us  [per_device(): got = lax.ppermute(send, 'row', swap)]
  transfers between devices with their start and end apart: 4 -> 6, of which waited for: 3 -> 6; matrix products, arithmetic and copies ran while one was open for 0% -> 0% of each run, Pallas kernels for 2% -> 2%
where the time goes in v1:
time: 118 us; the launch traced here: 117 us
  blocking collectives  74.9 us (63%)
  waiting for transfers between devices  21.2 us (18%)
  Pallas kernels  10.4 us (9%)
  starting transfers between devices  7.52 us (6%)
  local copies, waits for them, and re-layouts  1.62 us (1%)
  between operations  1.47 us (1%)
    all_to_all x1, blocking collectives, per_device(): exchange(row_part.reshape(col_devices, node_dev, feature_count), 'col')  26.1 us
    all_to_all x1, blocking collectives, per_device(): exchange(scaled, 'row', axis_index_groups=same_core)  20.6 us
    all_to_all x1, blocking collectives, per_device(): exchange(spread, both, axis_index_groups=col_near)  15.5 us
    all_to_all x1, blocking collectives, per_device(): back_parts = exchange(joined, 'row', axis_index_groups=row_near)  12.7 us
    ppermute x1, waiting for transfers between devices, per_device(): lax.ppermute(far_sums, 'row', row_far)  8.71 us
    ppermute x1, waiting for transfers between devices, per_device(): far = lax.ppermute(near, both, col_far)  7.84 us
    pallas_call x1, Pallas kernels, per_device(): pl.pallas_call(forward_kernel, out_shape=shape((col_devices * node_dev, f...  3.27 us
    pallas_call x1, Pallas kernels, per_device(): pl.pallas_call(backward_kernel, out_shape=(shape((half, edge), f32), shap...  2.84 us
  transfers between devices with their start and end apart: 6, of which 6 were waited for; matrix products, arithmetic and copies ran while one was open for 0% of the time, Pallas kernels for 2%

profile of v1, /device:TPU:1, one launch (start us, length us, event | category | flops | bytes accessed | tf_op | source)
XLA Modules:
  0.0 117.2 jit_solution(15222922269172464015)
XLA Ops:
  0.6 0.9 copy-done.2
  1.5 0.7 copy-done.3
  2.2 0.4 shard_map.138
  2.7 20.6 %all_to_all.20 = bf16[8,512,128]{2,1,0:T(8,128)(2,1)S(1)} all-to-all(bf16[8,512,128]{2,1,0:T(8,128)(2,1)S(1)} %shard_map.138), channel_id=1, replica_groups={{0,16,32,48,64,80,96,112},{8,24,40,56,72,88,104,120},{1,17,33,49,65,81,..., dimensions={0} | all-to-all | bytes 2097152 | tf_op jit(solution)/shard_map/all_to_all | solution.py:391
  23.3 1.9 %collective-permute-start = (bf16[4096,128]{1,0:T(8,128)(2,1)S(1)}, bf16[4096,128]{1,0:T(8,128)(2,1)}, u32[]{:S(2)}, u32[]{:S(2)}) collective-permute-start(bf16[4096,128]{1,0:T(8,128)(2,1)S(1)} %bitcast.12), channel_id=1, source_target_pairs={{0,8},{8,0},{16,24},{24,16},{32,40},{40,32},{48,56},{56,48},{64,72... | collective-permute-start | bytes 3145736 | tf_op jit(solution)/shard_map/ppermute | solution.py:392
  25.9 1.7 %collective-permute-done.other_ref = bf16[4096,128]{1,0:T(8,128)(2,1)} collective-permute-done((bf16[4096,128]{1,0:T(8,128)(2,1)S(1)}, bf16[4096,128]{1,0:T(8,128)(2,1)}, u32[]{:S(2)}, u32[]{:S(2)}) %collective-permute-start) | collective-permute-done | bytes 1048608 | tf_op jit(solution)/shard_map/ppermute | solution.py:392
  27.6 3.3 %shard_map.139 = bf16[4096,128]{1,0:T(8,128)(2,1)S(1)} custom-call(s32[1,1]{1,0:T(1,128)} %copy.17.live_ref, s32[512]{0:T(512)S(1)} %fusion.9.slots_ref, bf16[64,128,128]{2,1,0:T(8,128)(2,1)S(1)} %copy-done.6, bf16[4096,128]{1,0:T(8,128)(2,1)S(1)} %bitcast.13, bf16[4096,128]{1,0:T(8,128)(2,1)} %collective-permute-done.other_ref), custom_call_target="tpu_custom_call" | custom-call | flops 2147483648 | bytes 6291456 | tf_op jit(solution)/shard_map/pallas_call | solution.py:393
  30.8 0.0 copy-start
  30.9 0.0 copy-start.1
  30.9 0.0 copy-start.5
  30.9 26.1 %all_to_all.21.parts_ref = bf16[8,512,128]{2,1,0:T(8,128)(2,1)S(1)} all-to-all(bf16[8,512,128]{2,1,0:T(8,128)(2,1)S(1)} %bitcast.14), channel_id=1, replica_groups=mesh['row'=16,'col'=8] {'col'}, dimensions={0} | all-to-all | bytes 2097152 | tf_op jit(solution)/shard_map/all_to_all | solution.py:405
  57.0 0.9 shard_map.140
  57.9 2.6 %collective-permute-start.1 = (bf16[144,128]{1,0:T(8,128)(2,1)S(1)}, bf16[144,128]{1,0:T(8,128)(2,1)S(1)}, u32[]{:S(2)}, u32[]{:S(2)}) collective-permute-start(bf16[144,128]{1,0:T(8,128)(2,1)S(1)} %get-tuple-element.21), channel_id=1, source_target_pairs={{0,8},{8,0},{16,24},{24,16},{32,40},{40,32},{48,56},{56,48},{64,72... | collective-permute-start | bytes 110600 | tf_op jit(solution)/shard_map/ppermute | solution.py:419
  60.5 0.2 shard_map.141.spread_ref
  60.8 0.6 collective-permute-done.1.got_ref
  61.4 15.5 %all_to_all.22.parts_ref = bf16[4,656,128]{2,1,0:T(8,128)(2,1)S(1)} all-to-all(bf16[4,656,128]{2,1,0:T(8,128)(2,1)S(1)} %shard_map.142), channel_id=1, replica_groups={{0,1,2,3},{4,5,6,7},{8,9,14,15},{10,11,12,13},{16,17,18,19},{20,21,22,2..., dimensions={0} | all-to-all | bytes 1343488 | tf_op jit(solution)/shard_map/all_to_all | solution.py:441
  77.0 0.1 shard_map.143.near_ref
  77.0 0.1 collective-permute-start.2
  77.1 0.9 shard_map.144
  78.0 7.8 %collective-permute-done.2.far_ref = bf16[2192,128]{1,0:T(8,128)(2,1)S(1)} collective-permute-done((bf16[2192,128]{1,0:T(8,128)(2,1)S(1)}, bf16[2192,128]{1,0:T(8,128)(2,1)S(1)}, u32[]{:S(2)}, u32[]{:S(2)}) %collective-permute-start.2) | collective-permute-done | bytes 561184 | tf_op jit(solution)/shard_map/ppermute | solution.py:443
  85.8 2.8 %shard_map.145 = (f32[4096,128]{1,0:T(8,128)S(1)}, bf16[4096,128]{1,0:T(8,128)(2,1)S(1)}, bf16[144,128]{1,0:T(8,128)(2,1)S(1)}) custom-call(s32[1,1]{1,0:T(1,128)} %copy.17.live_ref, s32[512]{0:T(512)S(1)} %fusion.9.slots_ref, bf16[64,128,128]{2,1,0:T(8,128)(2,1)S(1)} %copy-done.6, bf16[2192,128]{1,0:T(8,128)(2,1)S(1)} %shard_map.143.near_ref, ...), custom_call_target="tpu_custom_call" | custom-call | flops 2147483648 | bytes 6291456 | tf_op jit(solution)/shard_map/pallas_call | solution.py:452
  88.7 1.0 collective-permute-start.3
  89.7 2.3 %collective-permute-done.3.got_ref = bf16[4096,128]{1,0:T(8,128)(2,1)S(1)} collective-permute-done((bf16[4096,128]{1,0:T(8,128)(2,1)S(1)}, bf16[4096,128]{1,0:T(8,128)(2,1)S(1)}, u32[]{:S(2)}, u32[]{:S(2)}) %collective-permute-start.3) | collective-permute-done | bytes 1048608 | tf_op jit(solution)/shard_map/ppermute | solution.py:468
  91.9 0.2 shard_map.146
  92.2 0.1 collective-permute-start.4
  92.3 8.7 %collective-permute-done.4.got_ref = bf16[2192,128]{1,0:T(8,128)(2,1)S(1)} collective-permute-done((bf16[2192,128]{1,0:T(8,128)(2,1)S(1)}, bf16[2192,128]{1,0:T(8,128)(2,1)S(1)}, u32[]{:S(2)}, u32[]{:S(2)}) %collective-permute-start.4) | collective-permute-done | bytes 561184 | tf_op jit(solution)/shard_map/ppermute | solution.py:482
  101.0 0.1 shard_map.147
  101.1 12.7 %all_to_all.23.parts_ref = bf16[4,656,128]{2,1,0:T(8,128)(2,1)S(1)} all-to-all(bf16[4,656,128]{2,1,0:T(8,128)(2,1)S(1)} %shard_map.147), channel_id=1, replica_groups={{0,64,16,80},{32,96,48,112},{8,72,56,120},{24,88,40,104},{1,65,17,81},{..., dimensions={0} | all-to-all | bytes 1343488 | tf_op jit(solution)/shard_map/all_to_all | solution.py:483
  113.8 1.9 %collective-permute-start.5 = (f32[136,128]{1,0:T(8,128)S(1)}, f32[136,128]{1,0:T(8,128)S(1)}, u32[]{:S(2)}, u32[]{:S(2)}) collective-permute-start(f32[136,128]{1,0:T(8,128)S(1)} %shard_map.149.mine_ref), channel_id=1, source_target_pairs={{0,8},{8,0},{16,24},{24,16},{32,40},{40,32},{48,56},{56,48},{64,72... | collective-permute-start | bytes 208904 | tf_op jit(solution)/shard_map/ppermute | solution.py:492
  115.6 0.8 shard_map.148
  116.4 0.1 collective-permute-done.5.other_ref
  116.6 0.7 shard_map.150
  (21 shorter events, 0.1 us)
Async XLA Ops:
  0.6 0.9 copy-start.2
  1.5 0.7 copy-start.3
  2.2 23.6 %copy-start.7 = (s32[1,1,512]{2,1,0:T(1,128)S(1)}, s32[1,1,512]{2,1,0:T(1,128)}, u32[]{:S(2)}) copy-start(s32[1,1,512]{2,1,0:T(1,128)} %param.19) | copy-start | bytes 6148
  2.2 23.6 %copy-start.8 = (s32[1,1,512]{2,1,0:T(1,128)S(1)}, s32[1,1,512]{2,1,0:T(1,128)}, u32[]{:S(2)}) copy-start(s32[1,1,512]{2,1,0:T(1,128)} %param.20) | copy-start | bytes 6148
  2.2 23.6 %copy-start.9 = (s32[1,1,512]{2,1,0:T(1,128)S(1)}, s32[1,1,512]{2,1,0:T(1,128)}, u32[]{:S(2)}) copy-start(s32[1,1,512]{2,1,0:T(1,128)} %param.17) | copy-start | bytes 6148
  2.2 23.6 %copy-start.10 = (s32[1,1,512]{2,1,0:T(1,128)S(1)}, s32[1,1,512]{2,1,0:T(1,128)}, u32[]{:S(2)}) copy-start(s32[1,1,512]{2,1,0:T(1,128)} %param.18) | copy-start | bytes 6148
  2.2 25.3 %copy-start.6 = (bf16[64,128,128]{2,1,0:T(8,128)(2,1)S(1)}, bf16[64,128,128]{2,1,0:T(8,128)(2,1)}, u32[]{:S(2)}) copy-start(bf16[64,128,128]{2,1,0:T(8,128)(2,1)} %patterns_ref.3) | copy-start | bytes 6291460
  23.3 4.3 %collective-permute-start = (bf16[4096,128]{1,0:T(8,128)(2,1)S(1)}, bf16[4096,128]{1,0:T(8,128)(2,1)}, u32[]{:S(2)}, u32[]{:S(2)}) collective-permute-start(bf16[4096,128]{1,0:T(8,128)(2,1)S(1)} %bitcast.12), channel_id=1, source_target_pairs={{0,8},{8,0},{16,24},{24,16},{32,40},{40,32},{48,56},{56,48},{64,72... | collective-permute-start | bytes 3145736 | tf_op jit(solution)/shard_map/ppermute | solution.py:392
  30.8 26.2 %copy-start = (bf16[512,256]{1,0:T(8,128)(2,1)S(1)}, bf16[512,256]{1,0:T(8,128)(2,1)}, u32[]{:S(2)}) copy-start(bf16[512,256]{1,0:T(8,128)(2,1)} %cotangent_ref.1) | copy-start | bytes 786436
  30.9 26.2 %copy-start.1 = (bf16[128,256]{1,0:T(8,128)(2,1)S(1)}, bf16[128,256]{1,0:T(8,128)(2,1)}, u32[]{:S(2)}) copy-start(bf16[128,256]{1,0:T(8,128)(2,1)} %weight_ref.3) | copy-start | bytes 196612
  30.9 26.2 %copy-start.4 = (s32[512]{0:T(512)S(1)}, s32[512]{0:T(512)}, u32[]{:S(2)}) copy-start(s32[512]{0:T(512)} %param.12) | copy-start | bytes 6148
  30.9 26.2 %copy-start.5 = (f32[256]{0:T(256)S(1)}, f32[256]{0:T(256)}, u32[]{:S(2)}) copy-start(f32[256]{0:T(256)} %param.15) | copy-start | bytes 3076
  57.9 3.5 %collective-permute-start.1 = (bf16[144,128]{1,0:T(8,128)(2,1)S(1)}, bf16[144,128]{1,0:T(8,128)(2,1)S(1)}, u32[]{:S(2)}, u32[]{:S(2)}) collective-permute-start(bf16[144,128]{1,0:T(8,128)(2,1)S(1)} %get-tuple-element.21), channel_id=1, source_target_pairs={{0,8},{8,0},{16,24},{24,16},{32,40},{40,32},{48,56},{56,48},{64,72... | collective-permute-start | bytes 110600 | tf_op jit(solution)/shard_map/ppermute | solution.py:419
  77.0 8.8 %collective-permute-start.2 = (bf16[2192,128]{1,0:T(8,128)(2,1)S(1)}, bf16[2192,128]{1,0:T(8,128)(2,1)S(1)}, u32[]{:S(2)}, u32[]{:S(2)}) collective-permute-start(bf16[2192,128]{1,0:T(8,128)(2,1)S(1)} %shard_map.143.near_ref), channel_id=1, source_target_pairs={{0,6},{1,7},{2,4},{3,5},{4,2},{5,3},{6,0},{7,1},{8,10},{9,11},{10,... | collective-permute-start | bytes 1683464 | tf_op jit(solution)/shard_map/ppermute | solution.py:443
  88.7 3.3 %collective-permute-start.3 = (bf16[4096,128]{1,0:T(8,128)(2,1)S(1)}, bf16[4096,128]{1,0:T(8,128)(2,1)S(1)}, u32[]{:S(2)}, u32[]{:S(2)}) collective-permute-start(bf16[4096,128]{1,0:T(8,128)(2,1)S(1)} %get-tuple-element.28), channel_id=1, source_target_pairs={{0,8},{8,0},{16,24},{24,16},{32,40},{40,32},{48,56},{56,48},{64,72... | collective-permute-start | bytes 3145736 | tf_op jit(solution)/shard_map/ppermute | solution.py:468
  92.2 8.8 %collective-permute-start.4 = (bf16[2192,128]{1,0:T(8,128)(2,1)S(1)}, bf16[2192,128]{1,0:T(8,128)(2,1)S(1)}, u32[]{:S(2)}, u32[]{:S(2)}) collective-permute-start(bf16[2192,128]{1,0:T(8,128)(2,1)S(1)} %get-tuple-element.31), channel_id=1, source_target_pairs={{0,48},{8,24},{16,32},{24,8},{32,16},{40,56},{48,0},{56,40},{64,11... | collective-permute-start | bytes 1683464 | tf_op jit(solution)/shard_map/ppermute | solution.py:482
  113.8 2.8 %collective-permute-start.5 = (f32[136,128]{1,0:T(8,128)S(1)}, f32[136,128]{1,0:T(8,128)S(1)}, u32[]{:S(2)}, u32[]{:S(2)}) collective-permute-start(f32[136,128]{1,0:T(8,128)S(1)} %shard_map.149.mine_ref), channel_id=1, source_target_pairs={{0,8},{8,0},{16,24},{24,16},{32,40},{40,32},{48,56},{56,48},{64,72... | collective-permute-start | bytes 208904 | tf_op jit(solution)/shard_map/ppermute | solution.py:492

commit v2 on v1

--- a/solution.py
+++ b/solution.py
@@ -13,6 +13,9 @@
 ROOT_2_PI = math.sqrt(2.0 / math.pi)
 CUBIC = 0.044715
 BIAS_ROWS = 16
+PER_SHARD = 4
+ORDERED = 640
+BOUNDS = 600
 PAIRS = (((0, 1), (2, 3)), ((0, 3), (1, 2)))
 ANY = pl.BlockSpec(memory_space=pl.ANY)
 VMEM = pl.BlockSpec(memory_space=pltpu.VMEM)
@@ -32,32 +35,101 @@
     return place ^ 3 if core == 0 else place ^ 1
 
 
-def pack_slots(tile_row, tile_col, tile_pattern, tile_weight, live, per_shard, row, col):
+def order_kernel(place_ref, live_ref, row_ref, col_ref, pattern_ref, weight_ref, out_ref):
+    row, col = place_ref[0], place_ref[1]
     core = row % 2
+    per_shard = PER_SHARD
+    rows, edge = row_ref.shape
+    tile_col, tile_row = col_ref[...], row_ref[...]
     shard = tile_col // per_shard
     parity = shard % 2
     chip = shard // 2
-    tile = tile_col % per_shard
-    half = parity ^ core
-    forward = (half * 8 + chip) * per_shard + tile
     ring = chip % 4
-    far = (pair_of(ring, parity) != pair_of((row // 2) % 4, parity)).astype(jnp.int32)
+    column_far = (pair_of(ring, parity) != pair_of((row // 2) % 4, parity)).astype(jnp.int32)
     rank = pair_index(ring, parity) * 2 + chip // 4
-    target = ((half * 2 + far) * 4 + rank) * per_shard + tile
+    column = (((parity ^ core) * 2 + column_far) * 4 + rank) * per_shard + tile_col % per_shard
     peer = tile_row // per_shard
-    far = (pair_of(peer // 2, core) != pair_of(col // 2, core)).astype(jnp.int32)
+    row_far = (pair_of(peer // 2, core) != pair_of(col // 2, core)).astype(jnp.int32)
     rank = pair_index(peer // 2, core) * 2 + peer % 2
-    source = (far * 4 + rank) * per_shard + tile_row % per_shard
-    slots = tile_col.shape[0]
-    factor = jnp.where(jnp.arange(slots, dtype=jnp.int32) < live, tile_weight, 0)
-    return (
-        forward
-        | (tile_row << 6)
-        | (tile_pattern << 11)
-        | (factor << 17)
-        | (target << 20)
-        | (source << 26)
-    )
+    source = (row_far * 4 + rank) * per_shard + tile_row % per_shard
+    word = tile_row | (pattern_ref[...] << 5) | (weight_ref[...] << 11) | (column << 14) | (source << 20)
+    slot = lax.broadcasted_iota(jnp.int32, (rows, edge), 0) * edge
+    slot += lax.broadcasted_iota(jnp.int32, (rows, edge), 1)
+    alive = slot < live_ref[0, 0]
+    word = jnp.where(alive, word, 0)
+    kind = jnp.where(alive, column_far * 2 + row_far, 4)
+
+    flags = [(kind == index).astype(jnp.float32) for index in range(5)]
+    stacked = jnp.concatenate(flags + [jnp.zeros((4, edge), jnp.float32)], 0)
+    before = lax.broadcasted_iota(jnp.int32, (edge, edge), 0) < lax.broadcasted_iota(
+        jnp.int32, (edge, edge), 1
+    )
+    earlier = jnp.dot(
+        stacked.astype(jnp.bfloat16),
+        before.astype(jnp.float32).astype(jnp.bfloat16),
+        preferred_element_type=jnp.float32,
+    )
+    counts = jnp.sum(stacked, axis=1, keepdims=True)
+    start = jnp.zeros((1, 1), jnp.float32)
+    ends = []
+    position = [jnp.zeros((1, edge), jnp.float32) for _ in range(rows)]
+    for index in range(5):
+        for line in range(rows):
+            at = index * rows + line
+            position[line] += flags[index][line : line + 1] * (start + earlier[at : at + 1])
+            start = start + counts[at : at + 1]
+        ends.append(start)
+    turned = jnp.concatenate(position + [jnp.zeros((8 - rows, edge), jnp.float32)], 0).T
+    slots = rows * edge
+    lanes = lax.broadcasted_iota(jnp.int32, (edge, slots), 1).astype(jnp.float32)
+    pieces = jnp.zeros((8, slots), jnp.float32)
+    for line in range(rows):
+        chosen = (turned[:, line : line + 1] == lanes).astype(jnp.float32).astype(jnp.bfloat16)
+        parts = [(word[line : line + 1] >> shift) & 127 for shift in (0, 7, 14, 21)]
+        parts = jnp.concatenate(parts + [jnp.zeros((4, edge), jnp.int32)], 0)
+        parts = parts.astype(jnp.float32).astype(jnp.bfloat16)
+        pieces += jnp.dot(parts, chosen, preferred_element_type=jnp.float32)
+    pieces = pieces.astype(jnp.int32)
+    out_ref[:, :slots] = (
+        pieces[0:1] | (pieces[1:2] << 7) | (pieces[2:3] << 14) | (pieces[3:4] << 21)
+    )
+    lane = lax.broadcasted_iota(jnp.int32, (1, out_ref.shape[1] - slots), 1) + slots
+    tail = jnp.zeros(lane.shape, jnp.int32)
+    for index in range(4):
+        tail = jnp.where(lane == BOUNDS + index, ends[index].astype(jnp.int32), tail)
+    out_ref[:, slots:] = tail
+
+
+def add_products(slots_ref, runs, product_of, place_of, sums):
+    edge = sums.shape[1]
+    (first, end), (first_b, end_b) = runs
+    turns = (end - first + GROUP - 1) // GROUP
+    turns_b = (end_b - first_b + GROUP - 1) // GROUP
+
+    def one_group(turn, carry):
+        is_a = turn < turns
+        start = jnp.where(is_a, first + turn * GROUP, first_b + (turn - turns) * GROUP)
+        stop = jnp.where(is_a, end, end_b)
+        terms = []
+        for member in range(GROUP):
+            slot = start + member
+            word = slots_ref[0, slot]
+            factor = jnp.where(slot < stop, (word >> 11) & 7, 0).astype(jnp.float32)
+            terms.append((place_of(word), factor, product_of(word)))
+        for place, factor, product in terms:
+            rows = pl.ds(pl.multiple_of(place * edge, edge), edge)
+            sums[rows, :] += factor * product
+        return carry
+
+    lax.fori_loop(0, turns + turns_b, one_group, 0)
+
+
+def tile_of(ref, place, edge):
+    return ref[pl.ds(pl.multiple_of(place * edge, edge), edge), :]
+
+
+def class_bounds(slots_ref):
+    return [0] + [slots_ref[0, BOUNDS + index] for index in range(4)]
 
 
 def root_columns(degree):
@@ -85,65 +157,63 @@
             out_ref[copy, rows, :] = scaled
 
 
-def forward_kernel(live_ref, slots_ref, patterns_ref, own_ref, other_ref, out_ref, panel, sums):
+def forward_sums(slots_ref, patterns_ref, own_ref, other_ref, panel, sums, far):
     edge = patterns_ref.shape[1]
     half = own_ref.shape[0]
     panel[:half, :] = own_ref[...]
     panel[half:, :] = other_ref[...]
-    sums[...] = jnp.zeros_like(sums)
-
-    def one_group(group, carry):
-        terms = []
-        for member in range(GROUP):
-            word = slots_ref[group * GROUP + member]
-            place, row, pattern = word & 63, (word >> 6) & 31, (word >> 11) & 63
-            factor = ((word >> 17) & 7).astype(jnp.float32)
-            block = panel[pl.ds(pl.multiple_of(place * edge, edge), edge), :]
-            product = jnp.dot(patterns_ref[pattern], block, preferred_element_type=jnp.float32)
-            terms.append((row, factor, product))
-        for row, factor, product in terms:
-            rows = pl.ds(pl.multiple_of(row * edge, edge), edge)
-            sums[rows, :] += factor * product
-        return carry
-
-    lax.fori_loop(0, (live_ref[0, 0] + GROUP - 1) // GROUP, one_group, 0)
+    bounds = class_bounds(slots_ref)
+
+    def product_of(word):
+        place = ((word >> 15) & 16) | ((word >> 14) & 15)
+        return jnp.dot(
+            patterns_ref[(word >> 5) & 63],
+            tile_of(panel, place, edge),
+            preferred_element_type=jnp.float32,
+        )
+
+    run = (bounds[2], bounds[4]) if far else (bounds[0], bounds[2])
+    add_products(slots_ref, (run, (0, 0)), product_of, lambda word: word & 31, sums)
+
+
+def forward_near_kernel(slots_ref, patterns_ref, own_ref, other_ref, out_ref, panel):
+    out_ref[...] = jnp.zeros_like(out_ref)
+    forward_sums(slots_ref, patterns_ref, own_ref, other_ref, panel, out_ref, False)
+
+
+def forward_far_kernel(slots_ref, patterns_ref, own_ref, other_ref, so_far_ref, out_ref, panel, sums):
+    sums[...] = so_far_ref[...]
+    forward_sums(slots_ref, patterns_ref, own_ref, other_ref, panel, sums, True)
     out_ref[...] = sums[...].astype(jnp.bfloat16)
 
 
-def backward_kernel(
-    live_ref,
-    slots_ref,
-    patterns_ref,
-    near_ref,
-    far_ref,
-    keep_ref,
-    send_ref,
-    grads_ref,
-    panel,
-    sums,
+def backward_sums(slots_ref, patterns_ref, panel_ref, sums, far):
+    edge = patterns_ref.shape[1]
+    bounds = class_bounds(slots_ref)
+
+    def product_of(word):
+        return jnp.dot(
+            tile_of(panel_ref, (word >> 20) & 15, edge),
+            patterns_ref[(word >> 5) & 63],
+            preferred_element_type=jnp.float32,
+        )
+
+    runs = [(bounds[index], bounds[index + 1]) for index in ((1, 3) if far else (0, 2))]
+    add_products(slots_ref, runs, product_of, lambda word: (word >> 14) & 63, sums)
+
+
+def backward_near_kernel(slots_ref, patterns_ref, near_ref, out_ref):
+    out_ref[...] = jnp.zeros_like(out_ref)
+    backward_sums(slots_ref, patterns_ref, near_ref, out_ref, False)
+
+
+def backward_far_kernel(
+    slots_ref, patterns_ref, near_ref, far_ref, so_far_ref, keep_ref, send_ref, grads_ref, sums
 ):
-    edge = patterns_ref.shape[1]
     half = keep_ref.shape[0]
-    part = panel.shape[0] // 2
-    panel[:part, :] = near_ref[:part, :]
-    panel[part:, :] = far_ref[:part, :]
-    sums[...] = jnp.zeros_like(sums)
-
-    def one_group(group, carry):
-        terms = []
-        for member in range(GROUP):
-            word = slots_ref[group * GROUP + member]
-            pattern, target, source = (word >> 11) & 63, (word >> 20) & 63, (word >> 26) & 31
-            factor = ((word >> 17) & 7).astype(jnp.float32)
-            block = panel[pl.ds(pl.multiple_of(source * edge, edge), edge), :]
-            product = jnp.dot(block, patterns_ref[pattern], preferred_element_type=jnp.float32)
-            terms.append((target, factor, product))
-        for target, factor, product in terms:
-            rows = pl.ds(pl.multiple_of(target * edge, edge), edge)
-            sums[rows, :] += factor * product
-        return carry
-
-    lax.fori_loop(0, (live_ref[0, 0] + GROUP - 1) // GROUP, one_group, 0)
+    part = near_ref.shape[0] - grads_ref.shape[0]
+    sums[...] = so_far_ref[...]
+    backward_sums(slots_ref, patterns_ref, far_ref, sums, True)
     keep_ref[...] = sums[:half, :]
     send_ref[...] = sums[half:, :].astype(jnp.bfloat16)
     grads = near_ref[part:, :].astype(jnp.float32) + far_ref[part:, :].astype(jnp.float32)
@@ -194,9 +264,9 @@
         square, bent, half = activate(pre_act)
         rise = 0.5 * pre_act * (1.0 - bent * bent) * (ROOT_2_PI * (1.0 + 3.0 * CUBIC * square))
         slope = cotangent_ref[rows, :].astype(jnp.float32) * (half + rise)
-        upstream = (inv_root * slope).astype(jnp.bfloat16)
+        upstream = inv_root * slope
         upstream_ref[rows, :] = upstream
-        grads += split_product(sums, upstream, ((0,), (0,)))
+        grads += split_product(sums, upstream.astype(jnp.bfloat16), ((0,), (0,)))
         bias_row += jnp.sum(slope, axis=0, keepdims=True)
     width = keep_ref.shape[1]
     bias_high = bias_row.astype(jnp.bfloat16).astype(jnp.float32)
@@ -224,11 +294,14 @@
     edge = out_ref.shape[2]
     for tile in range(upstream_ref.shape[0] // edge):
         rows = pl.ds(tile * edge, edge)
-        spread = lax.dot_general(
-            weight_ref[...],
-            upstream_ref[rows, :],
-            (((1,), (1,)), ((), ())),
-            preferred_element_type=jnp.float32,
+        upstream = upstream_ref[rows, :]
+        high = upstream.astype(jnp.bfloat16)
+        low = (upstream - high.astype(jnp.float32)).astype(jnp.bfloat16)
+        spread = sum(
+            lax.dot_general(
+                weight_ref[...], part, (((1,), (1,)), ((), ())), preferred_element_type=jnp.float32
+            )
+            for part in (high, low)
         ).astype(jnp.bfloat16)
         for shard in range(out_ref.shape[0]):
             out_ref[shard, rows, :] = spread
@@ -329,7 +402,6 @@
     per_shard = node_dev // edge
     row, col = lax.axis_index("row"), lax.axis_index("col")
     core = row % 2
-    same_core = [list(range(first, row_devices, 2)) for first in range(2)]
     swap = [(index, index ^ 1) for index in range(row_devices)]
     row_near = [
         [(low * 4 + ring) * 2 + core_index for ring in pair for low in range(2)]
@@ -360,25 +432,15 @@
     bf16, f32 = jnp.bfloat16, jnp.float32
     shape = jax.ShapeDtypeStruct
     degree_tiles = degree.reshape(per_shard, edge)
-    slots = pack_slots(
-        tile_row[0, 0],
-        tile_col[0, 0],
-        tile_pattern[0, 0],
-        tile_weight[0, 0],
-        tile_count[0, 0],
-        per_shard,
-        row,
-        col,
-    )
     tile_cost = pl.CostEstimate(
-        flops=2 * slots.shape[0] * edge * edge * feature_count,
+        flops=tile_row.size // (row_devices * col_devices) * edge * edge * feature_count,
         bytes_accessed=patterns.size * 2 + 4 * half * feature_count * 2,
         transcendentals=0,
     )
 
     scaled = pl.pallas_call(
         scale_kernel,
-        out_shape=shape((chips, node_dev, feature_count), bf16),
+        out_shape=shape((4, node_dev, feature_count), bf16),
         in_specs=[ANY] * 2,
         out_specs=VMEM,
         scratch_shapes=[
@@ -388,27 +450,54 @@
         ],
         compiler_params=PARAMS,
     )(features, degree_tiles)
-    own_panel = exchange(scaled, "row", axis_index_groups=same_core).reshape(half, feature_count)
-    other_panel = lax.ppermute(own_panel, "row", swap)
+    near_own = exchange(scaled, "row", axis_index_groups=row_near).reshape(half // 2, feature_count)
+    near_other = lax.ppermute(near_own, "row", swap)
+    far_own = lax.ppermute(near_own, "row", row_far)
+    row_tiles, near_own = lax.optimization_barrier((tile_row.reshape(per_shard, edge), near_own))
+    place = jnp.stack([row, col]).astype(jnp.int32)
+    slots = pl.pallas_call(
+        order_kernel,
+        out_shape=shape((1, ORDERED), jnp.int32),
+        in_specs=[SMEM] * 2 + [VMEM] * 4,
+        out_specs=VMEM,
+        compiler_params=PARAMS,
+    )(
+        place,
+        tile_count,
+        row_tiles,
+        tile_col.reshape(per_shard, edge),
+        tile_pattern.reshape(per_shard, edge),
+        tile_weight.reshape(per_shard, edge),
+    )
+    forward_panel = pltpu.VMEM((half, feature_count), bf16)
+    row_sums = shape((col_devices * node_dev, feature_count), f32)
+    near_sums = pl.pallas_call(
+        forward_near_kernel,
+        out_shape=row_sums,
+        in_specs=[SMEM] + [VMEM] * 3,
+        out_specs=VMEM,
+        scratch_shapes=[forward_panel],
+        compiler_params=PARAMS,
+        cost_estimate=tile_cost,
+    )(slots, patterns, near_own, near_other)
+    far_own, near_sums = lax.optimization_barrier((far_own, near_sums))
+    far_other = lax.ppermute(far_own, "row", swap)
     row_part = pl.pallas_call(
-        forward_kernel,
-        out_shape=shape((col_devices * node_dev, feature_count), bf16),
-        in_specs=[SMEM] * 2 + [VMEM] * 3,
-        out_specs=VMEM,
-        scratch_shapes=[
-            pltpu.VMEM((2 * half, feature_count), bf16),
-            pltpu.VMEM((col_devices * node_dev, feature_count), f32),
-        ],
+        forward_far_kernel,
+        out_shape=shape(row_sums.shape, bf16),
+        in_specs=[SMEM] + [VMEM] * 4,
+        out_specs=VMEM,
+        scratch_shapes=[forward_panel, pltpu.VMEM(row_sums.shape, f32)],
         compiler_params=PARAMS,
         cost_estimate=tile_cost,
-    )(tile_count, slots, patterns, own_panel, other_panel)
+    )(slots, patterns, far_own, far_other, near_sums)
     parts = exchange(row_part.reshape(col_devices, node_dev, feature_count), "col")
     core_word = core.astype(jnp.int32).reshape(1)
     pre_act, upstream, keep_terms, send_terms = pl.pallas_call(
         middle_kernel,
         out_shape=(
             shape((node_dev, hidden), f32),
-            shape((node_dev, hidden), bf16),
+            shape((node_dev, hidden), f32),
             shape((extra, edge), f32),
             shape((extra, edge), bf16),
         ),
@@ -448,23 +537,29 @@
         out_specs=VMEM,
         compiler_params=PARAMS,
     )(pre_act)
-    far, activations = lax.optimization_barrier((far, activations))
+    back_sums = shape((2 * half, edge), f32)
+    back_near = pl.pallas_call(
+        backward_near_kernel,
+        out_shape=back_sums,
+        in_specs=[SMEM] + [VMEM] * 2,
+        out_specs=VMEM,
+        compiler_params=PARAMS,
+        cost_estimate=tile_cost,
+    )(slots, patterns, near)
+    far, activations, back_near = lax.optimization_barrier((far, activations, back_near))
     keep, send, grads = pl.pallas_call(
-        backward_kernel,
+        backward_far_kernel,
         out_shape=(
             shape((half, edge), f32),
             shape((half, edge), bf16),
             shape((extra, edge), bf16),
         ),
-        in_specs=[SMEM] * 2 + [VMEM] * 3,
+        in_specs=[SMEM] + [VMEM] * 4,
         out_specs=(VMEM,) * 3,
-        scratch_shapes=[
-            pltpu.VMEM((col_devices * node_dev, edge), bf16),
-            pltpu.VMEM((2 * half, edge), f32),
-        ],
+        scratch_shapes=[pltpu.VMEM(back_sums.shape, f32)],
         compiler_params=PARAMS,
         cost_estimate=tile_cost,
-    )(tile_count, slots, patterns, near, far)
+    )(slots, patterns, near, far, back_near)
     got = lax.ppermute(send, "row", swap)
     near_sums, far_sums = pl.pallas_call(
         split_kernel,

time: 118 us -> 119 us (level)
  blocking collectives: 74.9 us -> 40.3 us
  waiting for transfers between devices: 21.2 us -> 33.9 us
  starting transfers between devices: 7.52 us -> 18.4 us
  Pallas kernels: 10.4 us -> 17.1 us
  local copies, waits for them, and re-layouts: 1.62 us -> 5.91 us
    all_to_all x2 -> x1, blocking collectives: 46.7 us -> 13.8 us  [per_device(): exchange(scaled, 'row', axis_index_groups=row_near)]
    all_to_all x0 -> x1, waiting for transfers between devices: none -> 15.4 us  [per_device(): exchange(row_part.reshape(col_devices, node_dev, feature_count), 'col')]
    all_to_all x0 -> x1, starting transfers between devices: none -> 9.1 us  [per_device(): exchange(row_part.reshape(col_devices, node_dev, feature_count), 'col')]
    pallas_call x3 -> x6, Pallas kernels: 6.55 us -> 13.2 us  [the longest x1 3.64 us: per_device(): pl.pallas_call(forward_far_kernel, out_shape=shape(row_sums.shape, bf16),...]
    unnamed x22 -> x24, local copies, waits for them, and re-layouts: 1.62 us -> 5.91 us
    ppermute x1, waiting for transfers between devices: 7.84 us -> 5.25 us  [per_device(): far = lax.ppermute(near, both, col_far)]
    all_to_all x1, blocking collectives: 12.7 us -> 10.9 us  [per_device(): back_parts = exchange(joined, 'row', axis_index_groups=row_near)]
    ppermute x1 -> x3, starting transfers between devices: 1.87 us -> 2.51 us  [the longest x1 1.97 us: per_device(): far_other = lax.ppermute(far_own, 'row', swap)]
  transfers between devices with their start and end apart: 6 -> 9, of which waited for: 6 -> 7; matrix products, arithmetic and copies ran while one was open for 0% -> 0% of each run, Pallas kernels for 2% -> 7%
where the time goes in v2:
time: 119 us; the launch traced here: 117 us
  blocking collectives  40.3 us (34%)
  waiting for transfers between devices  33.9 us (28%)
  starting transfers between devices  18.4 us (15%)
  Pallas kernels  17.1 us (14%)
  local copies, waits for them, and re-layouts  5.91 us (5%)
  between operations  1.43 us (1%)
    all_to_all x1, blocking collectives, per_device(): exchange(spread, both, axis_index_groups=col_near)  15.6 us
    all_to_all x1, waiting for transfers between devices, per_device(): exchange(row_part.reshape(col_devices, node_dev, feature_count), 'col')  15.4 us
    all_to_all x1, blocking collectives, per_device(): exchange(scaled, 'row', axis_index_groups=row_near)  13.8 us
    all_to_all x1, blocking collectives, per_device(): back_parts = exchange(joined, 'row', axis_index_groups=row_near)  10.9 us
    all_to_all x1, starting transfers between devices, per_device(): exchange(row_part.reshape(col_devices, node_dev, feature_count), 'col')  9.1 us
    ppermute x1, waiting for transfers between devices, per_device(): lax.ppermute(far_sums, 'row', row_far)  8.71 us
    unnamed x24, local copies, waits for them, and re-layouts  5.91 us
    ppermute x1, waiting for transfers between devices, per_device(): far = lax.ppermute(near, both, col_far)  5.25 us
  transfers between devices with their start and end apart: 9, of which 7 were waited for; matrix products, arithmetic and copies ran while one was open for 0% of the time, Pallas kernels for 7%

profile of v2, /device:TPU:1, one launch (start us, length us, event | category | flops | bytes accessed | tf_op | source)
XLA Modules:
  0.0 117.1 jit_solution(15943163032982925796)
XLA Ops:
  0.6 0.9 copy-done.4
  1.5 0.7 copy-done.5
  2.2 0.4 shard_map.138
  2.6 13.8 %all_to_all.20 = bf16[4,512,128]{2,1,0:T(8,128)(2,1)S(1)} all-to-all(bf16[4,512,128]{2,1,0:T(8,128)(2,1)S(1)} %shard_map.138), channel_id=1, replica_groups={{0,64,16,80},{32,96,48,112},{8,72,56,120},{24,88,40,104},{1,65,17,81},{..., dimensions={0} | all-to-all | bytes 1048576 | tf_op jit(solution)/shard_map/all_to_all | solution.py:453
  16.4 0.5 collective-permute-start.1
  17.7 0.7 copy-done.7
  18.4 0.7 copy-done.8
  19.1 0.7 copy-done.9
  19.7 0.7 copy-done.10
  20.4 1.1 shard_map.139.slots_ref
  21.6 1.6 %copy-done = bf16[64,128,128]{2,1,0:T(8,128)(2,1)S(1)} copy-done((bf16[64,128,128]{2,1,0:T(8,128)(2,1)S(1)}, bf16[64,128,128]{2,1,0:T(8,128)(2,1)}, u32[]{:S(2)}) %copy-start) | copy-done | bytes 2097176
  23.1 2.5 %shard_map.140.so_far_ref = f32[4096,128]{1,0:T(8,128)S(1)} custom-call(s32[1,640]{1,0:T(1,128)S(1)} %shard_map.139.slots_ref, bf16[64,128,128]{2,1,0:T(8,128)(2,1)S(1)} %copy-done, bf16[2048,128]{1,0:T(8,128)(2,1)S(1)} %bitcast.14, bf16[2048,128]{1,0:T(8,128)(2,1)S(1)} %collective-permute-done.1.other_ref), custom_call_target="tpu_custom_call" | custom-call | flops 8388608 | bytes 6291456 | tf_op jit(solution)/shard_map/pallas_call | solution.py:474
  25.7 2.0 %collective-permute-start.2 = (bf16[2048,128]{1,0:T(8,128)(2,1)S(1)}, bf16[2048,128]{1,0:T(8,128)(2,1)S(1)}, u32[]{:S(2)}, u32[]{:S(2)}) collective-permute-start(bf16[2048,128]{1,0:T(8,128)(2,1)S(1)} %collective-permute-done.own_ref), channel_id=1, source_target_pairs={{0,8},{8,0},{16,24},{24,16},{32,40},{40,32},{48,56},{56,48},{64,72... | collective-permute-start | bytes 1572872 | tf_op jit(solution)/shard_map/ppermute | solution.py:484
  27.7 1.5 %collective-permute-done.2.other_ref = bf16[2048,128]{1,0:T(8,128)(2,1)S(1)} collective-permute-done((bf16[2048,128]{1,0:T(8,128)(2,1)S(1)}, bf16[2048,128]{1,0:T(8,128)(2,1)S(1)}, u32[]{:S(2)}, u32[]{:S(2)}) %collective-permute-start.2) | collective-permute-done | bytes 524320 | tf_op jit(solution)/shard_map/ppermute | solution.py:484
  29.2 3.6 %shard_map.141 = bf16[4096,128]{1,0:T(8,128)(2,1)} custom-call(s32[1,640]{1,0:T(1,128)S(1)} %shard_map.139.slots_ref, bf16[64,128,128]{2,1,0:T(8,128)(2,1)S(1)} %copy-done, bf16[2048,128]{1,0:T(8,128)(2,1)S(1)} %collective-permute-done.own_ref, bf16[2048,128]{1,0:T(8,128)(2,1)S(1)} %collective-permute-done.2.other_ref, f32[4096,128]{1,0:T(8,128)S(1)} %shard_map.140.so_far_ref), custom_call_target="tpu_custom_call" | custom-call | flops 8388608 | bytes 6291456 | tf_op jit(solution)/shard_map/pallas_call | solution.py:485
  32.8 9.1 %all-to-all-start.1 = ((bf16[8,512,128]{2,1,0:T(8,128)(2,1)}), bf16[8,512,128]{2,1,0:T(8,128)(2,1)S(1)}, u32[]{:S(2)}, u32[]{:S(2)}) async-start(bf16[8,512,128]{2,1,0:T(8,128)(2,1)} %bitcast.9), calls=%async_computation.1 | async-start | bytes 2097152 | tf_op jit(solution)/shard_map/all_to_all | solution.py:494
  42.0 15.4 %all-to-all-done.1.parts_ref = bf16[8,512,128]{2,1,0:T(8,128)(2,1)S(1)} async-done(((bf16[8,512,128]{2,1,0:T(8,128)(2,1)}), bf16[8,512,128]{2,1,0:T(8,128)(2,1)S(1)}, u32[]{:S(2)}, u32[]{:S(2)}) %all-to-all-start.1) | async-done | bytes 1048608 | tf_op jit(solution)/shard_map/all_to_all | solution.py:494
  57.4 0.9 shard_map.142
  58.3 2.8 %collective-permute-start.3 = (bf16[144,128]{1,0:T(8,128)(2,1)S(1)}, bf16[144,128]{1,0:T(8,128)(2,1)S(1)}, u32[]{:S(2)}, u32[]{:S(2)}) collective-permute-start(bf16[144,128]{1,0:T(8,128)(2,1)S(1)} %get-tuple-element.30), channel_id=1, source_target_pairs={{0,8},{8,0},{16,24},{24,16},{32,40},{40,32},{48,56},{56,48},{64,72... | collective-permute-start | bytes 110600 | tf_op jit(solution)/shard_map/ppermute | solution.py:508
  61.4 0.6 collective-permute-done.3.got_ref
  62.0 15.6 %all_to_all.21.parts_ref = bf16[4,656,128]{2,1,0:T(8,128)(2,1)S(1)} all-to-all(bf16[4,656,128]{2,1,0:T(8,128)(2,1)S(1)} %shard_map.144), channel_id=1, replica_groups={{0,1,2,3},{4,5,6,7},{8,9,14,15},{10,11,12,13},{16,17,18,19},{20,21,22,2..., dimensions={0} | all-to-all | bytes 1343488 | tf_op jit(solution)/shard_map/all_to_all | solution.py:530
  77.8 0.9 shard_map.146
  78.6 2.6 %shard_map.147.so_far_ref = f32[8192,128]{1,0:T(8,128)S(1)} custom-call(s32[1,640]{1,0:T(1,128)S(1)} %shard_map.139.slots_ref, bf16[64,128,128]{2,1,0:T(8,128)(2,1)S(1)} %copy-done.1, bf16[2192,128]{1,0:T(8,128)(2,1)S(1)} %shard_map.145.near_ref), custom_call_target="tpu_custom_call" | custom-call | flops 8388608 | bytes 6291456 | tf_op jit(solution)/shard_map/pallas_call | solution.py:541
  81.2 5.3 %collective-permute-done.4.far_ref = bf16[2192,128]{1,0:T(8,128)(2,1)S(1)} collective-permute-done((bf16[2192,128]{1,0:T(8,128)(2,1)S(1)}, bf16[2192,128]{1,0:T(8,128)(2,1)S(1)}, u32[]{:S(2)}, u32[]{:S(2)}) %collective-permute-start.4) | collective-permute-done | bytes 561184 | tf_op jit(solution)/shard_map/ppermute | solution.py:532
  86.5 2.9 %shard_map.148 = (f32[4096,128]{1,0:T(8,128)S(1)}, bf16[4096,128]{1,0:T(8,128)(2,1)S(1)}, bf16[144,128]{1,0:T(8,128)(2,1)S(1)}) custom-call(s32[1,640]{1,0:T(1,128)S(1)} %shard_map.139.slots_ref, bf16[64,128,128]{2,1,0:T(8,128)(2,1)S(1)} %copy-done.1, bf16[2192,128]{1,0:T(8,128)(2,1)S(1)} %shard_map.145.near_ref, ...), custom_call_target="tpu_custom_call" | custom-call | flops 8388608 | bytes 6291456 | tf_op jit(solution)/shard_map/pallas_call | solution.py:550
  89.4 1.0 collective-permute-start.5
  90.4 2.3 %collective-permute-done.5.got_ref = bf16[4096,128]{1,0:T(8,128)(2,1)S(1)} collective-permute-done((bf16[4096,128]{1,0:T(8,128)(2,1)S(1)}, bf16[4096,128]{1,0:T(8,128)(2,1)S(1)}, u32[]{:S(2)}, u32[]{:S(2)}) %collective-permute-start.5) | collective-permute-done | bytes 1048608 | tf_op jit(solution)/shard_map/ppermute | solution.py:563
  93.0 8.7 %collective-permute-done.6.got_ref = bf16[2192,128]{1,0:T(8,128)(2,1)S(1)} collective-permute-done((bf16[2192,128]{1,0:T(8,128)(2,1)S(1)}, bf16[2192,128]{1,0:T(8,128)(2,1)S(1)}, u32[]{:S(2)}, u32[]{:S(2)}) %collective-permute-start.6) | collective-permute-done | bytes 561184 | tf_op jit(solution)/shard_map/ppermute | solution.py:577
  101.8 10.9 %all_to_all.22.parts_ref = bf16[4,656,128]{2,1,0:T(8,128)(2,1)S(1)} all-to-all(bf16[4,656,128]{2,1,0:T(8,128)(2,1)S(1)} %shard_map.150), channel_id=1, replica_groups={{0,64,16,80},{32,96,48,112},{8,72,56,120},{24,88,40,104},{1,65,17,81},{..., dimensions={0} | all-to-all | bytes 1343488 | tf_op jit(solution)/shard_map/all_to_all | solution.py:578
  112.7 2.8 %collective-permute-start.7 = (f32[136,128]{1,0:T(8,128)S(1)}, f32[136,128]{1,0:T(8,128)S(1)}, u32[]{:S(2)}, u32[]{:S(2)}) collective-permute-start(f32[136,128]{1,0:T(8,128)S(1)} %shard_map.152.mine_ref), channel_id=1, source_target_pairs={{0,8},{8,0},{16,24},{24,16},{32,40},{40,32},{48,56},{56,48},{64,72... | collective-permute-start | bytes 208904 | tf_op jit(solution)/shard_map/ppermute | solution.py:587
  115.6 0.8 shard_map.151
  116.5 0.7 shard_map.153
  (30 shorter events, 1.2 us)
Async XLA Ops:
  0.6 0.9 copy-start.4
  1.5 0.7 copy-start.5
  16.4 5.1 %collective-permute-start.1 = (bf16[2048,128]{1,0:T(8,128)(2,1)S(1)}, bf16[2048,128]{1,0:T(8,128)(2,1)S(1)}, u32[]{:S(2)}, u32[]{:S(2)}) collective-permute-start(bf16[2048,128]{1,0:T(8,128)(2,1)S(1)} %bitcast.12), channel_id=1, source_target_pairs={{0,8},{8,0},{16,24},{24,16},{32,40},{40,32},{48,56},{56,48},{64,72... | collective-permute-start | bytes 1572872 | tf_op jit(solution)/shard_map/ppermute | solution.py:454
  17.0 8.7 %collective-permute-start = (bf16[2048,128]{1,0:T(8,128)(2,1)S(1)}, bf16[2048,128]{1,0:T(8,128)(2,1)S(1)}, u32[]{:S(2)}, u32[]{:S(2)}) collective-permute-start(bf16[2048,128]{1,0:T(8,128)(2,1)S(1)} %bitcast.13), channel_id=1, source_target_pairs={{0,48},{8,24},{16,32},{24,8},{32,16},{40,56},{48,0},{56,40},{64,11... | collective-permute-start | bytes 1572872 | tf_op jit(solution)/shard_map/ppermute | solution.py:455
  17.7 0.7 copy-start.7
  18.4 0.7 copy-start.8
  19.1 0.7 copy-start.9
  19.7 0.7 copy-start.10
  21.5 1.6 %copy-start = (bf16[64,128,128]{2,1,0:T(8,128)(2,1)S(1)}, bf16[64,128,128]{2,1,0:T(8,128)(2,1)}, u32[]{:S(2)}) copy-start(bf16[64,128,128]{2,1,0:T(8,128)(2,1)} %patterns_ref.7) | copy-start | bytes 6291460
  25.7 3.5 %collective-permute-start.2 = (bf16[2048,128]{1,0:T(8,128)(2,1)S(1)}, bf16[2048,128]{1,0:T(8,128)(2,1)S(1)}, u32[]{:S(2)}, u32[]{:S(2)}) collective-permute-start(bf16[2048,128]{1,0:T(8,128)(2,1)S(1)} %collective-permute-done.own_ref), channel_id=1, source_target_pairs={{0,8},{8,0},{16,24},{24,16},{32,40},{40,32},{48,56},{56,48},{64,72... | collective-permute-start | bytes 1572872 | tf_op jit(solution)/shard_map/ppermute | solution.py:484
  32.8 24.5 %copy-start.2 = (bf16[128,256]{1,0:T(8,128)(2,1)S(1)}, bf16[128,256]{1,0:T(8,128)(2,1)}, u32[]{:S(2)}) copy-start(bf16[128,256]{1,0:T(8,128)(2,1)} %weight_ref.3) | copy-start | bytes 196612
  32.8 24.5 %copy-start.3 = (bf16[512,256]{1,0:T(8,128)(2,1)S(1)}, bf16[512,256]{1,0:T(8,128)(2,1)}, u32[]{:S(2)}) copy-start(bf16[512,256]{1,0:T(8,128)(2,1)} %cotangent_ref.1) | copy-start | bytes 786436
  32.8 24.5 %copy-start.6 = (s32[512]{0:T(512)S(1)}, s32[512]{0:T(512)}, u32[]{:S(2)}) copy-start(s32[512]{0:T(512)} %param.12) | copy-start | bytes 6148
  32.8 24.5 %copy-start.11 = (f32[256]{0:T(256)S(1)}, f32[256]{0:T(256)}, u32[]{:S(2)}) copy-start(f32[256]{0:T(256)} %param.15) | copy-start | bytes 3076
  32.8 24.5 %all-to-all-start.1 = ((bf16[8,512,128]{2,1,0:T(8,128)(2,1)}), bf16[8,512,128]{2,1,0:T(8,128)(2,1)S(1)}, u32[]{:S(2)}, u32[]{:S(2)}) async-start(bf16[8,512,128]{2,1,0:T(8,128)(2,1)} %bitcast.9), calls=%async_computation.1 | async-start | bytes 2097152 | tf_op jit(solution)/shard_map/all_to_all | solution.py:494
  58.3 3.7 %collective-permute-start.3 = (bf16[144,128]{1,0:T(8,128)(2,1)S(1)}, bf16[144,128]{1,0:T(8,128)(2,1)S(1)}, u32[]{:S(2)}, u32[]{:S(2)}) collective-permute-start(bf16[144,128]{1,0:T(8,128)(2,1)S(1)} %get-tuple-element.30), channel_id=1, source_target_pairs={{0,8},{8,0},{16,24},{24,16},{32,40},{40,32},{48,56},{56,48},{64,72... | collective-permute-start | bytes 110600 | tf_op jit(solution)/shard_map/ppermute | solution.py:508
  61.9 16.7 %copy-start.1 = (bf16[64,128,128]{2,1,0:T(8,128)(2,1)S(1)}, bf16[64,128,128]{2,1,0:T(8,128)(2,1)}, u32[]{:S(2)}) copy-start(bf16[64,128,128]{2,1,0:T(8,128)(2,1)} %patterns_ref.7) | copy-start | bytes 6291460
  77.7 8.8 %collective-permute-start.4 = (bf16[2192,128]{1,0:T(8,128)(2,1)S(1)}, bf16[2192,128]{1,0:T(8,128)(2,1)S(1)}, u32[]{:S(2)}, u32[]{:S(2)}) collective-permute-start(bf16[2192,128]{1,0:T(8,128)(2,1)S(1)} %shard_map.145.near_ref), channel_id=1, source_target_pairs={{0,6},{1,7},{2,4},{3,5},{4,2},{5,3},{6,0},{7,1},{8,10},{9,11},{10,... | collective-permute-start | bytes 1683464 | tf_op jit(solution)/shard_map/ppermute | solution.py:532
  89.4 3.3 %collective-permute-start.5 = (bf16[4096,128]{1,0:T(8,128)(2,1)S(1)}, bf16[4096,128]{1,0:T(8,128)(2,1)S(1)}, u32[]{:S(2)}, u32[]{:S(2)}) collective-permute-start(bf16[4096,128]{1,0:T(8,128)(2,1)S(1)} %get-tuple-element.38), channel_id=1, source_target_pairs={{0,8},{8,0},{16,24},{24,16},{32,40},{40,32},{48,56},{56,48},{64,72... | collective-permute-start | bytes 3145736 | tf_op jit(solution)/shard_map/ppermute | solution.py:563
  92.9 8.8 %collective-permute-start.6 = (bf16[2192,128]{1,0:T(8,128)(2,1)S(1)}, bf16[2192,128]{1,0:T(8,128)(2,1)S(1)}, u32[]{:S(2)}, u32[]{:S(2)}) collective-permute-start(bf16[2192,128]{1,0:T(8,128)(2,1)S(1)} %get-tuple-element.41), channel_id=1, source_target_pairs={{0,48},{8,24},{16,32},{24,8},{32,16},{40,56},{48,0},{56,40},{64,11... | collective-permute-start | bytes 1683464 | tf_op jit(solution)/shard_map/ppermute | solution.py:577
  112.7 3.7 %collective-permute-start.7 = (f32[136,128]{1,0:T(8,128)S(1)}, f32[136,128]{1,0:T(8,128)S(1)}, u32[]{:S(2)}, u32[]{:S(2)}) collective-permute-start(f32[136,128]{1,0:T(8,128)S(1)} %shard_map.152.mine_ref), channel_id=1, source_target_pairs={{0,8},{8,0},{16,24},{24,16},{32,40},{40,32},{48,56},{56,48},{64,72... | collective-permute-start | bytes 208904 | tf_op jit(solution)/shard_map/ppermute | solution.py:587

commit v3 on v2

v3 whole, which is shorter than its diff:
```python
import functools
import math

import jax
import jax.numpy as jnp
from jax import lax
from jax.experimental import pallas as pl
from jax.experimental.pallas import tpu as pltpu
from jax.sharding import PartitionSpec as P

GROUP = 64
SMALL_GROUP = 32
CLASSES = 8
VMEM_LIMIT = 20 * 1024 * 1024
ROOT_2_PI = math.sqrt(2.0 / math.pi)
CUBIC = 0.044715
BIAS_ROWS = 16
PER_SHARD = 4
ORDERED = 640
BOUNDS = 600
ANY = pl.BlockSpec(memory_space=pl.ANY)
VMEM = pl.BlockSpec(memory_space=pltpu.VMEM)
SMEM = pl.BlockSpec(memory_space=pltpu.SMEM)
PARAMS = pltpu.CompilerParams(vmem_limit_bytes=VMEM_LIMIT)


def order_kernel(core_ref, live_ref, row_ref, col_ref, pattern_ref, weight_ref, out_ref):
    rows, edge = row_ref.shape
    tile_col, tile_row = col_ref[...], row_ref[...]
    shard = tile_col // PER_SHARD
    other = (shard % 2) ^ core_ref[0]
    column = (other * 8 + shard // 2) * PER_SHARD + tile_col % PER_SHARD
    word = tile_row | (pattern_ref[...] << 5) | (weight_ref[...] << 11) | (column << 14)
    slot = lax.broadcasted_iota(jnp.int32, (rows, edge), 0) * edge
    slot += lax.broadcasted_iota(jnp.int32, (rows, edge), 1)
    alive = slot < live_ref[0, 0]
    word = jnp.where(alive, word, 0)
    second = PER_SHARD // 2
    kind = ((column % PER_SHARD) // second) * 4 + ((tile_row % PER_SHARD) // second) * 2 + other
    kind = jnp.where(alive, kind, CLASSES)

    flags = [(kind == index).astype(jnp.float32) for index in range(CLASSES + 1)]
    stacked = jnp.concatenate(flags + [jnp.zeros((4, edge), jnp.float32)], 0)
    before = lax.broadcasted_iota(jnp.int32, (edge, edge), 0) < lax.broadcasted_iota(
        jnp.int32, (edge, edge), 1
    )
    earlier = jnp.dot(
        stacked.astype(jnp.bfloat16),
        before.astype(jnp.float32).astype(jnp.bfloat16),
        preferred_element_type=jnp.float32,
    )
    counts = jnp.sum(stacked, axis=1, keepdims=True)
    start = jnp.zeros((1, 1), jnp.float32)
    ends = []
    position = [jnp.zeros((1, edge), jnp.float32) for _ in range(rows)]
    for index in range(CLASSES + 1):
        for line in range(rows):
            at = index * rows + line
            position[line] += flags[index][line : line + 1] * (start + earlier[at : at + 1])
            start = start + counts[at : at + 1]
        ends.append(start)
    turned = jnp.concatenate(position + [jnp.zeros((8 - rows, edge), jnp.float32)], 0).T
    slots = rows * edge
    lanes = lax.broadcasted_iota(jnp.int32, (edge, slots), 1).astype(jnp.float32)
    pieces = jnp.zeros((8, slots), jnp.float32)
    for line in range(rows):
        chosen = (turned[:, line : line + 1] == lanes).astype(jnp.float32).astype(jnp.bfloat16)
        parts = [(word[line : line + 1] >> shift) & 127 for shift in (0, 7, 14)]
        parts = jnp.concatenate(parts + [jnp.zeros((5, edge), jnp.int32)], 0)
        parts = parts.astype(jnp.float32).astype(jnp.bfloat16)
        pieces += jnp.dot(parts, chosen, preferred_element_type=jnp.float32)
    pieces = pieces.astype(jnp.int32)
    out_ref[:, :slots] = pieces[0:1] | (pieces[1:2] << 7) | (pieces[2:3] << 14)
    lane = lax.broadcasted_iota(jnp.int32, (1, out_ref.shape[1] - slots), 1) + slots
    tail = jnp.zeros(lane.shape, jnp.int32)
    for index in range(CLASSES):
        tail = jnp.where(lane == BOUNDS + index, ends[index].astype(jnp.int32), tail)
    out_ref[:, slots:] = tail


def add_products(slots_ref, runs, product_of, place_of, sums, size):
    edge = sums.shape[1]
    (first, end), (first_b, end_b) = runs
    turns = (end - first + size - 1) // size
    turns_b = (end_b - first_b + size - 1) // size

    def one_group(turn, carry):
        is_a = turn < turns
        start = jnp.where(is_a, first + turn * size, first_b + (turn - turns) * size)
        stop = jnp.where(is_a, end, end_b)
        terms = []
        for member in range(size):
            slot = start + member
            word = slots_ref[0, slot]
            factor = jnp.where(slot < stop, (word >> 11) & 7, 0).astype(jnp.float32)
            terms.append((place_of(word), factor, product_of(word)))
        for place, factor, product in terms:
            rows = pl.ds(pl.multiple_of(place * edge, edge), edge)
            sums[rows, :] += factor * product
        return carry

    lax.fori_loop(0, turns + turns_b, one_group, 0)


def tile_of(ref, place, edge):
    return ref[pl.ds(pl.multiple_of(place * edge, edge), edge), :]


def class_bounds(slots_ref):
    return [0] + [slots_ref[0, BOUNDS + index] for index in range(CLASSES)]


def root_columns(degree):
    rows = lax.rsqrt(degree.astype(jnp.float32))
    rows = jnp.concatenate([rows, jnp.ones((8 - rows.shape[0], rows.shape[1]), jnp.float32)], 0)
    return rows.T


def scale_kernel(
    features_hbm, degree_hbm, first_ref, second_ref, features_ref, degree_ref, sems
):
    copies = (
        pltpu.make_async_copy(degree_hbm, degree_ref, sems.at[0]),
        pltpu.make_async_copy(features_hbm, features_ref, sems.at[1]),
    )
    for copy in copies:
        copy.start()
    copies[0].wait()
    roots = root_columns(degree_ref[...])
    copies[1].wait()
    tiles, edge = degree_ref.shape
    for tile in range(tiles):
        scaled = features_ref[pl.ds(tile * edge, edge), :].astype(jnp.float32)
        scaled = (scaled * roots[:, tile : tile + 1]).astype(jnp.bfloat16)
        out_ref, at = (first_ref, tile) if 2 * tile < tiles else (second_ref, tile - tiles // 2)
        for copy in range(out_ref.shape[0]):
            out_ref[copy, pl.ds(at * edge, edge), :] = scaled


def forward_sums(slots_ref, patterns_ref, own_ref, other_ref, panel, sums, second):
    edge = patterns_ref.shape[1]
    half = own_ref.shape[0]
    panel[:half, :] = own_ref[...]
    panel[half:, :] = other_ref[...]
    bounds = class_bounds(slots_ref)

    def product_of(word):
        place = ((word >> 16) << 1) | ((word >> 14) & 1)
        return jnp.dot(
            patterns_ref[(word >> 5) & 63],
            tile_of(panel, place, edge),
            preferred_element_type=jnp.float32,
        )

    run = (bounds[4], bounds[8]) if second else (bounds[0], bounds[4])
    add_products(slots_ref, (run, (0, 0)), product_of, lambda word: word & 31, sums, GROUP)


def forward_first_kernel(slots_ref, patterns_ref, own_ref, other_ref, out_ref, panel):
    out_ref[...] = jnp.zeros_like(out_ref)
    forward_sums(slots_ref, patterns_ref, own_ref, other_ref, panel, out_ref, False)


def forward_second_kernel(
    slots_ref, patterns_ref, own_ref, other_ref, so_far_ref, out_ref, panel, sums
):
    sums[...] = so_far_ref[...]
    forward_sums(slots_ref, patterns_ref, own_ref, other_ref, panel, sums, True)
    out_ref[...] = sums[...].astype(jnp.bfloat16)


def backward_sums(slots_ref, patterns_ref, spread_ref, sums, runs, size):
    edge = patterns_ref.shape[1]
    mask = sums.shape[0] // edge - 1

    def product_of(word):
        start = pl.multiple_of((word & 1) * edge, edge)
        return jnp.dot(
            spread_ref[(word >> 2) & 7, pl.ds(start, edge), :],
            patterns_ref[(word >> 5) & 63],
            preferred_element_type=jnp.float32,
        )

    add_products(slots_ref, runs, product_of, lambda word: (word >> 14) & mask, sums, size)


def backward_first_kernel(slots_ref, patterns_ref, spread_ref, out_ref):
    out_ref[...] = jnp.zeros_like(out_ref)
    bounds = class_bounds(slots_ref)
    runs = ((bounds[0], bounds[2]), (bounds[4], bounds[6]))
    backward_sums(slots_ref, patterns_ref, spread_ref, out_ref, runs, GROUP)


def backward_send_kernel(slots_ref, patterns_ref, spread_ref, so_far_ref, send_ref, sums):
    half = sums.shape[0]
    sums[...] = so_far_ref[half:, :]
    bounds = class_bounds(slots_ref)
    runs = ((bounds[3], bounds[4]), (bounds[7], bounds[8]))
    backward_sums(slots_ref, patterns_ref, spread_ref, sums, runs, SMALL_GROUP)
    send_ref[...] = sums[...].astype(jnp.bfloat16)


def backward_keep_kernel(slots_ref, patterns_ref, spread_ref, so_far_ref, keep_ref, grads_ref):
    keep_ref[...] = so_far_ref[: keep_ref.shape[0], :]
    bounds = class_bounds(slots_ref)
    runs = ((bounds[2], bounds[3]), (bounds[6], bounds[7]))
    backward_sums(slots_ref, patterns_ref, spread_ref, keep_ref, runs, SMALL_GROUP)
    shards, rows_in_shard, _ = spread_ref.shape
    own = rows_in_shard - grads_ref.shape[0]
    grads = spread_ref[0, own:, :].astype(jnp.float32)
    for shard in range(1, shards):
        grads += spread_ref[shard, own:, :].astype(jnp.float32)
    grads_ref[...] = grads.astype(jnp.bfloat16)


def split_product(left, right, dims):
    high = left.astype(jnp.bfloat16)
    low = (left - high.astype(jnp.float32)).astype(jnp.bfloat16)
    return lax.dot_general(
        high, right, (dims, ((), ())), preferred_element_type=jnp.float32
    ) + lax.dot_general(low, right, (dims, ((), ())), preferred_element_type=jnp.float32)


def activate(pre_act):
    square = pre_act * pre_act
    bent = jnp.tanh(ROOT_2_PI * (pre_act + CUBIC * (pre_act * square)))
    return square, bent, 0.5 * (1.0 + bent)


def middle_tiles(
    tiles, parts_ref, degree_ref, cotangent_ref, weight_ref, bias_ref, pre_ref, out_ref
):
    edge = degree_ref.shape[1]
    shards = parts_ref.shape[0]
    weight = weight_ref[...]
    roots = root_columns(degree_ref[...])
    grads = jnp.zeros(weight.shape, jnp.float32)
    bias_row = jnp.zeros(bias_ref.shape, jnp.float32)
    for index, tile in enumerate(tiles):
        rows = pl.ds(tile * edge, edge)
        own_rows = pl.ds(index * edge, edge)
        sums = parts_ref[0, rows, :].astype(jnp.float32)
        for shard in range(1, shards):
            sums += parts_ref[shard, rows, :].astype(jnp.float32)
        inv_root = roots[:, tile : tile + 1]
        pre_act = inv_root * split_product(sums, weight, ((1,), (0,))) + bias_ref[...]
        pre_ref[own_rows, :] = pre_act
        square, bent, half = activate(pre_act)
        rise = 0.5 * pre_act * (1.0 - bent * bent) * (ROOT_2_PI * (1.0 + 3.0 * CUBIC * square))
        slope = cotangent_ref[rows, :].astype(jnp.float32) * (half + rise)
        upstream = inv_root * slope
        high = upstream.astype(jnp.bfloat16)
        low = (upstream - high.astype(jnp.float32)).astype(jnp.bfloat16)
        spread = sum(
            lax.dot_general(
                weight, part, (((1,), (1,)), ((), ())), preferred_element_type=jnp.float32
            )
            for part in (high, low)
        ).astype(jnp.bfloat16)
        for shard in range(shards):
            out_ref[shard, own_rows, :] = spread
        grads += split_product(sums, high, ((0,), (0,)))
        bias_row += jnp.sum(slope, axis=0, keepdims=True)
    return grads, bias_row


def middle_first_kernel(
    parts_ref,
    degree_ref,
    cotangent_ref,
    weight_ref,
    bias_ref,
    pre_ref,
    out_ref,
    grads_ref,
    bias_out_ref,
):
    tiles = range(degree_ref.shape[0] // 2)
    grads_ref[...], bias_out_ref[...] = middle_tiles(
        tiles, parts_ref, degree_ref, cotangent_ref, weight_ref, bias_ref, pre_ref, out_ref
    )


def middle_second_kernel(
    core_ref,
    parts_ref,
    degree_ref,
    cotangent_ref,
    weight_ref,
    bias_ref,
    grads_ref,
    bias_so_far_ref,
    pre_ref,
    out_ref,
    keep_ref,
    send_ref,
):
    tiles = range(degree_ref.shape[0] // 2, degree_ref.shape[0])
    grads, bias_row = middle_tiles(
        tiles, parts_ref, degree_ref, cotangent_ref, weight_ref, bias_ref, pre_ref, out_ref
    )
    grads += grads_ref[...]
    bias_row += bias_so_far_ref[...]
    height, width = weight_ref.shape[0], keep_ref.shape[1]
    bias_high = bias_row.astype(jnp.bfloat16).astype(jnp.float32)
    bias_low = bias_row - bias_high
    first = core_ref[0] == 0

    def put(target, left):
        pick = lambda whole: jnp.where(left, whole[:, :width], whole[:, width:])
        target[:height, :] = pick(grads).astype(target.dtype)
        row_ids = lax.broadcasted_iota(jnp.int32, (BIAS_ROWS, width), 0)
        block = jnp.where(row_ids == 0, pick(bias_high), 0.0)
        block = jnp.where(row_ids == 1, pick(bias_low), block)
        target[height:, :] = block.astype(target.dtype)

    put(keep_ref, first)
    put(send_ref, jnp.logical_not(first))


def activation_kernel(first_ref, second_ref, act_ref):
    half = first_ref.shape[0]
    for ref, rows in ((first_ref, pl.ds(0, half)), (second_ref, pl.ds(half, half))):
        pre_act = ref[...]
        act_ref[rows, :] = (pre_act * activate(pre_act)[2]).astype(jnp.bfloat16)


def append_kernel(keep_ref, got_ref, spread_ref, out_ref):
    terms = (keep_ref[...] + got_ref[...].astype(jnp.float32)).astype(jnp.bfloat16)
    rows = pl.ds(out_ref.shape[1] - terms.shape[0], terms.shape[0])
    for shard in range(out_ref.shape[0]):
        out_ref[shard, rows, :] = terms


def sum_of_parts(parts_ref, rows):
    total = parts_ref[0, rows, :].astype(jnp.float32)
    for shard in range(1, parts_ref.shape[0]):
        total += parts_ref[shard, rows, :].astype(jnp.float32)
    return total


def join_kernel(keep_ref, got_ref, grads_ref, out_ref):
    shards = out_ref.shape[0]
    own = keep_ref.shape[0] // shards
    for shard in range(shards):
        rows = pl.ds(shard * own, own)
        total = keep_ref[rows, :] + got_ref[rows, :].astype(jnp.float32)
        out_ref[shard, pl.ds(0, own), :] = total.astype(jnp.bfloat16)
        out_ref[shard, pl.ds(own, grads_ref.shape[0]), :] = grads_ref[...]


def total_kernel(scale_factor, parts_ref, half_ref):
    extra = half_ref.shape[0] - 8 + BIAS_ROWS
    tail = sum_of_parts(parts_ref, pl.ds(parts_ref.shape[1] - extra, extra))
    tail = tail * scale_factor
    height = half_ref.shape[0] - 8
    half_ref[:height, :] = tail[:height, :]
    bias_row = tail[height : height + 1, :] + tail[height + 1 : height + 2, :]
    half_ref[height:, :] = jnp.broadcast_to(bias_row, (8, bias_row.shape[1]))


def features_kernel(parts_ref, degree_ref, features_ref):
    tiles, edge = degree_ref.shape
    roots = lax.rsqrt(degree_ref[...].astype(jnp.float32))
    for tile in range(tiles):
        rows = pl.ds(tile * edge, edge)
        total = sum_of_parts(parts_ref, rows)
        features_ref[rows, :] = (total * roots[tile : tile + 1, :]).T.astype(jnp.bfloat16)


def lay_out_kernel(core_ref, mine_ref, other_ref, grads_ref, bias_ref):
    first = core_ref[0] == 0
    height = grads_ref.shape[0]
    width = mine_ref.shape[1]
    mine, other = mine_ref[...], other_ref[...]
    halves = (jnp.where(first, mine, other), jnp.where(first, other, mine))
    for index, half in enumerate(halves):
        lanes = pl.ds(index * width, width)
        grads_ref[:, lanes] = half[:height, :]
        bias_ref[:, lanes] = half[height : height + 1, :]


def per_device(
    features,
    degree,
    cotangent,
    weight,
    layer_bias,
    patterns,
    tile_row,
    tile_col,
    tile_pattern,
    tile_weight,
    tile_count,
):
    node_dev, feature_count = features.shape
    hidden = weight.shape[1]
    row_devices = lax.axis_size("row")
    col_devices = lax.axis_size("col")
    chips = row_devices // 2
    edge = patterns.shape[1]
    per_shard = node_dev // edge
    core = lax.axis_index("row") % 2
    same_core = [list(range(first, row_devices, 2)) for first in range(2)]
    swap = [(index, index ^ 1) for index in range(row_devices)]
    exchange = functools.partial(lax.all_to_all, split_axis=0, concat_axis=0)
    across_chips = functools.partial(exchange, axis_name="row", axis_index_groups=same_core)
    across_cols = functools.partial(exchange, axis_name="col")
    extra = feature_count + BIAS_ROWS
    half = chips * node_dev
    bf16, f32 = jnp.bfloat16, jnp.float32
    shape = jax.ShapeDtypeStruct
    degree_tiles = degree.reshape(per_shard, edge)
    tile_cost = pl.CostEstimate(
        flops=tile_row.size // (row_devices * col_devices) * edge * edge * feature_count,
        bytes_accessed=patterns.size * 2 + 4 * half * feature_count * 2,
        transcendentals=0,
    )

    core_word = core.astype(jnp.int32).reshape(1)
    half_shard = node_dev // 2
    copies = shape((chips, half_shard, feature_count), bf16)
    first, second = pl.pallas_call(
        scale_kernel,
        out_shape=(copies, copies),
        in_specs=[ANY] * 2,
        out_specs=(VMEM,) * 2,
        scratch_shapes=[
            pltpu.VMEM(features.shape, bf16),
            pltpu.VMEM(degree_tiles.shape, jnp.int32),
            pltpu.SemaphoreType.DMA((2,)),
        ],
        compiler_params=PARAMS,
    )(features, degree_tiles)
    first_own = across_chips(first).reshape(half // 2, feature_count)
    second_own = across_chips(second).reshape(half // 2, feature_count)
    slots = pl.pallas_call(
        order_kernel,
        out_shape=shape((1, ORDERED), jnp.int32),
        in_specs=[SMEM] * 2 + [VMEM] * 4,
        out_specs=VMEM,
        compiler_params=PARAMS,
    )(
        core_word,
        tile_count,
        tile_row.reshape(per_shard, edge),
        tile_col.reshape(per_shard, edge),
        tile_pattern.reshape(per_shard, edge),
        tile_weight.reshape(per_shard, edge),
    )
    first_own, slots = lax.optimization_barrier((first_own, slots))
    first_other = lax.ppermute(first_own, "row", swap)
    forward_panel = pltpu.VMEM((half, feature_count), bf16)
    row_sums = shape((col_devices * node_dev, feature_count), f32)
    so_far = pl.pallas_call(
        forward_first_kernel,
        out_shape=row_sums,
        in_specs=[SMEM] + [VMEM] * 3,
        out_specs=VMEM,
        scratch_shapes=[forward_panel],
        compiler_params=PARAMS,
        cost_estimate=tile_cost,
    )(slots, patterns, first_own, first_other)
    second_own, so_far = lax.optimization_barrier((second_own, so_far))
    second_other = lax.ppermute(second_own, "row", swap)
    row_part = pl.pallas_call(
        forward_second_kernel,
        out_shape=shape(row_sums.shape, bf16),
        in_specs=[SMEM] + [VMEM] * 4,
        out_specs=VMEM,
        scratch_shapes=[forward_panel, pltpu.VMEM(row_sums.shape, f32)],
        compiler_params=PARAMS,
        cost_estimate=tile_cost,
    )(slots, patterns, second_own, second_other, so_far)
    parts = across_cols(row_part.reshape(col_devices, node_dev, feature_count))

    middle_inputs = (parts, degree_tiles, cotangent, weight, layer_bias[None, :])
    pre_shape = shape((half_shard, hidden), f32)
    pre_first, spread, grads, bias_row = pl.pallas_call(
        middle_first_kernel,
        out_shape=(
            pre_shape,
            shape((col_devices, half_shard, edge), bf16),
            shape((feature_count, hidden), f32),
            shape((1, hidden), f32),
        ),
        in_specs=[VMEM] * 5,
        out_specs=(VMEM,) * 4,
        compiler_params=PARAMS,
    )(*middle_inputs)
    spread_first = across_cols(spread)
    pre_second, spread, keep_terms, send_terms = pl.pallas_call(
        middle_second_kernel,
        out_shape=(
            pre_shape,
            shape((col_devices, half_shard + extra, edge), bf16),
            shape((extra, edge), f32),
            shape((extra, edge), bf16),
        ),
        in_specs=[SMEM] + [VMEM] * 7,
        out_specs=(VMEM,) * 4,
        compiler_params=PARAMS,
    )(core_word, *middle_inputs, grads, bias_row)
    got_terms = lax.ppermute(send_terms, "row", swap)
    spread = pl.pallas_call(
        append_kernel,
        out_shape=shape(spread.shape, bf16),
        in_specs=[VMEM] * 3,
        out_specs=VMEM,
        input_output_aliases={2: 0},
        compiler_params=PARAMS,
    )(keep_terms, got_terms, spread)
    spread_first, spread = lax.optimization_barrier((spread_first, spread))
    spread_second = across_cols(spread)
    back_sums = pl.pallas_call(
        backward_first_kernel,
        out_shape=shape((2 * half, edge), f32),
        in_specs=[SMEM] + [VMEM] * 2,
        out_specs=VMEM,
        compiler_params=PARAMS,
        cost_estimate=tile_cost,
    )(slots, patterns, spread_first)
    spread_second, back_sums = lax.optimization_barrier((spread_second, back_sums))
    send = pl.pallas_call(
        backward_send_kernel,
        out_shape=shape((half, edge), bf16),
        in_specs=[SMEM] + [VMEM] * 3,
        out_specs=VMEM,
        scratch_shapes=[pltpu.VMEM((half, edge), f32)],
        compiler_params=PARAMS,
        cost_estimate=tile_cost,
    )(slots, patterns, spread_second, back_sums)
    back_sums, send = lax.optimization_barrier((back_sums, send))
    got = lax.ppermute(send, "row", swap)
    keep, grads = pl.pallas_call(
        backward_keep_kernel,
        out_shape=(shape((half, edge), f32), shape((extra, edge), bf16)),
        in_specs=[SMEM] + [VMEM] * 3,
        out_specs=(VMEM,) * 2,
        compiler_params=PARAMS,
        cost_estimate=tile_cost,
    )(slots, patterns, spread_second, back_sums)
    got, keep = lax.optimization_barrier((got, keep))
    joined = pl.pallas_call(
        join_kernel,
        out_shape=shape((chips, node_dev + extra, edge), bf16),
        in_specs=[VMEM] * 3,
        out_specs=VMEM,
        compiler_params=PARAMS,
    )(keep, got, grads)
    joined, pre_first, pre_second = lax.optimization_barrier((joined, pre_first, pre_second))
    back_parts = across_chips(joined)
    activations = pl.pallas_call(
        activation_kernel,
        out_shape=shape((node_dev, hidden), bf16),
        in_specs=[VMEM] * 2,
        out_specs=VMEM,
        compiler_params=PARAMS,
    )(pre_first, pre_second)
    back_parts, activations = lax.optimization_barrier((back_parts, activations))
    scale_factor = 1.0 / math.sqrt(node_dev * row_devices * col_devices)
    mine = pl.pallas_call(
        functools.partial(total_kernel, scale_factor),
        out_shape=shape((feature_count + 8, edge), f32),
        in_specs=[VMEM],
        out_specs=VMEM,
        compiler_params=PARAMS,
    )(back_parts)
    other = lax.ppermute(mine, "row", swap)
    grad_features = pl.pallas_call(
        features_kernel,
        out_shape=shape((node_dev, feature_count), bf16),
        in_specs=[VMEM] * 2,
        out_specs=VMEM,
        compiler_params=PARAMS,
    )(back_parts, degree_tiles)
    grad_weight, grad_bias = pl.pallas_call(
        lay_out_kernel,
        out_shape=(shape((feature_count, hidden), f32), shape((1, hidden), f32)),
        in_specs=[SMEM] + [VMEM] * 2,
        out_specs=(VMEM,) * 2,
        compiler_params=PARAMS,
    )(core_word, mine, other)
    return (activations, grad_features, grad_weight, grad_bias[0])


def solution(mesh):
    in_specs = (
        P(("row", "col"), None),
        P(("row", "col")),
        P(("row", "col"), None),
        P(),
        P(),
        P(),
        P("row", "col", None),
        P("row", "col", None),
        P("row", "col", None),
        P("row", "col", None),
        P("row", "col"),
    )
    out_specs = (P(("row", "col"), None), P(("row", "col"), None), P(), P())
    return jax.shard_map(
        per_device, mesh=mesh, in_specs=in_specs, out_specs=out_specs, check_vma=False
    )
```

time: 119 us -> 137 us (1.15)
  blocking collectives: 40.3 us -> 24.7 us
  starting transfers between devices: 18.4 us -> 31.1 us
  local copies, waits for them, and re-layouts: 5.91 us -> 17.1 us
  waiting for transfers between devices: 33.9 us -> 44 us
    all_to_all x1 -> x5, waiting for transfers between devices: 15.4 us -> 41.1 us  [the longest x1 18.2 us: per_device(): back_parts = across_chips(joined)]
    all_to_all x3 -> x1, blocking collectives: 40.3 us -> 24.7 us  [per_device(): parts = across_cols(row_part.reshape(col_devices, node_dev, feature_count))]
    ppermute x5 -> x2, waiting for transfers between devices: 15.5 us -> 1.54 us  [the longest x1 1.54 us: per_device(): second_other = lax.ppermute(second_own, 'row', swap)]
    all_to_all x1 -> x5, starting transfers between devices: 9.1 us -> 21.8 us  [the longest x1 5.86 us: per_device(): first_own = across_chips(first).reshape(half // 2, feature_count)]
    unnamed x24 -> x48, local copies, waits for them, and re-layouts: 5.91 us -> 17.1 us
    ppermute x1, starting transfers between devices: 0.99 us -> 4.54 us  [per_device(): got = lax.ppermute(send, 'row', swap)]
    ppermute x1, starting transfers between devices: 2.82 us -> 0.84 us  [per_device(): other = lax.ppermute(mine, 'row', swap)]
    ppermute x1, waiting for transfers between devices: 2.29 us -> 0.52 us  [per_device(): got = lax.ppermute(send, 'row', swap)]
  transfers between devices with their start and end apart: 9 -> 10, of which waited for: 7 -> 8; matrix products, arithmetic and copies ran while one was open for 0% -> 0% of each run, Pallas kernels for 7% -> 7%
where the time goes in v3:
time: 137 us; the launch traced here: 136 us
  waiting for transfers between devices  44 us (32%)
  starting transfers between devices  31.1 us (23%)
  blocking collectives  24.7 us (18%)
  Pallas kernels  17.7 us (13%)
  local copies, waits for them, and re-layouts  17.1 us (12%)
  between operations  1.54 us (1%)
    all_to_all x1, blocking collectives, per_device(): parts = across_cols(row_part.reshape(col_devices, node_dev, feature_count))  24.7 us
    all_to_all x1, waiting for transfers between devices, per_device(): back_parts = across_chips(joined)  18.2 us
    unnamed x48, local copies, waits for them, and re-layouts  17.1 us
    all_to_all x1, waiting for transfers between devices, per_device(): spread_second = across_cols(spread)  7.29 us
    all_to_all x1, waiting for transfers between devices, per_device(): second_own = across_chips(second).reshape(half // 2, feature_count)  6.79 us
    all_to_all x1, waiting for transfers between devices, per_device(): first_own = across_chips(first).reshape(half // 2, feature_count)  6.2 us
    all_to_all x1, starting transfers between devices, per_device(): first_own = across_chips(first).reshape(half // 2, feature_count)  5.86 us
    ppermute x1, starting transfers between devices, per_device(): got = lax.ppermute(send, 'row', swap)  4.54 us
  transfers between devices with their start and end apart: 10, of which 8 were waited for; matrix products, arithmetic and copies ran while one was open for 0% of the time, Pallas kernels for 7%

profile of v3, /device:TPU:1, one launch (start us, length us, event | category | flops | bytes accessed | tf_op | source)
XLA Modules:
  0.0 136.2 jit_solution(10425556478047448961)
XLA Ops:
  0.7 1.0 copy-done.14
  2.4 1.2 shard_map.138
  4.3 5.9 %all-to-all-start = ((bf16[8,256,128]{2,1,0:T(8,128)(2,1)}), bf16[8,256,128]{2,1,0:T(8,128)(2,1)S(1)}, u32[]{:S(2)}, u32[]{:S(2)}) async-start(bf16[8,256,128]{2,1,0:T(8,128)(2,1)} %get-tuple-element.35), calls=%async_computation | async-start | bytes 1048576 | tf_op jit(solution)/shard_map/all_to_all | solution.py:435
  14.2 6.2 %all-to-all-done = bf16[8,256,128]{2,1,0:T(8,128)(2,1)S(1)} async-done(((bf16[8,256,128]{2,1,0:T(8,128)(2,1)}), bf16[8,256,128]{2,1,0:T(8,128)(2,1)S(1)}, u32[]{:S(2)}, u32[]{:S(2)}) %all-to-all-start) | async-done | bytes 524320 | tf_op jit(solution)/shard_map/all_to_all | solution.py:435
  21.2 3.5 %all-to-all-start.1 = ((bf16[8,256,128]{2,1,0:T(8,128)(2,1)}), bf16[8,256,128]{2,1,0:T(8,128)(2,1)S(1)}, u32[]{:S(2)}, u32[]{:S(2)}) async-start(bf16[8,256,128]{2,1,0:T(8,128)(2,1)} %copy-done.7), calls=%async_computation.1 | async-start | bytes 1048576 | tf_op jit(solution)/shard_map/all_to_all | solution.py:436
  24.8 2.1 %shard_map.140.so_far_ref = f32[4096,128]{1,0:T(8,128)S(1)} custom-call(s32[1,640]{1,0:T(1,128)S(1)} %shard_map.139.slots_ref, bf16[64,128,128]{2,1,0:T(8,128)(2,1)S(1)} %copy-done, bf16[2048,128]{1,0:T(8,128)(2,1)S(1)} %bitcast.13, bf16[2048,128]{1,0:T(8,128)(2,1)} %collective-permute-done.other_ref), custom_call_target="tpu_custom_call" | custom-call | flops 8388608 | bytes 6291456 | tf_op jit(solution)/shard_map/pallas_call | solution.py:455
  26.9 1.4 copy-done.3
  28.2 6.8 %all-to-all-done.1 = bf16[8,256,128]{2,1,0:T(8,128)(2,1)S(1)} async-done(((bf16[8,256,128]{2,1,0:T(8,128)(2,1)}), bf16[8,256,128]{2,1,0:T(8,128)(2,1)S(1)}, u32[]{:S(2)}, u32[]{:S(2)}) %all-to-all-start.1) | async-done | bytes 524320 | tf_op jit(solution)/shard_map/all_to_all | solution.py:436
  35.7 1.5 %collective-permute-done.1.other_ref = bf16[2048,128]{1,0:T(8,128)(2,1)S(1)} collective-permute-done((bf16[2048,128]{1,0:T(8,128)(2,1)S(1)}, bf16[2048,128]{1,0:T(8,128)(2,1)S(1)}, u32[]{:S(2)}, u32[]{:S(2)}) %collective-permute-start.1) | collective-permute-done | bytes 524320 | tf_op jit(solution)/shard_map/ppermute | solution.py:465
  37.3 1.6 %copy-done.4 = f32[4096,128]{1,0:T(8,128)S(1)} copy-done((f32[4096,128]{1,0:T(8,128)S(1)}, f32[4096,128]{1,0:T(8,128)}, u32[]{:S(2)}) %copy-start.4) | copy-done | bytes 2097176
  38.9 1.7 %shard_map.141 = bf16[4096,128]{1,0:T(8,128)(2,1)S(1)} custom-call(s32[1,640]{1,0:T(1,128)S(1)} %shard_map.139.slots_ref, bf16[64,128,128]{2,1,0:T(8,128)(2,1)S(1)} %copy-done, bf16[2048,128]{1,0:T(8,128)(2,1)S(1)} %bitcast.15, bf16[2048,128]{1,0:T(8,128)(2,1)S(1)} %collective-permute-done.1.other_ref, f32[4096,128]{1,0:T(8,128)S(1)} %copy-done.4), custom_call_target="tpu_custom_call" | custom-call | flops 8388608 | bytes 6291456 | tf_op jit(solution)/shard_map/pallas_call | solution.py:466
  40.6 24.7 %all_to_all.30.parts_ref = bf16[8,512,128]{2,1,0:T(8,128)(2,1)S(1)} all-to-all(bf16[8,512,128]{2,1,0:T(8,128)(2,1)S(1)} %bitcast.11), channel_id=1, replica_groups=mesh['row'=16,'col'=8] {'col'}, dimensions={0} | all-to-all | bytes 2097152 | tf_op jit(solution)/shard_map/all_to_all | solution.py:475
  65.4 0.9 shard_map.142
  68.5 4.1 %all-to-all-start.3 = ((bf16[8,256,128]{2,1,0:T(8,128)(2,1)}), bf16[8,256,128]{2,1,0:T(8,128)(2,1)}, u32[]{:S(2)}, u32[]{:S(2)}) async-start(bf16[8,256,128]{2,1,0:T(8,128)(2,1)} %copy-done.8), calls=%async_computation.3 | async-start | bytes 1048576 | tf_op jit(solution)/shard_map/all_to_all | solution.py:491
  72.6 0.9 copy-done.16
  73.5 0.9 shard_map.143
  75.1 2.4 %collective-permute-start.2 = (bf16[144,128]{1,0:T(8,128)(2,1)S(1)}, bf16[144,128]{1,0:T(8,128)(2,1)S(1)}, u32[]{:S(2)}, u32[]{:S(2)}) collective-permute-start(bf16[144,128]{1,0:T(8,128)(2,1)S(1)} %get-tuple-element.45), channel_id=1, source_target_pairs={{0,8},{8,0},{16,24},{24,16},{32,40},{40,32},{48,56},{56,48},{64,72... | collective-permute-start | bytes 110600 | tf_op jit(solution)/shard_map/ppermute | solution.py:504
  78.5 0.9 copy-done.5
  79.4 2.6 %all-to-all-done.3.spread_ref = bf16[8,256,128]{2,1,0:T(8,128)(2,1)} async-done(((bf16[8,256,128]{2,1,0:T(8,128)(2,1)}), bf16[8,256,128]{2,1,0:T(8,128)(2,1)}, u32[]{:S(2)}, u32[]{:S(2)}) %all-to-all-start.3) | async-done | bytes 524320 | tf_op jit(solution)/shard_map/all_to_all | solution.py:491
  82.0 4.2 %all-to-all-start.4 = ((bf16[8,400,128]{2,1,0:T(8,128)(2,1)}), bf16[8,400,128]{2,1,0:T(8,128)(2,1)S(1)}, u32[]{:S(2)}, u32[]{:S(2)}) async-start(bf16[8,400,128]{2,1,0:T(8,128)(2,1)} %copy-done.5), calls=%async_computation.4 | async-start | bytes 1638400 | tf_op jit(solution)/shard_map/all_to_all | solution.py:514
  86.2 3.0 %shard_map.145.so_far_ref = f32[8192,128]{1,0:T(8,128)S(1)} custom-call(s32[1,640]{1,0:T(1,128)S(1)} %shard_map.139.slots_ref, bf16[64,128,128]{2,1,0:T(8,128)(2,1)S(1)} %copy-done, bf16[8,256,128]{2,1,0:T(8,128)(2,1)} %all-to-all-done.3.spread_ref), custom_call_target="tpu_custom_call" | custom-call | flops 8388608 | bytes 6291456 | tf_op jit(solution)/shard_map/pallas_call | solution.py:515
  89.2 2.0 %copy-done.1 = f32[8192,128]{1,0:T(8,128)} copy-done((f32[8192,128]{1,0:T(8,128)}, f32[8192,128]{1,0:T(8,128)S(1)}, u32[]{:S(2)}) %copy-start.1) | copy-done | bytes 4194328
  91.2 7.3 %all-to-all-done.4.spread_ref = bf16[8,400,128]{2,1,0:T(8,128)(2,1)S(1)} async-done(((bf16[8,400,128]{2,1,0:T(8,128)(2,1)}), bf16[8,400,128]{2,1,0:T(8,128)(2,1)S(1)}, u32[]{:S(2)}, u32[]{:S(2)}) %all-to-all-start.4) | async-done | bytes 819232 | tf_op jit(solution)/shard_map/all_to_all | solution.py:514
  98.5 2.2 %copy-done.2 = f32[8192,128]{1,0:T(8,128)S(1)} copy-done((f32[8192,128]{1,0:T(8,128)S(1)}, f32[8192,128]{1,0:T(8,128)}, u32[]{:S(2)}) %copy-start.2) | copy-done | bytes 4194328
  100.6 1.8 %shard_map.146 = bf16[4096,128]{1,0:T(8,128)(2,1)S(1)} custom-call(s32[1,640]{1,0:T(1,128)S(1)} %shard_map.139.slots_ref, bf16[64,128,128]{2,1,0:T(8,128)(2,1)S(1)} %copy-done, bf16[8,400,128]{2,1,0:T(8,128)(2,1)S(1)} %all-to-all-done.4.spread_ref, f32[8192,128]{1,0:T(8,128)S(1)} %copy-done.2), custom_call_target="tpu_custom_call" | custom-call | flops 8388608 | bytes 6291456 | tf_op jit(solution)/shard_map/pallas_call | solution.py:524
  102.5 4.5 %collective-permute-start.3 = (bf16[4096,128]{1,0:T(8,128)(2,1)S(1)}, bf16[4096,128]{1,0:T(8,128)(2,1)S(1)}, u32[]{:S(2)}, u32[]{:S(2)}) collective-permute-start(bf16[4096,128]{1,0:T(8,128)(2,1)S(1)} %shard_map.146), channel_id=1, source_target_pairs={{0,8},{8,0},{16,24},{24,16},{32,40},{40,32},{48,56},{56,48},{64,72... | collective-permute-start | bytes 3145736 | tf_op jit(solution)/shard_map/ppermute | solution.py:534
  107.0 1.8 %shard_map.147 = (f32[4096,128]{1,0:T(8,128)S(1)}, bf16[144,128]{1,0:T(8,128)(2,1)S(1)}) custom-call(s32[1,640]{1,0:T(1,128)S(1)} %shard_map.139.slots_ref, bf16[64,128,128]{2,1,0:T(8,128)(2,1)S(1)} %copy-done, bf16[8,400,128]{2,1,0:T(8,128)(2,1)S(1)} %all-to-all-done.4.spread_ref, f32[8192,128]{1,0:T(8,128)S(1)} %copy-done.2), custom_call_target="tpu_custom_call" | custom-call | flops 8388608 | bytes 6291456 | tf_op jit(solution)/shard_map/pallas_call | solution.py:535
  109.3 1.3 shard_map.148
  110.6 4.1 %all-to-all-start.5 = ((bf16[8,656,128]{2,1,0:T(8,128)(2,1)}), bf16[8,656,128]{2,1,0:T(8,128)(2,1)S(1)}, u32[]{:S(2)}, u32[]{:S(2)}) async-start(bf16[8,656,128]{2,1,0:T(8,128)(2,1)} %shard_map.148), calls=%async_computation.5 | async-start | bytes 2686976 | tf_op jit(solution)/shard_map/all_to_all | solution.py:552
  114.7 0.9 shard_map.149
  115.6 18.2 %all-to-all-done.5.parts_ref = bf16[8,656,128]{2,1,0:T(8,128)(2,1)S(1)} async-done(((bf16[8,656,128]{2,1,0:T(8,128)(2,1)}), bf16[8,656,128]{2,1,0:T(8,128)(2,1)S(1)}, u32[]{:S(2)}, u32[]{:S(2)}) %all-to-all-start.5) | async-done | bytes 1343520 | tf_op jit(solution)/shard_map/all_to_all | solution.py:552
  134.6 0.9 shard_map.150
  (52 shorter events, 12.3 us)
Async XLA Ops:
  0.6 24.1 %copy-start = (bf16[64,128,128]{2,1,0:T(8,128)(2,1)S(1)}, bf16[64,128,128]{2,1,0:T(8,128)(2,1)}, u32[]{:S(2)}) copy-start(bf16[64,128,128]{2,1,0:T(8,128)(2,1)} %patterns_ref.9) | copy-start | bytes 6291460
  0.6 1.1 copy-start.14
  1.7 0.7 copy-start.17
  3.5 0.8 copy-start.7
  4.3 16.1 %all-to-all-start = ((bf16[8,256,128]{2,1,0:T(8,128)(2,1)}), bf16[8,256,128]{2,1,0:T(8,128)(2,1)S(1)}, u32[]{:S(2)}, u32[]{:S(2)}) async-start(bf16[8,256,128]{2,1,0:T(8,128)(2,1)} %get-tuple-element.35), calls=%async_computation | async-start | bytes 1048576 | tf_op jit(solution)/shard_map/all_to_all | solution.py:435
  10.9 0.7 copy-start.20
  11.5 0.7 copy-start.21
  12.2 0.7 copy-start.22
  20.4 4.3 %collective-permute-start = (bf16[2048,128]{1,0:T(8,128)(2,1)S(1)}, bf16[2048,128]{1,0:T(8,128)(2,1)}, u32[]{:S(2)}, u32[]{:S(2)}) collective-permute-start(bf16[2048,128]{1,0:T(8,128)(2,1)S(1)} %bitcast.12), channel_id=1, source_target_pairs={{0,8},{8,0},{16,24},{24,16},{32,40},{40,32},{48,56},{56,48},{64,72... | collective-permute-start | bytes 1572872 | tf_op jit(solution)/shard_map/ppermute | solution.py:452
  21.2 13.8 %all-to-all-start.1 = ((bf16[8,256,128]{2,1,0:T(8,128)(2,1)}), bf16[8,256,128]{2,1,0:T(8,128)(2,1)S(1)}, u32[]{:S(2)}, u32[]{:S(2)}) async-start(bf16[8,256,128]{2,1,0:T(8,128)(2,1)} %copy-done.7), calls=%async_computation.1 | async-start | bytes 1048576 | tf_op jit(solution)/shard_map/all_to_all | solution.py:436
  26.9 1.4 copy-start.3
  35.0 2.2 %collective-permute-start.1 = (bf16[2048,128]{1,0:T(8,128)(2,1)S(1)}, bf16[2048,128]{1,0:T(8,128)(2,1)S(1)}, u32[]{:S(2)}, u32[]{:S(2)}) collective-permute-start(bf16[2048,128]{1,0:T(8,128)(2,1)S(1)} %bitcast.14), channel_id=1, source_target_pairs={{0,8},{8,0},{16,24},{24,16},{32,40},{40,32},{48,56},{56,48},{64,72... | collective-permute-start | bytes 1572872 | tf_op jit(solution)/shard_map/ppermute | solution.py:465
  37.3 1.6 %copy-start.4 = (f32[4096,128]{1,0:T(8,128)S(1)}, f32[4096,128]{1,0:T(8,128)}, u32[]{:S(2)}) copy-start(f32[4096,128]{1,0:T(8,128)} %copy-done.3) | copy-start | bytes 6291460
  40.6 24.8 %copy-start.6 = (bf16[512,256]{1,0:T(8,128)(2,1)S(1)}, bf16[512,256]{1,0:T(8,128)(2,1)}, u32[]{:S(2)}) copy-start(bf16[512,256]{1,0:T(8,128)(2,1)} %cotangent_ref.3) | copy-start | bytes 786436
  40.6 24.8 %copy-start.13 = (bf16[128,256]{1,0:T(8,128)(2,1)S(1)}, bf16[128,256]{1,0:T(8,128)(2,1)}, u32[]{:S(2)}) copy-start(bf16[128,256]{1,0:T(8,128)(2,1)} %weight_ref.3) | copy-start | bytes 196612
  40.6 24.7 %copy-start.18 = (s32[512]{0:T(512)S(1)}, s32[512]{0:T(512)}, u32[]{:S(2)}) copy-start(s32[512]{0:T(512)} %param.12) | copy-start | bytes 6148
  40.6 24.7 %copy-start.19 = (f32[256]{0:T(256)S(1)}, f32[256]{0:T(256)}, u32[]{:S(2)}) copy-start(f32[256]{0:T(256)} %param.15) | copy-start | bytes 3076
  66.3 0.8 copy-start.8
  67.1 0.7 copy-start.9
  68.5 13.5 %all-to-all-start.3 = ((bf16[8,256,128]{2,1,0:T(8,128)(2,1)}), bf16[8,256,128]{2,1,0:T(8,128)(2,1)}, u32[]{:S(2)}, u32[]{:S(2)}) async-start(bf16[8,256,128]{2,1,0:T(8,128)(2,1)} %copy-done.8), calls=%async_computation.3 | async-start | bytes 1048576 | tf_op jit(solution)/shard_map/all_to_all | solution.py:491
  72.6 0.9 copy-start.16
  74.4 0.7 copy-start.11
  75.1 3.3 %collective-permute-start.2 = (bf16[144,128]{1,0:T(8,128)(2,1)S(1)}, bf16[144,128]{1,0:T(8,128)(2,1)S(1)}, u32[]{:S(2)}, u32[]{:S(2)}) collective-permute-start(bf16[144,128]{1,0:T(8,128)(2,1)S(1)} %get-tuple-element.45), channel_id=1, source_target_pairs={{0,8},{8,0},{16,24},{24,16},{32,40},{40,32},{48,56},{56,48},{64,72... | collective-permute-start | bytes 110600 | tf_op jit(solution)/shard_map/ppermute | solution.py:504
  78.4 0.9 copy-start.5
  82.0 16.4 %all-to-all-start.4 = ((bf16[8,400,128]{2,1,0:T(8,128)(2,1)}), bf16[8,400,128]{2,1,0:T(8,128)(2,1)S(1)}, u32[]{:S(2)}, u32[]{:S(2)}) async-start(bf16[8,400,128]{2,1,0:T(8,128)(2,1)} %copy-done.5), calls=%async_computation.4 | async-start | bytes 1638400 | tf_op jit(solution)/shard_map/all_to_all | solution.py:514
  89.2 2.0 %copy-start.1 = (f32[8192,128]{1,0:T(8,128)}, f32[8192,128]{1,0:T(8,128)S(1)}, u32[]{:S(2)}) copy-start(f32[8192,128]{1,0:T(8,128)S(1)} %shard_map.145.so_far_ref) | copy-start | bytes 12582916
  98.5 2.2 %copy-start.2 = (f32[8192,128]{1,0:T(8,128)S(1)}, f32[8192,128]{1,0:T(8,128)}, u32[]{:S(2)}) copy-start(f32[8192,128]{1,0:T(8,128)} %copy-done.1) | copy-start | bytes 12582916
  102.5 6.8 %collective-permute-start.3 = (bf16[4096,128]{1,0:T(8,128)(2,1)S(1)}, bf16[4096,128]{1,0:T(8,128)(2,1)S(1)}, u32[]{:S(2)}, u32[]{:S(2)}) collective-permute-start(bf16[4096,128]{1,0:T(8,128)(2,1)S(1)} %shard_map.146), channel_id=1, source_target_pairs={{0,8},{8,0},{16,24},{24,16},{32,40},{40,32},{48,56},{56,48},{64,72... | collective-permute-start | bytes 3145736 | tf_op jit(solution)/shard_map/ppermute | solution.py:534
  110.6 4.1 %copy-start.10 = (f32[256,256]{1,0:T(8,128)S(1)}, f32[256,256]{1,0:T(8,128)}, u32[]{:S(2)}) copy-start(f32[256,256]{1,0:T(8,128)} %copy-done.9) | copy-start | bytes 786436
  110.6 4.1 %copy-start.12 = (f32[256,256]{1,0:T(8,128)S(1)}, f32[256,256]{1,0:T(8,128)}, u32[]{:S(2)}) copy-start(f32[256,256]{1,0:T(8,128)} %copy-done.11) | copy-start | bytes 786436
  110.6 23.2 %all-to-all-start.5 = ((bf16[8,656,128]{2,1,0:T(8,128)(2,1)}), bf16[8,656,128]{2,1,0:T(8,128)(2,1)S(1)}, u32[]{:S(2)}, u32[]{:S(2)}) async-start(bf16[8,656,128]{2,1,0:T(8,128)(2,1)} %shard_map.148), calls=%async_computation.5 | async-start | bytes 2686976 | tf_op jit(solution)/shard_map/all_to_all | solution.py:552
  133.8 1.8 %collective-permute-start.4 = (f32[136,128]{1,0:T(8,128)S(1)}, f32[136,128]{1,0:T(8,128)S(1)}, u32[]{:S(2)}, u32[]{:S(2)}) collective-permute-start(f32[136,128]{1,0:T(8,128)S(1)} %shard_map.151.mine_ref), channel_id=1, source_target_pairs={{0,8},{8,0},{16,24},{24,16},{32,40},{40,32},{48,56},{56,48},{64,72... | collective-permute-start | bytes 208904 | tf_op jit(solution)/shard_map/ppermute | solution.py:569
  (2 other events, 1.3 us)

commit v4 on v2

--- a/solution.py
+++ b/solution.py
@@ -14,10 +14,11 @@
 CUBIC = 0.044715
 BIAS_ROWS = 16
 PER_SHARD = 4
+CLASSES = 2
 ORDERED = 640
 BOUNDS = 600
 PAIRS = (((0, 1), (2, 3)), ((0, 3), (1, 2)))
-ANY = pl.BlockSpec(memory_space=pl.ANY)
+HBM = pl.BlockSpec(memory_space=pltpu.HBM)
 VMEM = pl.BlockSpec(memory_space=pltpu.VMEM)
 SMEM = pl.BlockSpec(memory_space=pltpu.SMEM)
 PARAMS = pltpu.CompilerParams(vmem_limit_bytes=VMEM_LIMIT)
@@ -35,31 +36,39 @@
     return place ^ 3 if core == 0 else place ^ 1
 
 
-def order_kernel(place_ref, live_ref, row_ref, col_ref, pattern_ref, weight_ref, out_ref):
-    row, col = place_ref[0], place_ref[1]
-    core = row % 2
-    per_shard = PER_SHARD
-    rows, edge = row_ref.shape
-    tile_col, tile_row = col_ref[...], row_ref[...]
-    shard = tile_col // per_shard
+def order_kernel(
+    place_ref, live_ref, row_hbm, col_hbm, pattern_hbm, weight_hbm, out_ref, fields, sems
+):
+    sources = (row_hbm, col_hbm, pattern_hbm, weight_hbm)
+    copies = [
+        pltpu.make_async_copy(source, fields.at[index], sems.at[index])
+        for index, source in enumerate(sources)
+    ]
+    for copy in copies:
+        copy.start()
+    for copy in copies:
+        copy.wait()
+    row = place_ref[0]
+    _, rows, edge = fields.shape
+    tile_row, tile_col = fields[0], fields[1]
+    shard = tile_col // PER_SHARD
     parity = shard % 2
     chip = shard // 2
     ring = chip % 4
-    column_far = (pair_of(ring, parity) != pair_of((row // 2) % 4, parity)).astype(jnp.int32)
+    tile = tile_col % PER_SHARD
+    half = parity ^ (row % 2)
+    far = (pair_of(ring, parity) != pair_of((row // 2) % 4, parity)).astype(jnp.int32)
     rank = pair_index(ring, parity) * 2 + chip // 4
-    column = (((parity ^ core) * 2 + column_far) * 4 + rank) * per_shard + tile_col % per_shard
-    peer = tile_row // per_shard
-    row_far = (pair_of(peer // 2, core) != pair_of(col // 2, core)).astype(jnp.int32)
-    rank = pair_index(peer // 2, core) * 2 + peer % 2
-    source = (row_far * 4 + rank) * per_shard + tile_row % per_shard
-    word = tile_row | (pattern_ref[...] << 5) | (weight_ref[...] << 11) | (column << 14) | (source << 20)
+    place = (half * 4 + rank) * PER_SHARD + tile
+    target = (half * 8 + chip) * PER_SHARD + tile
+    word = tile_row | (fields[2] << 5) | (fields[3] << 11) | (place << 14) | (target << 19)
     slot = lax.broadcasted_iota(jnp.int32, (rows, edge), 0) * edge
     slot += lax.broadcasted_iota(jnp.int32, (rows, edge), 1)
     alive = slot < live_ref[0, 0]
     word = jnp.where(alive, word, 0)
-    kind = jnp.where(alive, column_far * 2 + row_far, 4)
-
-    flags = [(kind == index).astype(jnp.float32) for index in range(5)]
+    kind = jnp.where(alive, far, CLASSES)
+
+    flags = [(kind == index).astype(jnp.float32) for index in range(CLASSES + 1)]
     stacked = jnp.concatenate(flags + [jnp.zeros((4, edge), jnp.float32)], 0)
     before = lax.broadcasted_iota(jnp.int32, (edge, edge), 0) < lax.broadcasted_iota(
         jnp.int32, (edge, edge), 1
@@ -73,7 +82,7 @@
     start = jnp.zeros((1, 1), jnp.float32)
     ends = []
     position = [jnp.zeros((1, edge), jnp.float32) for _ in range(rows)]
-    for index in range(5):
+    for index in range(CLASSES + 1):
         for line in range(rows):
             at = index * rows + line
             position[line] += flags[index][line : line + 1] * (start + earlier[at : at + 1])
@@ -95,41 +104,9 @@
     )
     lane = lax.broadcasted_iota(jnp.int32, (1, out_ref.shape[1] - slots), 1) + slots
     tail = jnp.zeros(lane.shape, jnp.int32)
-    for index in range(4):
+    for index in range(CLASSES):
         tail = jnp.where(lane == BOUNDS + index, ends[index].astype(jnp.int32), tail)
     out_ref[:, slots:] = tail
-
-
-def add_products(slots_ref, runs, product_of, place_of, sums):
-    edge = sums.shape[1]
-    (first, end), (first_b, end_b) = runs
-    turns = (end - first + GROUP - 1) // GROUP
-    turns_b = (end_b - first_b + GROUP - 1) // GROUP
-
-    def one_group(turn, carry):
-        is_a = turn < turns
-        start = jnp.where(is_a, first + turn * GROUP, first_b + (turn - turns) * GROUP)
-        stop = jnp.where(is_a, end, end_b)
-        terms = []
-        for member in range(GROUP):
-            slot = start + member
-            word = slots_ref[0, slot]
-            factor = jnp.where(slot < stop, (word >> 11) & 7, 0).astype(jnp.float32)
-            terms.append((place_of(word), factor, product_of(word)))
-        for place, factor, product in terms:
-            rows = pl.ds(pl.multiple_of(place * edge, edge), edge)
-            sums[rows, :] += factor * product
-        return carry
-
-    lax.fori_loop(0, turns + turns_b, one_group, 0)
-
-
-def tile_of(ref, place, edge):
-    return ref[pl.ds(pl.multiple_of(place * edge, edge), edge), :]
-
-
-def class_bounds(slots_ref):
-    return [0] + [slots_ref[0, BOUNDS + index] for index in range(4)]
 
 
 def root_columns(degree):
@@ -157,23 +134,44 @@
             out_ref[copy, rows, :] = scaled
 
 
+def add_products(slots_ref, first, end, product_of, place_of, sums):
+    edge = sums.shape[1]
+
+    def one_group(turn, carry):
+        terms = []
+        for member in range(GROUP):
+            slot = first + turn * GROUP + member
+            word = slots_ref[0, slot]
+            factor = jnp.where(slot < end, (word >> 11) & 7, 0).astype(jnp.float32)
+            terms.append((place_of(word), factor, product_of(word)))
+        for place, factor, product in terms:
+            rows = pl.ds(pl.multiple_of(place * edge, edge), edge)
+            sums[rows, :] += factor * product
+        return carry
+
+    lax.fori_loop(0, (end - first + GROUP - 1) // GROUP, one_group, 0)
+
+
+def tile_of(ref, place, edge):
+    return ref[pl.ds(pl.multiple_of(place * edge, edge), edge), :]
+
+
 def forward_sums(slots_ref, patterns_ref, own_ref, other_ref, panel, sums, far):
     edge = patterns_ref.shape[1]
     half = own_ref.shape[0]
     panel[:half, :] = own_ref[...]
     panel[half:, :] = other_ref[...]
-    bounds = class_bounds(slots_ref)
+    middle, end = slots_ref[0, BOUNDS], slots_ref[0, BOUNDS + 1]
 
     def product_of(word):
-        place = ((word >> 15) & 16) | ((word >> 14) & 15)
         return jnp.dot(
             patterns_ref[(word >> 5) & 63],
-            tile_of(panel, place, edge),
+            tile_of(panel, (word >> 14) & 31, edge),
             preferred_element_type=jnp.float32,
         )
 
-    run = (bounds[2], bounds[4]) if far else (bounds[0], bounds[2])
-    add_products(slots_ref, (run, (0, 0)), product_of, lambda word: word & 31, sums)
+    first, end = (middle, end) if far else (0, middle)
+    add_products(slots_ref, first, end, product_of, lambda word: word & 31, sums)
 
 
 def forward_near_kernel(slots_ref, patterns_ref, own_ref, other_ref, out_ref, panel):
@@ -187,36 +185,28 @@
     out_ref[...] = sums[...].astype(jnp.bfloat16)
 
 
-def backward_sums(slots_ref, patterns_ref, panel_ref, sums, far):
+def backward_kernel(slots_ref, patterns_ref, spread_ref, keep_ref, send_ref, grads_ref, sums):
     edge = patterns_ref.shape[1]
-    bounds = class_bounds(slots_ref)
+    shards, rows_in_shard, _ = spread_ref.shape
+    half = sums.shape[0] // 2
+    own = rows_in_shard - grads_ref.shape[0]
+    sums[...] = jnp.zeros_like(sums)
 
     def product_of(word):
+        start = pl.multiple_of((word & 3) * edge, edge)
         return jnp.dot(
-            tile_of(panel_ref, (word >> 20) & 15, edge),
+            spread_ref[(word >> 2) & 7, pl.ds(start, edge), :],
             patterns_ref[(word >> 5) & 63],
             preferred_element_type=jnp.float32,
         )
 
-    runs = [(bounds[index], bounds[index + 1]) for index in ((1, 3) if far else (0, 2))]
-    add_products(slots_ref, runs, product_of, lambda word: (word >> 14) & 63, sums)
-
-
-def backward_near_kernel(slots_ref, patterns_ref, near_ref, out_ref):
-    out_ref[...] = jnp.zeros_like(out_ref)
-    backward_sums(slots_ref, patterns_ref, near_ref, out_ref, False)
-
-
-def backward_far_kernel(
-    slots_ref, patterns_ref, near_ref, far_ref, so_far_ref, keep_ref, send_ref, grads_ref, sums
-):
-    half = keep_ref.shape[0]
-    part = near_ref.shape[0] - grads_ref.shape[0]
-    sums[...] = so_far_ref[...]
-    backward_sums(slots_ref, patterns_ref, far_ref, sums, True)
+    end = slots_ref[0, BOUNDS + CLASSES - 1]
+    add_products(slots_ref, 0, end, product_of, lambda word: (word >> 19) & 63, sums)
     keep_ref[...] = sums[:half, :]
     send_ref[...] = sums[half:, :].astype(jnp.bfloat16)
-    grads = near_ref[part:, :].astype(jnp.float32) + far_ref[part:, :].astype(jnp.float32)
+    grads = spread_ref[0, own:, :].astype(jnp.float32)
+    for shard in range(1, shards):
+        grads += spread_ref[shard, own:, :].astype(jnp.float32)
     grads_ref[...] = grads.astype(jnp.bfloat16)
 
 
@@ -235,7 +225,7 @@
 
 
 def middle_kernel(
-    core_ref,
+    place_ref,
     parts_ref,
     degree_ref,
     cotangent_ref,
@@ -271,7 +261,7 @@
     width = keep_ref.shape[1]
     bias_high = bias_row.astype(jnp.bfloat16).astype(jnp.float32)
     bias_low = bias_row - bias_high
-    first = core_ref[0] == 0
+    first = place_ref[0] % 2 == 0
 
     def put(target, left):
         pick = lambda whole: jnp.where(left, whole[:, :width], whole[:, width:])
@@ -314,44 +304,22 @@
         out_ref[shard, rows, :] = terms
 
 
-def sum_of_four(parts_ref, rows):
-    part = lambda index: parts_ref[index, rows, :].astype(jnp.float32)
-    return (part(0) + part(2)) + (part(1) + part(3))
-
-
-def gather_kernel(parts_ref, out_ref):
-    shards, rows_in_shard, _ = parts_ref.shape
-    extra = (shards * rows_in_shard - out_ref.shape[0]) // (shards - 1)
-    own = rows_in_shard - extra
-    for shard in range(shards):
-        out_ref[pl.ds(shard * own, own), :] = parts_ref[shard, :own, :]
-    out_ref[shards * own :, :] = sum_of_four(parts_ref, pl.ds(own, extra)).astype(jnp.bfloat16)
-
-
-def split_kernel(keep_ref, got_ref, grads_ref, near_ref, far_ref):
-    half = near_ref.shape[0]
-    near_ref[...] = keep_ref[:half, :] + got_ref[:half, :].astype(jnp.float32)
-    far = keep_ref[half:, :] + got_ref[half:, :].astype(jnp.float32)
-    far_ref[:half, :] = far.astype(jnp.bfloat16)
-    far_ref[half:, :] = grads_ref[...]
-
-
-def join_kernel(near_ref, got_ref, grads_ref, out_ref):
+def join_kernel(keep_ref, got_ref, grads_ref, out_ref):
     shards = out_ref.shape[0]
-    half = near_ref.shape[0]
-    own = half // shards
-    grads = grads_ref[...].astype(jnp.float32) + got_ref[half:, :].astype(jnp.float32)
-    grads = grads.astype(jnp.bfloat16)
+    own = keep_ref.shape[0] // shards
     for shard in range(shards):
         rows = pl.ds(shard * own, own)
-        total = near_ref[rows, :] + got_ref[rows, :].astype(jnp.float32)
+        total = keep_ref[rows, :] + got_ref[rows, :].astype(jnp.float32)
         out_ref[shard, pl.ds(0, own), :] = total.astype(jnp.bfloat16)
-        out_ref[shard, pl.ds(own, grads.shape[0]), :] = grads
+        out_ref[shard, pl.ds(own, grads_ref.shape[0]), :] = grads_ref[...]
 
 
 def total_kernel(scale_factor, parts_ref, half_ref):
-    extra = half_ref.shape[0] - 8 + BIAS_ROWS
-    tail = sum_of_four(parts_ref, pl.ds(parts_ref.shape[1] - extra, extra))
+    shards = parts_ref.shape[0]
+    own = parts_ref.shape[1] - (half_ref.shape[0] - 8 + BIAS_ROWS)
+    tail = parts_ref[0, own:, :].astype(jnp.float32)
+    for shard in range(1, shards):
+        tail += parts_ref[shard, own:, :].astype(jnp.float32)
     tail = tail * scale_factor
     height = half_ref.shape[0] - 8
     half_ref[:height, :] = tail[:height, :]
@@ -364,12 +332,14 @@
     roots = lax.rsqrt(degree_ref[...].astype(jnp.float32))
     for tile in range(tiles):
         rows = pl.ds(tile * edge, edge)
-        total = sum_of_four(parts_ref, rows)
+        total = parts_ref[0, rows, :].astype(jnp.float32)
+        for shard in range(1, parts_ref.shape[0]):
+            total += parts_ref[shard, rows, :].astype(jnp.float32)
         features_ref[rows, :] = (total * roots[tile : tile + 1, :]).T.astype(jnp.bfloat16)
 
 
-def lay_out_kernel(core_ref, mine_ref, other_ref, grads_ref, bias_ref):
-    first = core_ref[0] == 0
+def lay_out_kernel(place_ref, mine_ref, other_ref, grads_ref, bias_ref):
+    first = place_ref[0] % 2 == 0
     height = grads_ref.shape[0]
     width = mine_ref.shape[1]
     mine, other = mine_ref[...], other_ref[...]
@@ -400,8 +370,7 @@
     chips = row_devices // 2
     edge = patterns.shape[1]
     per_shard = node_dev // edge
-    row, col = lax.axis_index("row"), lax.axis_index("col")
-    core = row % 2
+    row = lax.axis_index("row")
     swap = [(index, index ^ 1) for index in range(row_devices)]
     row_near = [
         [(low * 4 + ring) * 2 + core_index for ring in pair for low in range(2)]
@@ -412,21 +381,8 @@
         (index, (index // 8 * 4 + far_neighbour(index // 2 % 4, index % 2)) * 2 + index % 2)
         for index in range(row_devices)
     ]
-    col_near = [
-        [index * col_devices + ring * 2 + high for ring in pair for high in range(2)]
-        for index in range(row_devices)
-        for pair in PAIRS[index % 2]
-    ]
-    col_far = [
-        (
-            index * col_devices + place,
-            index * col_devices + far_neighbour(place // 2, index % 2) * 2 + place % 2,
-        )
-        for index in range(row_devices)
-        for place in range(col_devices)
-    ]
     exchange = functools.partial(lax.all_to_all, split_axis=0, concat_axis=0)
-    both = ("row", "col")
+    same_core = [list(range(first, row_devices, 2)) for first in range(2)]
     extra = feature_count + BIAS_ROWS
     half = chips * node_dev
     bf16, f32 = jnp.bfloat16, jnp.float32
@@ -441,7 +397,7 @@
     scaled = pl.pallas_call(
         scale_kernel,
         out_shape=shape((4, node_dev, feature_count), bf16),
-        in_specs=[ANY] * 2,
+        in_specs=[HBM] * 2,
         out_specs=VMEM,
         scratch_shapes=[
             pltpu.VMEM(features.shape, bf16),
@@ -454,12 +410,16 @@
     near_other = lax.ppermute(near_own, "row", swap)
     far_own = lax.ppermute(near_own, "row", row_far)
     row_tiles, near_own = lax.optimization_barrier((tile_row.reshape(per_shard, edge), near_own))
-    place = jnp.stack([row, col]).astype(jnp.int32)
+    place = row.astype(jnp.int32).reshape(1)
     slots = pl.pallas_call(
         order_kernel,
         out_shape=shape((1, ORDERED), jnp.int32),
-        in_specs=[SMEM] * 2 + [VMEM] * 4,
-        out_specs=VMEM,
+        in_specs=[SMEM] * 2 + [HBM] * 4,
+        out_specs=VMEM,
+        scratch_shapes=[
+            pltpu.VMEM((4, per_shard, edge), jnp.int32),
+            pltpu.SemaphoreType.DMA((4,)),
+        ],
         compiler_params=PARAMS,
     )(
         place,
@@ -492,7 +452,6 @@
         cost_estimate=tile_cost,
     )(slots, patterns, far_own, far_other, near_sums)
     parts = exchange(row_part.reshape(col_devices, node_dev, feature_count), "col")
-    core_word = core.astype(jnp.int32).reshape(1)
     pre_act, upstream, keep_terms, send_terms = pl.pallas_call(
         middle_kernel,
         out_shape=(
@@ -504,11 +463,11 @@
         in_specs=[SMEM] + [VMEM] * 5,
         out_specs=(VMEM,) * 4,
         compiler_params=PARAMS,
-    )(core_word, parts, degree_tiles, cotangent, weight, layer_bias[None, :])
+    )(place, parts, degree_tiles, cotangent, weight, layer_bias[None, :])
     got_terms = lax.ppermute(send_terms, "row", swap)
     spread = pl.pallas_call(
         spread_kernel,
-        out_shape=shape((4, node_dev + extra, edge), bf16),
+        out_shape=shape((col_devices, node_dev + extra, edge), bf16),
         in_specs=[VMEM] * 2,
         out_specs=VMEM,
         compiler_params=PARAMS,
@@ -521,61 +480,38 @@
         input_output_aliases={2: 0},
         compiler_params=PARAMS,
     )(keep_terms, got_terms, spread)
-    near = pl.pallas_call(
-        gather_kernel,
-        out_shape=shape((4 * node_dev + extra, edge), bf16),
-        in_specs=[VMEM],
-        out_specs=VMEM,
-        compiler_params=PARAMS,
-    )(exchange(spread, both, axis_index_groups=col_near))
-    pre_act, near = lax.optimization_barrier((pre_act, near))
-    far = lax.ppermute(near, both, col_far)
-    activations = pl.pallas_call(
-        activation_kernel,
-        out_shape=shape((node_dev, hidden), bf16),
-        in_specs=[VMEM],
-        out_specs=VMEM,
-        compiler_params=PARAMS,
-    )(pre_act)
-    back_sums = shape((2 * half, edge), f32)
-    back_near = pl.pallas_call(
-        backward_near_kernel,
-        out_shape=back_sums,
-        in_specs=[SMEM] + [VMEM] * 2,
-        out_specs=VMEM,
-        compiler_params=PARAMS,
-        cost_estimate=tile_cost,
-    )(slots, patterns, near)
-    far, activations, back_near = lax.optimization_barrier((far, activations, back_near))
+    spread_all = exchange(spread, "col")
     keep, send, grads = pl.pallas_call(
-        backward_far_kernel,
+        backward_kernel,
         out_shape=(
             shape((half, edge), f32),
             shape((half, edge), bf16),
             shape((extra, edge), bf16),
         ),
-        in_specs=[SMEM] + [VMEM] * 4,
+        in_specs=[SMEM] + [VMEM] * 2,
         out_specs=(VMEM,) * 3,
-        scratch_shapes=[pltpu.VMEM(back_sums.shape, f32)],
+        scratch_shapes=[pltpu.VMEM((2 * half, edge), f32)],
         compiler_params=PARAMS,
         cost_estimate=tile_cost,
-    )(slots, patterns, near, far, back_near)
+    )(slots, patterns, spread_all)
     got = lax.ppermute(send, "row", swap)
-    near_sums, far_sums = pl.pallas_call(
-        split_kernel,
-        out_shape=(shape((half // 2, edge), f32), shape((half // 2 + extra, edge), bf16)),
-        in_specs=[VMEM] * 3,
-        out_specs=(VMEM,) * 2,
-        compiler_params=PARAMS,
-    )(keep, got, grads)
+    pre_act, keep = lax.optimization_barrier((pre_act, keep))
+    activations = pl.pallas_call(
+        activation_kernel,
+        out_shape=shape((node_dev, hidden), bf16),
+        in_specs=[VMEM],
+        out_specs=VMEM,
+        compiler_params=PARAMS,
+    )(pre_act)
+    got, activations = lax.optimization_barrier((got, activations))
     joined = pl.pallas_call(
         join_kernel,
-        out_shape=shape((4, node_dev + extra, edge), bf16),
+        out_shape=shape((chips, node_dev + extra, edge), bf16),
         in_specs=[VMEM] * 3,
         out_specs=VMEM,
         compiler_params=PARAMS,
-    )(near_sums, lax.ppermute(far_sums, "row", row_far), grads)
-    back_parts = exchange(joined, "row", axis_index_groups=row_near)
+    )(keep, got, grads)
+    back_parts = exchange(joined, "row", axis_index_groups=same_core)
     scale_factor = 1.0 / math.sqrt(node_dev * row_devices * col_devices)
     mine = pl.pallas_call(
         functools.partial(total_kernel, scale_factor),
@@ -598,7 +534,7 @@
         in_specs=[SMEM] + [VMEM] * 2,
         out_specs=(VMEM,) * 2,
         compiler_params=PARAMS,
-    )(core_word, mine, other)
+    )(place, mine, other)
     return (activations, grad_features, grad_weight, grad_bias[0])
 
 

time: 119 us -> 118 us (level); the launches traced: 117 us -> 118 us
  blocking collectives: 40.3 us -> 86 us
  waiting for transfers between devices: 33.9 us -> 6.42 us
  starting transfers between devices: 18.4 us -> 6.92 us
  Pallas kernels: 17.1 us -> 14 us
  local copies, waits for them, and re-layouts: 5.91 us -> 3.22 us
    all_to_all x2 -> x3, blocking collectives: 26.5 us -> 72.2 us  [the longest x1 26.6 us: per_device(): back_parts = exchange(joined, 'row', axis_index_groups=same_core)]
    all_to_all x1 -> x0, waiting for transfers between devices: 15.4 us -> none  [per_device(): exchange(row_part.reshape(col_devices, node_dev, feature_count), 'col')]
    ppermute x2 -> x0, waiting for transfers between devices: 14 us -> none  [the longest x1 8.71 us: per_device(): lax.ppermute(far_sums, 'row', row_far)]
    all_to_all x1 -> x0, starting transfers between devices: 9.1 us -> none  [per_device(): exchange(row_part.reshape(col_devices, node_dev, feature_count), 'col')]
    unnamed x24, local copies, waits for them, and re-layouts: 5.91 us -> 3.22 us
    ppermute x1, waiting for transfers between devices: 0.01 us -> 2.66 us  [per_device(): far_own = lax.ppermute(near_own, 'row', row_far)]
    pallas_call x6 -> x3, Pallas kernels: 6.18 us -> 4.37 us  [the longest x1 3.8 us: per_device(): pl.pallas_call(backward_kernel, out_shape=(shape((half, edge), f32), shap...]
    ppermute x1, starting transfers between devices: 2.82 us -> 1.14 us  [per_device(): other = lax.ppermute(mine, 'row', swap)]
  transfers between devices with their start and end apart: 9 -> 6, of which waited for: 7 -> 5; matrix products, arithmetic and copies ran while one was open for 0% -> 0% of each run, Pallas kernels for 7% -> 4%
where the time goes in v4:
time: 118 us
  blocking collectives  86 us (73%)
  Pallas kernels  14 us (12%)
  starting transfers between devices  6.92 us (6%)
  waiting for transfers between devices  6.42 us (5%)
  local copies, waits for them, and re-layouts  3.22 us (3%)
  between operations  1.45 us (1%)
    all_to_all x1, blocking collectives, per_device(): back_parts = exchange(joined, 'row', axis_index_groups=same_core)  26.6 us
    all_to_all x1, blocking collectives, per_device(): exchange(row_part.reshape(col_devices, node_dev, feature_count), 'col')  23 us
    all_to_all x1, blocking collectives, per_device(): spread_all = exchange(spread, 'col')  22.6 us
    all_to_all x1, blocking collectives, per_device(): exchange(scaled, 'row', axis_index_groups=row_near)  13.8 us
    pallas_call x1, Pallas kernels, per_device(): pl.pallas_call(backward_kernel, out_shape=(shape((half, edge), f32), shap...  3.8 us
    unnamed x24, local copies, waits for them, and re-layouts  3.22 us
    ppermute x1, waiting for transfers between devices, per_device(): far_own = lax.ppermute(near_own, 'row', row_far)  2.66 us
    pallas_call x1, Pallas kernels, per_device(): pl.pallas_call(forward_far_kernel, out_shape=shape(row_sums.shape, bf16),...  2.65 us
  transfers between devices with their start and end apart: 6, of which 5 were waited for; matrix products, arithmetic and copies ran while one was open for 0% of the time, Pallas kernels for 4%

profile of v4, /device:TPU:1, one launch (start us, length us, event | category | flops | bytes accessed | tf_op | source)
XLA Modules:
  0.0 118.0 jit_solution(13636066720464179478)
XLA Ops:
  0.6 0.9 copy-done.4
  1.5 0.7 copy-done.5
  2.2 0.4 shard_map.138
  2.7 13.8 %all_to_all.20 = bf16[4,512,128]{2,1,0:T(8,128)(2,1)S(1)} all-to-all(bf16[4,512,128]{2,1,0:T(8,128)(2,1)S(1)} %shard_map.138), channel_id=1, replica_groups={{0,64,16,80},{32,96,48,112},{8,72,56,120},{24,88,40,104},{1,65,17,81},{..., dimensions={0} | all-to-all | bytes 1048576 | tf_op jit(solution)/shard_map/all_to_all | solution.py:409
  16.5 0.5 collective-permute-start.1
  17.7 0.6 shard_map.139.slots_ref
  18.3 0.2 collective-permute-done.1.other_ref
  18.5 1.6 %copy-done = bf16[64,128,128]{2,1,0:T(8,128)(2,1)S(1)} copy-done((bf16[64,128,128]{2,1,0:T(8,128)(2,1)S(1)}, bf16[64,128,128]{2,1,0:T(8,128)(2,1)}, u32[]{:S(2)}) %copy-start) | copy-done | bytes 2097176
  20.1 2.5 %shard_map.140.so_far_ref = f32[4096,128]{1,0:T(8,128)S(1)} custom-call(s32[1,640]{1,0:T(1,128)S(1)} %shard_map.139.slots_ref, bf16[64,128,128]{2,1,0:T(8,128)(2,1)S(1)} %copy-done, bf16[2048,128]{1,0:T(8,128)(2,1)S(1)} %bitcast.13, bf16[2048,128]{1,0:T(8,128)(2,1)S(1)} %collective-permute-done.1.other_ref), custom_call_target="tpu_custom_call" | custom-call | flops 8388608 | bytes 6291456 | tf_op jit(solution)/shard_map/pallas_call | solution.py:434
  22.7 2.7 %collective-permute-done.own_ref = bf16[2048,128]{1,0:T(8,128)(2,1)S(1)} collective-permute-done((bf16[2048,128]{1,0:T(8,128)(2,1)S(1)}, bf16[2048,128]{1,0:T(8,128)(2,1)S(1)}, u32[]{:S(2)}, u32[]{:S(2)}) %collective-permute-start) | collective-permute-done | bytes 524320 | tf_op jit(solution)/shard_map/ppermute | solution.py:411
  25.3 2.1 %collective-permute-start.2 = (bf16[2048,128]{1,0:T(8,128)(2,1)S(1)}, bf16[2048,128]{1,0:T(8,128)(2,1)S(1)}, u32[]{:S(2)}, u32[]{:S(2)}) collective-permute-start(bf16[2048,128]{1,0:T(8,128)(2,1)S(1)} %collective-permute-done.own_ref), channel_id=1, source_target_pairs={{0,8},{8,0},{16,24},{24,16},{32,40},{40,32},{48,56},{56,48},{64,72... | collective-permute-start | bytes 1572872 | tf_op jit(solution)/shard_map/ppermute | solution.py:444
  27.4 1.5 %collective-permute-done.2.other_ref = bf16[2048,128]{1,0:T(8,128)(2,1)S(1)} collective-permute-done((bf16[2048,128]{1,0:T(8,128)(2,1)S(1)}, bf16[2048,128]{1,0:T(8,128)(2,1)S(1)}, u32[]{:S(2)}, u32[]{:S(2)}) %collective-permute-start.2) | collective-permute-done | bytes 524320 | tf_op jit(solution)/shard_map/ppermute | solution.py:444
  28.9 2.7 %shard_map.141 = bf16[4096,128]{1,0:T(8,128)(2,1)S(1)} custom-call(s32[1,640]{1,0:T(1,128)S(1)} %shard_map.139.slots_ref, bf16[64,128,128]{2,1,0:T(8,128)(2,1)S(1)} %copy-done, bf16[2048,128]{1,0:T(8,128)(2,1)S(1)} %collective-permute-done.own_ref, bf16[2048,128]{1,0:T(8,128)(2,1)S(1)} %collective-permute-done.2.other_ref, f32[4096,128]{1,0:T(8,128)S(1)} %shard_map.140.so_far_ref), custom_call_target="tpu_custom_call" | custom-call | flops 8388608 | bytes 6291456 | tf_op jit(solution)/shard_map/pallas_call | solution.py:445
  31.6 0.0 copy-start.2
  31.6 0.0 copy-start.3
  31.6 0.0 copy-start.6
  31.6 23.0 %all_to_all.21.parts_ref = bf16[8,512,128]{2,1,0:T(8,128)(2,1)S(1)} all-to-all(bf16[8,512,128]{2,1,0:T(8,128)(2,1)S(1)} %bitcast.10), channel_id=1, replica_groups=mesh['row'=16,'col'=8] {'col'}, dimensions={0} | all-to-all | bytes 2097152 | tf_op jit(solution)/shard_map/all_to_all | solution.py:454
  54.6 0.9 shard_map.142
  55.5 2.6 %collective-permute-start.3 = (bf16[144,128]{1,0:T(8,128)(2,1)S(1)}, bf16[144,128]{1,0:T(8,128)(2,1)S(1)}, u32[]{:S(2)}, u32[]{:S(2)}) collective-permute-start(bf16[144,128]{1,0:T(8,128)(2,1)S(1)} %get-tuple-element.26), channel_id=1, source_target_pairs={{0,8},{8,0},{16,24},{24,16},{32,40},{40,32},{48,56},{56,48},{64,72... | collective-permute-start | bytes 110600 | tf_op jit(solution)/shard_map/ppermute | solution.py:467
  58.1 0.3 shard_map.143.spread_ref
  58.4 0.5 collective-permute-done.3.got_ref
  59.0 22.6 %all_to_all.22.spread_ref = bf16[8,656,128]{2,1,0:T(8,128)(2,1)S(1)} all-to-all(bf16[8,656,128]{2,1,0:T(8,128)(2,1)S(1)} %shard_map.144), channel_id=1, replica_groups=mesh['row'=16,'col'=8] {'col'}, dimensions={0} | all-to-all | bytes 2686976 | tf_op jit(solution)/shard_map/all_to_all | solution.py:483
  81.6 3.8 %shard_map.145 = (f32[4096,128]{1,0:T(8,128)S(1)}, bf16[4096,128]{1,0:T(8,128)(2,1)S(1)}, bf16[144,128]{1,0:T(8,128)(2,1)S(1)}) custom-call(s32[1,640]{1,0:T(1,128)S(1)} %shard_map.139.slots_ref, bf16[64,128,128]{2,1,0:T(8,128)(2,1)S(1)} %copy-done.1, bf16[8,656,128]{2,1,0:T(8,128)(2,1)S(1)} %all_to_all.22.spread_ref), custom_call_target="tpu_custom_call" | custom-call | flops 8388608 | bytes 6291456 | tf_op jit(solution)/shard_map/pallas_call | solution.py:484
  85.4 0.6 collective-permute-start.4
  86.0 0.9 shard_map.146
  86.9 1.4 %collective-permute-done.4.got_ref = bf16[4096,128]{1,0:T(8,128)(2,1)S(1)} collective-permute-done((bf16[4096,128]{1,0:T(8,128)(2,1)S(1)}, bf16[4096,128]{1,0:T(8,128)(2,1)S(1)}, u32[]{:S(2)}, u32[]{:S(2)}) %collective-permute-start.4) | collective-permute-done | bytes 1048608 | tf_op jit(solution)/shard_map/ppermute | solution.py:497
  88.3 0.3 shard_map.147
  88.6 26.6 %all_to_all.23.parts_ref = bf16[8,656,128]{2,1,0:T(8,128)(2,1)S(1)} all-to-all(bf16[8,656,128]{2,1,0:T(8,128)(2,1)S(1)} %shard_map.147), channel_id=1, replica_groups={{0,16,32,48,64,80,96,112},{8,24,40,56,72,88,104,120},{1,17,33,49,65,81,..., dimensions={0} | all-to-all | bytes 2686976 | tf_op jit(solution)/shard_map/all_to_all | solution.py:514
  115.3 1.1 collective-permute-start.5
  116.4 0.9 shard_map.148
  117.3 0.0 collective-permute-done.5.other_ref
  117.3 0.7 shard_map.150
  (21 shorter events, 0.1 us)
Async XLA Ops:
  0.6 0.9 copy-start.4
  1.5 0.7 copy-start.5
  2.2 15.4 %copy-start.7 = (s32[1,1,512]{2,1,0:T(1,128)S(1)}, s32[1,1,512]{2,1,0:T(1,128)}, u32[]{:S(2)}) copy-start(s32[1,1,512]{2,1,0:T(1,128)} %param.17) | copy-start | bytes 6148
  2.2 15.4 %copy-start.8 = (s32[1,1,512]{2,1,0:T(1,128)S(1)}, s32[1,1,512]{2,1,0:T(1,128)}, u32[]{:S(2)}) copy-start(s32[1,1,512]{2,1,0:T(1,128)} %param.18) | copy-start | bytes 6148
  2.2 15.4 %copy-start.9 = (s32[1,1,512]{2,1,0:T(1,128)S(1)}, s32[1,1,512]{2,1,0:T(1,128)}, u32[]{:S(2)}) copy-start(s32[1,1,512]{2,1,0:T(1,128)} %param.19) | copy-start | bytes 6148
  2.2 15.5 %copy-start.10 = (s32[1,1,512]{2,1,0:T(1,128)S(1)}, s32[1,1,512]{2,1,0:T(1,128)}, u32[]{:S(2)}) copy-start(s32[1,1,512]{2,1,0:T(1,128)} %param.20) | copy-start | bytes 6148
  16.5 2.1 %collective-permute-start.1 = (bf16[2048,128]{1,0:T(8,128)(2,1)S(1)}, bf16[2048,128]{1,0:T(8,128)(2,1)S(1)}, u32[]{:S(2)}, u32[]{:S(2)}) collective-permute-start(bf16[2048,128]{1,0:T(8,128)(2,1)S(1)} %bitcast.11), channel_id=1, source_target_pairs={{0,8},{8,0},{16,24},{24,16},{32,40},{40,32},{48,56},{56,48},{64,72... | collective-permute-start | bytes 1572872 | tf_op jit(solution)/shard_map/ppermute | solution.py:410
  17.0 8.3 %collective-permute-start = (bf16[2048,128]{1,0:T(8,128)(2,1)S(1)}, bf16[2048,128]{1,0:T(8,128)(2,1)S(1)}, u32[]{:S(2)}, u32[]{:S(2)}) collective-permute-start(bf16[2048,128]{1,0:T(8,128)(2,1)S(1)} %bitcast.12), channel_id=1, source_target_pairs={{0,48},{8,24},{16,32},{24,8},{32,16},{40,56},{48,0},{56,40},{64,11... | collective-permute-start | bytes 1572872 | tf_op jit(solution)/shard_map/ppermute | solution.py:411
  18.5 1.6 %copy-start = (bf16[64,128,128]{2,1,0:T(8,128)(2,1)S(1)}, bf16[64,128,128]{2,1,0:T(8,128)(2,1)}, u32[]{:S(2)}) copy-start(bf16[64,128,128]{2,1,0:T(8,128)(2,1)} %patterns_ref.5) | copy-start | bytes 6291460
  25.3 3.6 %collective-permute-start.2 = (bf16[2048,128]{1,0:T(8,128)(2,1)S(1)}, bf16[2048,128]{1,0:T(8,128)(2,1)S(1)}, u32[]{:S(2)}, u32[]{:S(2)}) collective-permute-start(bf16[2048,128]{1,0:T(8,128)(2,1)S(1)} %collective-permute-done.own_ref), channel_id=1, source_target_pairs={{0,8},{8,0},{16,24},{24,16},{32,40},{40,32},{48,56},{56,48},{64,72... | collective-permute-start | bytes 1572872 | tf_op jit(solution)/shard_map/ppermute | solution.py:444
  31.6 23.0 %copy-start.2 = (bf16[512,256]{1,0:T(8,128)(2,1)S(1)}, bf16[512,256]{1,0:T(8,128)(2,1)}, u32[]{:S(2)}) copy-start(bf16[512,256]{1,0:T(8,128)(2,1)} %cotangent_ref.1) | copy-start | bytes 786436
  31.6 23.0 %copy-start.3 = (bf16[128,256]{1,0:T(8,128)(2,1)S(1)}, bf16[128,256]{1,0:T(8,128)(2,1)}, u32[]{:S(2)}) copy-start(bf16[128,256]{1,0:T(8,128)(2,1)} %weight_ref.3) | copy-start | bytes 196612
  31.6 23.0 %copy-start.6 = (s32[512]{0:T(512)S(1)}, s32[512]{0:T(512)}, u32[]{:S(2)}) copy-start(s32[512]{0:T(512)} %param.12) | copy-start | bytes 6148
  31.6 23.0 %copy-start.11 = (f32[256]{0:T(256)S(1)}, f32[256]{0:T(256)}, u32[]{:S(2)}) copy-start(f32[256]{0:T(256)} %param.15) | copy-start | bytes 3076
  55.5 3.4 %collective-permute-start.3 = (bf16[144,128]{1,0:T(8,128)(2,1)S(1)}, bf16[144,128]{1,0:T(8,128)(2,1)S(1)}, u32[]{:S(2)}, u32[]{:S(2)}) collective-permute-start(bf16[144,128]{1,0:T(8,128)(2,1)S(1)} %get-tuple-element.26), channel_id=1, source_target_pairs={{0,8},{8,0},{16,24},{24,16},{32,40},{40,32},{48,56},{56,48},{64,72... | collective-permute-start | bytes 110600 | tf_op jit(solution)/shard_map/ppermute | solution.py:467
  59.0 22.6 %copy-start.1 = (bf16[64,128,128]{2,1,0:T(8,128)(2,1)S(1)}, bf16[64,128,128]{2,1,0:T(8,128)(2,1)}, u32[]{:S(2)}) copy-start(bf16[64,128,128]{2,1,0:T(8,128)(2,1)} %patterns_ref.5) | copy-start | bytes 6291460
  85.4 2.9 %collective-permute-start.4 = (bf16[4096,128]{1,0:T(8,128)(2,1)S(1)}, bf16[4096,128]{1,0:T(8,128)(2,1)S(1)}, u32[]{:S(2)}, u32[]{:S(2)}) collective-permute-start(bf16[4096,128]{1,0:T(8,128)(2,1)S(1)} %get-tuple-element.28), channel_id=1, source_target_pairs={{0,8},{8,0},{16,24},{24,16},{32,40},{40,32},{48,56},{56,48},{64,72... | collective-permute-start | bytes 3145736 | tf_op jit(solution)/shard_map/ppermute | solution.py:497
  115.3 2.1 %collective-permute-start.5 = (f32[136,128]{1,0:T(8,128)S(1)}, f32[136,128]{1,0:T(8,128)S(1)}, u32[]{:S(2)}, u32[]{:S(2)}) collective-permute-start(f32[136,128]{1,0:T(8,128)S(1)} %shard_map.149.mine_ref), channel_id=1, source_target_pairs={{0,8},{8,0},{16,24},{24,16},{32,40},{40,32},{48,56},{56,48},{64,72... | collective-permute-start | bytes 208904 | tf_op jit(solution)/shard_map/ppermute | solution.py:523

commit v5 on v4

--- a/solution.py
+++ b/solution.py
@@ -60,8 +60,7 @@
     far = (pair_of(ring, parity) != pair_of((row // 2) % 4, parity)).astype(jnp.int32)
     rank = pair_index(ring, parity) * 2 + chip // 4
     place = (half * 4 + rank) * PER_SHARD + tile
-    target = (half * 8 + chip) * PER_SHARD + tile
-    word = tile_row | (fields[2] << 5) | (fields[3] << 11) | (place << 14) | (target << 19)
+    word = tile_row | (fields[2] << 5) | (fields[3] << 11) | (place << 14)
     slot = lax.broadcasted_iota(jnp.int32, (rows, edge), 0) * edge
     slot += lax.broadcasted_iota(jnp.int32, (rows, edge), 1)
     alive = slot < live_ref[0, 0]
@@ -94,14 +93,12 @@
     pieces = jnp.zeros((8, slots), jnp.float32)
     for line in range(rows):
         chosen = (turned[:, line : line + 1] == lanes).astype(jnp.float32).astype(jnp.bfloat16)
-        parts = [(word[line : line + 1] >> shift) & 127 for shift in (0, 7, 14, 21)]
-        parts = jnp.concatenate(parts + [jnp.zeros((4, edge), jnp.int32)], 0)
+        parts = [(word[line : line + 1] >> shift) & 127 for shift in (0, 7, 14)]
+        parts = jnp.concatenate(parts + [jnp.zeros((5, edge), jnp.int32)], 0)
         parts = parts.astype(jnp.float32).astype(jnp.bfloat16)
         pieces += jnp.dot(parts, chosen, preferred_element_type=jnp.float32)
     pieces = pieces.astype(jnp.int32)
-    out_ref[:, :slots] = (
-        pieces[0:1] | (pieces[1:2] << 7) | (pieces[2:3] << 14) | (pieces[3:4] << 21)
-    )
+    out_ref[:, :slots] = pieces[0:1] | (pieces[1:2] << 7) | (pieces[2:3] << 14)
     lane = lax.broadcasted_iota(jnp.int32, (1, out_ref.shape[1] - slots), 1) + slots
     tail = jnp.zeros(lane.shape, jnp.int32)
     for index in range(CLASSES):
@@ -185,12 +182,11 @@
     out_ref[...] = sums[...].astype(jnp.bfloat16)
 
 
-def backward_kernel(slots_ref, patterns_ref, spread_ref, keep_ref, send_ref, grads_ref, sums):
+def backward_sums(slots_ref, patterns_ref, spread_ref, keep_ref, send_ref, sums, far):
     edge = patterns_ref.shape[1]
-    shards, rows_in_shard, _ = spread_ref.shape
     half = sums.shape[0] // 2
-    own = rows_in_shard - grads_ref.shape[0]
     sums[...] = jnp.zeros_like(sums)
+    middle, end = slots_ref[0, BOUNDS], slots_ref[0, BOUNDS + 1]
 
     def product_of(word):
         start = pl.multiple_of((word & 3) * edge, edge)
@@ -200,14 +196,23 @@
             preferred_element_type=jnp.float32,
         )
 
-    end = slots_ref[0, BOUNDS + CLASSES - 1]
-    add_products(slots_ref, 0, end, product_of, lambda word: (word >> 19) & 63, sums)
+    first, end = (middle, end) if far else (0, middle)
+    add_products(slots_ref, first, end, product_of, lambda word: (word >> 14) & 31, sums)
     keep_ref[...] = sums[:half, :]
     send_ref[...] = sums[half:, :].astype(jnp.bfloat16)
+
+
+def backward_far_kernel(slots_ref, patterns_ref, spread_ref, keep_ref, send_ref, grads_ref, sums):
+    backward_sums(slots_ref, patterns_ref, spread_ref, keep_ref, send_ref, sums, True)
+    own = spread_ref.shape[1] - grads_ref.shape[0]
     grads = spread_ref[0, own:, :].astype(jnp.float32)
-    for shard in range(1, shards):
+    for shard in range(1, spread_ref.shape[0]):
         grads += spread_ref[shard, own:, :].astype(jnp.float32)
     grads_ref[...] = grads.astype(jnp.bfloat16)
+
+
+def backward_near_kernel(slots_ref, patterns_ref, spread_ref, keep_ref, send_ref, sums):
+    backward_sums(slots_ref, patterns_ref, spread_ref, keep_ref, send_ref, sums, False)
 
 
 def split_product(left, right, dims):
@@ -304,22 +309,34 @@
         out_ref[shard, rows, :] = terms
 
 
-def join_kernel(keep_ref, got_ref, grads_ref, out_ref):
+def sum_of_four(parts_ref, rows):
+    part = lambda index: parts_ref[index, rows, :].astype(jnp.float32)
+    return (part(0) + part(2)) + (part(1) + part(3))
+
+
+def far_join_kernel(keep_ref, got_ref, grads_ref, out_ref):
+    half = keep_ref.shape[0]
+    out_ref[:half, :] = (keep_ref[...] + got_ref[...].astype(jnp.float32)).astype(jnp.bfloat16)
+    out_ref[half:, :] = grads_ref[...]
+
+
+def near_join_kernel(keep_ref, got_ref, far_ref, grads_ref, out_ref):
     shards = out_ref.shape[0]
-    own = keep_ref.shape[0] // shards
+    half = keep_ref.shape[0]
+    own = half // shards
+    grads = grads_ref[...].astype(jnp.float32) + far_ref[half:, :].astype(jnp.float32)
+    grads = grads.astype(jnp.bfloat16)
     for shard in range(shards):
         rows = pl.ds(shard * own, own)
         total = keep_ref[rows, :] + got_ref[rows, :].astype(jnp.float32)
+        total += far_ref[rows, :].astype(jnp.float32)
         out_ref[shard, pl.ds(0, own), :] = total.astype(jnp.bfloat16)
-        out_ref[shard, pl.ds(own, grads_ref.shape[0]), :] = grads_ref[...]
+        out_ref[shard, pl.ds(own, grads.shape[0]), :] = grads
 
 
 def total_kernel(scale_factor, parts_ref, half_ref):
-    shards = parts_ref.shape[0]
-    own = parts_ref.shape[1] - (half_ref.shape[0] - 8 + BIAS_ROWS)
-    tail = parts_ref[0, own:, :].astype(jnp.float32)
-    for shard in range(1, shards):
-        tail += parts_ref[shard, own:, :].astype(jnp.float32)
+    extra = half_ref.shape[0] - 8 + BIAS_ROWS
+    tail = sum_of_four(parts_ref, pl.ds(parts_ref.shape[1] - extra, extra))
     tail = tail * scale_factor
     height = half_ref.shape[0] - 8
     half_ref[:height, :] = tail[:height, :]
@@ -332,9 +349,7 @@
     roots = lax.rsqrt(degree_ref[...].astype(jnp.float32))
     for tile in range(tiles):
         rows = pl.ds(tile * edge, edge)
-        total = parts_ref[0, rows, :].astype(jnp.float32)
-        for shard in range(1, parts_ref.shape[0]):
-            total += parts_ref[shard, rows, :].astype(jnp.float32)
+        total = sum_of_four(parts_ref, rows)
         features_ref[rows, :] = (total * roots[tile : tile + 1, :]).T.astype(jnp.bfloat16)
 
 
@@ -382,7 +397,6 @@
         for index in range(row_devices)
     ]
     exchange = functools.partial(lax.all_to_all, split_axis=0, concat_axis=0)
-    same_core = [list(range(first, row_devices, 2)) for first in range(2)]
     extra = feature_count + BIAS_ROWS
     half = chips * node_dev
     bf16, f32 = jnp.bfloat16, jnp.float32
@@ -481,16 +495,13 @@
         compiler_params=PARAMS,
     )(keep_terms, got_terms, spread)
     spread_all = exchange(spread, "col")
+    kept, sent = shape((half // 2, edge), f32), shape((half // 2, edge), bf16)
     keep, send, grads = pl.pallas_call(
-        backward_kernel,
-        out_shape=(
-            shape((half, edge), f32),
-            shape((half, edge), bf16),
-            shape((extra, edge), bf16),
-        ),
+        backward_far_kernel,
+        out_shape=(kept, sent, shape((extra, edge), bf16)),
         in_specs=[SMEM] + [VMEM] * 2,
         out_specs=(VMEM,) * 3,
-        scratch_shapes=[pltpu.VMEM((2 * half, edge), f32)],
+        scratch_shapes=[pltpu.VMEM((half, edge), f32)],
         compiler_params=PARAMS,
         cost_estimate=tile_cost,
     )(slots, patterns, spread_all)
@@ -504,14 +515,34 @@
         compiler_params=PARAMS,
     )(pre_act)
     got, activations = lax.optimization_barrier((got, activations))
+    far_sums = pl.pallas_call(
+        far_join_kernel,
+        out_shape=shape((half // 2 + extra, edge), bf16),
+        in_specs=[VMEM] * 3,
+        out_specs=VMEM,
+        compiler_params=PARAMS,
+    )(keep, got, grads)
+    far_sums, spread_all = lax.optimization_barrier((far_sums, spread_all))
+    far_got = lax.ppermute(far_sums, "row", row_far)
+    keep, send = pl.pallas_call(
+        backward_near_kernel,
+        out_shape=(kept, sent),
+        in_specs=[SMEM] + [VMEM] * 2,
+        out_specs=(VMEM,) * 2,
+        scratch_shapes=[pltpu.VMEM((half, edge), f32)],
+        compiler_params=PARAMS,
+        cost_estimate=tile_cost,
+    )(slots, patterns, spread_all)
+    got = lax.ppermute(send, "row", swap)
+    got, far_got = lax.optimization_barrier((got, far_got))
     joined = pl.pallas_call(
-        join_kernel,
-        out_shape=shape((chips, node_dev + extra, edge), bf16),
-        in_specs=[VMEM] * 3,
-        out_specs=VMEM,
-        compiler_params=PARAMS,
-    )(keep, got, grads)
-    back_parts = exchange(joined, "row", axis_index_groups=same_core)
+        near_join_kernel,
+        out_shape=shape((4, node_dev + extra, edge), bf16),
+        in_specs=[VMEM] * 4,
+        out_specs=VMEM,
+        compiler_params=PARAMS,
+    )(keep, got, far_got, grads)
+    back_parts = exchange(joined, "row", axis_index_groups=row_near)
     scale_factor = 1.0 / math.sqrt(node_dev * row_devices * col_devices)
     mine = pl.pallas_call(
         functools.partial(total_kernel, scale_factor),

time: 118 us -> 114 us (0.966)
  blocking collectives: 86 us -> 74.3 us
  starting transfers between devices: 6.92 us -> 14.9 us
  Pallas kernels: 14 us -> 11.8 us
  waiting for transfers between devices: 6.42 us -> 8.16 us
    all_to_all x1, blocking collectives: 26.6 us -> 14.6 us  [per_device(): back_parts = exchange(joined, 'row', axis_index_groups=row_near)]
    ppermute x1 -> x2, starting transfers between devices: 0.6 us -> 7.02 us  [per_device(): got = lax.ppermute(send, 'row', swap)]
    pallas_call x2 -> x4, Pallas kernels: 4.06 us -> 3.78 us  [the longest x1 1.76 us: per_device(): pl.pallas_call(backward_far_kernel, out_shape=(kept, sent, shape((extra,...]
  transfers between devices with their start and end apart: 6 -> 8, of which waited for: 5 -> 7; matrix products, arithmetic and copies ran while one was open for 0% -> 0% of each run, Pallas kernels for 4% -> 5%
where the time goes in v5:
time: 114 us
  blocking collectives  74.3 us (65%)
  starting transfers between devices  14.9 us (13%)
  Pallas kernels  11.8 us (10%)
  waiting for transfers between devices  8.16 us (7%)
  local copies, waits for them, and re-layouts  3.22 us (3%)
  between operations  1.47 us (1%)
    all_to_all x1, blocking collectives, per_device(): exchange(row_part.reshape(col_devices, node_dev, feature_count), 'col')  23.4 us
    all_to_all x1, blocking collectives, per_device(): spread_all = exchange(spread, 'col')  22.6 us
    all_to_all x1, blocking collectives, per_device(): back_parts = exchange(joined, 'row', axis_index_groups=row_near)  14.6 us
    all_to_all x1, blocking collectives, per_device(): exchange(scaled, 'row', axis_index_groups=row_near)  13.8 us
    ppermute x2, starting transfers between devices, per_device(): got = lax.ppermute(send, 'row', swap)  7.02 us
    ppermute x1, waiting for transfers between devices, per_device(): far_own = lax.ppermute(near_own, 'row', row_far)  3.53 us
    ppermute x1, starting transfers between devices, per_device(): got_terms = lax.ppermute(send_terms, 'row', swap)  3.44 us
    unnamed x24, local copies, waits for them, and re-layouts  3.22 us
  transfers between devices with their start and end apart: 8, of which 7 were waited for; matrix products, arithmetic and copies ran while one was open for 0% of the time, Pallas kernels for 5%

profile of v5, /device:TPU:1, one launch (start us, length us, event | category | flops | bytes accessed | tf_op | source)
XLA Modules:
  0.0 113.9 jit_solution(11960892857044123853)
XLA Ops:
  0.6 0.9 copy-done.4
  1.5 0.7 copy-done.5
  2.2 0.4 shard_map.138
  2.7 13.8 %all_to_all.20 = bf16[4,512,128]{2,1,0:T(8,128)(2,1)S(1)} all-to-all(bf16[4,512,128]{2,1,0:T(8,128)(2,1)S(1)} %shard_map.138), channel_id=1, replica_groups={{0,64,16,80},{32,96,48,112},{8,72,56,120},{24,88,40,104},{1,65,17,81},{..., dimensions={0} | all-to-all | bytes 1048576 | tf_op jit(solution)/shard_map/all_to_all | solution.py:423
  16.5 0.5 collective-permute-start.1
  17.7 0.6 shard_map.139.slots_ref
  18.3 0.2 collective-permute-done.1.other_ref
  18.5 1.6 %copy-done = bf16[64,128,128]{2,1,0:T(8,128)(2,1)S(1)} copy-done((bf16[64,128,128]{2,1,0:T(8,128)(2,1)S(1)}, bf16[64,128,128]{2,1,0:T(8,128)(2,1)}, u32[]{:S(2)}) %copy-start) | copy-done | bytes 2097176
  20.1 1.7 %shard_map.140.so_far_ref = f32[4096,128]{1,0:T(8,128)S(1)} custom-call(s32[1,640]{1,0:T(1,128)S(1)} %shard_map.139.slots_ref, bf16[64,128,128]{2,1,0:T(8,128)(2,1)S(1)} %copy-done, bf16[2048,128]{1,0:T(8,128)(2,1)S(1)} %bitcast.13, bf16[2048,128]{1,0:T(8,128)(2,1)S(1)} %collective-permute-done.1.other_ref), custom_call_target="tpu_custom_call" | custom-call | flops 8388608 | bytes 6291456 | tf_op jit(solution)/shard_map/pallas_call | solution.py:448
  21.8 3.5 %collective-permute-done.own_ref = bf16[2048,128]{1,0:T(8,128)(2,1)S(1)} collective-permute-done((bf16[2048,128]{1,0:T(8,128)(2,1)S(1)}, bf16[2048,128]{1,0:T(8,128)(2,1)S(1)}, u32[]{:S(2)}, u32[]{:S(2)}) %collective-permute-start) | collective-permute-done | bytes 524320 | tf_op jit(solution)/shard_map/ppermute | solution.py:425
  25.3 2.1 %collective-permute-start.2 = (bf16[2048,128]{1,0:T(8,128)(2,1)S(1)}, bf16[2048,128]{1,0:T(8,128)(2,1)S(1)}, u32[]{:S(2)}, u32[]{:S(2)}) collective-permute-start(bf16[2048,128]{1,0:T(8,128)(2,1)S(1)} %collective-permute-done.own_ref), channel_id=1, source_target_pairs={{0,8},{8,0},{16,24},{24,16},{32,40},{40,32},{48,56},{56,48},{64,72... | collective-permute-start | bytes 1572872 | tf_op jit(solution)/shard_map/ppermute | solution.py:458
  27.4 1.5 %collective-permute-done.2.other_ref = bf16[2048,128]{1,0:T(8,128)(2,1)S(1)} collective-permute-done((bf16[2048,128]{1,0:T(8,128)(2,1)S(1)}, bf16[2048,128]{1,0:T(8,128)(2,1)S(1)}, u32[]{:S(2)}, u32[]{:S(2)}) %collective-permute-start.2) | collective-permute-done | bytes 524320 | tf_op jit(solution)/shard_map/ppermute | solution.py:458
  28.9 1.8 %shard_map.141 = bf16[4096,128]{1,0:T(8,128)(2,1)S(1)} custom-call(s32[1,640]{1,0:T(1,128)S(1)} %shard_map.139.slots_ref, bf16[64,128,128]{2,1,0:T(8,128)(2,1)S(1)} %copy-done, bf16[2048,128]{1,0:T(8,128)(2,1)S(1)} %collective-permute-done.own_ref, bf16[2048,128]{1,0:T(8,128)(2,1)S(1)} %collective-permute-done.2.other_ref, f32[4096,128]{1,0:T(8,128)S(1)} %shard_map.140.so_far_ref), custom_call_target="tpu_custom_call" | custom-call | flops 8388608 | bytes 6291456 | tf_op jit(solution)/shard_map/pallas_call | solution.py:459
  30.8 23.4 %all_to_all.21.parts_ref = bf16[8,512,128]{2,1,0:T(8,128)(2,1)S(1)} all-to-all(bf16[8,512,128]{2,1,0:T(8,128)(2,1)S(1)} %bitcast.10), channel_id=1, replica_groups=mesh['row'=16,'col'=8] {'col'}, dimensions={0} | all-to-all | bytes 2097152 | tf_op jit(solution)/shard_map/all_to_all | solution.py:468
  54.1 0.9 shard_map.142
  55.0 3.4 %collective-permute-start.3 = (bf16[144,128]{1,0:T(8,128)(2,1)S(1)}, bf16[144,128]{1,0:T(8,128)(2,1)S(1)}, u32[]{:S(2)}, u32[]{:S(2)}) collective-permute-start(bf16[144,128]{1,0:T(8,128)(2,1)S(1)} %get-tuple-element.32), channel_id=1, source_target_pairs={{0,8},{8,0},{16,24},{24,16},{32,40},{40,32},{48,56},{56,48},{64,72... | collective-permute-start | bytes 110600 | tf_op jit(solution)/shard_map/ppermute | solution.py:481
  58.5 0.3 shard_map.143.spread_ref
  58.8 0.6 collective-permute-done.3.got_ref
  59.4 22.6 %all_to_all.22.spread_ref = bf16[8,656,128]{2,1,0:T(8,128)(2,1)S(1)} all-to-all(bf16[8,656,128]{2,1,0:T(8,128)(2,1)S(1)} %shard_map.144), channel_id=1, replica_groups=mesh['row'=16,'col'=8] {'col'}, dimensions={0} | all-to-all | bytes 2686976 | tf_op jit(solution)/shard_map/all_to_all | solution.py:497
  82.0 1.8 %shard_map.145 = (f32[2048,128]{1,0:T(8,128)S(1)}, bf16[2048,128]{1,0:T(8,128)(2,1)S(1)}, bf16[144,128]{1,0:T(8,128)(2,1)S(1)}) custom-call(s32[1,640]{1,0:T(1,128)S(1)} %shard_map.139.slots_ref, bf16[64,128,128]{2,1,0:T(8,128)(2,1)S(1)} %copy-done.1, bf16[8,656,128]{2,1,0:T(8,128)(2,1)S(1)} %all_to_all.22.spread_ref), custom_call_target="tpu_custom_call" | custom-call | flops 8388608 | bytes 6291456 | tf_op jit(solution)/shard_map/pallas_call | solution.py:499
  83.7 1.5 %collective-permute-start.4 = (bf16[2048,128]{1,0:T(8,128)(2,1)S(1)}, bf16[2048,128]{1,0:T(8,128)(2,1)S(1)}, u32[]{:S(2)}, u32[]{:S(2)}) collective-permute-start(bf16[2048,128]{1,0:T(8,128)(2,1)S(1)} %get-tuple-element.34), channel_id=1, source_target_pairs={{0,8},{8,0},{16,24},{24,16},{32,40},{40,32},{48,56},{56,48},{64,72... | collective-permute-start | bytes 1572872 | tf_op jit(solution)/shard_map/ppermute | solution.py:508
  85.3 0.9 shard_map.146
  86.1 0.7 collective-permute-done.4.got_ref
  86.8 0.1 shard_map.147
  87.0 1.7 %shard_map.148 = (f32[2048,128]{1,0:T(8,128)S(1)}, bf16[2048,128]{1,0:T(8,128)(2,1)S(1)}) custom-call(s32[1,640]{1,0:T(1,128)S(1)} %shard_map.139.slots_ref, bf16[64,128,128]{2,1,0:T(8,128)(2,1)S(1)} %copy-done.1, bf16[8,656,128]{2,1,0:T(8,128)(2,1)S(1)} %all_to_all.22.spread_ref), custom_call_target="tpu_custom_call" | custom-call | flops 8388608 | bytes 6291456 | tf_op jit(solution)/shard_map/pallas_call | solution.py:527
  88.7 5.5 %collective-permute-start.5 = (bf16[2048,128]{1,0:T(8,128)(2,1)S(1)}, bf16[2048,128]{1,0:T(8,128)(2,1)S(1)}, u32[]{:S(2)}, u32[]{:S(2)}) collective-permute-start(bf16[2048,128]{1,0:T(8,128)(2,1)S(1)} %get-tuple-element.44), channel_id=1, source_target_pairs={{0,8},{8,0},{16,24},{24,16},{32,40},{40,32},{48,56},{56,48},{64,72... | collective-permute-start | bytes 1572872 | tf_op jit(solution)/shard_map/ppermute | solution.py:536
  94.2 1.5 %collective-permute-done.5.got_ref = bf16[2048,128]{1,0:T(8,128)(2,1)S(1)} collective-permute-done((bf16[2048,128]{1,0:T(8,128)(2,1)S(1)}, bf16[2048,128]{1,0:T(8,128)(2,1)S(1)}, u32[]{:S(2)}, u32[]{:S(2)}) %collective-permute-start.5) | collective-permute-done | bytes 524320 | tf_op jit(solution)/shard_map/ppermute | solution.py:536
  95.8 0.2 shard_map.149
  96.0 14.6 %all_to_all.23.parts_ref = bf16[4,656,128]{2,1,0:T(8,128)(2,1)S(1)} all-to-all(bf16[4,656,128]{2,1,0:T(8,128)(2,1)S(1)} %shard_map.149), channel_id=1, replica_groups={{0,64,16,80},{32,96,48,112},{8,72,56,120},{24,88,40,104},{1,65,17,81},{..., dimensions={0} | all-to-all | bytes 1343488 | tf_op jit(solution)/shard_map/all_to_all | solution.py:545
  110.6 1.8 %collective-permute-start.7 = (f32[136,128]{1,0:T(8,128)S(1)}, f32[136,128]{1,0:T(8,128)S(1)}, u32[]{:S(2)}, u32[]{:S(2)}) collective-permute-start(f32[136,128]{1,0:T(8,128)S(1)} %shard_map.151.mine_ref), channel_id=1, source_target_pairs={{0,8},{8,0},{16,24},{24,16},{32,40},{40,32},{48,56},{56,48},{64,72... | collective-permute-start | bytes 208904 | tf_op jit(solution)/shard_map/ppermute | solution.py:554
  112.4 0.8 shard_map.150
  113.3 0.7 shard_map.152
  (27 shorter events, 0.3 us)
Async XLA Ops:
  0.6 0.9 copy-start.4
  1.5 0.7 copy-start.5
  2.2 15.4 %copy-start.7 = (s32[1,1,512]{2,1,0:T(1,128)S(1)}, s32[1,1,512]{2,1,0:T(1,128)}, u32[]{:S(2)}) copy-start(s32[1,1,512]{2,1,0:T(1,128)} %param.17) | copy-start | bytes 6148
  2.2 15.4 %copy-start.8 = (s32[1,1,512]{2,1,0:T(1,128)S(1)}, s32[1,1,512]{2,1,0:T(1,128)}, u32[]{:S(2)}) copy-start(s32[1,1,512]{2,1,0:T(1,128)} %param.18) | copy-start | bytes 6148
  2.2 15.4 %copy-start.9 = (s32[1,1,512]{2,1,0:T(1,128)S(1)}, s32[1,1,512]{2,1,0:T(1,128)}, u32[]{:S(2)}) copy-start(s32[1,1,512]{2,1,0:T(1,128)} %param.19) | copy-start | bytes 6148
  2.2 15.5 %copy-start.10 = (s32[1,1,512]{2,1,0:T(1,128)S(1)}, s32[1,1,512]{2,1,0:T(1,128)}, u32[]{:S(2)}) copy-start(s32[1,1,512]{2,1,0:T(1,128)} %param.20) | copy-start | bytes 6148
  16.5 2.1 %collective-permute-start.1 = (bf16[2048,128]{1,0:T(8,128)(2,1)S(1)}, bf16[2048,128]{1,0:T(8,128)(2,1)S(1)}, u32[]{:S(2)}, u32[]{:S(2)}) collective-permute-start(bf16[2048,128]{1,0:T(8,128)(2,1)S(1)} %bitcast.11), channel_id=1, source_target_pairs={{0,8},{8,0},{16,24},{24,16},{32,40},{40,32},{48,56},{56,48},{64,72... | collective-permute-start | bytes 1572872 | tf_op jit(solution)/shard_map/ppermute | solution.py:424
  17.0 8.3 %collective-permute-start = (bf16[2048,128]{1,0:T(8,128)(2,1)S(1)}, bf16[2048,128]{1,0:T(8,128)(2,1)S(1)}, u32[]{:S(2)}, u32[]{:S(2)}) collective-permute-start(bf16[2048,128]{1,0:T(8,128)(2,1)S(1)} %bitcast.12), channel_id=1, source_target_pairs={{0,48},{8,24},{16,32},{24,8},{32,16},{40,56},{48,0},{56,40},{64,11... | collective-permute-start | bytes 1572872 | tf_op jit(solution)/shard_map/ppermute | solution.py:425
  18.5 1.6 %copy-start = (bf16[64,128,128]{2,1,0:T(8,128)(2,1)S(1)}, bf16[64,128,128]{2,1,0:T(8,128)(2,1)}, u32[]{:S(2)}) copy-start(bf16[64,128,128]{2,1,0:T(8,128)(2,1)} %patterns_ref.7) | copy-start | bytes 6291460
  25.3 3.6 %collective-permute-start.2 = (bf16[2048,128]{1,0:T(8,128)(2,1)S(1)}, bf16[2048,128]{1,0:T(8,128)(2,1)S(1)}, u32[]{:S(2)}, u32[]{:S(2)}) collective-permute-start(bf16[2048,128]{1,0:T(8,128)(2,1)S(1)} %collective-permute-done.own_ref), channel_id=1, source_target_pairs={{0,8},{8,0},{16,24},{24,16},{32,40},{40,32},{48,56},{56,48},{64,72... | collective-permute-start | bytes 1572872 | tf_op jit(solution)/shard_map/ppermute | solution.py:458
  30.7 23.4 %copy-start.2 = (bf16[512,256]{1,0:T(8,128)(2,1)S(1)}, bf16[512,256]{1,0:T(8,128)(2,1)}, u32[]{:S(2)}) copy-start(bf16[512,256]{1,0:T(8,128)(2,1)} %cotangent_ref.1) | copy-start | bytes 786436
  30.7 23.4 %copy-start.3 = (bf16[128,256]{1,0:T(8,128)(2,1)S(1)}, bf16[128,256]{1,0:T(8,128)(2,1)}, u32[]{:S(2)}) copy-start(bf16[128,256]{1,0:T(8,128)(2,1)} %weight_ref.3) | copy-start | bytes 196612
  30.7 23.4 %copy-start.6 = (s32[512]{0:T(512)S(1)}, s32[512]{0:T(512)}, u32[]{:S(2)}) copy-start(s32[512]{0:T(512)} %param.12) | copy-start | bytes 6148
  30.7 23.4 %copy-start.11 = (f32[256]{0:T(256)S(1)}, f32[256]{0:T(256)}, u32[]{:S(2)}) copy-start(f32[256]{0:T(256)} %param.15) | copy-start | bytes 3076
  55.0 4.3 %collective-permute-start.3 = (bf16[144,128]{1,0:T(8,128)(2,1)S(1)}, bf16[144,128]{1,0:T(8,128)(2,1)S(1)}, u32[]{:S(2)}, u32[]{:S(2)}) collective-permute-start(bf16[144,128]{1,0:T(8,128)(2,1)S(1)} %get-tuple-element.32), channel_id=1, source_target_pairs={{0,8},{8,0},{16,24},{24,16},{32,40},{40,32},{48,56},{56,48},{64,72... | collective-permute-start | bytes 110600 | tf_op jit(solution)/shard_map/ppermute | solution.py:481
  59.3 22.6 %copy-start.1 = (bf16[64,128,128]{2,1,0:T(8,128)(2,1)S(1)}, bf16[64,128,128]{2,1,0:T(8,128)(2,1)}, u32[]{:S(2)}) copy-start(bf16[64,128,128]{2,1,0:T(8,128)(2,1)} %patterns_ref.7) | copy-start | bytes 6291460
  83.7 3.1 %collective-permute-start.4 = (bf16[2048,128]{1,0:T(8,128)(2,1)S(1)}, bf16[2048,128]{1,0:T(8,128)(2,1)S(1)}, u32[]{:S(2)}, u32[]{:S(2)}) collective-permute-start(bf16[2048,128]{1,0:T(8,128)(2,1)S(1)} %get-tuple-element.34), channel_id=1, source_target_pairs={{0,8},{8,0},{16,24},{24,16},{32,40},{40,32},{48,56},{56,48},{64,72... | collective-permute-start | bytes 1572872 | tf_op jit(solution)/shard_map/ppermute | solution.py:508
  86.9 8.8 %collective-permute-start.6 = (bf16[2192,128]{1,0:T(8,128)(2,1)S(1)}, bf16[2192,128]{1,0:T(8,128)(2,1)S(1)}, u32[]{:S(2)}, u32[]{:S(2)}) collective-permute-start(bf16[2192,128]{1,0:T(8,128)(2,1)S(1)} %shard_map.147), channel_id=1, source_target_pairs={{0,48},{8,24},{16,32},{24,8},{32,16},{40,56},{48,0},{56,40},{64,11... | collective-permute-start | bytes 1683464 | tf_op jit(solution)/shard_map/ppermute | solution.py:526
  88.7 7.0 %collective-permute-start.5 = (bf16[2048,128]{1,0:T(8,128)(2,1)S(1)}, bf16[2048,128]{1,0:T(8,128)(2,1)S(1)}, u32[]{:S(2)}, u32[]{:S(2)}) collective-permute-start(bf16[2048,128]{1,0:T(8,128)(2,1)S(1)} %get-tuple-element.44), channel_id=1, source_target_pairs={{0,8},{8,0},{16,24},{24,16},{32,40},{40,32},{48,56},{56,48},{64,72... | collective-permute-start | bytes 1572872 | tf_op jit(solution)/shard_map/ppermute | solution.py:536
  110.6 2.7 %collective-permute-start.7 = (f32[136,128]{1,0:T(8,128)S(1)}, f32[136,128]{1,0:T(8,128)S(1)}, u32[]{:S(2)}, u32[]{:S(2)}) collective-permute-start(f32[136,128]{1,0:T(8,128)S(1)} %shard_map.151.mine_ref), channel_id=1, source_target_pairs={{0,8},{8,0},{16,24},{24,16},{32,40},{40,32},{48,56},{56,48},{64,72... | collective-permute-start | bytes 208904 | tf_op jit(solution)/shard_map/ppermute | solution.py:554

commit v6 on v5

--- a/solution.py
+++ b/solution.py
@@ -14,7 +14,7 @@
 CUBIC = 0.044715
 BIAS_ROWS = 16
 PER_SHARD = 4
-CLASSES = 2
+CLASSES = 4
 ORDERED = 640
 BOUNDS = 600
 PAIRS = (((0, 1), (2, 3)), ((0, 3), (1, 2)))
@@ -48,7 +48,8 @@
         copy.start()
     for copy in copies:
         copy.wait()
-    row = place_ref[0]
+    row, col = place_ref[0], place_ref[1]
+    core = row % 2
     _, rows, edge = fields.shape
     tile_row, tile_col = fields[0], fields[1]
     shard = tile_col // PER_SHARD
@@ -56,16 +57,20 @@
     chip = shard // 2
     ring = chip % 4
     tile = tile_col % PER_SHARD
-    half = parity ^ (row % 2)
+    half = parity ^ core
     far = (pair_of(ring, parity) != pair_of((row // 2) % 4, parity)).astype(jnp.int32)
     rank = pair_index(ring, parity) * 2 + chip // 4
     place = (half * 4 + rank) * PER_SHARD + tile
-    word = tile_row | (fields[2] << 5) | (fields[3] << 11) | (place << 14)
+    peer = tile_row // PER_SHARD
+    row_far = (pair_of(peer // 2, core) != pair_of(col // 2, core)).astype(jnp.int32)
+    rank = pair_index(peer // 2, core) * 2 + peer % 2
+    target = (row_far * 4 + rank) * PER_SHARD + tile_row % PER_SHARD
+    word = tile_row | (fields[2] << 5) | (fields[3] << 11) | (place << 14) | (target << 19)
     slot = lax.broadcasted_iota(jnp.int32, (rows, edge), 0) * edge
     slot += lax.broadcasted_iota(jnp.int32, (rows, edge), 1)
     alive = slot < live_ref[0, 0]
     word = jnp.where(alive, word, 0)
-    kind = jnp.where(alive, far, CLASSES)
+    kind = jnp.where(alive, far * 2 + row_far, CLASSES)
 
     flags = [(kind == index).astype(jnp.float32) for index in range(CLASSES + 1)]
     stacked = jnp.concatenate(flags + [jnp.zeros((4, edge), jnp.float32)], 0)
@@ -93,12 +98,14 @@
     pieces = jnp.zeros((8, slots), jnp.float32)
     for line in range(rows):
         chosen = (turned[:, line : line + 1] == lanes).astype(jnp.float32).astype(jnp.bfloat16)
-        parts = [(word[line : line + 1] >> shift) & 127 for shift in (0, 7, 14)]
-        parts = jnp.concatenate(parts + [jnp.zeros((5, edge), jnp.int32)], 0)
+        parts = [(word[line : line + 1] >> shift) & 127 for shift in (0, 7, 14, 21)]
+        parts = jnp.concatenate(parts + [jnp.zeros((4, edge), jnp.int32)], 0)
         parts = parts.astype(jnp.float32).astype(jnp.bfloat16)
         pieces += jnp.dot(parts, chosen, preferred_element_type=jnp.float32)
     pieces = pieces.astype(jnp.int32)
-    out_ref[:, :slots] = pieces[0:1] | (pieces[1:2] << 7) | (pieces[2:3] << 14)
+    out_ref[:, :slots] = (
+        pieces[0:1] | (pieces[1:2] << 7) | (pieces[2:3] << 14) | (pieces[3:4] << 21)
+    )
     lane = lax.broadcasted_iota(jnp.int32, (1, out_ref.shape[1] - slots), 1) + slots
     tail = jnp.zeros(lane.shape, jnp.int32)
     for index in range(CLASSES):
@@ -153,12 +160,16 @@
     return ref[pl.ds(pl.multiple_of(place * edge, edge), edge), :]
 
 
-def forward_sums(slots_ref, patterns_ref, own_ref, other_ref, panel, sums, far):
+def class_end(slots_ref, index):
+    return slots_ref[0, BOUNDS + index]
+
+
+def forward_sums(slots_ref, patterns_ref, own_ref, other_ref, panel, sums, first, end):
     edge = patterns_ref.shape[1]
     half = own_ref.shape[0]
     panel[:half, :] = own_ref[...]
     panel[half:, :] = other_ref[...]
-    middle, end = slots_ref[0, BOUNDS], slots_ref[0, BOUNDS + 1]
+    mask = sums.shape[0] // edge - 1
 
     def product_of(word):
         return jnp.dot(
@@ -167,26 +178,43 @@
             preferred_element_type=jnp.float32,
         )
 
-    first, end = (middle, end) if far else (0, middle)
-    add_products(slots_ref, first, end, product_of, lambda word: word & 31, sums)
+    add_products(slots_ref, first, end, product_of, lambda word: (word >> 19) & mask, sums)
 
 
 def forward_near_kernel(slots_ref, patterns_ref, own_ref, other_ref, out_ref, panel):
     out_ref[...] = jnp.zeros_like(out_ref)
-    forward_sums(slots_ref, patterns_ref, own_ref, other_ref, panel, out_ref, False)
-
-
-def forward_far_kernel(slots_ref, patterns_ref, own_ref, other_ref, so_far_ref, out_ref, panel, sums):
-    sums[...] = so_far_ref[...]
-    forward_sums(slots_ref, patterns_ref, own_ref, other_ref, panel, sums, True)
+    end = class_end(slots_ref, 1)
+    forward_sums(slots_ref, patterns_ref, own_ref, other_ref, panel, out_ref, 0, end)
+
+
+def forward_send_kernel(
+    slots_ref, patterns_ref, own_ref, other_ref, so_far_ref, out_ref, panel, sums
+):
+    sums[...] = so_far_ref[sums.shape[0] :, :]
+    first, end = class_end(slots_ref, 2), class_end(slots_ref, 3)
+    forward_sums(slots_ref, patterns_ref, own_ref, other_ref, panel, sums, first, end)
     out_ref[...] = sums[...].astype(jnp.bfloat16)
+
+
+def forward_keep_kernel(slots_ref, patterns_ref, own_ref, other_ref, so_far_ref, out_ref, panel):
+    out_ref[...] = so_far_ref[: out_ref.shape[0], :]
+    first, end = class_end(slots_ref, 1), class_end(slots_ref, 2)
+    forward_sums(slots_ref, patterns_ref, own_ref, other_ref, panel, out_ref, first, end)
+
+
+def row_join_kernel(keep_ref, got_ref, out_ref):
+    shards, own, _ = out_ref.shape
+    for shard in range(shards):
+        rows = pl.ds(shard * own, own)
+        total = keep_ref[rows, :] + got_ref[rows, :].astype(jnp.float32)
+        out_ref[shard] = total.astype(jnp.bfloat16)
 
 
 def backward_sums(slots_ref, patterns_ref, spread_ref, keep_ref, send_ref, sums, far):
     edge = patterns_ref.shape[1]
     half = sums.shape[0] // 2
     sums[...] = jnp.zeros_like(sums)
-    middle, end = slots_ref[0, BOUNDS], slots_ref[0, BOUNDS + 1]
+    middle, end = class_end(slots_ref, 1), class_end(slots_ref, 3)
 
     def product_of(word):
         start = pl.multiple_of((word & 3) * edge, edge)
@@ -385,7 +413,7 @@
     chips = row_devices // 2
     edge = patterns.shape[1]
     per_shard = node_dev // edge
-    row = lax.axis_index("row")
+    row, col = lax.axis_index("row"), lax.axis_index("col")
     swap = [(index, index ^ 1) for index in range(row_devices)]
     row_near = [
         [(low * 4 + ring) * 2 + core_index for ring in pair for low in range(2)]
@@ -395,6 +423,19 @@
     row_far = [
         (index, (index // 8 * 4 + far_neighbour(index // 2 % 4, index % 2)) * 2 + index % 2)
         for index in range(row_devices)
+    ]
+    col_near = [
+        [index * col_devices + ring * 2 + high for ring in pair for high in range(2)]
+        for index in range(row_devices)
+        for pair in PAIRS[index % 2]
+    ]
+    col_far = [
+        (
+            index * col_devices + place,
+            index * col_devices + far_neighbour(place // 2, index % 2) * 2 + place % 2,
+        )
+        for index in range(row_devices)
+        for place in range(col_devices)
     ]
     exchange = functools.partial(lax.all_to_all, split_axis=0, concat_axis=0)
     extra = feature_count + BIAS_ROWS
@@ -424,7 +465,7 @@
     near_other = lax.ppermute(near_own, "row", swap)
     far_own = lax.ppermute(near_own, "row", row_far)
     row_tiles, near_own = lax.optimization_barrier((tile_row.reshape(per_shard, edge), near_own))
-    place = row.astype(jnp.int32).reshape(1)
+    place = jnp.stack([row, col]).astype(jnp.int32)
     slots = pl.pallas_call(
         order_kernel,
         out_shape=shape((1, ORDERED), jnp.int32),
@@ -456,16 +497,35 @@
     )(slots, patterns, near_own, near_other)
     far_own, near_sums = lax.optimization_barrier((far_own, near_sums))
     far_other = lax.ppermute(far_own, "row", swap)
-    row_part = pl.pallas_call(
-        forward_far_kernel,
-        out_shape=shape(row_sums.shape, bf16),
+    row_half = shape((col_devices // 2 * node_dev, feature_count), f32)
+    far_sums = pl.pallas_call(
+        forward_send_kernel,
+        out_shape=shape(row_half.shape, bf16),
         in_specs=[SMEM] + [VMEM] * 4,
         out_specs=VMEM,
-        scratch_shapes=[forward_panel, pltpu.VMEM(row_sums.shape, f32)],
+        scratch_shapes=[forward_panel, pltpu.VMEM(row_half.shape, f32)],
         compiler_params=PARAMS,
         cost_estimate=tile_cost,
     )(slots, patterns, far_own, far_other, near_sums)
-    parts = exchange(row_part.reshape(col_devices, node_dev, feature_count), "col")
+    far_sums, near_sums = lax.optimization_barrier((far_sums, near_sums))
+    got = lax.ppermute(far_sums, ("row", "col"), col_far)
+    keep = pl.pallas_call(
+        forward_keep_kernel,
+        out_shape=row_half,
+        in_specs=[SMEM] + [VMEM] * 4,
+        out_specs=VMEM,
+        scratch_shapes=[forward_panel],
+        compiler_params=PARAMS,
+        cost_estimate=tile_cost,
+    )(slots, patterns, far_own, far_other, near_sums)
+    row_part = pl.pallas_call(
+        row_join_kernel,
+        out_shape=shape((4, node_dev, feature_count), bf16),
+        in_specs=[VMEM] * 2,
+        out_specs=VMEM,
+        compiler_params=PARAMS,
+    )(keep, got)
+    parts = exchange(row_part, ("row", "col"), axis_index_groups=col_near)
     pre_act, upstream, keep_terms, send_terms = pl.pallas_call(
         middle_kernel,
         out_shape=(

time: 114 us -> 115 us (level)
  waiting for transfers between devices: 8.16 us -> 15.1 us
  blocking collectives: 74.3 us -> 68.1 us
  starting transfers between devices: 14.9 us -> 11.7 us
  Pallas kernels: 11.8 us -> 15 us
    all_to_all x1, blocking collectives: 23.4 us -> 16.5 us  [per_device(): parts = exchange(row_part, ('row', 'col'), axis_index_groups=col_near)]
    ppermute x0 -> x1, waiting for transfers between devices: none -> 5.21 us  [per_device(): got = lax.ppermute(far_sums, ('row', 'col'), col_far)]
    ppermute x2, starting transfers between devices: 7.02 us -> 3.25 us  [per_device(): got = lax.ppermute(send, 'row', swap)]
    ppermute x1, starting transfers between devices: 3.44 us -> 1.04 us  [per_device(): got_terms = lax.ppermute(send_terms, 'row', swap)]
    ppermute x1, waiting for transfers between devices: 0.01 us -> 2.4 us  [per_device(): far_got = lax.ppermute(far_sums, 'row', row_far)]
    all_to_all x1, blocking collectives: 22.6 us -> 24.4 us  [per_device(): spread_all = exchange(spread, 'col')]
    ppermute x0 -> x1, starting transfers between devices: none -> 1.71 us  [per_device(): got = lax.ppermute(far_sums, ('row', 'col'), col_far)]
    ppermute x1, starting transfers between devices: 0.09 us -> 1.71 us  [per_device(): far_got = lax.ppermute(far_sums, 'row', row_far)]
  transfers between devices with their start and end apart: 8 -> 9, of which waited for: 7 -> 8; matrix products, arithmetic and copies ran while one was open for 0% -> 0% of each run, Pallas kernels for 5% -> 7%
where the time goes in v6:
time: 115 us
  blocking collectives  68.1 us (59%)
  waiting for transfers between devices  15.1 us (13%)
  Pallas kernels  15 us (13%)
  starting transfers between devices  11.7 us (10%)
  local copies, waits for them, and re-layouts  3.21 us (3%)
  between operations  1.47 us (1%)
    all_to_all x1, blocking collectives, per_device(): spread_all = exchange(spread, 'col')  24.4 us
    all_to_all x1, blocking collectives, per_device(): parts = exchange(row_part, ('row', 'col'), axis_index_groups=col_near)  16.5 us
    all_to_all x1, blocking collectives, per_device(): exchange(scaled, 'row', axis_index_groups=row_near)  13.8 us
    all_to_all x1, blocking collectives, per_device(): back_parts = exchange(joined, 'row', axis_index_groups=row_near)  13.4 us
    ppermute x1, waiting for transfers between devices, per_device(): got = lax.ppermute(far_sums, ('row', 'col'), col_far)  5.21 us
    ppermute x2, starting transfers between devices, per_device(): got = lax.ppermute(send, 'row', swap)  3.25 us
    unnamed x24, local copies, waits for them, and re-layouts  3.21 us
    ppermute x1, waiting for transfers between devices, per_device(): far_own = lax.ppermute(near_own, 'row', row_far)  3.13 us
  transfers between devices with their start and end apart: 9, of which 8 were waited for; matrix products, arithmetic and copies ran while one was open for 0% of the time, Pallas kernels for 7%

profile of v6, /device:TPU:1, one launch (start us, length us, event | category | flops | bytes accessed | tf_op | source)
XLA Modules:
  0.0 114.7 jit_solution(225128993198677193)
XLA Ops:
  0.6 0.9 copy-done.4
  1.5 0.7 copy-done.5
  2.7 13.8 %all_to_all.20 = bf16[4,512,128]{2,1,0:T(8,128)(2,1)S(1)} all-to-all(bf16[4,512,128]{2,1,0:T(8,128)(2,1)S(1)} %shard_map.138), channel_id=1, replica_groups={{0,64,16,80},{32,96,48,112},{8,72,56,120},{24,88,40,104},{1,65,17,81},{..., dimensions={0} | all-to-all | bytes 1048576 | tf_op jit(solution)/shard_map/all_to_all | solution.py:464
  16.5 0.5 collective-permute-start.1
  17.7 1.2 %shard_map.139.slots_ref = s32[1,640]{1,0:T(1,128)S(1)} custom-call(s32[2]{0:T(128)S(1)} %pad_add_fusion.place_ref, s32[1,1]{1,0:T(1,128)S(6)} %copy.17.live_ref, s32[4,128]{1,0:T(4,128)S(1)} %bitcast.16, s32[4,128]{1,0:T(4,128)S(1)} %bitcast.17, s32[4,128]{1,0:T(4,128)S(1)} %bitcast.18, s32[4,128]{1,0:T(4,128)S(1)} %bitcast.19), custom_call_target="tpu_custom_call" | custom-call | tf_op jit(solution)/shard_map/pallas_call | solution.py:469
  18.9 1.6 %copy-done = bf16[64,128,128]{2,1,0:T(8,128)(2,1)S(1)} copy-done((bf16[64,128,128]{2,1,0:T(8,128)(2,1)S(1)}, bf16[64,128,128]{2,1,0:T(8,128)(2,1)}, u32[]{:S(2)}) %copy-start) | copy-done | bytes 2097176
  20.5 1.7 %shard_map.140.so_far_ref = f32[4096,128]{1,0:T(8,128)S(1)} custom-call(s32[1,640]{1,0:T(1,128)S(1)} %shard_map.139.slots_ref, bf16[64,128,128]{2,1,0:T(8,128)(2,1)S(1)} %copy-done, bf16[2048,128]{1,0:T(8,128)(2,1)S(1)} %bitcast.12, bf16[2048,128]{1,0:T(8,128)(2,1)S(1)} %collective-permute-done.1.other_ref), custom_call_target="tpu_custom_call" | custom-call | flops 8388608 | bytes 6291456 | tf_op jit(solution)/shard_map/pallas_call | solution.py:489
  22.2 3.1 %collective-permute-done.own_ref = bf16[2048,128]{1,0:T(8,128)(2,1)S(1)} collective-permute-done((bf16[2048,128]{1,0:T(8,128)(2,1)S(1)}, bf16[2048,128]{1,0:T(8,128)(2,1)S(1)}, u32[]{:S(2)}, u32[]{:S(2)}) %collective-permute-start) | collective-permute-done | bytes 524320 | tf_op jit(solution)/shard_map/ppermute | solution.py:466
  25.3 2.1 %collective-permute-start.2 = (bf16[2048,128]{1,0:T(8,128)(2,1)S(1)}, bf16[2048,128]{1,0:T(8,128)(2,1)S(1)}, u32[]{:S(2)}, u32[]{:S(2)}) collective-permute-start(bf16[2048,128]{1,0:T(8,128)(2,1)S(1)} %collective-permute-done.own_ref), channel_id=1, source_target_pairs={{0,8},{8,0},{16,24},{24,16},{32,40},{40,32},{48,56},{56,48},{64,72... | collective-permute-start | bytes 1572872 | tf_op jit(solution)/shard_map/ppermute | solution.py:499
  27.4 1.5 %collective-permute-done.2.other_ref = bf16[2048,128]{1,0:T(8,128)(2,1)S(1)} collective-permute-done((bf16[2048,128]{1,0:T(8,128)(2,1)S(1)}, bf16[2048,128]{1,0:T(8,128)(2,1)S(1)}, u32[]{:S(2)}, u32[]{:S(2)}) %collective-permute-start.2) | collective-permute-done | bytes 524320 | tf_op jit(solution)/shard_map/ppermute | solution.py:499
  28.9 1.6 %shard_map.141 = bf16[2048,128]{1,0:T(8,128)(2,1)S(1)} custom-call(s32[1,640]{1,0:T(1,128)S(1)} %shard_map.139.slots_ref, bf16[64,128,128]{2,1,0:T(8,128)(2,1)S(1)} %copy-done, bf16[2048,128]{1,0:T(8,128)(2,1)S(1)} %collective-permute-done.own_ref, bf16[2048,128]{1,0:T(8,128)(2,1)S(1)} %collective-permute-done.2.other_ref, f32[4096,128]{1,0:T(8,128)S(1)} %shard_map.140.so_far_ref), custom_call_target="tpu_custom_call" | custom-call | flops 8388608 | bytes 6291456 | tf_op jit(solution)/shard_map/pallas_call | solution.py:501
  30.6 1.7 %collective-permute-start.3 = (bf16[2048,128]{1,0:T(8,128)(2,1)S(1)}, bf16[2048,128]{1,0:T(8,128)(2,1)S(1)}, u32[]{:S(2)}, u32[]{:S(2)}) collective-permute-start(bf16[2048,128]{1,0:T(8,128)(2,1)S(1)} %shard_map.141), channel_id=1, source_target_pairs={{0,6},{1,7},{2,4},{3,5},{4,2},{5,3},{6,0},{7,1},{8,10},{9,11},{10,... | collective-permute-start | bytes 1572872 | tf_op jit(solution)/shard_map/ppermute | solution.py:511
  32.3 1.6 %shard_map.142.keep_ref = f32[2048,128]{1,0:T(8,128)S(1)} custom-call(s32[1,640]{1,0:T(1,128)S(1)} %shard_map.139.slots_ref, bf16[64,128,128]{2,1,0:T(8,128)(2,1)S(1)} %copy-done, bf16[2048,128]{1,0:T(8,128)(2,1)S(1)} %collective-permute-done.own_ref, bf16[2048,128]{1,0:T(8,128)(2,1)S(1)} %collective-permute-done.2.other_ref, ...), custom_call_target="tpu_custom_call" | custom-call | flops 8388608 | bytes 6291456 | tf_op jit(solution)/shard_map/pallas_call | solution.py:512
  34.0 5.2 %collective-permute-done.3.got_ref = bf16[2048,128]{1,0:T(8,128)(2,1)S(1)} collective-permute-done((bf16[2048,128]{1,0:T(8,128)(2,1)S(1)}, bf16[2048,128]{1,0:T(8,128)(2,1)S(1)}, u32[]{:S(2)}, u32[]{:S(2)}) %collective-permute-start.3) | collective-permute-done | bytes 524320 | tf_op jit(solution)/shard_map/ppermute | solution.py:511
  39.3 16.5 %all_to_all.21.parts_ref = bf16[4,512,128]{2,1,0:T(8,128)(2,1)S(1)} all-to-all(bf16[4,512,128]{2,1,0:T(8,128)(2,1)S(1)} %shard_map.143), channel_id=1, replica_groups={{0,1,2,3},{4,5,6,7},{8,9,14,15},{10,11,12,13},{16,17,18,19},{20,21,22,2..., dimensions={0} | all-to-all | bytes 1048576 | tf_op jit(solution)/shard_map/all_to_all | solution.py:528
  55.7 1.4 %shard_map.144 = (f32[512,256]{1,0:T(8,128)S(1)}, f32[512,256]{1,0:T(8,128)S(1)}, f32[144,128]{1,0:T(8,128)S(1)}, bf16[144,128]{1,0:T(8,128)(2,1)S(1)}) custom-call(s32[2]{0:T(128)S(1)} %pad_add_fusion.place_ref, bf16[4,512,128]{2,1,0:T(8,128)(2,1)S(1)} %all_to_all.21.parts_ref, s32[4,128]{1,0:T(4,128)S(1)} %bitcast.14, bf16[512,256]{1,0:T(8,128)(2,1)S(1)} %copy-done.2, ...), custom_call_target="tpu_custom_call" | custom-call | tf_op jit(solution)/shard_map/pallas_call | solution.py:529
  57.1 1.0 collective-permute-start.4
  58.5 0.5 collective-permute-done.4.got_ref
  59.1 24.4 %all_to_all.22.spread_ref = bf16[8,656,128]{2,1,0:T(8,128)(2,1)S(1)} all-to-all(bf16[8,656,128]{2,1,0:T(8,128)(2,1)S(1)} %shard_map.146), channel_id=1, replica_groups=mesh['row'=16,'col'=8] {'col'}, dimensions={0} | all-to-all | bytes 2686976 | tf_op jit(solution)/shard_map/all_to_all | solution.py:557
  83.5 1.8 %shard_map.147 = (f32[2048,128]{1,0:T(8,128)S(1)}, bf16[2048,128]{1,0:T(8,128)(2,1)S(1)}, bf16[144,128]{1,0:T(8,128)(2,1)S(1)}) custom-call(s32[1,640]{1,0:T(1,128)S(1)} %shard_map.139.slots_ref, bf16[64,128,128]{2,1,0:T(8,128)(2,1)S(1)} %copy-done.1, bf16[8,656,128]{2,1,0:T(8,128)(2,1)S(1)} %all_to_all.22.spread_ref), custom_call_target="tpu_custom_call" | custom-call | flops 8388608 | bytes 6291456 | tf_op jit(solution)/shard_map/pallas_call | solution.py:559
  85.3 1.6 %collective-permute-start.5 = (bf16[2048,128]{1,0:T(8,128)(2,1)S(1)}, bf16[2048,128]{1,0:T(8,128)(2,1)S(1)}, u32[]{:S(2)}, u32[]{:S(2)}) collective-permute-start(bf16[2048,128]{1,0:T(8,128)(2,1)S(1)} %get-tuple-element.38), channel_id=1, source_target_pairs={{0,8},{8,0},{16,24},{24,16},{32,40},{40,32},{48,56},{56,48},{64,72... | collective-permute-start | bytes 1572872 | tf_op jit(solution)/shard_map/ppermute | solution.py:568
  87.0 0.9 shard_map.148
  87.8 0.7 collective-permute-done.5.got_ref
  88.6 1.7 %collective-permute-start.7 = (bf16[2192,128]{1,0:T(8,128)(2,1)S(1)}, bf16[2192,128]{1,0:T(8,128)(2,1)S(1)}, u32[]{:S(2)}, u32[]{:S(2)}) collective-permute-start(bf16[2192,128]{1,0:T(8,128)(2,1)S(1)} %shard_map.149), channel_id=1, source_target_pairs={{0,48},{8,24},{16,32},{24,8},{32,16},{40,56},{48,0},{56,40},{64,11... | collective-permute-start | bytes 1683464 | tf_op jit(solution)/shard_map/ppermute | solution.py:586
  90.3 1.7 %shard_map.150 = (f32[2048,128]{1,0:T(8,128)S(1)}, bf16[2048,128]{1,0:T(8,128)(2,1)S(1)}) custom-call(s32[1,640]{1,0:T(1,128)S(1)} %shard_map.139.slots_ref, bf16[64,128,128]{2,1,0:T(8,128)(2,1)S(1)} %copy-done.1, bf16[8,656,128]{2,1,0:T(8,128)(2,1)S(1)} %all_to_all.22.spread_ref), custom_call_target="tpu_custom_call" | custom-call | flops 8388608 | bytes 6291456 | tf_op jit(solution)/shard_map/pallas_call | solution.py:587
  92.0 1.6 %collective-permute-start.6 = (bf16[2048,128]{1,0:T(8,128)(2,1)S(1)}, bf16[2048,128]{1,0:T(8,128)(2,1)S(1)}, u32[]{:S(2)}, u32[]{:S(2)}) collective-permute-start(bf16[2048,128]{1,0:T(8,128)(2,1)S(1)} %get-tuple-element.48), channel_id=1, source_target_pairs={{0,8},{8,0},{16,24},{24,16},{32,40},{40,32},{48,56},{56,48},{64,72... | collective-permute-start | bytes 1572872 | tf_op jit(solution)/shard_map/ppermute | solution.py:596
  93.7 1.5 %collective-permute-done.6.got_ref = bf16[2048,128]{1,0:T(8,128)(2,1)S(1)} collective-permute-done((bf16[2048,128]{1,0:T(8,128)(2,1)S(1)}, bf16[2048,128]{1,0:T(8,128)(2,1)S(1)}, u32[]{:S(2)}, u32[]{:S(2)}) %collective-permute-start.6) | collective-permute-done | bytes 524320 | tf_op jit(solution)/shard_map/ppermute | solution.py:596
  95.2 2.4 %collective-permute-done.7.far_ref = bf16[2192,128]{1,0:T(8,128)(2,1)S(1)} collective-permute-done((bf16[2192,128]{1,0:T(8,128)(2,1)S(1)}, bf16[2192,128]{1,0:T(8,128)(2,1)S(1)}, u32[]{:S(2)}, u32[]{:S(2)}) %collective-permute-start.7) | collective-permute-done | bytes 561184 | tf_op jit(solution)/shard_map/ppermute | solution.py:586
  97.8 13.4 %all_to_all.23.parts_ref = bf16[4,656,128]{2,1,0:T(8,128)(2,1)S(1)} all-to-all(bf16[4,656,128]{2,1,0:T(8,128)(2,1)S(1)} %shard_map.151), channel_id=1, replica_groups={{0,64,16,80},{32,96,48,112},{8,72,56,120},{24,88,40,104},{1,65,17,81},{..., dimensions={0} | all-to-all | bytes 1343488 | tf_op jit(solution)/shard_map/all_to_all | solution.py:605
  111.2 1.4 %collective-permute-start.8 = (f32[136,128]{1,0:T(8,128)S(1)}, f32[136,128]{1,0:T(8,128)S(1)}, u32[]{:S(2)}, u32[]{:S(2)}) collective-permute-start(f32[136,128]{1,0:T(8,128)S(1)} %shard_map.153.mine_ref), channel_id=1, source_target_pairs={{0,8},{8,0},{16,24},{24,16},{32,40},{40,32},{48,56},{56,48},{64,72... | collective-permute-start | bytes 208904 | tf_op jit(solution)/shard_map/ppermute | solution.py:614
  112.6 0.8 shard_map.152
  113.5 1.2 %shard_map.154 = (f32[128,256]{1,0:T(8,128)}, f32[1,256]{1,0:T(1,128)}) custom-call(s32[2]{0:T(128)S(1)} %pad_add_fusion.place_ref, f32[136,128]{1,0:T(8,128)S(1)} %shard_map.153.mine_ref, f32[136,128]{1,0:T(8,128)S(1)} %collective-permute-done.8.other_ref), custom_call_target="tpu_custom_call" | custom-call | tf_op jit(solution)/shard_map/pallas_call | solution.py:622
  (32 shorter events, 1.4 us)
Async XLA Ops:
  0.6 0.9 copy-start.4
  1.5 0.7 copy-start.5
  2.2 15.5 %copy-start.7 = (s32[1,1,512]{2,1,0:T(1,128)S(1)}, s32[1,1,512]{2,1,0:T(1,128)}, u32[]{:S(2)}) copy-start(s32[1,1,512]{2,1,0:T(1,128)} %param.17) | copy-start | bytes 6148
  2.2 15.5 %copy-start.8 = (s32[1,1,512]{2,1,0:T(1,128)S(1)}, s32[1,1,512]{2,1,0:T(1,128)}, u32[]{:S(2)}) copy-start(s32[1,1,512]{2,1,0:T(1,128)} %param.18) | copy-start | bytes 6148
  2.2 15.5 %copy-start.9 = (s32[1,1,512]{2,1,0:T(1,128)S(1)}, s32[1,1,512]{2,1,0:T(1,128)}, u32[]{:S(2)}) copy-start(s32[1,1,512]{2,1,0:T(1,128)} %param.19) | copy-start | bytes 6148
  2.2 15.5 %copy-start.10 = (s32[1,1,512]{2,1,0:T(1,128)S(1)}, s32[1,1,512]{2,1,0:T(1,128)}, u32[]{:S(2)}) copy-start(s32[1,1,512]{2,1,0:T(1,128)} %param.20) | copy-start | bytes 6148
  16.5 2.5 %collective-permute-start.1 = (bf16[2048,128]{1,0:T(8,128)(2,1)S(1)}, bf16[2048,128]{1,0:T(8,128)(2,1)S(1)}, u32[]{:S(2)}, u32[]{:S(2)}) collective-permute-start(bf16[2048,128]{1,0:T(8,128)(2,1)S(1)} %bitcast.10), channel_id=1, source_target_pairs={{0,8},{8,0},{16,24},{24,16},{32,40},{40,32},{48,56},{56,48},{64,72... | collective-permute-start | bytes 1572872 | tf_op jit(solution)/shard_map/ppermute | solution.py:465
  17.0 8.3 %collective-permute-start = (bf16[2048,128]{1,0:T(8,128)(2,1)S(1)}, bf16[2048,128]{1,0:T(8,128)(2,1)S(1)}, u32[]{:S(2)}, u32[]{:S(2)}) collective-permute-start(bf16[2048,128]{1,0:T(8,128)(2,1)S(1)} %bitcast.11), channel_id=1, source_target_pairs={{0,48},{8,24},{16,32},{24,8},{32,16},{40,56},{48,0},{56,40},{64,11... | collective-permute-start | bytes 1572872 | tf_op jit(solution)/shard_map/ppermute | solution.py:466
  18.9 1.6 %copy-start = (bf16[64,128,128]{2,1,0:T(8,128)(2,1)S(1)}, bf16[64,128,128]{2,1,0:T(8,128)(2,1)}, u32[]{:S(2)}) copy-start(bf16[64,128,128]{2,1,0:T(8,128)(2,1)} %patterns_ref.9) | copy-start | bytes 6291460
  25.3 3.6 %collective-permute-start.2 = (bf16[2048,128]{1,0:T(8,128)(2,1)S(1)}, bf16[2048,128]{1,0:T(8,128)(2,1)S(1)}, u32[]{:S(2)}, u32[]{:S(2)}) collective-permute-start(bf16[2048,128]{1,0:T(8,128)(2,1)S(1)} %collective-permute-done.own_ref), channel_id=1, source_target_pairs={{0,8},{8,0},{16,24},{24,16},{32,40},{40,32},{48,56},{56,48},{64,72... | collective-permute-start | bytes 1572872 | tf_op jit(solution)/shard_map/ppermute | solution.py:499
  30.6 8.6 %collective-permute-start.3 = (bf16[2048,128]{1,0:T(8,128)(2,1)S(1)}, bf16[2048,128]{1,0:T(8,128)(2,1)S(1)}, u32[]{:S(2)}, u32[]{:S(2)}) collective-permute-start(bf16[2048,128]{1,0:T(8,128)(2,1)S(1)} %shard_map.141), channel_id=1, source_target_pairs={{0,6},{1,7},{2,4},{3,5},{4,2},{5,3},{6,0},{7,1},{8,10},{9,11},{10,... | collective-permute-start | bytes 1572872 | tf_op jit(solution)/shard_map/ppermute | solution.py:511
  33.9 21.8 %copy-start.2 = (bf16[512,256]{1,0:T(8,128)(2,1)S(1)}, bf16[512,256]{1,0:T(8,128)(2,1)}, u32[]{:S(2)}) copy-start(bf16[512,256]{1,0:T(8,128)(2,1)} %cotangent_ref.1) | copy-start | bytes 786436
  33.9 21.8 %copy-start.3 = (bf16[128,256]{1,0:T(8,128)(2,1)S(1)}, bf16[128,256]{1,0:T(8,128)(2,1)}, u32[]{:S(2)}) copy-start(bf16[128,256]{1,0:T(8,128)(2,1)} %weight_ref.3) | copy-start | bytes 196612
  33.9 21.8 %copy-start.6 = (s32[512]{0:T(512)S(1)}, s32[512]{0:T(512)}, u32[]{:S(2)}) copy-start(s32[512]{0:T(512)} %param.12) | copy-start | bytes 6148
  33.9 21.8 %copy-start.11 = (f32[256]{0:T(256)S(1)}, f32[256]{0:T(256)}, u32[]{:S(2)}) copy-start(f32[256]{0:T(256)} %param.15) | copy-start | bytes 3076
  57.1 1.9 %collective-permute-start.4 = (bf16[144,128]{1,0:T(8,128)(2,1)S(1)}, bf16[144,128]{1,0:T(8,128)(2,1)S(1)}, u32[]{:S(2)}, u32[]{:S(2)}) collective-permute-start(bf16[144,128]{1,0:T(8,128)(2,1)S(1)} %get-tuple-element.36), channel_id=1, source_target_pairs={{0,8},{8,0},{16,24},{24,16},{32,40},{40,32},{48,56},{56,48},{64,72... | collective-permute-start | bytes 110600 | tf_op jit(solution)/shard_map/ppermute | solution.py:541
  59.1 24.5 %copy-start.1 = (bf16[64,128,128]{2,1,0:T(8,128)(2,1)S(1)}, bf16[64,128,128]{2,1,0:T(8,128)(2,1)}, u32[]{:S(2)}) copy-start(bf16[64,128,128]{2,1,0:T(8,128)(2,1)} %patterns_ref.9) | copy-start | bytes 6291460
  85.3 3.2 %collective-permute-start.5 = (bf16[2048,128]{1,0:T(8,128)(2,1)S(1)}, bf16[2048,128]{1,0:T(8,128)(2,1)S(1)}, u32[]{:S(2)}, u32[]{:S(2)}) collective-permute-start(bf16[2048,128]{1,0:T(8,128)(2,1)S(1)} %get-tuple-element.38), channel_id=1, source_target_pairs={{0,8},{8,0},{16,24},{24,16},{32,40},{40,32},{48,56},{56,48},{64,72... | collective-permute-start | bytes 1572872 | tf_op jit(solution)/shard_map/ppermute | solution.py:568
  88.6 9.0 %collective-permute-start.7 = (bf16[2192,128]{1,0:T(8,128)(2,1)S(1)}, bf16[2192,128]{1,0:T(8,128)(2,1)S(1)}, u32[]{:S(2)}, u32[]{:S(2)}) collective-permute-start(bf16[2192,128]{1,0:T(8,128)(2,1)S(1)} %shard_map.149), channel_id=1, source_target_pairs={{0,48},{8,24},{16,32},{24,8},{32,16},{40,56},{48,0},{56,40},{64,11... | collective-permute-start | bytes 1683464 | tf_op jit(solution)/shard_map/ppermute | solution.py:586
  92.0 3.1 %collective-permute-start.6 = (bf16[2048,128]{1,0:T(8,128)(2,1)S(1)}, bf16[2048,128]{1,0:T(8,128)(2,1)S(1)}, u32[]{:S(2)}, u32[]{:S(2)}) collective-permute-start(bf16[2048,128]{1,0:T(8,128)(2,1)S(1)} %get-tuple-element.48), channel_id=1, source_target_pairs={{0,8},{8,0},{16,24},{24,16},{32,40},{40,32},{48,56},{56,48},{64,72... | collective-permute-start | bytes 1572872 | tf_op jit(solution)/shard_map/ppermute | solution.py:596
  111.2 2.3 %collective-permute-start.8 = (f32[136,128]{1,0:T(8,128)S(1)}, f32[136,128]{1,0:T(8,128)S(1)}, u32[]{:S(2)}, u32[]{:S(2)}) collective-permute-start(f32[136,128]{1,0:T(8,128)S(1)} %shard_map.153.mine_ref), channel_id=1, source_target_pairs={{0,8},{8,0},{16,24},{24,16},{32,40},{40,32},{48,56},{56,48},{64,72... | collective-permute-start | bytes 208904 | tf_op jit(solution)/shard_map/ppermute | solution.py:614

commit v7 on v5

--- a/solution.py
+++ b/solution.py
@@ -202,13 +202,8 @@
     send_ref[...] = sums[half:, :].astype(jnp.bfloat16)
 
 
-def backward_far_kernel(slots_ref, patterns_ref, spread_ref, keep_ref, send_ref, grads_ref, sums):
+def backward_far_kernel(slots_ref, patterns_ref, spread_ref, keep_ref, send_ref, sums):
     backward_sums(slots_ref, patterns_ref, spread_ref, keep_ref, send_ref, sums, True)
-    own = spread_ref.shape[1] - grads_ref.shape[0]
-    grads = spread_ref[0, own:, :].astype(jnp.float32)
-    for shard in range(1, spread_ref.shape[0]):
-        grads += spread_ref[shard, own:, :].astype(jnp.float32)
-    grads_ref[...] = grads.astype(jnp.bfloat16)
 
 
 def backward_near_kernel(slots_ref, patterns_ref, spread_ref, keep_ref, send_ref, sums):
@@ -227,6 +222,44 @@
     square = pre_act * pre_act
     bent = jnp.tanh(ROOT_2_PI * (pre_act + CUBIC * (pre_act * square)))
     return square, bent, 0.5 * (1.0 + bent)
+
+
+def middle_tile(tile, roots, parts_ref, cotangent_ref, weight, bias_ref):
+    edge = roots.shape[0]
+    rows = pl.ds(tile * edge, edge)
+    sums = parts_ref[0, rows, :].astype(jnp.float32)
+    for shard in range(1, parts_ref.shape[0]):
+        sums += parts_ref[shard, rows, :].astype(jnp.float32)
+    inv_root = roots[:, tile : tile + 1]
+    pre_act = inv_root * split_product(sums, weight, ((1,), (0,))) + bias_ref[...]
+    square, bent, half = activate(pre_act)
+    rise = 0.5 * pre_act * (1.0 - bent * bent) * (ROOT_2_PI * (1.0 + 3.0 * CUBIC * square))
+    slope = cotangent_ref[rows, :].astype(jnp.float32) * (half + rise)
+    return sums, pre_act * half, slope, inv_root
+
+
+def spread_kernel(
+    parts_ref, degree_ref, cotangent_ref, weight_ref, bias_ref, out_ref, done_ref
+):
+    tiles, edge = degree_ref.shape
+    weight = weight_ref[...]
+    roots = root_columns(degree_ref[...])
+    for tile in range(tiles):
+        _, _, slope, inv_root = middle_tile(
+            tile, roots, parts_ref, cotangent_ref, weight, bias_ref
+        )
+        upstream = inv_root * slope
+        high = upstream.astype(jnp.bfloat16)
+        low = (upstream - high.astype(jnp.float32)).astype(jnp.bfloat16)
+        spread = sum(
+            lax.dot_general(
+                weight, part, (((1,), (1,)), ((), ())), preferred_element_type=jnp.float32
+            )
+            for part in (high, low)
+        ).astype(jnp.bfloat16)
+        for shard in range(out_ref.shape[0]):
+            out_ref[shard, pl.ds(tile * edge, edge), :] = spread
+    done_ref[...] = jnp.zeros_like(done_ref)
 
 
 def middle_kernel(
@@ -236,77 +269,35 @@
     cotangent_ref,
     weight_ref,
     bias_ref,
-    pre_ref,
-    upstream_ref,
+    act_ref,
     keep_ref,
     send_ref,
 ):
     tiles, edge = degree_ref.shape
-    shards = parts_ref.shape[0]
     weight = weight_ref[...]
     height = weight.shape[0]
     roots = root_columns(degree_ref[...])
     grads = jnp.zeros(weight.shape, jnp.float32)
     bias_row = jnp.zeros(bias_ref.shape, jnp.float32)
     for tile in range(tiles):
-        rows = pl.ds(tile * edge, edge)
-        sums = parts_ref[0, rows, :].astype(jnp.float32)
-        for shard in range(1, shards):
-            sums += parts_ref[shard, rows, :].astype(jnp.float32)
-        inv_root = roots[:, tile : tile + 1]
-        pre_act = inv_root * split_product(sums, weight, ((1,), (0,))) + bias_ref[...]
-        pre_ref[rows, :] = pre_act
-        square, bent, half = activate(pre_act)
-        rise = 0.5 * pre_act * (1.0 - bent * bent) * (ROOT_2_PI * (1.0 + 3.0 * CUBIC * square))
-        slope = cotangent_ref[rows, :].astype(jnp.float32) * (half + rise)
-        upstream = inv_root * slope
-        upstream_ref[rows, :] = upstream
-        grads += split_product(sums, upstream.astype(jnp.bfloat16), ((0,), (0,)))
+        sums, activations, slope, inv_root = middle_tile(
+            tile, roots, parts_ref, cotangent_ref, weight, bias_ref
+        )
+        act_ref[pl.ds(tile * edge, edge), :] = activations.astype(jnp.bfloat16)
+        upstream = (inv_root * slope).astype(jnp.bfloat16)
+        grads += split_product(sums, upstream, ((0,), (0,)))
         bias_row += jnp.sum(slope, axis=0, keepdims=True)
     width = keep_ref.shape[1]
-    bias_high = bias_row.astype(jnp.bfloat16).astype(jnp.float32)
-    bias_low = bias_row - bias_high
     first = place_ref[0] % 2 == 0
 
     def put(target, left):
         pick = lambda whole: jnp.where(left, whole[:, :width], whole[:, width:])
-        target[:height, :] = pick(grads).astype(target.dtype)
+        target[:height, :] = pick(grads)
         row_ids = lax.broadcasted_iota(jnp.int32, (BIAS_ROWS, width), 0)
-        block = jnp.where(row_ids == 0, pick(bias_high), 0.0)
-        block = jnp.where(row_ids == 1, pick(bias_low), block)
-        target[height:, :] = block.astype(target.dtype)
+        target[height:, :] = jnp.where(row_ids == 0, pick(bias_row), 0.0)
 
     put(keep_ref, first)
     put(send_ref, jnp.logical_not(first))
-
-
-def activation_kernel(pre_ref, act_ref):
-    pre_act = pre_ref[...]
-    act_ref[...] = (pre_act * activate(pre_act)[2]).astype(jnp.bfloat16)
-
-
-def spread_kernel(upstream_ref, weight_ref, out_ref):
-    edge = out_ref.shape[2]
-    for tile in range(upstream_ref.shape[0] // edge):
-        rows = pl.ds(tile * edge, edge)
-        upstream = upstream_ref[rows, :]
-        high = upstream.astype(jnp.bfloat16)
-        low = (upstream - high.astype(jnp.float32)).astype(jnp.bfloat16)
-        spread = sum(
-            lax.dot_general(
-                weight_ref[...], part, (((1,), (1,)), ((), ())), preferred_element_type=jnp.float32
-            )
-            for part in (high, low)
-        ).astype(jnp.bfloat16)
-        for shard in range(out_ref.shape[0]):
-            out_ref[shard, rows, :] = spread
-
-
-def append_kernel(keep_ref, got_ref, spread_ref, out_ref):
-    terms = (keep_ref[...] + got_ref[...].astype(jnp.float32)).astype(jnp.bfloat16)
-    rows = pl.ds(out_ref.shape[1] - terms.shape[0], terms.shape[0])
-    for shard in range(out_ref.shape[0]):
-        out_ref[shard, rows, :] = terms
 
 
 def sum_of_four(parts_ref, rows):
@@ -314,10 +305,22 @@
     return (part(0) + part(2)) + (part(1) + part(3))
 
 
-def far_join_kernel(keep_ref, got_ref, grads_ref, out_ref):
+def terms_to_send(grads_ref):
+    height = grads_ref.shape[0] - BIAS_ROWS
+    bias = grads_ref[height:, :]
+    high = bias.astype(jnp.bfloat16).astype(jnp.float32)
+    row_ids = lax.broadcasted_iota(jnp.int32, bias.shape, 0)
+    low = jnp.broadcast_to((bias - high)[0:1, :], bias.shape)
+    bias = jnp.where(row_ids == 1, low, high)
+    return jnp.concatenate([grads_ref[:height, :], bias], 0).astype(jnp.bfloat16)
+
+
+def far_join_kernel(keep_ref, got_ref, grads_ref, out_ref, terms_ref):
     half = keep_ref.shape[0]
     out_ref[:half, :] = (keep_ref[...] + got_ref[...].astype(jnp.float32)).astype(jnp.bfloat16)
-    out_ref[half:, :] = grads_ref[...]
+    terms = terms_to_send(grads_ref)
+    out_ref[half:, :] = terms
+    terms_ref[...] = terms
 
 
 def near_join_kernel(keep_ref, got_ref, far_ref, grads_ref, out_ref):
@@ -396,6 +399,18 @@
         (index, (index // 8 * 4 + far_neighbour(index // 2 % 4, index % 2)) * 2 + index % 2)
         for index in range(row_devices)
     ]
+    col_far, col_close, col_high = (
+        [
+            (index * col_devices + place, index * col_devices + peer(place, index % 2))
+            for index in range(row_devices)
+            for place in range(col_devices)
+        ]
+        for peer in (
+            lambda place, core: far_neighbour(place // 2, core) * 2 + place % 2,
+            lambda place, core: far_neighbour(place // 2, 1 - core) * 2 + place % 2,
+            lambda place, core: place ^ 1,
+        )
+    )
     exchange = functools.partial(lax.all_to_all, split_axis=0, concat_axis=0)
     extra = feature_count + BIAS_ROWS
     half = chips * node_dev
@@ -466,60 +481,44 @@
         cost_estimate=tile_cost,
     )(slots, patterns, far_own, far_other, near_sums)
     parts = exchange(row_part.reshape(col_devices, node_dev, feature_count), "col")
-    pre_act, upstream, keep_terms, send_terms = pl.pallas_call(
+    middle_inputs = (parts, degree_tiles, cotangent, weight, layer_bias[None, :])
+    spread, done = pl.pallas_call(
+        spread_kernel,
+        out_shape=(shape((col_devices, node_dev, edge), bf16), shape((8, edge), f32)),
+        in_specs=[VMEM] * 5,
+        out_specs=(VMEM,) * 2,
+        compiler_params=PARAMS,
+    )(*middle_inputs)
+    spread_all = exchange(spread, "col")
+    middle_inputs, _ = lax.optimization_barrier((middle_inputs, done))
+    terms = shape((extra, edge), f32)
+    activations, keep_terms, send_terms = pl.pallas_call(
         middle_kernel,
-        out_shape=(
-            shape((node_dev, hidden), f32),
-            shape((node_dev, hidden), f32),
-            shape((extra, edge), f32),
-            shape((extra, edge), bf16),
-        ),
+        out_shape=(shape((node_dev, hidden), bf16), terms, terms),
         in_specs=[SMEM] + [VMEM] * 5,
-        out_specs=(VMEM,) * 4,
-        compiler_params=PARAMS,
-    )(place, parts, degree_tiles, cotangent, weight, layer_bias[None, :])
-    got_terms = lax.ppermute(send_terms, "row", swap)
-    spread = pl.pallas_call(
-        spread_kernel,
-        out_shape=shape((col_devices, node_dev + extra, edge), bf16),
-        in_specs=[VMEM] * 2,
-        out_specs=VMEM,
-        compiler_params=PARAMS,
-    )(upstream, weight)
-    spread = pl.pallas_call(
-        append_kernel,
-        out_shape=shape(spread.shape, bf16),
-        in_specs=[VMEM] * 3,
-        out_specs=VMEM,
-        input_output_aliases={2: 0},
-        compiler_params=PARAMS,
-    )(keep_terms, got_terms, spread)
-    spread_all = exchange(spread, "col")
+        out_specs=(VMEM,) * 3,
+        compiler_params=PARAMS,
+    )(place, *middle_inputs)
+    grads = keep_terms + lax.ppermute(send_terms, "row", swap)
+    for pairs in (col_far, col_close, col_high):
+        grads = grads + lax.ppermute(grads, ("row", "col"), pairs)
+    spread_all, grads, activations = lax.optimization_barrier((spread_all, grads, activations))
     kept, sent = shape((half // 2, edge), f32), shape((half // 2, edge), bf16)
-    keep, send, grads = pl.pallas_call(
+    keep, send = pl.pallas_call(
         backward_far_kernel,
-        out_shape=(kept, sent, shape((extra, edge), bf16)),
+        out_shape=(kept, sent),
         in_specs=[SMEM] + [VMEM] * 2,
-        out_specs=(VMEM,) * 3,
+        out_specs=(VMEM,) * 2,
         scratch_shapes=[pltpu.VMEM((half, edge), f32)],
         compiler_params=PARAMS,
         cost_estimate=tile_cost,
     )(slots, patterns, spread_all)
     got = lax.ppermute(send, "row", swap)
-    pre_act, keep = lax.optimization_barrier((pre_act, keep))
-    activations = pl.pallas_call(
-        activation_kernel,
-        out_shape=shape((node_dev, hidden), bf16),
-        in_specs=[VMEM],
-        out_specs=VMEM,
-        compiler_params=PARAMS,
-    )(pre_act)
-    got, activations = lax.optimization_barrier((got, activations))
-    far_sums = pl.pallas_call(
+    far_sums, grads = pl.pallas_call(
         far_join_kernel,
-        out_shape=shape((half // 2 + extra, edge), bf16),
+        out_shape=(shape((half // 2 + extra, edge), bf16), shape((extra, edge), bf16)),
         in_specs=[VMEM] * 3,
-        out_specs=VMEM,
+        out_specs=(VMEM,) * 2,
         compiler_params=PARAMS,
     )(keep, got, grads)
     far_sums, spread_all = lax.optimization_barrier((far_sums, spread_all))

time: 114 us -> 118 us (1.035)
  blocking collectives: 74.3 us -> 49.4 us
  waiting for transfers between devices: 8.16 us -> 24.2 us
  local copies, waits for them, and re-layouts: 3.22 us -> 8.11 us
  starting transfers between devices: 14.9 us -> 18.6 us
  Pallas kernels: 11.8 us -> 15.5 us
    all_to_all x1 -> x0, blocking collectives: 22.6 us -> none  [per_device(): spread_all = exchange(spread, 'col')]
    ppermute x1 -> x4, waiting for transfers between devices: 0.55 us -> 15.3 us  [the longest x3 14.4 us: per_device(): grads = grads + lax.ppermute(grads, ('row', 'col'), pairs)]
    unnamed x24 -> x30, local copies, waits for them, and re-layouts: 3.22 us -> 8.11 us
    ppermute x2, starting transfers between devices: 7.02 us -> 2.95 us  [per_device(): got = lax.ppermute(send, 'row', swap)]
    ppermute x1, waiting for transfers between devices: 0.01 us -> 3.93 us  [per_device(): far_got = lax.ppermute(far_sums, 'row', row_far)]
    all_to_all x1, blocking collectives: 14.6 us -> 10.9 us  [per_device(): back_parts = exchange(joined, 'row', axis_index_groups=row_near)]
    all_to_all x0 -> x1, starting transfers between devices: none -> 3.69 us  [per_device(): spread_all = exchange(spread, 'col')]
    ppermute x1, waiting for transfers between devices: 3.53 us -> 0.27 us  [per_device(): far_own = lax.ppermute(near_own, 'row', row_far)]
  transfers between devices with their start and end apart: 8 -> 12, of which waited for: 7 -> 10; matrix products, arithmetic and copies ran while one was open for 0% -> 0% of each run, Pallas kernels for 5% -> 7%
where the time goes in v7:
time: 118 us; the launch traced here: 117 us
  blocking collectives  49.4 us (42%)
  waiting for transfers between devices  24.2 us (21%)
  starting transfers between devices  18.6 us (16%)
  Pallas kernels  15.5 us (13%)
  local copies, waits for them, and re-layouts  8.11 us (7%)
  between operations  1.48 us (1%)
    all_to_all x1, blocking collectives, per_device(): exchange(row_part.reshape(col_devices, node_dev, feature_count), 'col')  24.8 us
    ppermute x3, waiting for transfers between devices, per_device(): grads = grads + lax.ppermute(grads, ('row', 'col'), pairs)  14.4 us
    all_to_all x1, blocking collectives, per_device(): exchange(scaled, 'row', axis_index_groups=row_near)  13.8 us
    all_to_all x1, blocking collectives, per_device(): back_parts = exchange(joined, 'row', axis_index_groups=row_near)  10.9 us
    unnamed x30, local copies, waits for them, and re-layouts  8.11 us
    ppermute x3, starting transfers between devices, per_device(): grads = grads + lax.ppermute(grads, ('row', 'col'), pairs)  5.53 us
    ppermute x1, waiting for transfers between devices, per_device(): far_got = lax.ppermute(far_sums, 'row', row_far)  3.93 us
    all_to_all x1, starting transfers between devices, per_device(): spread_all = exchange(spread, 'col')  3.69 us
  transfers between devices with their start and end apart: 12, of which 10 were waited for; matrix products, arithmetic and copies ran while one was open for 0% of the time, Pallas kernels for 7%

profile of v7, /device:TPU:1, one launch (start us, length us, event | category | flops | bytes accessed | tf_op | source)
XLA Modules:
  0.0 117.4 jit_solution(16673493888896557390)
XLA Ops:
  0.6 0.9 copy-done.7
  2.6 13.8 %all_to_all.20 = bf16[4,512,128]{2,1,0:T(8,128)(2,1)S(1)} all-to-all(bf16[4,512,128]{2,1,0:T(8,128)(2,1)S(1)} %shard_map.138), channel_id=1, replica_groups={{0,64,16,80},{32,96,48,112},{8,72,56,120},{24,88,40,104},{1,65,17,81},{..., dimensions={0} | all-to-all | bytes 1048576 | tf_op jit(solution)/shard_map/all_to_all | solution.py:438
  18.3 0.7 copy-done.12
  19.0 0.7 copy-done.13
  21.0 1.6 %copy-done = bf16[64,128,128]{2,1,0:T(8,128)(2,1)S(1)} copy-done((bf16[64,128,128]{2,1,0:T(8,128)(2,1)S(1)}, bf16[64,128,128]{2,1,0:T(8,128)(2,1)}, u32[]{:S(2)}) %copy-start) | copy-done | bytes 2097176
  22.6 2.4 %shard_map.140.so_far_ref = f32[4096,128]{1,0:T(8,128)S(1)} custom-call(s32[1,640]{1,0:T(1,128)S(1)} %shard_map.139.slots_ref, bf16[64,128,128]{2,1,0:T(8,128)(2,1)S(1)} %copy-done, bf16[2048,128]{1,0:T(8,128)(2,1)S(1)} %bitcast.13, bf16[2048,128]{1,0:T(8,128)(2,1)S(1)} %collective-permute-done.1.other_ref), custom_call_target="tpu_custom_call" | custom-call | flops 8388608 | bytes 6291456 | tf_op jit(solution)/shard_map/pallas_call | solution.py:463
  25.3 2.6 %collective-permute-start.2 = (bf16[2048,128]{1,0:T(8,128)(2,1)S(1)}, bf16[2048,128]{1,0:T(8,128)(2,1)S(1)}, u32[]{:S(2)}, u32[]{:S(2)}) collective-permute-start(bf16[2048,128]{1,0:T(8,128)(2,1)S(1)} %collective-permute-done.own_ref), channel_id=1, source_target_pairs={{0,8},{8,0},{16,24},{24,16},{32,40},{40,32},{48,56},{56,48},{64,72... | collective-permute-start | bytes 1572872 | tf_op jit(solution)/shard_map/ppermute | solution.py:473
  27.9 1.5 %collective-permute-done.2.other_ref = bf16[2048,128]{1,0:T(8,128)(2,1)S(1)} collective-permute-done((bf16[2048,128]{1,0:T(8,128)(2,1)S(1)}, bf16[2048,128]{1,0:T(8,128)(2,1)S(1)}, u32[]{:S(2)}, u32[]{:S(2)}) %collective-permute-start.2) | collective-permute-done | bytes 524320 | tf_op jit(solution)/shard_map/ppermute | solution.py:473
  29.4 2.6 %shard_map.141 = bf16[4096,128]{1,0:T(8,128)(2,1)S(1)} custom-call(s32[1,640]{1,0:T(1,128)S(1)} %shard_map.139.slots_ref, bf16[64,128,128]{2,1,0:T(8,128)(2,1)S(1)} %copy-done, bf16[2048,128]{1,0:T(8,128)(2,1)S(1)} %collective-permute-done.own_ref, bf16[2048,128]{1,0:T(8,128)(2,1)S(1)} %collective-permute-done.2.other_ref, f32[4096,128]{1,0:T(8,128)S(1)} %shard_map.140.so_far_ref), custom_call_target="tpu_custom_call" | custom-call | flops 8388608 | bytes 6291456 | tf_op jit(solution)/shard_map/pallas_call | solution.py:474
  32.0 24.8 %all_to_all.21.parts_ref = bf16[8,512,128]{2,1,0:T(8,128)(2,1)S(1)} all-to-all(bf16[8,512,128]{2,1,0:T(8,128)(2,1)S(1)} %bitcast.10), channel_id=1, replica_groups=mesh['row'=16,'col'=8] {'col'}, dimensions={0} | all-to-all | bytes 2097152 | tf_op jit(solution)/shard_map/all_to_all | solution.py:483
  56.8 1.3 %shard_map.142 = (bf16[8,512,128]{2,1,0:T(8,128)(2,1)S(1)}, f32[8,128]{1,0:T(8,128)}) custom-call(bf16[8,512,128]{2,1,0:T(8,128)(2,1)S(1)} %all_to_all.21.parts_ref, s32[4,128]{1,0:T(4,128)S(1)} %bitcast.15, bf16[512,256]{1,0:T(8,128)(2,1)S(1)} %copy-done.5, bf16[128,256]{1,0:T(8,128)(2,1)S(1)} %copy-done.6, f32[1,256]{1,0:T(1,128)S(1)} %bitcast.18), custom_call_target="tpu_custom_call" | custom-call | tf_op jit(solution)/shard_map/pallas_call | solution.py:485
  58.1 1.0 copy-done.4
  59.1 3.7 %all-to-all-start.2 = ((bf16[8,512,128]{2,1,0:T(8,128)(2,1)}), bf16[8,512,128]{2,1,0:T(8,128)(2,1)S(1)}, u32[]{:S(2)}, u32[]{:S(2)}) async-start(bf16[8,512,128]{2,1,0:T(8,128)(2,1)} %copy-done.4), calls=%async_computation.2 | async-start | bytes 2097152 | tf_op jit(solution)/shard_map/all_to_all | solution.py:492
  62.8 1.2 %copy-done.3 = bf16[8,512,128]{2,1,0:T(8,128)(2,1)S(1)} copy-done((bf16[8,512,128]{2,1,0:T(8,128)(2,1)S(1)}, bf16[8,512,128]{2,1,0:T(8,128)(2,1)}, u32[]{:S(2)}) %copy-start.3) | copy-done | bytes 1048600
  64.0 1.4 %shard_map.143 = (bf16[512,256]{1,0:T(8,128)(2,1)}, f32[144,128]{1,0:T(8,128)S(1)}, f32[144,128]{1,0:T(8,128)S(1)}) custom-call(s32[1]{0:T(128)} %bitcast.place_ref, bf16[8,512,128]{2,1,0:T(8,128)(2,1)S(1)} %copy-done.3, s32[4,128]{1,0:T(4,128)S(1)} %bitcast.16, bf16[512,256]{1,0:T(8,128)(2,1)S(1)} %copy-done.5, bf16[128,256]{1,0:T(8,128)(2,1)S(1)} %copy-done.6, ...), custom_call_target="tpu_custom_call" | custom-call | tf_op jit(solution)/shard_map/pallas_call | solution.py:495
  65.8 0.9 collective-permute-done.3
  66.7 1.7 %collective-permute-start.4 = (f32[144,128]{1,0:T(8,128)S(1)}, f32[144,128]{1,0:T(8,128)S(1)}, u32[]{:S(2)}, u32[]{:S(2)}) collective-permute-start(f32[144,128]{1,0:T(8,128)S(1)} %add.12), channel_id=1, source_target_pairs={{0,6},{1,7},{2,4},{3,5},{4,2},{5,3},{6,0},{7,1},{8,10},{9,11},{10,... | collective-permute-start | bytes 221192 | tf_op jit(solution)/shard_map/ppermute | solution.py:504
  68.4 8.9 %collective-permute-done.4 = f32[144,128]{1,0:T(8,128)S(1)} collective-permute-done((f32[144,128]{1,0:T(8,128)S(1)}, f32[144,128]{1,0:T(8,128)S(1)}, u32[]{:S(2)}, u32[]{:S(2)}) %collective-permute-start.4) | collective-permute-done | bytes 73760 | tf_op jit(solution)/shard_map/ppermute | solution.py:504
  77.4 0.7 collective-permute-start.5
  78.1 3.8 %collective-permute-done.5 = f32[144,128]{1,0:T(8,128)S(1)} collective-permute-done((f32[144,128]{1,0:T(8,128)S(1)}, f32[144,128]{1,0:T(8,128)S(1)}, u32[]{:S(2)}, u32[]{:S(2)}) %collective-permute-start.5) | collective-permute-done | bytes 73760 | tf_op jit(solution)/shard_map/ppermute | solution.py:504
  81.9 3.1 %collective-permute-start.6 = (f32[144,128]{1,0:T(8,128)S(1)}, f32[144,128]{1,0:T(8,128)S(1)}, u32[]{:S(2)}, u32[]{:S(2)}) collective-permute-start(f32[144,128]{1,0:T(8,128)S(1)} %add.14), channel_id=1, source_target_pairs={{0,1},{1,0},{2,3},{3,2},{4,5},{5,4},{6,7},{7,6},{8,9},{9,8},{10,11... | collective-permute-start | bytes 221192 | tf_op jit(solution)/shard_map/ppermute | solution.py:504
  85.0 1.7 %collective-permute-done.6 = f32[144,128]{1,0:T(8,128)S(1)} collective-permute-done((f32[144,128]{1,0:T(8,128)S(1)}, f32[144,128]{1,0:T(8,128)S(1)}, u32[]{:S(2)}, u32[]{:S(2)}) %collective-permute-start.6) | collective-permute-done | bytes 73760 | tf_op jit(solution)/shard_map/ppermute | solution.py:504
  86.7 2.5 %shard_map.144 = (f32[2048,128]{1,0:T(8,128)S(1)}, bf16[2048,128]{1,0:T(8,128)(2,1)S(1)}) custom-call(s32[1,640]{1,0:T(1,128)S(1)} %shard_map.139.slots_ref, bf16[64,128,128]{2,1,0:T(8,128)(2,1)S(1)} %copy-done.1, bf16[8,512,128]{2,1,0:T(8,128)(2,1)S(1)} %all-to-all-done.2.spread_ref), custom_call_target="tpu_custom_call" | custom-call | flops 8388608 | bytes 6291456 | tf_op jit(solution)/shard_map/pallas_call | solution.py:507
  89.2 2.2 %collective-permute-start.7 = (bf16[2048,128]{1,0:T(8,128)(2,1)S(1)}, bf16[2048,128]{1,0:T(8,128)(2,1)S(1)}, u32[]{:S(2)}, u32[]{:S(2)}) collective-permute-start(bf16[2048,128]{1,0:T(8,128)(2,1)S(1)} %get-tuple-element.48), channel_id=1, source_target_pairs={{0,8},{8,0},{16,24},{24,16},{32,40},{40,32},{48,56},{56,48},{64,72... | collective-permute-start | bytes 1572872 | tf_op jit(solution)/shard_map/ppermute | solution.py:516
  91.4 1.5 %collective-permute-done.7.got_ref = bf16[2048,128]{1,0:T(8,128)(2,1)S(1)} collective-permute-done((bf16[2048,128]{1,0:T(8,128)(2,1)S(1)}, bf16[2048,128]{1,0:T(8,128)(2,1)S(1)}, u32[]{:S(2)}, u32[]{:S(2)}) %collective-permute-start.7) | collective-permute-done | bytes 524320 | tf_op jit(solution)/shard_map/ppermute | solution.py:516
  93.2 2.5 %shard_map.146 = (f32[2048,128]{1,0:T(8,128)S(1)}, bf16[2048,128]{1,0:T(8,128)(2,1)S(1)}) custom-call(s32[1,640]{1,0:T(1,128)S(1)} %shard_map.139.slots_ref, bf16[64,128,128]{2,1,0:T(8,128)(2,1)S(1)} %copy-done.1, bf16[8,512,128]{2,1,0:T(8,128)(2,1)S(1)} %all-to-all-done.2.spread_ref), custom_call_target="tpu_custom_call" | custom-call | flops 8388608 | bytes 6291456 | tf_op jit(solution)/shard_map/pallas_call | solution.py:526
  95.7 0.7 collective-permute-start.8
  96.4 1.5 %collective-permute-done.8.got_ref = bf16[2048,128]{1,0:T(8,128)(2,1)S(1)} collective-permute-done((bf16[2048,128]{1,0:T(8,128)(2,1)S(1)}, bf16[2048,128]{1,0:T(8,128)(2,1)S(1)}, u32[]{:S(2)}, u32[]{:S(2)}) %collective-permute-start.8) | collective-permute-done | bytes 524320 | tf_op jit(solution)/shard_map/ppermute | solution.py:535
  97.9 3.9 %collective-permute-done.9.far_ref = bf16[2192,128]{1,0:T(8,128)(2,1)S(1)} collective-permute-done((bf16[2192,128]{1,0:T(8,128)(2,1)S(1)}, bf16[2192,128]{1,0:T(8,128)(2,1)S(1)}, u32[]{:S(2)}, u32[]{:S(2)}) %collective-permute-start.9) | collective-permute-done | bytes 561184 | tf_op jit(solution)/shard_map/ppermute | solution.py:525
  102.1 10.9 %all_to_all.22.parts_ref = bf16[4,656,128]{2,1,0:T(8,128)(2,1)S(1)} all-to-all(bf16[4,656,128]{2,1,0:T(8,128)(2,1)S(1)} %shard_map.147), channel_id=1, replica_groups={{0,64,16,80},{32,96,48,112},{8,72,56,120},{24,88,40,104},{1,65,17,81},{..., dimensions={0} | all-to-all | bytes 1343488 | tf_op jit(solution)/shard_map/all_to_all | solution.py:544
  113.0 2.8 %collective-permute-start.10 = (f32[136,128]{1,0:T(8,128)S(1)}, f32[136,128]{1,0:T(8,128)S(1)}, u32[]{:S(2)}, u32[]{:S(2)}) collective-permute-start(f32[136,128]{1,0:T(8,128)S(1)} %shard_map.149.mine_ref), channel_id=1, source_target_pairs={{0,8},{8,0},{16,24},{24,16},{32,40},{40,32},{48,56},{56,48},{64,72... | collective-permute-start | bytes 208904 | tf_op jit(solution)/shard_map/ppermute | solution.py:553
  115.8 0.8 shard_map.148
  (42 shorter events, 5.5 us)
Async XLA Ops:
  0.6 0.9 copy-start.7
  1.5 0.7 copy-start.8
  16.4 4.5 %collective-permute-start.1 = (bf16[2048,128]{1,0:T(8,128)(2,1)S(1)}, bf16[2048,128]{1,0:T(8,128)(2,1)S(1)}, u32[]{:S(2)}, u32[]{:S(2)}) collective-permute-start(bf16[2048,128]{1,0:T(8,128)(2,1)S(1)} %bitcast.11), channel_id=1, source_target_pairs={{0,8},{8,0},{16,24},{24,16},{32,40},{40,32},{48,56},{56,48},{64,72... | collective-permute-start | bytes 1572872 | tf_op jit(solution)/shard_map/ppermute | solution.py:439
  17.0 8.3 %collective-permute-start = (bf16[2048,128]{1,0:T(8,128)(2,1)S(1)}, bf16[2048,128]{1,0:T(8,128)(2,1)S(1)}, u32[]{:S(2)}, u32[]{:S(2)}) collective-permute-start(bf16[2048,128]{1,0:T(8,128)(2,1)S(1)} %bitcast.12), channel_id=1, source_target_pairs={{0,48},{8,24},{16,32},{24,8},{32,16},{40,56},{48,0},{56,40},{64,11... | collective-permute-start | bytes 1572872 | tf_op jit(solution)/shard_map/ppermute | solution.py:440
  17.6 0.7 copy-start.11
  18.3 0.7 copy-start.12
  19.0 0.7 copy-start.13
  19.7 0.7 copy-start.14
  21.0 1.6 %copy-start = (bf16[64,128,128]{2,1,0:T(8,128)(2,1)S(1)}, bf16[64,128,128]{2,1,0:T(8,128)(2,1)}, u32[]{:S(2)}) copy-start(bf16[64,128,128]{2,1,0:T(8,128)(2,1)} %patterns_ref.7) | copy-start | bytes 6291460
  25.3 4.1 %collective-permute-start.2 = (bf16[2048,128]{1,0:T(8,128)(2,1)S(1)}, bf16[2048,128]{1,0:T(8,128)(2,1)S(1)}, u32[]{:S(2)}, u32[]{:S(2)}) collective-permute-start(bf16[2048,128]{1,0:T(8,128)(2,1)S(1)} %collective-permute-done.own_ref), channel_id=1, source_target_pairs={{0,8},{8,0},{16,24},{24,16},{32,40},{40,32},{48,56},{56,48},{64,72... | collective-permute-start | bytes 1572872 | tf_op jit(solution)/shard_map/ppermute | solution.py:473
  32.0 24.8 %copy-start.5 = (bf16[512,256]{1,0:T(8,128)(2,1)S(1)}, bf16[512,256]{1,0:T(8,128)(2,1)}, u32[]{:S(2)}) copy-start(bf16[512,256]{1,0:T(8,128)(2,1)} %cotangent_ref.2) | copy-start | bytes 786436
  32.0 24.8 %copy-start.6 = (bf16[128,256]{1,0:T(8,128)(2,1)S(1)}, bf16[128,256]{1,0:T(8,128)(2,1)}, u32[]{:S(2)}) copy-start(bf16[128,256]{1,0:T(8,128)(2,1)} %weight_ref.2) | copy-start | bytes 196612
  32.0 24.8 %copy-start.9 = (s32[512]{0:T(512)S(1)}, s32[512]{0:T(512)}, u32[]{:S(2)}) copy-start(s32[512]{0:T(512)} %param.12) | copy-start | bytes 6148
  32.0 24.8 %copy-start.10 = (f32[256]{0:T(256)S(1)}, f32[256]{0:T(256)}, u32[]{:S(2)}) copy-start(f32[256]{0:T(256)} %param.15) | copy-start | bytes 3076
  56.8 1.3 %copy-start.2 = (bf16[8,512,128]{2,1,0:T(8,128)(2,1)}, bf16[8,512,128]{2,1,0:T(8,128)(2,1)S(1)}, u32[]{:S(2)}) copy-start(bf16[8,512,128]{2,1,0:T(8,128)(2,1)S(1)} %all_to_all.21.parts_ref) | copy-start | bytes 3145732
  58.1 1.0 copy-start.4
  59.1 27.6 %copy-start.1 = (bf16[64,128,128]{2,1,0:T(8,128)(2,1)S(1)}, bf16[64,128,128]{2,1,0:T(8,128)(2,1)}, u32[]{:S(2)}) copy-start(bf16[64,128,128]{2,1,0:T(8,128)(2,1)} %patterns_ref.7) | copy-start | bytes 6291460
  59.1 27.6 %all-to-all-start.2 = ((bf16[8,512,128]{2,1,0:T(8,128)(2,1)}), bf16[8,512,128]{2,1,0:T(8,128)(2,1)S(1)}, u32[]{:S(2)}, u32[]{:S(2)}) async-start(bf16[8,512,128]{2,1,0:T(8,128)(2,1)} %copy-done.4), calls=%async_computation.2 | async-start | bytes 2097152 | tf_op jit(solution)/shard_map/all_to_all | solution.py:492
  62.8 1.2 %copy-start.3 = (bf16[8,512,128]{2,1,0:T(8,128)(2,1)S(1)}, bf16[8,512,128]{2,1,0:T(8,128)(2,1)}, u32[]{:S(2)}) copy-start(bf16[8,512,128]{2,1,0:T(8,128)(2,1)} %copy-done.2) | copy-start | bytes 3145732
  65.4 1.3 %collective-permute-start.3 = (f32[144,128]{1,0:T(8,128)S(1)}, f32[144,128]{1,0:T(8,128)S(1)}, u32[]{:S(2)}, u32[]{:S(2)}) collective-permute-start(f32[144,128]{1,0:T(8,128)S(1)} %get-tuple-element.43), channel_id=1, source_target_pairs={{0,8},{8,0},{16,24},{24,16},{32,40},{40,32},{48,56},{56,48},{64,72... | collective-permute-start | bytes 221192 | tf_op jit(solution)/shard_map/ppermute | solution.py:502
  66.7 10.6 %collective-permute-start.4 = (f32[144,128]{1,0:T(8,128)S(1)}, f32[144,128]{1,0:T(8,128)S(1)}, u32[]{:S(2)}, u32[]{:S(2)}) collective-permute-start(f32[144,128]{1,0:T(8,128)S(1)} %add.12), channel_id=1, source_target_pairs={{0,6},{1,7},{2,4},{3,5},{4,2},{5,3},{6,0},{7,1},{8,10},{9,11},{10,... | collective-permute-start | bytes 221192 | tf_op jit(solution)/shard_map/ppermute | solution.py:504
  77.4 4.5 %collective-permute-start.5 = (f32[144,128]{1,0:T(8,128)S(1)}, f32[144,128]{1,0:T(8,128)S(1)}, u32[]{:S(2)}, u32[]{:S(2)}) collective-permute-start(f32[144,128]{1,0:T(8,128)S(1)} %add.13), channel_id=1, source_target_pairs={{0,2},{1,3},{2,0},{3,1},{4,6},{5,7},{6,4},{7,5},{8,14},{9,15},{10,... | collective-permute-start | bytes 221192 | tf_op jit(solution)/shard_map/ppermute | solution.py:504
  81.9 4.8 %collective-permute-start.6 = (f32[144,128]{1,0:T(8,128)S(1)}, f32[144,128]{1,0:T(8,128)S(1)}, u32[]{:S(2)}, u32[]{:S(2)}) collective-permute-start(f32[144,128]{1,0:T(8,128)S(1)} %add.14), channel_id=1, source_target_pairs={{0,1},{1,0},{2,3},{3,2},{4,5},{5,4},{6,7},{7,6},{8,9},{9,8},{10,11... | collective-permute-start | bytes 221192 | tf_op jit(solution)/shard_map/ppermute | solution.py:504
  89.2 3.7 %collective-permute-start.7 = (bf16[2048,128]{1,0:T(8,128)(2,1)S(1)}, bf16[2048,128]{1,0:T(8,128)(2,1)S(1)}, u32[]{:S(2)}, u32[]{:S(2)}) collective-permute-start(bf16[2048,128]{1,0:T(8,128)(2,1)S(1)} %get-tuple-element.48), channel_id=1, source_target_pairs={{0,8},{8,0},{16,24},{24,16},{32,40},{40,32},{48,56},{56,48},{64,72... | collective-permute-start | bytes 1572872 | tf_op jit(solution)/shard_map/ppermute | solution.py:516
  93.1 8.8 %collective-permute-start.9 = (bf16[2192,128]{1,0:T(8,128)(2,1)S(1)}, bf16[2192,128]{1,0:T(8,128)(2,1)S(1)}, u32[]{:S(2)}, u32[]{:S(2)}) collective-permute-start(bf16[2192,128]{1,0:T(8,128)(2,1)S(1)} %get-tuple-element.54), channel_id=1, source_target_pairs={{0,48},{8,24},{16,32},{24,8},{32,16},{40,56},{48,0},{56,40},{64,11... | collective-permute-start | bytes 1683464 | tf_op jit(solution)/shard_map/ppermute | solution.py:525
  95.7 2.3 %collective-permute-start.8 = (bf16[2048,128]{1,0:T(8,128)(2,1)S(1)}, bf16[2048,128]{1,0:T(8,128)(2,1)S(1)}, u32[]{:S(2)}, u32[]{:S(2)}) collective-permute-start(bf16[2048,128]{1,0:T(8,128)(2,1)S(1)} %get-tuple-element.53), channel_id=1, source_target_pairs={{0,8},{8,0},{16,24},{24,16},{32,40},{40,32},{48,56},{56,48},{64,72... | collective-permute-start | bytes 1572872 | tf_op jit(solution)/shard_map/ppermute | solution.py:535
  113.0 3.8 %collective-permute-start.10 = (f32[136,128]{1,0:T(8,128)S(1)}, f32[136,128]{1,0:T(8,128)S(1)}, u32[]{:S(2)}, u32[]{:S(2)}) collective-permute-start(f32[136,128]{1,0:T(8,128)S(1)} %shard_map.149.mine_ref), channel_id=1, source_target_pairs={{0,8},{8,0},{16,24},{24,16},{32,40},{40,32},{48,56},{56,48},{64,72... | collective-permute-start | bytes 208904 | tf_op jit(solution)/shard_map/ppermute | solution.py:553

commit v8 on v7

--- a/solution.py
+++ b/solution.py
@@ -323,28 +323,18 @@
     terms_ref[...] = terms
 
 
-def near_join_kernel(keep_ref, got_ref, far_ref, grads_ref, out_ref):
-    shards = out_ref.shape[0]
-    half = keep_ref.shape[0]
-    own = half // shards
-    grads = grads_ref[...].astype(jnp.float32) + far_ref[half:, :].astype(jnp.float32)
-    grads = grads.astype(jnp.bfloat16)
+def near_join_kernel(keep_ref, got_ref, far_ref, terms_ref, out_ref, grads_ref):
+    shards, own, _ = out_ref.shape
     for shard in range(shards):
         rows = pl.ds(shard * own, own)
         total = keep_ref[rows, :] + got_ref[rows, :].astype(jnp.float32)
-        total += far_ref[rows, :].astype(jnp.float32)
-        out_ref[shard, pl.ds(0, own), :] = total.astype(jnp.bfloat16)
-        out_ref[shard, pl.ds(own, grads.shape[0]), :] = grads
-
-
-def total_kernel(scale_factor, parts_ref, half_ref):
-    extra = half_ref.shape[0] - 8 + BIAS_ROWS
-    tail = sum_of_four(parts_ref, pl.ds(parts_ref.shape[1] - extra, extra))
-    tail = tail * scale_factor
-    height = half_ref.shape[0] - 8
-    half_ref[:height, :] = tail[:height, :]
-    bias_row = tail[height : height + 1, :] + tail[height + 1 : height + 2, :]
-    half_ref[height:, :] = jnp.broadcast_to(bias_row, (8, bias_row.shape[1]))
+        out_ref[shard] = (total + far_ref[rows, :].astype(jnp.float32)).astype(jnp.bfloat16)
+    grads = terms_ref[...].astype(jnp.float32)
+    grads += far_ref[shards * own :, :].astype(jnp.float32)
+    height = grads.shape[0] - BIAS_ROWS
+    grads_ref[:height, :] = grads[:height, :]
+    bias = grads[height : height + 1, :] + grads[height + 1 : height + 2, :]
+    grads_ref[height:, :] = jnp.broadcast_to(bias, (BIAS_ROWS, bias.shape[1]))
 
 
 def features_kernel(parts_ref, degree_ref, features_ref):
@@ -399,7 +389,7 @@
         (index, (index // 8 * 4 + far_neighbour(index // 2 % 4, index % 2)) * 2 + index % 2)
         for index in range(row_devices)
     ]
-    col_far, col_close, col_high = (
+    col_steps = [
         [
             (index * col_devices + place, index * col_devices + peer(place, index % 2))
             for index in range(row_devices)
@@ -410,7 +400,13 @@
             lambda place, core: far_neighbour(place // 2, 1 - core) * 2 + place % 2,
             lambda place, core: place ^ 1,
         )
-    )
+    ]
+    row_close = [
+        (index, (index // 8 * 4 + far_neighbour(index // 2 % 4, 1 - index % 2)) * 2 + index % 2)
+        for index in range(row_devices)
+    ]
+    row_low = [(index, index ^ 8) for index in range(row_devices)]
+    both = ("row", "col")
     exchange = functools.partial(lax.all_to_all, split_axis=0, concat_axis=0)
     extra = feature_count + BIAS_ROWS
     half = chips * node_dev
@@ -500,8 +496,8 @@
         compiler_params=PARAMS,
     )(place, *middle_inputs)
     grads = keep_terms + lax.ppermute(send_terms, "row", swap)
-    for pairs in (col_far, col_close, col_high):
-        grads = grads + lax.ppermute(grads, ("row", "col"), pairs)
+    for pairs in (row_close, row_low):
+        grads = grads + lax.ppermute(grads, "row", pairs)
     spread_all, grads, activations = lax.optimization_barrier((spread_all, grads, activations))
     kept, sent = shape((half // 2, edge), f32), shape((half // 2, edge), bf16)
     keep, send = pl.pallas_call(
@@ -513,14 +509,18 @@
         compiler_params=PARAMS,
         cost_estimate=tile_cost,
     )(slots, patterns, spread_all)
+    send, step = lax.optimization_barrier((send, lax.ppermute(grads, both, col_steps[0])))
+    grads = grads + step
     got = lax.ppermute(send, "row", swap)
-    far_sums, grads = pl.pallas_call(
+    step = lax.ppermute(grads, both, col_steps[1])
+    got, step = lax.optimization_barrier((got, step))
+    far_sums, own_terms = pl.pallas_call(
         far_join_kernel,
         out_shape=(shape((half // 2 + extra, edge), bf16), shape((extra, edge), bf16)),
         in_specs=[VMEM] * 3,
         out_specs=(VMEM,) * 2,
         compiler_params=PARAMS,
-    )(keep, got, grads)
+    )(keep, got, grads + step)
     far_sums, spread_all = lax.optimization_barrier((far_sums, spread_all))
     far_got = lax.ppermute(far_sums, "row", row_far)
     keep, send = pl.pallas_call(
@@ -534,22 +534,18 @@
     )(slots, patterns, spread_all)
     got = lax.ppermute(send, "row", swap)
     got, far_got = lax.optimization_barrier((got, far_got))
-    joined = pl.pallas_call(
+    joined, grads = pl.pallas_call(
         near_join_kernel,
-        out_shape=shape((4, node_dev + extra, edge), bf16),
+        out_shape=(shape((4, node_dev, edge), bf16), terms),
         in_specs=[VMEM] * 4,
-        out_specs=VMEM,
-        compiler_params=PARAMS,
-    )(keep, got, far_got, grads)
+        out_specs=(VMEM,) * 2,
+        compiler_params=PARAMS,
+    )(keep, got, far_got, own_terms)
+    step = lax.ppermute(grads, both, col_steps[2])
     back_parts = exchange(joined, "row", axis_index_groups=row_near)
+    back_parts, step = lax.optimization_barrier((back_parts, step))
     scale_factor = 1.0 / math.sqrt(node_dev * row_devices * col_devices)
-    mine = pl.pallas_call(
-        functools.partial(total_kernel, scale_factor),
-        out_shape=shape((feature_count + 8, edge), f32),
-        in_specs=[VMEM],
-        out_specs=VMEM,
-        compiler_params=PARAMS,
-    )(back_parts)
+    mine = (grads + step) * scale_factor
     other = lax.ppermute(mine, "row", swap)
     grad_features = pl.pallas_call(
         features_kernel,

time: 118 us -> 120 us (1.017)
  blocking collectives: 49.4 us -> 38.1 us
  waiting for transfers between devices: 24.2 us -> 30.8 us
  starting transfers between devices: 18.6 us -> 24 us
  local copies, waits for them, and re-layouts: 8.11 us -> 10.9 us
  Pallas kernels: 15.5 us -> 13.4 us
    all_to_all x1 -> x0, blocking collectives: 10.9 us -> none  [per_device(): back_parts = exchange(joined, 'row', axis_index_groups=row_near)]
    ppermute x3 -> x5, waiting for transfers between devices: 14.4 us -> 21.1 us  [the longest x2 8.21 us: per_device(): grads = grads + lax.ppermute(grads, 'row', pairs)]
    ppermute x3 -> x5, starting transfers between devices: 5.53 us -> 1.75 us  [the longest x1 0.58 us: per_device(): step = lax.ppermute(grads, both, col_steps[1])]
    ppermute x2, starting transfers between devices: 2.95 us -> 6.69 us  [per_device(): got = lax.ppermute(send, 'row', swap)]
    all_to_all x0 -> x1, starting transfers between devices: none -> 3.47 us  [per_device(): back_parts = exchange(joined, 'row', axis_index_groups=row_near)]
    unnamed x30 -> x34, local copies, waits for them, and re-layouts: 8.11 us -> 10.9 us
    ppermute x2, waiting for transfers between devices: 3.07 us -> 1.54 us  [per_device(): got = lax.ppermute(send, 'row', swap)]
    ppermute x1, starting transfers between devices: 0.36 us -> 1.83 us  [per_device(): grads = keep_terms + lax.ppermute(send_terms, 'row', swap)]
  transfers between devices with their start and end apart: 12 -> 15, of which waited for: 10 -> 11; matrix products, arithmetic and copies ran while one was open for 0% -> 0% of each run, Pallas kernels for 7% -> 7%
where the time goes in v8:
time: 120 us; the launch traced here: 119 us
  blocking collectives  38.1 us (32%)
  waiting for transfers between devices  30.8 us (26%)
  starting transfers between devices  24 us (20%)
  Pallas kernels  13.4 us (11%)
  local copies, waits for them, and re-layouts  10.9 us (9%)
  between operations  1.51 us (1%)
    all_to_all x1, blocking collectives, per_device(): exchange(row_part.reshape(col_devices, node_dev, feature_count), 'col')  24.3 us
    all_to_all x1, blocking collectives, per_device(): exchange(scaled, 'row', axis_index_groups=row_near)  13.8 us
    unnamed x34, local copies, waits for them, and re-layouts  10.9 us
    ppermute x2, waiting for transfers between devices, per_device(): grads = grads + lax.ppermute(grads, 'row', pairs)  8.21 us
    ppermute x1, waiting for transfers between devices, per_device(): step = lax.ppermute(grads, both, col_steps[2])  7.68 us
    ppermute x2, starting transfers between devices, per_device(): got = lax.ppermute(send, 'row', swap)  6.69 us
    ppermute x1, waiting for transfers between devices, per_device(): far_got = lax.ppermute(far_sums, 'row', row_far)  4.53 us
    ppermute x1, waiting for transfers between devices, per_device(): step = lax.ppermute(grads, both, col_steps[1])  3.91 us
  transfers between devices with their start and end apart: 15, of which 11 were waited for; matrix products, arithmetic and copies ran while one was open for 0% of the time, Pallas kernels for 7%

profile of v8, /device:TPU:1, one launch (start us, length us, event | category | flops | bytes accessed | tf_op | source)
XLA Modules:
  0.0 118.7 jit_solution(303848337361626245)
XLA Ops:
  0.6 0.9 copy-done.9
  2.6 13.8 %all_to_all.20 = bf16[4,512,128]{2,1,0:T(8,128)(2,1)S(1)} all-to-all(bf16[4,512,128]{2,1,0:T(8,128)(2,1)S(1)} %shard_map.138), channel_id=1, replica_groups={{0,64,16,80},{32,96,48,112},{8,72,56,120},{24,88,40,104},{1,65,17,81},{..., dimensions={0} | all-to-all | bytes 1048576 | tf_op jit(solution)/shard_map/all_to_all | solution.py:434
  21.8 1.6 %copy-done = bf16[64,128,128]{2,1,0:T(8,128)(2,1)S(1)} copy-done((bf16[64,128,128]{2,1,0:T(8,128)(2,1)S(1)}, bf16[64,128,128]{2,1,0:T(8,128)(2,1)}, u32[]{:S(2)}) %copy-start) | copy-done | bytes 2097176
  23.4 1.0 copy-done.7
  24.4 1.6 %shard_map.140.so_far_ref = f32[4096,128]{1,0:T(8,128)S(1)} custom-call(s32[1,640]{1,0:T(1,128)S(1)} %shard_map.139.slots_ref, bf16[64,128,128]{2,1,0:T(8,128)(2,1)S(1)} %copy-done, bf16[2048,128]{1,0:T(8,128)(2,1)S(1)} %bitcast.13, bf16[2048,128]{1,0:T(8,128)(2,1)S(1)} %copy-done.7), custom_call_target="tpu_custom_call" | custom-call | flops 8388608 | bytes 6291456 | tf_op jit(solution)/shard_map/pallas_call | solution.py:459
  26.0 3.7 %collective-permute-start.2 = (bf16[2048,128]{1,0:T(8,128)(2,1)}, bf16[2048,128]{1,0:T(8,128)(2,1)S(1)}, u32[]{:S(2)}, u32[]{:S(2)}) collective-permute-start(bf16[2048,128]{1,0:T(8,128)(2,1)} %collective-permute-done.own_ref), channel_id=1, source_target_pairs={{0,8},{8,0},{16,24},{24,16},{32,40},{40,32},{48,56},{56,48},{64,72... | collective-permute-start | bytes 1572872 | tf_op jit(solution)/shard_map/ppermute | solution.py:469
  29.7 1.7 %collective-permute-done.2.other_ref = bf16[2048,128]{1,0:T(8,128)(2,1)S(1)} collective-permute-done((bf16[2048,128]{1,0:T(8,128)(2,1)}, bf16[2048,128]{1,0:T(8,128)(2,1)S(1)}, u32[]{:S(2)}, u32[]{:S(2)}) %collective-permute-start.2) | collective-permute-done | bytes 524320 | tf_op jit(solution)/shard_map/ppermute | solution.py:469
  31.5 2.2 %shard_map.141 = bf16[4096,128]{1,0:T(8,128)(2,1)S(1)} custom-call(s32[1,640]{1,0:T(1,128)S(1)} %shard_map.139.slots_ref, bf16[64,128,128]{2,1,0:T(8,128)(2,1)S(1)} %copy-done, bf16[2048,128]{1,0:T(8,128)(2,1)} %collective-permute-done.own_ref, bf16[2048,128]{1,0:T(8,128)(2,1)S(1)} %collective-permute-done.2.other_ref, f32[4096,128]{1,0:T(8,128)S(1)} %shard_map.140.so_far_ref), custom_call_target="tpu_custom_call" | custom-call | flops 8388608 | bytes 6291456 | tf_op jit(solution)/shard_map/pallas_call | solution.py:470
  33.7 24.3 %all_to_all.21.parts_ref = bf16[8,512,128]{2,1,0:T(8,128)(2,1)S(1)} all-to-all(bf16[8,512,128]{2,1,0:T(8,128)(2,1)S(1)} %bitcast.10), channel_id=1, replica_groups=mesh['row'=16,'col'=8] {'col'}, dimensions={0} | all-to-all | bytes 2097152 | tf_op jit(solution)/shard_map/all_to_all | solution.py:479
  58.0 1.3 %shard_map.142 = (bf16[8,512,128]{2,1,0:T(8,128)(2,1)S(1)}, f32[8,128]{1,0:T(8,128)}) custom-call(bf16[8,512,128]{2,1,0:T(8,128)(2,1)S(1)} %all_to_all.21.parts_ref, s32[4,128]{1,0:T(4,128)S(1)} %bitcast.15, bf16[512,256]{1,0:T(8,128)(2,1)S(1)} %copy-done.5, bf16[128,256]{1,0:T(8,128)(2,1)S(1)} %copy-done.8, f32[1,256]{1,0:T(1,128)S(1)} %bitcast.18), custom_call_target="tpu_custom_call" | custom-call | tf_op jit(solution)/shard_map/pallas_call | solution.py:481
  59.4 1.0 copy-done.2
  60.3 1.0 copy-done.4
  61.3 3.7 %all-to-all-start.2 = ((bf16[8,512,128]{2,1,0:T(8,128)(2,1)}), bf16[8,512,128]{2,1,0:T(8,128)(2,1)S(1)}, u32[]{:S(2)}, u32[]{:S(2)}) async-start(bf16[8,512,128]{2,1,0:T(8,128)(2,1)} %copy-done.4), calls=%async_computation.2 | async-start | bytes 2097152 | tf_op jit(solution)/shard_map/all_to_all | solution.py:488
  65.0 1.2 %copy-done.3 = bf16[8,512,128]{2,1,0:T(8,128)(2,1)S(1)} copy-done((bf16[8,512,128]{2,1,0:T(8,128)(2,1)S(1)}, bf16[8,512,128]{2,1,0:T(8,128)(2,1)}, u32[]{:S(2)}) %copy-start.3) | copy-done | bytes 1048600
  66.2 1.4 %shard_map.143 = (bf16[512,256]{1,0:T(8,128)(2,1)}, f32[144,128]{1,0:T(8,128)S(1)}, f32[144,128]{1,0:T(8,128)S(1)}) custom-call(s32[1]{0:T(128)} %bitcast.place_ref, bf16[8,512,128]{2,1,0:T(8,128)(2,1)S(1)} %copy-done.3, s32[4,128]{1,0:T(4,128)S(1)} %bitcast.16, bf16[512,256]{1,0:T(8,128)(2,1)S(1)} %copy-done.5, bf16[128,256]{1,0:T(8,128)(2,1)S(1)} %copy-done.8, ...), custom_call_target="tpu_custom_call" | custom-call | tf_op jit(solution)/shard_map/pallas_call | solution.py:491
  67.6 1.8 %collective-permute-start.3 = (f32[144,128]{1,0:T(8,128)S(1)}, f32[144,128]{1,0:T(8,128)S(1)}, u32[]{:S(2)}, u32[]{:S(2)}) collective-permute-start(f32[144,128]{1,0:T(8,128)S(1)} %get-tuple-element.51), channel_id=1, source_target_pairs={{0,8},{8,0},{16,24},{24,16},{32,40},{40,32},{48,56},{56,48},{64,72... | collective-permute-start | bytes 221192 | tf_op jit(solution)/shard_map/ppermute | solution.py:498
  69.5 0.9 collective-permute-done.3
  70.9 4.3 %collective-permute-done.4 = f32[144,128]{1,0:T(8,128)S(1)} collective-permute-done((f32[144,128]{1,0:T(8,128)S(1)}, f32[144,128]{1,0:T(8,128)S(1)}, u32[]{:S(2)}, u32[]{:S(2)}) %collective-permute-start.4) | collective-permute-done | bytes 73760 | tf_op jit(solution)/shard_map/ppermute | solution.py:500
  75.3 3.9 %collective-permute-done.5 = f32[144,128]{1,0:T(8,128)S(1)} collective-permute-done((f32[144,128]{1,0:T(8,128)S(1)}, f32[144,128]{1,0:T(8,128)S(1)}, u32[]{:S(2)}, u32[]{:S(2)}) %collective-permute-start.5) | collective-permute-done | bytes 73760 | tf_op jit(solution)/shard_map/ppermute | solution.py:500
  79.2 0.9 all-to-all-done.2.spread_ref
  80.6 1.7 %shard_map.144 = (f32[2048,128]{1,0:T(8,128)S(1)}, bf16[2048,128]{1,0:T(8,128)(2,1)S(1)}) custom-call(s32[1,640]{1,0:T(1,128)S(1)} %shard_map.139.slots_ref, bf16[64,128,128]{2,1,0:T(8,128)(2,1)S(1)} %copy-done.1, bf16[8,512,128]{2,1,0:T(8,128)(2,1)S(1)} %all-to-all-done.2.spread_ref), custom_call_target="tpu_custom_call" | custom-call | flops 8388608 | bytes 6291456 | tf_op jit(solution)/shard_map/pallas_call | solution.py:503
  82.2 1.3 %collective-permute-done.6 = f32[144,128]{1,0:T(8,128)S(1)} collective-permute-done((f32[144,128]{1,0:T(8,128)S(1)}, f32[144,128]{1,0:T(8,128)S(1)}, u32[]{:S(2)}, u32[]{:S(2)}) %collective-permute-start.6) | collective-permute-done | bytes 73760 | tf_op jit(solution)/shard_map/ppermute | solution.py:512
  83.5 6.0 %collective-permute-start.7 = (bf16[2048,128]{1,0:T(8,128)(2,1)S(1)}, bf16[2048,128]{1,0:T(8,128)(2,1)S(1)}, u32[]{:S(2)}, u32[]{:S(2)}) collective-permute-start(bf16[2048,128]{1,0:T(8,128)(2,1)S(1)} %get-tuple-element.58), channel_id=1, source_target_pairs={{0,8},{8,0},{16,24},{24,16},{32,40},{40,32},{48,56},{56,48},{64,72... | collective-permute-start | bytes 1572872 | tf_op jit(solution)/shard_map/ppermute | solution.py:514
  90.0 3.9 %collective-permute-done.8 = f32[144,128]{1,0:T(8,128)S(1)} collective-permute-done((f32[144,128]{1,0:T(8,128)S(1)}, f32[144,128]{1,0:T(8,128)S(1)}, u32[]{:S(2)}, u32[]{:S(2)}) %collective-permute-start.8) | collective-permute-done | bytes 73760 | tf_op jit(solution)/shard_map/ppermute | solution.py:515
  94.4 1.7 %shard_map.146 = (f32[2048,128]{1,0:T(8,128)S(1)}, bf16[2048,128]{1,0:T(8,128)(2,1)S(1)}) custom-call(s32[1,640]{1,0:T(1,128)S(1)} %shard_map.139.slots_ref, bf16[64,128,128]{2,1,0:T(8,128)(2,1)S(1)} %copy-done.1, bf16[8,512,128]{2,1,0:T(8,128)(2,1)S(1)} %all-to-all-done.2.spread_ref), custom_call_target="tpu_custom_call" | custom-call | flops 8388608 | bytes 6291456 | tf_op jit(solution)/shard_map/pallas_call | solution.py:526
  96.8 1.5 %collective-permute-done.9.got_ref = bf16[2048,128]{1,0:T(8,128)(2,1)S(1)} collective-permute-done((bf16[2048,128]{1,0:T(8,128)(2,1)S(1)}, bf16[2048,128]{1,0:T(8,128)(2,1)S(1)}, u32[]{:S(2)}, u32[]{:S(2)}) %collective-permute-start.9) | collective-permute-done | bytes 524320 | tf_op jit(solution)/shard_map/ppermute | solution.py:535
  98.3 4.5 %collective-permute-done.10.far_ref = bf16[2192,128]{1,0:T(8,128)(2,1)S(1)} collective-permute-done((bf16[2192,128]{1,0:T(8,128)(2,1)S(1)}, bf16[2192,128]{1,0:T(8,128)(2,1)S(1)}, u32[]{:S(2)}, u32[]{:S(2)}) %collective-permute-start.10) | collective-permute-done | bytes 561184 | tf_op jit(solution)/shard_map/ppermute | solution.py:525
  102.9 1.0 shard_map.147
  103.9 3.5 %all-to-all-start.3 = ((bf16[4,512,128]{2,1,0:T(8,128)(2,1)}), bf16[4,512,128]{2,1,0:T(8,128)(2,1)S(1)}, u32[]{:S(2)}, u32[]{:S(2)}) async-start(bf16[4,512,128]{2,1,0:T(8,128)(2,1)} %get-tuple-element.70), calls=%async_computation.3 | async-start | bytes 1048576 | tf_op jit(solution)/shard_map/all_to_all | solution.py:545
  107.5 7.7 %collective-permute-done.11 = f32[144,128]{1,0:T(8,128)S(1)} collective-permute-done((f32[144,128]{1,0:T(8,128)S(1)}, f32[144,128]{1,0:T(8,128)S(1)}, u32[]{:S(2)}, u32[]{:S(2)}) %collective-permute-start.11) | collective-permute-done | bytes 73760 | tf_op jit(solution)/shard_map/ppermute | solution.py:544
  115.2 2.0 %collective-permute-start.12 = (f32[144,128]{1,0:T(8,128)S(1)}, f32[144,128]{1,0:T(8,128)S(1)}, u32[]{:S(2)}, u32[]{:S(2)}) collective-permute-start(f32[144,128]{1,0:T(8,128)S(1)} %add_multiply_fusion.mine_ref), channel_id=1, source_target_pairs={{0,8},{8,0},{16,24},{24,16},{32,40},{40,32},{48,56},{56,48},{64,72... | collective-permute-start | bytes 221192 | tf_op jit(solution)/shard_map/ppermute | solution.py:549
  117.1 0.8 shard_map.148
  (52 shorter events, 9.6 us)
Async XLA Ops:
  0.6 0.9 copy-start.9
  1.5 0.7 copy-start.10
  16.4 4.5 %collective-permute-start.1 = (bf16[2048,128]{1,0:T(8,128)(2,1)S(1)}, bf16[2048,128]{1,0:T(8,128)(2,1)S(1)}, u32[]{:S(2)}, u32[]{:S(2)}) collective-permute-start(bf16[2048,128]{1,0:T(8,128)(2,1)S(1)} %bitcast.11), channel_id=1, source_target_pairs={{0,8},{8,0},{16,24},{24,16},{32,40},{40,32},{48,56},{56,48},{64,72... | collective-permute-start | bytes 1572872 | tf_op jit(solution)/shard_map/ppermute | solution.py:435
  17.0 9.1 %collective-permute-start = (bf16[2048,128]{1,0:T(8,128)(2,1)S(1)}, bf16[2048,128]{1,0:T(8,128)(2,1)}, u32[]{:S(2)}, u32[]{:S(2)}) collective-permute-start(bf16[2048,128]{1,0:T(8,128)(2,1)S(1)} %bitcast.12), channel_id=1, source_target_pairs={{0,48},{8,24},{16,32},{24,8},{32,16},{40,56},{48,0},{56,40},{64,11... | collective-permute-start | bytes 1572872 | tf_op jit(solution)/shard_map/ppermute | solution.py:436
  17.6 0.7 copy-start.13
  18.3 0.7 copy-start.14
  19.0 0.7 copy-start.15
  19.7 0.7 copy-start.16
  21.0 0.8 copy-start.6
  21.8 1.6 %copy-start = (bf16[64,128,128]{2,1,0:T(8,128)(2,1)S(1)}, bf16[64,128,128]{2,1,0:T(8,128)(2,1)}, u32[]{:S(2)}) copy-start(bf16[64,128,128]{2,1,0:T(8,128)(2,1)} %patterns_ref.7) | copy-start | bytes 6291460
  23.4 1.0 copy-start.7
  26.0 5.4 %collective-permute-start.2 = (bf16[2048,128]{1,0:T(8,128)(2,1)}, bf16[2048,128]{1,0:T(8,128)(2,1)S(1)}, u32[]{:S(2)}, u32[]{:S(2)}) collective-permute-start(bf16[2048,128]{1,0:T(8,128)(2,1)} %collective-permute-done.own_ref), channel_id=1, source_target_pairs={{0,8},{8,0},{16,24},{24,16},{32,40},{40,32},{48,56},{56,48},{64,72... | collective-permute-start | bytes 1572872 | tf_op jit(solution)/shard_map/ppermute | solution.py:469
  33.7 24.3 %copy-start.5 = (bf16[512,256]{1,0:T(8,128)(2,1)S(1)}, bf16[512,256]{1,0:T(8,128)(2,1)}, u32[]{:S(2)}) copy-start(bf16[512,256]{1,0:T(8,128)(2,1)} %cotangent_ref.2) | copy-start | bytes 786436
  33.7 24.3 %copy-start.8 = (bf16[128,256]{1,0:T(8,128)(2,1)S(1)}, bf16[128,256]{1,0:T(8,128)(2,1)}, u32[]{:S(2)}) copy-start(bf16[128,256]{1,0:T(8,128)(2,1)} %weight_ref.2) | copy-start | bytes 196612
  33.7 24.3 %copy-start.11 = (s32[512]{0:T(512)S(1)}, s32[512]{0:T(512)}, u32[]{:S(2)}) copy-start(s32[512]{0:T(512)} %param.12) | copy-start | bytes 6148
  33.7 24.3 %copy-start.12 = (f32[256]{0:T(256)S(1)}, f32[256]{0:T(256)}, u32[]{:S(2)}) copy-start(f32[256]{0:T(256)} %param.15) | copy-start | bytes 3076
  59.4 1.0 copy-start.2
  60.3 1.0 copy-start.4
  61.3 19.3 %copy-start.1 = (bf16[64,128,128]{2,1,0:T(8,128)(2,1)S(1)}, bf16[64,128,128]{2,1,0:T(8,128)(2,1)}, u32[]{:S(2)}) copy-start(bf16[64,128,128]{2,1,0:T(8,128)(2,1)} %patterns_ref.7) | copy-start | bytes 6291460
  61.3 18.7 %all-to-all-start.2 = ((bf16[8,512,128]{2,1,0:T(8,128)(2,1)}), bf16[8,512,128]{2,1,0:T(8,128)(2,1)S(1)}, u32[]{:S(2)}, u32[]{:S(2)}) async-start(bf16[8,512,128]{2,1,0:T(8,128)(2,1)} %copy-done.4), calls=%async_computation.2 | async-start | bytes 2097152 | tf_op jit(solution)/shard_map/all_to_all | solution.py:488
  65.0 1.2 %copy-start.3 = (bf16[8,512,128]{2,1,0:T(8,128)(2,1)S(1)}, bf16[8,512,128]{2,1,0:T(8,128)(2,1)}, u32[]{:S(2)}) copy-start(bf16[8,512,128]{2,1,0:T(8,128)(2,1)} %copy-done.2) | copy-start | bytes 3145732
  67.6 2.7 %collective-permute-start.3 = (f32[144,128]{1,0:T(8,128)S(1)}, f32[144,128]{1,0:T(8,128)S(1)}, u32[]{:S(2)}, u32[]{:S(2)}) collective-permute-start(f32[144,128]{1,0:T(8,128)S(1)} %get-tuple-element.51), channel_id=1, source_target_pairs={{0,8},{8,0},{16,24},{24,16},{32,40},{40,32},{48,56},{56,48},{64,72... | collective-permute-start | bytes 221192 | tf_op jit(solution)/shard_map/ppermute | solution.py:498
  70.4 4.8 %collective-permute-start.4 = (f32[144,128]{1,0:T(8,128)S(1)}, f32[144,128]{1,0:T(8,128)S(1)}, u32[]{:S(2)}, u32[]{:S(2)}) collective-permute-start(f32[144,128]{1,0:T(8,128)S(1)} %add.18), channel_id=1, source_target_pairs={{0,16},{8,56},{16,0},{24,40},{32,48},{40,24},{48,32},{56,8},{64,80... | collective-permute-start | bytes 221192 | tf_op jit(solution)/shard_map/ppermute | solution.py:500
  75.2 4.0 %collective-permute-start.5 = (f32[144,128]{1,0:T(8,128)S(1)}, f32[144,128]{1,0:T(8,128)S(1)}, u32[]{:S(2)}, u32[]{:S(2)}) collective-permute-start(f32[144,128]{1,0:T(8,128)S(1)} %add.19), channel_id=1, source_target_pairs={{0,64},{8,72},{16,80},{24,88},{32,96},{40,104},{48,112},{56,120},{... | collective-permute-start | bytes 221192 | tf_op jit(solution)/shard_map/ppermute | solution.py:500
  80.0 3.4 %collective-permute-start.6 = (f32[144,128]{1,0:T(8,128)S(1)}, f32[144,128]{1,0:T(8,128)S(1)}, u32[]{:S(2)}, u32[]{:S(2)}) collective-permute-start(f32[144,128]{1,0:T(8,128)S(1)} %add.20), channel_id=1, source_target_pairs={{0,6},{1,7},{2,4},{3,5},{4,2},{5,3},{6,0},{7,1},{8,10},{9,11},{10,... | collective-permute-start | bytes 221192 | tf_op jit(solution)/shard_map/ppermute | solution.py:512
  83.5 10.5 %collective-permute-start.7 = (bf16[2048,128]{1,0:T(8,128)(2,1)S(1)}, bf16[2048,128]{1,0:T(8,128)(2,1)S(1)}, u32[]{:S(2)}, u32[]{:S(2)}) collective-permute-start(bf16[2048,128]{1,0:T(8,128)(2,1)S(1)} %get-tuple-element.58), channel_id=1, source_target_pairs={{0,8},{8,0},{16,24},{24,16},{32,40},{40,32},{48,56},{56,48},{64,72... | collective-permute-start | bytes 1572872 | tf_op jit(solution)/shard_map/ppermute | solution.py:514
  89.5 4.5 %collective-permute-start.8 = (f32[144,128]{1,0:T(8,128)S(1)}, f32[144,128]{1,0:T(8,128)S(1)}, u32[]{:S(2)}, u32[]{:S(2)}) collective-permute-start(f32[144,128]{1,0:T(8,128)S(1)} %add.21), channel_id=1, source_target_pairs={{0,2},{1,3},{2,0},{3,1},{4,6},{5,7},{6,4},{7,5},{8,14},{9,15},{10,... | collective-permute-start | bytes 221192 | tf_op jit(solution)/shard_map/ppermute | solution.py:515
  94.1 8.8 %collective-permute-start.10 = (bf16[2192,128]{1,0:T(8,128)(2,1)S(1)}, bf16[2192,128]{1,0:T(8,128)(2,1)S(1)}, u32[]{:S(2)}, u32[]{:S(2)}) collective-permute-start(bf16[2192,128]{1,0:T(8,128)(2,1)S(1)} %get-tuple-element.66), channel_id=1, source_target_pairs={{0,48},{8,24},{16,32},{24,8},{32,16},{40,56},{48,0},{56,40},{64,11... | collective-permute-start | bytes 1683464 | tf_op jit(solution)/shard_map/ppermute | solution.py:525
  96.1 2.3 %collective-permute-start.9 = (bf16[2048,128]{1,0:T(8,128)(2,1)S(1)}, bf16[2048,128]{1,0:T(8,128)(2,1)S(1)}, u32[]{:S(2)}, u32[]{:S(2)}) collective-permute-start(bf16[2048,128]{1,0:T(8,128)(2,1)S(1)} %get-tuple-element.65), channel_id=1, source_target_pairs={{0,8},{8,0},{16,24},{24,16},{32,40},{40,32},{48,56},{56,48},{64,72... | collective-permute-start | bytes 1572872 | tf_op jit(solution)/shard_map/ppermute | solution.py:535
  103.9 11.3 %all-to-all-start.3 = ((bf16[4,512,128]{2,1,0:T(8,128)(2,1)}), bf16[4,512,128]{2,1,0:T(8,128)(2,1)S(1)}, u32[]{:S(2)}, u32[]{:S(2)}) async-start(bf16[4,512,128]{2,1,0:T(8,128)(2,1)} %get-tuple-element.70), calls=%async_computation.3 | async-start | bytes 1048576 | tf_op jit(solution)/shard_map/all_to_all | solution.py:545
  107.4 7.8 %collective-permute-start.11 = (f32[144,128]{1,0:T(8,128)S(1)}, f32[144,128]{1,0:T(8,128)S(1)}, u32[]{:S(2)}, u32[]{:S(2)}) collective-permute-start(f32[144,128]{1,0:T(8,128)S(1)} %get-tuple-element.71), channel_id=1, source_target_pairs={{0,1},{1,0},{2,3},{3,2},{4,5},{5,4},{6,7},{7,6},{8,9},{9,8},{10,11... | collective-permute-start | bytes 221192 | tf_op jit(solution)/shard_map/ppermute | solution.py:544
  115.2 2.9 %collective-permute-start.12 = (f32[144,128]{1,0:T(8,128)S(1)}, f32[144,128]{1,0:T(8,128)S(1)}, u32[]{:S(2)}, u32[]{:S(2)}) collective-permute-start(f32[144,128]{1,0:T(8,128)S(1)} %add_multiply_fusion.mine_ref), channel_id=1, source_target_pairs={{0,8},{8,0},{16,24},{24,16},{32,40},{40,32},{48,56},{56,48},{64,72... | collective-permute-start | bytes 221192 | tf_op jit(solution)/shard_map/ppermute | solution.py:549

commit v9 on v5

--- a/solution.py
+++ b/solution.py
@@ -14,7 +14,7 @@
 CUBIC = 0.044715
 BIAS_ROWS = 16
 PER_SHARD = 4
-CLASSES = 2
+CLASSES = 4
 ORDERED = 640
 BOUNDS = 600
 PAIRS = (((0, 1), (2, 3)), ((0, 3), (1, 2)))
@@ -65,7 +65,7 @@
     slot += lax.broadcasted_iota(jnp.int32, (rows, edge), 1)
     alive = slot < live_ref[0, 0]
     word = jnp.where(alive, word, 0)
-    kind = jnp.where(alive, far, CLASSES)
+    kind = jnp.where(alive, far * 2 + half, CLASSES)
 
     flags = [(kind == index).astype(jnp.float32) for index in range(CLASSES + 1)]
     stacked = jnp.concatenate(flags + [jnp.zeros((4, edge), jnp.float32)], 0)
@@ -149,16 +149,16 @@
     lax.fori_loop(0, (end - first + GROUP - 1) // GROUP, one_group, 0)
 
 
+def class_end(slots_ref, index):
+    return slots_ref[0, BOUNDS + index]
+
+
 def tile_of(ref, place, edge):
     return ref[pl.ds(pl.multiple_of(place * edge, edge), edge), :]
 
 
-def forward_sums(slots_ref, patterns_ref, own_ref, other_ref, panel, sums, far):
+def forward_sums(slots_ref, patterns_ref, panel, sums, first, end):
     edge = patterns_ref.shape[1]
-    half = own_ref.shape[0]
-    panel[:half, :] = own_ref[...]
-    panel[half:, :] = other_ref[...]
-    middle, end = slots_ref[0, BOUNDS], slots_ref[0, BOUNDS + 1]
 
     def product_of(word):
         return jnp.dot(
@@ -167,26 +167,40 @@
             preferred_element_type=jnp.float32,
         )
 
-    first, end = (middle, end) if far else (0, middle)
     add_products(slots_ref, first, end, product_of, lambda word: word & 31, sums)
 
 
-def forward_near_kernel(slots_ref, patterns_ref, own_ref, other_ref, out_ref, panel):
+def forward_near_kernel(
+    slots_from, patterns_ref, own_ref, other_ref, out_ref, slots_ref, sem, panel
+):
+    copy = pltpu.make_async_copy(slots_from, slots_ref, sem)
+    copy.start()
+    half = own_ref.shape[0]
+    panel[:half, :] = own_ref[...]
+    panel[half:, :] = other_ref[...]
     out_ref[...] = jnp.zeros_like(out_ref)
-    forward_sums(slots_ref, patterns_ref, own_ref, other_ref, panel, out_ref, False)
-
-
-def forward_far_kernel(slots_ref, patterns_ref, own_ref, other_ref, so_far_ref, out_ref, panel, sums):
+    copy.wait()
+    forward_sums(slots_ref, patterns_ref, panel, out_ref, 0, class_end(slots_ref, 1))
+
+
+def forward_far_kernel(
+    slots_from, patterns_ref, own_ref, other_ref, so_far_ref, out_ref, slots_ref, sem, panel, sums
+):
+    copy = pltpu.make_async_copy(slots_from, slots_ref, sem)
+    copy.start()
+    half = own_ref.shape[0]
+    panel[:half, :] = own_ref[...]
+    panel[half:, :] = other_ref[...]
     sums[...] = so_far_ref[...]
-    forward_sums(slots_ref, patterns_ref, own_ref, other_ref, panel, sums, True)
+    copy.wait()
+    first, end = class_end(slots_ref, 1), class_end(slots_ref, 3)
+    forward_sums(slots_ref, patterns_ref, panel, sums, first, end)
     out_ref[...] = sums[...].astype(jnp.bfloat16)
 
 
-def backward_sums(slots_ref, patterns_ref, spread_ref, keep_ref, send_ref, sums, far):
+def backward_sums(slots_ref, patterns_ref, spread_ref, sums, first, end):
     edge = patterns_ref.shape[1]
-    half = sums.shape[0] // 2
-    sums[...] = jnp.zeros_like(sums)
-    middle, end = slots_ref[0, BOUNDS], slots_ref[0, BOUNDS + 1]
+    mask = sums.shape[0] // edge - 1
 
     def product_of(word):
         start = pl.multiple_of((word & 3) * edge, edge)
@@ -196,23 +210,46 @@
             preferred_element_type=jnp.float32,
         )
 
-    first, end = (middle, end) if far else (0, middle)
-    add_products(slots_ref, first, end, product_of, lambda word: (word >> 14) & 31, sums)
-    keep_ref[...] = sums[:half, :]
-    send_ref[...] = sums[half:, :].astype(jnp.bfloat16)
-
-
-def backward_far_kernel(slots_ref, patterns_ref, spread_ref, keep_ref, send_ref, grads_ref, sums):
-    backward_sums(slots_ref, patterns_ref, spread_ref, keep_ref, send_ref, sums, True)
+    add_products(slots_ref, first, end, product_of, lambda word: (word >> 14) & mask, sums)
+
+
+def backward_send_kernel(
+    slots_from, patterns_ref, spread_ref, send_ref, grads_ref, slots_ref, sem, sums
+):
+    copy = pltpu.make_async_copy(slots_from, slots_ref, sem)
+    copy.start()
+    sums[...] = jnp.zeros_like(sums)
     own = spread_ref.shape[1] - grads_ref.shape[0]
     grads = spread_ref[0, own:, :].astype(jnp.float32)
     for shard in range(1, spread_ref.shape[0]):
         grads += spread_ref[shard, own:, :].astype(jnp.float32)
     grads_ref[...] = grads.astype(jnp.bfloat16)
-
-
-def backward_near_kernel(slots_ref, patterns_ref, spread_ref, keep_ref, send_ref, sums):
-    backward_sums(slots_ref, patterns_ref, spread_ref, keep_ref, send_ref, sums, False)
+    copy.wait()
+    first, end = class_end(slots_ref, 2), class_end(slots_ref, 3)
+    backward_sums(slots_ref, patterns_ref, spread_ref, sums, first, end)
+    send_ref[...] = sums[...].astype(jnp.bfloat16)
+
+
+def backward_keep_kernel(slots_from, patterns_ref, spread_ref, keep_ref, slots_ref, sem):
+    copy = pltpu.make_async_copy(slots_from, slots_ref, sem)
+    copy.start()
+    keep_ref[...] = jnp.zeros_like(keep_ref)
+    copy.wait()
+    first, end = class_end(slots_ref, 1), class_end(slots_ref, 2)
+    backward_sums(slots_ref, patterns_ref, spread_ref, keep_ref, first, end)
+
+
+def backward_near_kernel(
+    slots_from, patterns_ref, spread_ref, keep_ref, send_ref, slots_ref, sem, sums
+):
+    copy = pltpu.make_async_copy(slots_from, slots_ref, sem)
+    copy.start()
+    sums[...] = jnp.zeros_like(sums)
+    copy.wait()
+    backward_sums(slots_ref, patterns_ref, spread_ref, sums, 0, class_end(slots_ref, 1))
+    half = keep_ref.shape[0]
+    keep_ref[...] = sums[:half, :]
+    send_ref[...] = sums[half:, :].astype(jnp.bfloat16)
 
 
 def split_product(left, right, dims):
@@ -418,7 +455,7 @@
             pltpu.VMEM(degree_tiles.shape, jnp.int32),
             pltpu.SemaphoreType.DMA((2,)),
         ],
-        compiler_params=PARAMS,
+        compiler_params=pltpu.CompilerParams(vmem_limit_bytes=62 * 1024 * 1024),
     )(features, degree_tiles)
     near_own = exchange(scaled, "row", axis_index_groups=row_near).reshape(half // 2, feature_count)
     near_other = lax.ppermute(near_own, "row", swap)
@@ -443,14 +480,15 @@
         tile_pattern.reshape(per_shard, edge),
         tile_weight.reshape(per_shard, edge),
     )
+    slots_scratch = [pltpu.SMEM((1, ORDERED), jnp.int32), pltpu.SemaphoreType.DMA]
     forward_panel = pltpu.VMEM((half, feature_count), bf16)
     row_sums = shape((col_devices * node_dev, feature_count), f32)
     near_sums = pl.pallas_call(
         forward_near_kernel,
         out_shape=row_sums,
-        in_specs=[SMEM] + [VMEM] * 3,
-        out_specs=VMEM,
-        scratch_shapes=[forward_panel],
+        in_specs=[HBM] + [VMEM] * 3,
+        out_specs=VMEM,
+        scratch_shapes=[*slots_scratch, forward_panel],
         compiler_params=PARAMS,
         cost_estimate=tile_cost,
     )(slots, patterns, near_own, near_other)
@@ -459,9 +497,9 @@
     row_part = pl.pallas_call(
         forward_far_kernel,
         out_shape=shape(row_sums.shape, bf16),
-        in_specs=[SMEM] + [VMEM] * 4,
-        out_specs=VMEM,
-        scratch_shapes=[forward_panel, pltpu.VMEM(row_sums.shape, f32)],
+        in_specs=[HBM] + [VMEM] * 4,
+        out_specs=VMEM,
+        scratch_shapes=[*slots_scratch, forward_panel, pltpu.VMEM(row_sums.shape, f32)],
         compiler_params=PARAMS,
         cost_estimate=tile_cost,
     )(slots, patterns, far_own, far_other, near_sums)
@@ -496,12 +534,41 @@
     )(keep_terms, got_terms, spread)
     spread_all = exchange(spread, "col")
     kept, sent = shape((half // 2, edge), f32), shape((half // 2, edge), bf16)
-    keep, send, grads = pl.pallas_call(
-        backward_far_kernel,
-        out_shape=(kept, sent, shape((extra, edge), bf16)),
-        in_specs=[SMEM] + [VMEM] * 2,
-        out_specs=(VMEM,) * 3,
-        scratch_shapes=[pltpu.VMEM((half, edge), f32)],
+    send, grads = pl.pallas_call(
+        backward_send_kernel,
+        out_shape=(sent, shape((extra, edge), bf16)),
+        in_specs=[HBM] + [VMEM] * 2,
+        out_specs=(VMEM,) * 2,
+        scratch_shapes=[*slots_scratch, pltpu.VMEM(kept.shape, f32)],
+        compiler_params=PARAMS,
+        cost_estimate=tile_cost,
+    )(slots, patterns, spread_all)
+    send, spread_all = lax.optimization_barrier((send, spread_all))
+    got = lax.ppermute(send, "row", swap)
+    keep = pl.pallas_call(
+        backward_keep_kernel,
+        out_shape=kept,
+        in_specs=[HBM] + [VMEM] * 2,
+        out_specs=VMEM,
+        scratch_shapes=slots_scratch,
+        compiler_params=PARAMS,
+        cost_estimate=tile_cost,
+    )(slots, patterns, spread_all)
+    far_sums = pl.pallas_call(
+        far_join_kernel,
+        out_shape=shape((half // 2 + extra, edge), bf16),
+        in_specs=[VMEM] * 3,
+        out_specs=VMEM,
+        compiler_params=PARAMS,
+    )(keep, got, grads)
+    far_sums, spread_all = lax.optimization_barrier((far_sums, spread_all))
+    far_got = lax.ppermute(far_sums, "row", row_far)
+    keep, send = pl.pallas_call(
+        backward_near_kernel,
+        out_shape=(kept, sent),
+        in_specs=[HBM] + [VMEM] * 2,
+        out_specs=(VMEM,) * 2,
+        scratch_shapes=[*slots_scratch, pltpu.VMEM((half, edge), f32)],
         compiler_params=PARAMS,
         cost_estimate=tile_cost,
     )(slots, patterns, spread_all)
@@ -514,27 +581,7 @@
         out_specs=VMEM,
         compiler_params=PARAMS,
     )(pre_act)
-    got, activations = lax.optimization_barrier((got, activations))
-    far_sums = pl.pallas_call(
-        far_join_kernel,
-        out_shape=shape((half // 2 + extra, edge), bf16),
-        in_specs=[VMEM] * 3,
-        out_specs=VMEM,
-        compiler_params=PARAMS,
-    )(keep, got, grads)
-    far_sums, spread_all = lax.optimization_barrier((far_sums, spread_all))
-    far_got = lax.ppermute(far_sums, "row", row_far)
-    keep, send = pl.pallas_call(
-        backward_near_kernel,
-        out_shape=(kept, sent),
-        in_specs=[SMEM] + [VMEM] * 2,
-        out_specs=(VMEM,) * 2,
-        scratch_shapes=[pltpu.VMEM((half, edge), f32)],
-        compiler_params=PARAMS,
-        cost_estimate=tile_cost,
-    )(slots, patterns, spread_all)
-    got = lax.ppermute(send, "row", swap)
-    got, far_got = lax.optimization_barrier((got, far_got))
+    got, far_got, activations = lax.optimization_barrier((got, far_got, activations))
     joined = pl.pallas_call(
         near_join_kernel,
         out_shape=shape((4, node_dev + extra, edge), bf16),

time: 114 us -> 113 us (level)
  Pallas kernels: 11.8 us -> 16.7 us
  starting transfers between devices: 14.9 us -> 12 us
  local copies, waits for them, and re-layouts: 3.22 us -> 1.64 us
  blocking collectives: 74.3 us -> 73.1 us
    all_to_all x1, blocking collectives: 14.6 us -> 10.7 us  [per_device(): back_parts = exchange(joined, 'row', axis_index_groups=row_near)]
    ppermute x1, starting transfers between devices: 3.44 us -> 0.39 us  [per_device(): got_terms = lax.ppermute(send_terms, 'row', swap)]
    pallas_call x3 -> x4, Pallas kernels: 5.14 us -> 7.91 us  [the longest x1 2.52 us: per_device(): pl.pallas_call(backward_near_kernel, out_shape=(kept, sent), in_specs=[HB...]
    all_to_all x1, blocking collectives: 23.4 us -> 25.9 us  [per_device(): exchange(row_part.reshape(col_devices, node_dev, feature_count), 'col')]
    unnamed x24 -> x20, local copies, waits for them, and re-layouts: 3.22 us -> 1.64 us
    ppermute x2, waiting for transfers between devices: 2.2 us -> 0.7 us  [per_device(): got = lax.ppermute(send, 'row', swap)]
    ppermute x1, waiting for transfers between devices: 0.01 us -> 1.5 us  [per_device(): far_got = lax.ppermute(far_sums, 'row', row_far)]
    pallas_call x1, Pallas kernels: 0.44 us -> 1.9 us  [per_device(): pl.pallas_call(scale_kernel, out_shape=shape((4, node_dev, feature_count)...]
  transfers between devices with their start and end apart: 8 -> 8, of which waited for: 7 -> 7; matrix products, arithmetic and copies ran while one was open for 0% -> 0% of each run, Pallas kernels for 5% -> 8%
where the time goes in v9:
time: 113 us; the launch traced here: 112 us
  blocking collectives  73.1 us (65%)
  Pallas kernels  16.7 us (15%)
  starting transfers between devices  12 us (11%)
  waiting for transfers between devices  7.49 us (7%)
  local copies, waits for them, and re-layouts  1.64 us (1%)
  between operations  1.5 us (1%)
    all_to_all x1, blocking collectives, per_device(): exchange(row_part.reshape(col_devices, node_dev, feature_count), 'col')  25.9 us
    all_to_all x1, blocking collectives, per_device(): spread_all = exchange(spread, 'col')  22.6 us
    all_to_all x1, blocking collectives, per_device(): exchange(scaled, 'row', axis_index_groups=row_near)  14 us
    all_to_all x1, blocking collectives, per_device(): back_parts = exchange(joined, 'row', axis_index_groups=row_near)  10.7 us
    ppermute x2, starting transfers between devices, per_device(): got = lax.ppermute(send, 'row', swap)  5.7 us
    ppermute x1, starting transfers between devices, per_device(): other = lax.ppermute(mine, 'row', swap)  3.19 us
    ppermute x1, waiting for transfers between devices, per_device(): far_own = lax.ppermute(near_own, 'row', row_far)  2.85 us
    pallas_call x1, Pallas kernels, per_device(): pl.pallas_call(backward_near_kernel, out_shape=(kept, sent), in_specs=[HB...  2.52 us
  transfers between devices with their start and end apart: 8, of which 7 were waited for; matrix products, arithmetic and copies ran while one was open for 0% of the time, Pallas kernels for 8%

profile of v9, /device:TPU:1, one launch (start us, length us, event | category | flops | bytes accessed | tf_op | source)
XLA Modules:
  0.0 112.5 jit_solution(15052093843562905117)
XLA Ops:
  0.7 1.9 %shard_map.138 = bf16[4,512,128]{2,1,0:T(8,128)(2,1)} custom-call(bf16[512,128]{1,0:T(8,128)(2,1)} %features_hbm.1, s32[4,128]{1,0:T(4,128)} %bitcast.14), custom_call_target="tpu_custom_call" | custom-call | tf_op jit(solution)/shard_map/pallas_call | solution.py:448
  2.6 14.0 %all_to_all.20 = bf16[4,512,128]{2,1,0:T(8,128)(2,1)S(1)} all-to-all(bf16[4,512,128]{2,1,0:T(8,128)(2,1)} %shard_map.138), channel_id=1, replica_groups={{0,64,16,80},{32,96,48,112},{8,72,56,120},{24,88,40,104},{1,65,17,81},{..., dimensions={0} | all-to-all | bytes 1048576 | tf_op jit(solution)/shard_map/all_to_all | solution.py:460
  16.6 0.5 collective-permute-start.1
  17.8 0.6 shard_map.139.slots_from
  18.4 0.2 collective-permute-done.1.other_ref
  18.7 1.6 %copy-done = bf16[64,128,128]{2,1,0:T(8,128)(2,1)S(1)} copy-done((bf16[64,128,128]{2,1,0:T(8,128)(2,1)S(1)}, bf16[64,128,128]{2,1,0:T(8,128)(2,1)}, u32[]{:S(2)}) %copy-start) | copy-done | bytes 2097176
  20.2 2.3 %shard_map.140.so_far_ref = f32[4096,128]{1,0:T(8,128)S(1)} custom-call(s32[1,640]{1,0:T(1,128)S(1)} %shard_map.139.slots_from, bf16[64,128,128]{2,1,0:T(8,128)(2,1)S(1)} %copy-done, bf16[2048,128]{1,0:T(8,128)(2,1)S(1)} %bitcast.13, bf16[2048,128]{1,0:T(8,128)(2,1)S(1)} %collective-permute-done.1.other_ref), custom_call_target="tpu_custom_call" | custom-call | flops 8388608 | bytes 6291456 | tf_op jit(solution)/shard_map/pallas_call | solution.py:486
  22.6 2.9 %collective-permute-done.own_ref = bf16[2048,128]{1,0:T(8,128)(2,1)S(1)} collective-permute-done((bf16[2048,128]{1,0:T(8,128)(2,1)S(1)}, bf16[2048,128]{1,0:T(8,128)(2,1)S(1)}, u32[]{:S(2)}, u32[]{:S(2)}) %collective-permute-start) | collective-permute-done | bytes 524320 | tf_op jit(solution)/shard_map/ppermute | solution.py:462
  25.4 2.1 %collective-permute-start.2 = (bf16[2048,128]{1,0:T(8,128)(2,1)S(1)}, bf16[2048,128]{1,0:T(8,128)(2,1)S(1)}, u32[]{:S(2)}, u32[]{:S(2)}) collective-permute-start(bf16[2048,128]{1,0:T(8,128)(2,1)S(1)} %collective-permute-done.own_ref), channel_id=1, source_target_pairs={{0,8},{8,0},{16,24},{24,16},{32,40},{40,32},{48,56},{56,48},{64,72... | collective-permute-start | bytes 1572872 | tf_op jit(solution)/shard_map/ppermute | solution.py:496
  27.5 1.5 %collective-permute-done.2.other_ref = bf16[2048,128]{1,0:T(8,128)(2,1)S(1)} collective-permute-done((bf16[2048,128]{1,0:T(8,128)(2,1)S(1)}, bf16[2048,128]{1,0:T(8,128)(2,1)S(1)}, u32[]{:S(2)}, u32[]{:S(2)}) %collective-permute-start.2) | collective-permute-done | bytes 524320 | tf_op jit(solution)/shard_map/ppermute | solution.py:496
  29.0 2.4 %shard_map.141 = bf16[4096,128]{1,0:T(8,128)(2,1)S(1)} custom-call(s32[1,640]{1,0:T(1,128)S(1)} %shard_map.139.slots_from, bf16[64,128,128]{2,1,0:T(8,128)(2,1)S(1)} %copy-done, bf16[2048,128]{1,0:T(8,128)(2,1)S(1)} %collective-permute-done.own_ref, bf16[2048,128]{1,0:T(8,128)(2,1)S(1)} %collective-permute-done.2.other_ref, ...), custom_call_target="tpu_custom_call" | custom-call | flops 8388608 | bytes 6291456 | tf_op jit(solution)/shard_map/pallas_call | solution.py:497
  31.5 25.9 %all_to_all.21.parts_ref = bf16[8,512,128]{2,1,0:T(8,128)(2,1)S(1)} all-to-all(bf16[8,512,128]{2,1,0:T(8,128)(2,1)S(1)} %bitcast.10), channel_id=1, replica_groups=mesh['row'=16,'col'=8] {'col'}, dimensions={0} | all-to-all | bytes 2097152 | tf_op jit(solution)/shard_map/all_to_all | solution.py:506
  57.4 0.9 shard_map.142
  58.3 0.4 collective-permute-start.3
  58.7 0.3 shard_map.143.spread_ref
  59.0 0.6 collective-permute-done.3.got_ref
  59.7 22.6 %all_to_all.22.spread_ref = bf16[8,656,128]{2,1,0:T(8,128)(2,1)S(1)} all-to-all(bf16[8,656,128]{2,1,0:T(8,128)(2,1)S(1)} %shard_map.144), channel_id=1, replica_groups=mesh['row'=16,'col'=8] {'col'}, dimensions={0} | all-to-all | bytes 2686976 | tf_op jit(solution)/shard_map/all_to_all | solution.py:535
  82.2 1.6 %shard_map.145 = (bf16[2048,128]{1,0:T(8,128)(2,1)S(1)}, bf16[144,128]{1,0:T(8,128)(2,1)S(1)}) custom-call(s32[1,640]{1,0:T(1,128)S(1)} %shard_map.139.slots_from, bf16[64,128,128]{2,1,0:T(8,128)(2,1)S(1)} %copy-done.1, bf16[8,656,128]{2,1,0:T(8,128)(2,1)S(1)} %all_to_all.22.spread_ref), custom_call_target="tpu_custom_call" | custom-call | flops 8388608 | bytes 6291456 | tf_op jit(solution)/shard_map/pallas_call | solution.py:537
  83.8 2.6 %collective-permute-start.4 = (bf16[2048,128]{1,0:T(8,128)(2,1)S(1)}, bf16[2048,128]{1,0:T(8,128)(2,1)S(1)}, u32[]{:S(2)}, u32[]{:S(2)}) collective-permute-start(bf16[2048,128]{1,0:T(8,128)(2,1)S(1)} %get-tuple-element.36), channel_id=1, source_target_pairs={{0,8},{8,0},{16,24},{24,16},{32,40},{40,32},{48,56},{56,48},{64,72... | collective-permute-start | bytes 1572872 | tf_op jit(solution)/shard_map/ppermute | solution.py:547
  86.3 1.5 %shard_map.146.keep_ref = f32[2048,128]{1,0:T(8,128)S(1)} custom-call(s32[1,640]{1,0:T(1,128)S(1)} %shard_map.139.slots_from, bf16[64,128,128]{2,1,0:T(8,128)(2,1)S(1)} %copy-done.1, bf16[8,656,128]{2,1,0:T(8,128)(2,1)S(1)} %all_to_all.22.spread_ref), custom_call_target="tpu_custom_call" | custom-call | flops 8388608 | bytes 6291456 | tf_op jit(solution)/shard_map/pallas_call | solution.py:548
  87.9 0.1 shard_map.147
  88.1 2.5 %shard_map.148 = (f32[2048,128]{1,0:T(8,128)S(1)}, bf16[2048,128]{1,0:T(8,128)(2,1)S(1)}) custom-call(s32[1,640]{1,0:T(1,128)S(1)} %shard_map.139.slots_from, bf16[64,128,128]{2,1,0:T(8,128)(2,1)S(1)} %copy-done.1, bf16[8,656,128]{2,1,0:T(8,128)(2,1)S(1)} %all_to_all.22.spread_ref), custom_call_target="tpu_custom_call" | custom-call | flops 8388608 | bytes 6291456 | tf_op jit(solution)/shard_map/pallas_call | solution.py:566
  90.6 3.1 %collective-permute-start.5 = (bf16[2048,128]{1,0:T(8,128)(2,1)S(1)}, bf16[2048,128]{1,0:T(8,128)(2,1)S(1)}, u32[]{:S(2)}, u32[]{:S(2)}) collective-permute-start(bf16[2048,128]{1,0:T(8,128)(2,1)S(1)} %get-tuple-element.39), channel_id=1, source_target_pairs={{0,8},{8,0},{16,24},{24,16},{32,40},{40,32},{48,56},{56,48},{64,72... | collective-permute-start | bytes 1572872 | tf_op jit(solution)/shard_map/ppermute | solution.py:575
  93.7 0.9 shard_map.149
  94.6 0.7 collective-permute-done.5.got_ref
  95.3 1.5 %collective-permute-done.6.far_ref = bf16[2192,128]{1,0:T(8,128)(2,1)S(1)} collective-permute-done((bf16[2192,128]{1,0:T(8,128)(2,1)S(1)}, bf16[2192,128]{1,0:T(8,128)(2,1)S(1)}, u32[]{:S(2)}, u32[]{:S(2)}) %collective-permute-start.6) | collective-permute-done | bytes 561184 | tf_op jit(solution)/shard_map/ppermute | solution.py:565
  96.8 0.2 shard_map.150
  97.0 10.7 %all_to_all.23.parts_ref = bf16[4,656,128]{2,1,0:T(8,128)(2,1)S(1)} all-to-all(bf16[4,656,128]{2,1,0:T(8,128)(2,1)S(1)} %shard_map.150), channel_id=1, replica_groups={{0,64,16,80},{32,96,48,112},{8,72,56,120},{24,88,40,104},{1,65,17,81},{..., dimensions={0} | all-to-all | bytes 1343488 | tf_op jit(solution)/shard_map/all_to_all | solution.py:592
  107.7 3.2 %collective-permute-start.7 = (f32[136,128]{1,0:T(8,128)S(1)}, f32[136,128]{1,0:T(8,128)S(1)}, u32[]{:S(2)}, u32[]{:S(2)}) collective-permute-start(f32[136,128]{1,0:T(8,128)S(1)} %shard_map.152.mine_ref), channel_id=1, source_target_pairs={{0,8},{8,0},{16,24},{24,16},{32,40},{40,32},{48,56},{56,48},{64,72... | collective-permute-start | bytes 208904 | tf_op jit(solution)/shard_map/ppermute | solution.py:601
  110.9 0.8 shard_map.151
  111.7 0.1 collective-permute-done.7.other_ref
  111.8 0.7 shard_map.153
  (24 shorter events, 0.2 us)
Async XLA Ops:
  0.6 17.1 %copy-start.5 = (s32[1,1,512]{2,1,0:T(1,128)S(1)}, s32[1,1,512]{2,1,0:T(1,128)}, u32[]{:S(2)}) copy-start(s32[1,1,512]{2,1,0:T(1,128)} %param.17) | copy-start | bytes 6148
  0.6 17.1 %copy-start.8 = (s32[1,1,512]{2,1,0:T(1,128)S(1)}, s32[1,1,512]{2,1,0:T(1,128)}, u32[]{:S(2)}) copy-start(s32[1,1,512]{2,1,0:T(1,128)} %param.20) | copy-start | bytes 6148
  0.7 17.1 %copy-start.7 = (s32[1,1,512]{2,1,0:T(1,128)S(1)}, s32[1,1,512]{2,1,0:T(1,128)}, u32[]{:S(2)}) copy-start(s32[1,1,512]{2,1,0:T(1,128)} %param.19) | copy-start | bytes 6148
  0.7 17.1 %copy-start.6 = (s32[1,1,512]{2,1,0:T(1,128)S(1)}, s32[1,1,512]{2,1,0:T(1,128)}, u32[]{:S(2)}) copy-start(s32[1,1,512]{2,1,0:T(1,128)} %param.18) | copy-start | bytes 6148
  16.6 2.1 %collective-permute-start.1 = (bf16[2048,128]{1,0:T(8,128)(2,1)S(1)}, bf16[2048,128]{1,0:T(8,128)(2,1)S(1)}, u32[]{:S(2)}, u32[]{:S(2)}) collective-permute-start(bf16[2048,128]{1,0:T(8,128)(2,1)S(1)} %bitcast.11), channel_id=1, source_target_pairs={{0,8},{8,0},{16,24},{24,16},{32,40},{40,32},{48,56},{56,48},{64,72... | collective-permute-start | bytes 1572872 | tf_op jit(solution)/shard_map/ppermute | solution.py:461
  17.1 8.3 %collective-permute-start = (bf16[2048,128]{1,0:T(8,128)(2,1)S(1)}, bf16[2048,128]{1,0:T(8,128)(2,1)S(1)}, u32[]{:S(2)}, u32[]{:S(2)}) collective-permute-start(bf16[2048,128]{1,0:T(8,128)(2,1)S(1)} %bitcast.12), channel_id=1, source_target_pairs={{0,48},{8,24},{16,32},{24,8},{32,16},{40,56},{48,0},{56,40},{64,11... | collective-permute-start | bytes 1572872 | tf_op jit(solution)/shard_map/ppermute | solution.py:462
  18.7 1.6 %copy-start = (bf16[64,128,128]{2,1,0:T(8,128)(2,1)S(1)}, bf16[64,128,128]{2,1,0:T(8,128)(2,1)}, u32[]{:S(2)}) copy-start(bf16[64,128,128]{2,1,0:T(8,128)(2,1)} %patterns_ref.9) | copy-start | bytes 6291460
  25.4 3.6 %collective-permute-start.2 = (bf16[2048,128]{1,0:T(8,128)(2,1)S(1)}, bf16[2048,128]{1,0:T(8,128)(2,1)S(1)}, u32[]{:S(2)}, u32[]{:S(2)}) collective-permute-start(bf16[2048,128]{1,0:T(8,128)(2,1)S(1)} %collective-permute-done.own_ref), channel_id=1, source_target_pairs={{0,8},{8,0},{16,24},{24,16},{32,40},{40,32},{48,56},{56,48},{64,72... | collective-permute-start | bytes 1572872 | tf_op jit(solution)/shard_map/ppermute | solution.py:496
  31.5 25.9 %copy-start.2 = (bf16[512,256]{1,0:T(8,128)(2,1)S(1)}, bf16[512,256]{1,0:T(8,128)(2,1)}, u32[]{:S(2)}) copy-start(bf16[512,256]{1,0:T(8,128)(2,1)} %cotangent_ref.1) | copy-start | bytes 786436
  31.5 25.9 %copy-start.3 = (bf16[128,256]{1,0:T(8,128)(2,1)S(1)}, bf16[128,256]{1,0:T(8,128)(2,1)}, u32[]{:S(2)}) copy-start(bf16[128,256]{1,0:T(8,128)(2,1)} %weight_ref.3) | copy-start | bytes 196612
  31.5 25.9 %copy-start.4 = (s32[512]{0:T(512)S(1)}, s32[512]{0:T(512)}, u32[]{:S(2)}) copy-start(s32[512]{0:T(512)} %param.12) | copy-start | bytes 6148
  31.5 25.9 %copy-start.9 = (f32[256]{0:T(256)S(1)}, f32[256]{0:T(256)}, u32[]{:S(2)}) copy-start(f32[256]{0:T(256)} %param.15) | copy-start | bytes 3076
  58.3 1.3 %collective-permute-start.3 = (bf16[144,128]{1,0:T(8,128)(2,1)S(1)}, bf16[144,128]{1,0:T(8,128)(2,1)S(1)}, u32[]{:S(2)}, u32[]{:S(2)}) collective-permute-start(bf16[144,128]{1,0:T(8,128)(2,1)S(1)} %get-tuple-element.32), channel_id=1, source_target_pairs={{0,8},{8,0},{16,24},{24,16},{32,40},{40,32},{48,56},{56,48},{64,72... | collective-permute-start | bytes 110600 | tf_op jit(solution)/shard_map/ppermute | solution.py:519
  59.6 22.6 %copy-start.1 = (bf16[64,128,128]{2,1,0:T(8,128)(2,1)S(1)}, bf16[64,128,128]{2,1,0:T(8,128)(2,1)}, u32[]{:S(2)}) copy-start(bf16[64,128,128]{2,1,0:T(8,128)(2,1)} %patterns_ref.9) | copy-start | bytes 6291460
  83.8 4.1 %collective-permute-start.4 = (bf16[2048,128]{1,0:T(8,128)(2,1)S(1)}, bf16[2048,128]{1,0:T(8,128)(2,1)S(1)}, u32[]{:S(2)}, u32[]{:S(2)}) collective-permute-start(bf16[2048,128]{1,0:T(8,128)(2,1)S(1)} %get-tuple-element.36), channel_id=1, source_target_pairs={{0,8},{8,0},{16,24},{24,16},{32,40},{40,32},{48,56},{56,48},{64,72... | collective-permute-start | bytes 1572872 | tf_op jit(solution)/shard_map/ppermute | solution.py:547
  88.0 8.8 %collective-permute-start.6 = (bf16[2192,128]{1,0:T(8,128)(2,1)S(1)}, bf16[2192,128]{1,0:T(8,128)(2,1)S(1)}, u32[]{:S(2)}, u32[]{:S(2)}) collective-permute-start(bf16[2192,128]{1,0:T(8,128)(2,1)S(1)} %shard_map.147), channel_id=1, source_target_pairs={{0,48},{8,24},{16,32},{24,8},{32,16},{40,56},{48,0},{56,40},{64,11... | collective-permute-start | bytes 1683464 | tf_op jit(solution)/shard_map/ppermute | solution.py:565
  90.6 4.7 %collective-permute-start.5 = (bf16[2048,128]{1,0:T(8,128)(2,1)S(1)}, bf16[2048,128]{1,0:T(8,128)(2,1)S(1)}, u32[]{:S(2)}, u32[]{:S(2)}) collective-permute-start(bf16[2048,128]{1,0:T(8,128)(2,1)S(1)} %get-tuple-element.39), channel_id=1, source_target_pairs={{0,8},{8,0},{16,24},{24,16},{32,40},{40,32},{48,56},{56,48},{64,72... | collective-permute-start | bytes 1572872 | tf_op jit(solution)/shard_map/ppermute | solution.py:575
  107.7 4.1 %collective-permute-start.7 = (f32[136,128]{1,0:T(8,128)S(1)}, f32[136,128]{1,0:T(8,128)S(1)}, u32[]{:S(2)}, u32[]{:S(2)}) collective-permute-start(f32[136,128]{1,0:T(8,128)S(1)} %shard_map.152.mine_ref), channel_id=1, source_target_pairs={{0,8},{8,0},{16,24},{24,16},{32,40},{40,32},{48,56},{56,48},{64,72... | collective-permute-start | bytes 208904 | tf_op jit(solution)/shard_map/ppermute | solution.py:601

commit v10 on v9

--- a/solution.py
+++ b/solution.py
@@ -472,6 +472,7 @@
             pltpu.SemaphoreType.DMA((4,)),
         ],
         compiler_params=PARAMS,
+        cost_estimate=pl.CostEstimate(flops=1 << 31, bytes_accessed=8 << 20, transcendentals=0),
     )(
         place,
         tile_count,

time: 113 us -> 112 us (level)
  Pallas kernels: 16.7 us -> 19.5 us
  starting transfers between devices: 12 us -> 9.42 us
  waiting for transfers between devices: 7.49 us -> 9.1 us
  blocking collectives: 73.1 us -> 71.5 us
    ppermute x2, starting transfers between devices: 5.7 us -> 1.96 us  [per_device(): got = lax.ppermute(send, 'row', swap)]
    ppermute x1, starting transfers between devices: 0.39 us -> 2.55 us  [per_device(): got_terms = lax.ppermute(send_terms, 'row', swap)]
    all_to_all x1, blocking collectives: 25.9 us -> 23.9 us  [per_device(): exchange(row_part.reshape(col_devices, node_dev, feature_count), 'col')]
    ppermute x1, waiting for transfers between devices: 1.5 us -> 3.31 us  [per_device(): far_got = lax.ppermute(far_sums, 'row', row_far)]
  transfers between devices with their start and end apart: 8 -> 8, of which waited for: 7 -> 7; matrix products, arithmetic and copies ran while one was open for 0% -> 0% of each run, Pallas kernels for 8% -> 10%
where the time goes in v10:
time: 112 us
  blocking collectives  71.5 us (64%)
  Pallas kernels  19.5 us (17%)
  starting transfers between devices  9.42 us (8%)
  waiting for transfers between devices  9.1 us (8%)
  between operations  1.51 us (1%)
    all_to_all x1, blocking collectives, per_device(): exchange(row_part.reshape(col_devices, node_dev, feature_count), 'col')  23.9 us
    all_to_all x1, blocking collectives, per_device(): spread_all = exchange(spread, 'col')  22.5 us
    all_to_all x1, blocking collectives, per_device(): exchange(scaled, 'row', axis_index_groups=row_near)  14 us
    all_to_all x1, blocking collectives, per_device(): back_parts = exchange(joined, 'row', axis_index_groups=row_near)  11.1 us
    pallas_call x1, Pallas kernels, per_device(): pl.pallas_call(backward_near_kernel, out_shape=(kept, sent), in_specs=[HB...  3.39 us
    ppermute x1, waiting for transfers between devices, per_device(): far_got = lax.ppermute(far_sums, 'row', row_far)  3.31 us
    pallas_call x1, Pallas kernels, per_device(): pl.pallas_call(forward_near_kernel, out_shape=row_sums, in_specs=[HBM] +...  3.29 us
    ppermute x1, waiting for transfers between devices, per_device(): far_own = lax.ppermute(near_own, 'row', row_far)  2.73 us
  transfers between devices with their start and end apart: 8, of which 7 were waited for; matrix products, arithmetic and copies ran while one was open for 0% of the time, Pallas kernels for 10%

profile of v10, /device:TPU:1, one launch (start us, length us, event | category | flops | bytes accessed | tf_op | source)
XLA Modules:
  0.0 111.8 jit_solution(3567203595266134121)
XLA Ops:
  0.7 1.9 %shard_map.138 = bf16[4,512,128]{2,1,0:T(8,128)(2,1)} custom-call(bf16[512,128]{1,0:T(8,128)(2,1)} %features_hbm.1, s32[4,128]{1,0:T(4,128)} %bitcast.14), custom_call_target="tpu_custom_call" | custom-call | tf_op jit(solution)/shard_map/pallas_call | solution.py:448
  2.6 14.0 %all_to_all.20 = bf16[4,512,128]{2,1,0:T(8,128)(2,1)S(1)} all-to-all(bf16[4,512,128]{2,1,0:T(8,128)(2,1)} %shard_map.138), channel_id=1, replica_groups={{0,64,16,80},{32,96,48,112},{8,72,56,120},{24,88,40,104},{1,65,17,81},{..., dimensions={0} | all-to-all | bytes 1048576 | tf_op jit(solution)/shard_map/all_to_all | solution.py:460
  16.6 0.5 collective-permute-start.1
  17.8 0.6 shard_map.139.slots_from
  18.4 0.2 collective-permute-done.1.other_ref
  18.6 0.8 copy-done
  19.4 3.3 %shard_map.140.so_far_ref = f32[4096,128]{1,0:T(8,128)S(1)} custom-call(s32[1,640]{1,0:T(1,128)S(1)} %shard_map.139.slots_from, bf16[64,128,128]{2,1,0:T(8,128)(2,1)S(1)} %copy-done, bf16[2048,128]{1,0:T(8,128)(2,1)S(1)} %bitcast.13, bf16[2048,128]{1,0:T(8,128)(2,1)S(1)} %collective-permute-done.1.other_ref), custom_call_target="tpu_custom_call" | custom-call | flops 8388608 | bytes 6291456 | tf_op jit(solution)/shard_map/pallas_call | solution.py:487
  22.7 2.7 %collective-permute-done.own_ref = bf16[2048,128]{1,0:T(8,128)(2,1)S(1)} collective-permute-done((bf16[2048,128]{1,0:T(8,128)(2,1)S(1)}, bf16[2048,128]{1,0:T(8,128)(2,1)S(1)}, u32[]{:S(2)}, u32[]{:S(2)}) %collective-permute-start) | collective-permute-done | bytes 524320 | tf_op jit(solution)/shard_map/ppermute | solution.py:462
  25.4 2.1 %collective-permute-start.2 = (bf16[2048,128]{1,0:T(8,128)(2,1)S(1)}, bf16[2048,128]{1,0:T(8,128)(2,1)S(1)}, u32[]{:S(2)}, u32[]{:S(2)}) collective-permute-start(bf16[2048,128]{1,0:T(8,128)(2,1)S(1)} %collective-permute-done.own_ref), channel_id=1, source_target_pairs={{0,8},{8,0},{16,24},{24,16},{32,40},{40,32},{48,56},{56,48},{64,72... | collective-permute-start | bytes 1572872 | tf_op jit(solution)/shard_map/ppermute | solution.py:497
  27.5 1.5 %collective-permute-done.2.other_ref = bf16[2048,128]{1,0:T(8,128)(2,1)S(1)} collective-permute-done((bf16[2048,128]{1,0:T(8,128)(2,1)S(1)}, bf16[2048,128]{1,0:T(8,128)(2,1)S(1)}, u32[]{:S(2)}, u32[]{:S(2)}) %collective-permute-start.2) | collective-permute-done | bytes 524320 | tf_op jit(solution)/shard_map/ppermute | solution.py:497
  29.0 2.5 %shard_map.141 = bf16[4096,128]{1,0:T(8,128)(2,1)S(1)} custom-call(s32[1,640]{1,0:T(1,128)S(1)} %shard_map.139.slots_from, bf16[64,128,128]{2,1,0:T(8,128)(2,1)S(1)} %copy-done, bf16[2048,128]{1,0:T(8,128)(2,1)S(1)} %collective-permute-done.own_ref, bf16[2048,128]{1,0:T(8,128)(2,1)S(1)} %collective-permute-done.2.other_ref, ...), custom_call_target="tpu_custom_call" | custom-call | flops 8388608 | bytes 6291456 | tf_op jit(solution)/shard_map/pallas_call | solution.py:498
  31.6 23.9 %all_to_all.21.parts_ref = bf16[8,512,128]{2,1,0:T(8,128)(2,1)S(1)} all-to-all(bf16[8,512,128]{2,1,0:T(8,128)(2,1)S(1)} %bitcast.10), channel_id=1, replica_groups=mesh['row'=16,'col'=8] {'col'}, dimensions={0} | all-to-all | bytes 2097152 | tf_op jit(solution)/shard_map/all_to_all | solution.py:507
  55.5 0.9 shard_map.142
  56.3 2.6 %collective-permute-start.3 = (bf16[144,128]{1,0:T(8,128)(2,1)S(1)}, bf16[144,128]{1,0:T(8,128)(2,1)S(1)}, u32[]{:S(2)}, u32[]{:S(2)}) collective-permute-start(bf16[144,128]{1,0:T(8,128)(2,1)S(1)} %get-tuple-element.32), channel_id=1, source_target_pairs={{0,8},{8,0},{16,24},{24,16},{32,40},{40,32},{48,56},{56,48},{64,72... | collective-permute-start | bytes 110600 | tf_op jit(solution)/shard_map/ppermute | solution.py:520
  58.9 0.3 shard_map.143.spread_ref
  59.2 0.6 collective-permute-done.3.got_ref
  59.8 22.5 %all_to_all.22.spread_ref = bf16[8,656,128]{2,1,0:T(8,128)(2,1)S(1)} all-to-all(bf16[8,656,128]{2,1,0:T(8,128)(2,1)S(1)} %shard_map.144), channel_id=1, replica_groups=mesh['row'=16,'col'=8] {'col'}, dimensions={0} | all-to-all | bytes 2686976 | tf_op jit(solution)/shard_map/all_to_all | solution.py:536
  82.3 1.5 %shard_map.145 = (bf16[2048,128]{1,0:T(8,128)(2,1)S(1)}, bf16[144,128]{1,0:T(8,128)(2,1)S(1)}) custom-call(s32[1,640]{1,0:T(1,128)S(1)} %shard_map.139.slots_from, bf16[64,128,128]{2,1,0:T(8,128)(2,1)S(1)} %copy-done, bf16[8,656,128]{2,1,0:T(8,128)(2,1)S(1)} %all_to_all.22.spread_ref), custom_call_target="tpu_custom_call" | custom-call | flops 8388608 | bytes 6291456 | tf_op jit(solution)/shard_map/pallas_call | solution.py:538
  83.8 1.5 %collective-permute-start.4 = (bf16[2048,128]{1,0:T(8,128)(2,1)S(1)}, bf16[2048,128]{1,0:T(8,128)(2,1)S(1)}, u32[]{:S(2)}, u32[]{:S(2)}) collective-permute-start(bf16[2048,128]{1,0:T(8,128)(2,1)S(1)} %get-tuple-element.36), channel_id=1, source_target_pairs={{0,8},{8,0},{16,24},{24,16},{32,40},{40,32},{48,56},{56,48},{64,72... | collective-permute-start | bytes 1572872 | tf_op jit(solution)/shard_map/ppermute | solution.py:548
  85.3 2.4 %shard_map.146.keep_ref = f32[2048,128]{1,0:T(8,128)S(1)} custom-call(s32[1,640]{1,0:T(1,128)S(1)} %shard_map.139.slots_from, bf16[64,128,128]{2,1,0:T(8,128)(2,1)S(1)} %copy-done, bf16[8,656,128]{2,1,0:T(8,128)(2,1)S(1)} %all_to_all.22.spread_ref), custom_call_target="tpu_custom_call" | custom-call | flops 8388608 | bytes 6291456 | tf_op jit(solution)/shard_map/pallas_call | solution.py:549
  87.8 0.1 shard_map.147
  87.9 3.4 %shard_map.148 = (f32[2048,128]{1,0:T(8,128)S(1)}, bf16[2048,128]{1,0:T(8,128)(2,1)S(1)}) custom-call(s32[1,640]{1,0:T(1,128)S(1)} %shard_map.139.slots_from, bf16[64,128,128]{2,1,0:T(8,128)(2,1)S(1)} %copy-done, bf16[8,656,128]{2,1,0:T(8,128)(2,1)S(1)} %all_to_all.22.spread_ref), custom_call_target="tpu_custom_call" | custom-call | flops 8388608 | bytes 6291456 | tf_op jit(solution)/shard_map/pallas_call | solution.py:567
  91.3 0.5 collective-permute-start.5
  91.8 0.9 shard_map.149
  92.7 0.7 collective-permute-done.5.got_ref
  93.3 3.3 %collective-permute-done.6.far_ref = bf16[2192,128]{1,0:T(8,128)(2,1)S(1)} collective-permute-done((bf16[2192,128]{1,0:T(8,128)(2,1)S(1)}, bf16[2192,128]{1,0:T(8,128)(2,1)S(1)}, u32[]{:S(2)}, u32[]{:S(2)}) %collective-permute-start.6) | collective-permute-done | bytes 561184 | tf_op jit(solution)/shard_map/ppermute | solution.py:566
  96.7 0.2 shard_map.150
  96.9 11.1 %all_to_all.23.parts_ref = bf16[4,656,128]{2,1,0:T(8,128)(2,1)S(1)} all-to-all(bf16[4,656,128]{2,1,0:T(8,128)(2,1)S(1)} %shard_map.150), channel_id=1, replica_groups={{0,64,16,80},{32,96,48,112},{8,72,56,120},{24,88,40,104},{1,65,17,81},{..., dimensions={0} | all-to-all | bytes 1343488 | tf_op jit(solution)/shard_map/all_to_all | solution.py:593
  108.0 2.2 %collective-permute-start.7 = (f32[136,128]{1,0:T(8,128)S(1)}, f32[136,128]{1,0:T(8,128)S(1)}, u32[]{:S(2)}, u32[]{:S(2)}) collective-permute-start(f32[136,128]{1,0:T(8,128)S(1)} %shard_map.152.mine_ref), channel_id=1, source_target_pairs={{0,8},{8,0},{16,24},{24,16},{32,40},{40,32},{48,56},{56,48},{64,72... | collective-permute-start | bytes 208904 | tf_op jit(solution)/shard_map/ppermute | solution.py:602
  110.2 0.8 shard_map.151
  111.0 0.1 collective-permute-done.7.other_ref
  111.1 0.7 shard_map.153
  (22 shorter events, 0.2 us)
Async XLA Ops:
  0.6 17.1 %copy-start.5 = (s32[1,1,512]{2,1,0:T(1,128)S(1)}, s32[1,1,512]{2,1,0:T(1,128)}, u32[]{:S(2)}) copy-start(s32[1,1,512]{2,1,0:T(1,128)} %param.17) | copy-start | bytes 6148
  0.6 17.1 %copy-start.8 = (s32[1,1,512]{2,1,0:T(1,128)S(1)}, s32[1,1,512]{2,1,0:T(1,128)}, u32[]{:S(2)}) copy-start(s32[1,1,512]{2,1,0:T(1,128)} %param.20) | copy-start | bytes 6148
  0.7 17.1 %copy-start.7 = (s32[1,1,512]{2,1,0:T(1,128)S(1)}, s32[1,1,512]{2,1,0:T(1,128)}, u32[]{:S(2)}) copy-start(s32[1,1,512]{2,1,0:T(1,128)} %param.19) | copy-start | bytes 6148
  0.7 17.1 %copy-start.6 = (s32[1,1,512]{2,1,0:T(1,128)S(1)}, s32[1,1,512]{2,1,0:T(1,128)}, u32[]{:S(2)}) copy-start(s32[1,1,512]{2,1,0:T(1,128)} %param.18) | copy-start | bytes 6148
  16.6 2.1 %collective-permute-start.1 = (bf16[2048,128]{1,0:T(8,128)(2,1)S(1)}, bf16[2048,128]{1,0:T(8,128)(2,1)S(1)}, u32[]{:S(2)}, u32[]{:S(2)}) collective-permute-start(bf16[2048,128]{1,0:T(8,128)(2,1)S(1)} %bitcast.11), channel_id=1, source_target_pairs={{0,8},{8,0},{16,24},{24,16},{32,40},{40,32},{48,56},{56,48},{64,72... | collective-permute-start | bytes 1572872 | tf_op jit(solution)/shard_map/ppermute | solution.py:461
  17.1 8.3 %collective-permute-start = (bf16[2048,128]{1,0:T(8,128)(2,1)S(1)}, bf16[2048,128]{1,0:T(8,128)(2,1)S(1)}, u32[]{:S(2)}, u32[]{:S(2)}) collective-permute-start(bf16[2048,128]{1,0:T(8,128)(2,1)S(1)} %bitcast.12), channel_id=1, source_target_pairs={{0,48},{8,24},{16,32},{24,8},{32,16},{40,56},{48,0},{56,40},{64,11... | collective-permute-start | bytes 1572872 | tf_op jit(solution)/shard_map/ppermute | solution.py:462
  17.8 1.6 %copy-start = (bf16[64,128,128]{2,1,0:T(8,128)(2,1)S(1)}, bf16[64,128,128]{2,1,0:T(8,128)(2,1)}, u32[]{:S(2)}) copy-start(bf16[64,128,128]{2,1,0:T(8,128)(2,1)} %patterns_ref.9) | copy-start | bytes 6291460
  25.4 3.6 %collective-permute-start.2 = (bf16[2048,128]{1,0:T(8,128)(2,1)S(1)}, bf16[2048,128]{1,0:T(8,128)(2,1)S(1)}, u32[]{:S(2)}, u32[]{:S(2)}) collective-permute-start(bf16[2048,128]{1,0:T(8,128)(2,1)S(1)} %collective-permute-done.own_ref), channel_id=1, source_target_pairs={{0,8},{8,0},{16,24},{24,16},{32,40},{40,32},{48,56},{56,48},{64,72... | collective-permute-start | bytes 1572872 | tf_op jit(solution)/shard_map/ppermute | solution.py:497
  31.5 23.9 %copy-start.1 = (bf16[512,256]{1,0:T(8,128)(2,1)S(1)}, bf16[512,256]{1,0:T(8,128)(2,1)}, u32[]{:S(2)}) copy-start(bf16[512,256]{1,0:T(8,128)(2,1)} %cotangent_ref.1) | copy-start | bytes 786436
  31.5 23.9 %copy-start.2 = (bf16[128,256]{1,0:T(8,128)(2,1)S(1)}, bf16[128,256]{1,0:T(8,128)(2,1)}, u32[]{:S(2)}) copy-start(bf16[128,256]{1,0:T(8,128)(2,1)} %weight_ref.3) | copy-start | bytes 196612
  31.5 23.9 %copy-start.3 = (s32[512]{0:T(512)S(1)}, s32[512]{0:T(512)}, u32[]{:S(2)}) copy-start(s32[512]{0:T(512)} %param.12) | copy-start | bytes 6148
  31.6 23.9 %copy-start.4 = (f32[256]{0:T(256)S(1)}, f32[256]{0:T(256)}, u32[]{:S(2)}) copy-start(f32[256]{0:T(256)} %param.15) | copy-start | bytes 3076
  56.3 3.4 %collective-permute-start.3 = (bf16[144,128]{1,0:T(8,128)(2,1)S(1)}, bf16[144,128]{1,0:T(8,128)(2,1)S(1)}, u32[]{:S(2)}, u32[]{:S(2)}) collective-permute-start(bf16[144,128]{1,0:T(8,128)(2,1)S(1)} %get-tuple-element.32), channel_id=1, source_target_pairs={{0,8},{8,0},{16,24},{24,16},{32,40},{40,32},{48,56},{56,48},{64,72... | collective-permute-start | bytes 110600 | tf_op jit(solution)/shard_map/ppermute | solution.py:520
  83.8 3.9 %collective-permute-start.4 = (bf16[2048,128]{1,0:T(8,128)(2,1)S(1)}, bf16[2048,128]{1,0:T(8,128)(2,1)S(1)}, u32[]{:S(2)}, u32[]{:S(2)}) collective-permute-start(bf16[2048,128]{1,0:T(8,128)(2,1)S(1)} %get-tuple-element.36), channel_id=1, source_target_pairs={{0,8},{8,0},{16,24},{24,16},{32,40},{40,32},{48,56},{56,48},{64,72... | collective-permute-start | bytes 1572872 | tf_op jit(solution)/shard_map/ppermute | solution.py:548
  87.9 8.8 %collective-permute-start.6 = (bf16[2192,128]{1,0:T(8,128)(2,1)S(1)}, bf16[2192,128]{1,0:T(8,128)(2,1)S(1)}, u32[]{:S(2)}, u32[]{:S(2)}) collective-permute-start(bf16[2192,128]{1,0:T(8,128)(2,1)S(1)} %shard_map.147), channel_id=1, source_target_pairs={{0,48},{8,24},{16,32},{24,8},{32,16},{40,56},{48,0},{56,40},{64,11... | collective-permute-start | bytes 1683464 | tf_op jit(solution)/shard_map/ppermute | solution.py:566
  91.3 2.0 %collective-permute-start.5 = (bf16[2048,128]{1,0:T(8,128)(2,1)S(1)}, bf16[2048,128]{1,0:T(8,128)(2,1)S(1)}, u32[]{:S(2)}, u32[]{:S(2)}) collective-permute-start(bf16[2048,128]{1,0:T(8,128)(2,1)S(1)} %get-tuple-element.39), channel_id=1, source_target_pairs={{0,8},{8,0},{16,24},{24,16},{32,40},{40,32},{48,56},{56,48},{64,72... | collective-permute-start | bytes 1572872 | tf_op jit(solution)/shard_map/ppermute | solution.py:576
  108.0 3.1 %collective-permute-start.7 = (f32[136,128]{1,0:T(8,128)S(1)}, f32[136,128]{1,0:T(8,128)S(1)}, u32[]{:S(2)}, u32[]{:S(2)}) collective-permute-start(f32[136,128]{1,0:T(8,128)S(1)} %shard_map.152.mine_ref), channel_id=1, source_target_pairs={{0,8},{8,0},{16,24},{24,16},{32,40},{40,32},{48,56},{56,48},{64,72... | collective-permute-start | bytes 208904 | tf_op jit(solution)/shard_map/ppermute | solution.py:602

commit v11 on v9

--- a/solution.py
+++ b/solution.py
@@ -113,18 +113,21 @@
 
 
 def scale_kernel(features_hbm, degree_hbm, out_ref, features_ref, degree_ref, sems):
-    copies = (
-        pltpu.make_async_copy(degree_hbm, degree_ref, sems.at[0]),
-        pltpu.make_async_copy(features_hbm, features_ref, sems.at[1]),
-    )
-    for copy in copies:
-        copy.start()
-    copies[0].wait()
+    tiles, edge = degree_ref.shape
+    degree_copy = pltpu.make_async_copy(degree_hbm, degree_ref, sems.at[tiles])
+    degree_copy.start()
+    copies = []
+    for tile in range(tiles):
+        rows = pl.ds(tile * edge, edge)
+        copies.append(
+            pltpu.make_async_copy(features_hbm.at[rows], features_ref.at[rows], sems.at[tile])
+        )
+        copies[-1].start()
+    degree_copy.wait()
     roots = root_columns(degree_ref[...])
-    copies[1].wait()
-    edge = degree_ref.shape[1]
-    for tile in range(degree_ref.shape[0]):
+    for tile in range(tiles):
         rows = pl.ds(tile * edge, edge)
+        copies[tile].wait()
         scaled = features_ref[rows, :].astype(jnp.float32) * roots[:, tile : tile + 1]
         scaled = scaled.astype(jnp.bfloat16)
         for copy in range(out_ref.shape[0]):
@@ -453,7 +456,7 @@
         scratch_shapes=[
             pltpu.VMEM(features.shape, bf16),
             pltpu.VMEM(degree_tiles.shape, jnp.int32),
-            pltpu.SemaphoreType.DMA((2,)),
+            pltpu.SemaphoreType.DMA((per_shard + 1,)),
         ],
         compiler_params=pltpu.CompilerParams(vmem_limit_bytes=62 * 1024 * 1024),
     )(features, degree_tiles)

time: 113 us -> 112 us (level)
  starting transfers between devices: 12 us -> 8.73 us
  waiting for transfers between devices: 7.49 us -> 8.63 us
    ppermute x2, starting transfers between devices: 5.7 us -> 2.92 us  [per_device(): got = lax.ppermute(send, 'row', swap)]
    all_to_all x1, blocking collectives: 10.7 us -> 11.9 us  [per_device(): back_parts = exchange(joined, 'row', axis_index_groups=row_near)]
where the time goes in v11:
time: 112 us; the launch traced here: 111 us
  blocking collectives  73.6 us (66%)
  Pallas kernels  16.9 us (15%)
  starting transfers between devices  8.73 us (8%)
  waiting for transfers between devices  8.63 us (8%)
  local copies, waits for them, and re-layouts  1.64 us (1%)
  between operations  1.5 us (1%)
    all_to_all x1, blocking collectives, per_device(): exchange(row_part.reshape(col_devices, node_dev, feature_count), 'col')  25 us
    all_to_all x1, blocking collectives, per_device(): spread_all = exchange(spread, 'col')  22.7 us
    all_to_all x1, blocking collectives, per_device(): exchange(scaled, 'row', axis_index_groups=row_near)  14 us
    all_to_all x1, blocking collectives, per_device(): back_parts = exchange(joined, 'row', axis_index_groups=row_near)  11.9 us
    ppermute x2, starting transfers between devices, per_device(): got = lax.ppermute(send, 'row', swap)  2.92 us
    ppermute x1, waiting for transfers between devices, per_device(): far_own = lax.ppermute(near_own, 'row', row_far)  2.85 us
    pallas_call x1, Pallas kernels, per_device(): pl.pallas_call(backward_near_kernel, out_shape=(kept, sent), in_specs=[HB...  2.52 us
    pallas_call x1, Pallas kernels, per_device(): pl.pallas_call(forward_far_kernel, out_shape=shape(row_sums.shape, bf16),...  2.42 us
  transfers between devices with their start and end apart: 8, of which 7 were waited for; matrix products, arithmetic and copies ran while one was open for 0% of the time, Pallas kernels for 8%

profile of v11, /device:TPU:1, one launch (start us, length us, event | category | flops | bytes accessed | tf_op | source)
XLA Modules:
  0.0 111.0 jit_solution(12442569049387848059)
XLA Ops:
  0.7 2.0 %shard_map.138 = bf16[4,512,128]{2,1,0:T(8,128)(2,1)} custom-call(bf16[512,128]{1,0:T(8,128)(2,1)} %features_hbm.1, s32[4,128]{1,0:T(4,128)} %bitcast.14), custom_call_target="tpu_custom_call" | custom-call | tf_op jit(solution)/shard_map/pallas_call | solution.py:451
  2.7 14.0 %all_to_all.20 = bf16[4,512,128]{2,1,0:T(8,128)(2,1)S(1)} all-to-all(bf16[4,512,128]{2,1,0:T(8,128)(2,1)} %shard_map.138), channel_id=1, replica_groups={{0,64,16,80},{32,96,48,112},{8,72,56,120},{24,88,40,104},{1,65,17,81},{..., dimensions={0} | all-to-all | bytes 1048576 | tf_op jit(solution)/shard_map/all_to_all | solution.py:463
  16.7 0.5 collective-permute-start.1
  17.9 0.6 shard_map.139.slots_from
  18.5 0.2 collective-permute-done.1.other_ref
  18.8 1.6 %copy-done = bf16[64,128,128]{2,1,0:T(8,128)(2,1)S(1)} copy-done((bf16[64,128,128]{2,1,0:T(8,128)(2,1)S(1)}, bf16[64,128,128]{2,1,0:T(8,128)(2,1)}, u32[]{:S(2)}) %copy-start) | copy-done | bytes 2097176
  20.3 2.3 %shard_map.140.so_far_ref = f32[4096,128]{1,0:T(8,128)S(1)} custom-call(s32[1,640]{1,0:T(1,128)S(1)} %shard_map.139.slots_from, bf16[64,128,128]{2,1,0:T(8,128)(2,1)S(1)} %copy-done, bf16[2048,128]{1,0:T(8,128)(2,1)S(1)} %bitcast.13, bf16[2048,128]{1,0:T(8,128)(2,1)S(1)} %collective-permute-done.1.other_ref), custom_call_target="tpu_custom_call" | custom-call | flops 8388608 | bytes 6291456 | tf_op jit(solution)/shard_map/pallas_call | solution.py:489
  22.7 2.8 %collective-permute-done.own_ref = bf16[2048,128]{1,0:T(8,128)(2,1)S(1)} collective-permute-done((bf16[2048,128]{1,0:T(8,128)(2,1)S(1)}, bf16[2048,128]{1,0:T(8,128)(2,1)S(1)}, u32[]{:S(2)}, u32[]{:S(2)}) %collective-permute-start) | collective-permute-done | bytes 524320 | tf_op jit(solution)/shard_map/ppermute | solution.py:465
  25.5 2.1 %collective-permute-start.2 = (bf16[2048,128]{1,0:T(8,128)(2,1)S(1)}, bf16[2048,128]{1,0:T(8,128)(2,1)S(1)}, u32[]{:S(2)}, u32[]{:S(2)}) collective-permute-start(bf16[2048,128]{1,0:T(8,128)(2,1)S(1)} %collective-permute-done.own_ref), channel_id=1, source_target_pairs={{0,8},{8,0},{16,24},{24,16},{32,40},{40,32},{48,56},{56,48},{64,72... | collective-permute-start | bytes 1572872 | tf_op jit(solution)/shard_map/ppermute | solution.py:499
  27.6 1.5 %collective-permute-done.2.other_ref = bf16[2048,128]{1,0:T(8,128)(2,1)S(1)} collective-permute-done((bf16[2048,128]{1,0:T(8,128)(2,1)S(1)}, bf16[2048,128]{1,0:T(8,128)(2,1)S(1)}, u32[]{:S(2)}, u32[]{:S(2)}) %collective-permute-start.2) | collective-permute-done | bytes 524320 | tf_op jit(solution)/shard_map/ppermute | solution.py:499
  29.2 2.4 %shard_map.141 = bf16[4096,128]{1,0:T(8,128)(2,1)S(1)} custom-call(s32[1,640]{1,0:T(1,128)S(1)} %shard_map.139.slots_from, bf16[64,128,128]{2,1,0:T(8,128)(2,1)S(1)} %copy-done, bf16[2048,128]{1,0:T(8,128)(2,1)S(1)} %collective-permute-done.own_ref, bf16[2048,128]{1,0:T(8,128)(2,1)S(1)} %collective-permute-done.2.other_ref, ...), custom_call_target="tpu_custom_call" | custom-call | flops 8388608 | bytes 6291456 | tf_op jit(solution)/shard_map/pallas_call | solution.py:500
  31.6 25.0 %all_to_all.21.parts_ref = bf16[8,512,128]{2,1,0:T(8,128)(2,1)S(1)} all-to-all(bf16[8,512,128]{2,1,0:T(8,128)(2,1)S(1)} %bitcast.10), channel_id=1, replica_groups=mesh['row'=16,'col'=8] {'col'}, dimensions={0} | all-to-all | bytes 2097152 | tf_op jit(solution)/shard_map/all_to_all | solution.py:509
  56.7 0.9 shard_map.142
  57.7 0.3 shard_map.143.spread_ref
  58.0 0.9 collective-permute-done.3.got_ref
  58.9 22.7 %all_to_all.22.spread_ref = bf16[8,656,128]{2,1,0:T(8,128)(2,1)S(1)} all-to-all(bf16[8,656,128]{2,1,0:T(8,128)(2,1)S(1)} %shard_map.144), channel_id=1, replica_groups=mesh['row'=16,'col'=8] {'col'}, dimensions={0} | all-to-all | bytes 2686976 | tf_op jit(solution)/shard_map/all_to_all | solution.py:538
  81.6 1.6 %shard_map.145 = (bf16[2048,128]{1,0:T(8,128)(2,1)S(1)}, bf16[144,128]{1,0:T(8,128)(2,1)S(1)}) custom-call(s32[1,640]{1,0:T(1,128)S(1)} %shard_map.139.slots_from, bf16[64,128,128]{2,1,0:T(8,128)(2,1)S(1)} %copy-done.1, bf16[8,656,128]{2,1,0:T(8,128)(2,1)S(1)} %all_to_all.22.spread_ref), custom_call_target="tpu_custom_call" | custom-call | flops 8388608 | bytes 6291456 | tf_op jit(solution)/shard_map/pallas_call | solution.py:540
  83.2 1.4 %collective-permute-start.4 = (bf16[2048,128]{1,0:T(8,128)(2,1)S(1)}, bf16[2048,128]{1,0:T(8,128)(2,1)S(1)}, u32[]{:S(2)}, u32[]{:S(2)}) collective-permute-start(bf16[2048,128]{1,0:T(8,128)(2,1)S(1)} %get-tuple-element.36), channel_id=1, source_target_pairs={{0,8},{8,0},{16,24},{24,16},{32,40},{40,32},{48,56},{56,48},{64,72... | collective-permute-start | bytes 1572872 | tf_op jit(solution)/shard_map/ppermute | solution.py:550
  84.6 1.5 %shard_map.146.keep_ref = f32[2048,128]{1,0:T(8,128)S(1)} custom-call(s32[1,640]{1,0:T(1,128)S(1)} %shard_map.139.slots_from, bf16[64,128,128]{2,1,0:T(8,128)(2,1)S(1)} %copy-done.1, bf16[8,656,128]{2,1,0:T(8,128)(2,1)S(1)} %all_to_all.22.spread_ref), custom_call_target="tpu_custom_call" | custom-call | flops 8388608 | bytes 6291456 | tf_op jit(solution)/shard_map/pallas_call | solution.py:551
  86.2 0.1 shard_map.147
  86.2 0.9 collective-permute-start.6
  87.1 2.5 %shard_map.148 = (f32[2048,128]{1,0:T(8,128)S(1)}, bf16[2048,128]{1,0:T(8,128)(2,1)S(1)}) custom-call(s32[1,640]{1,0:T(1,128)S(1)} %shard_map.139.slots_from, bf16[64,128,128]{2,1,0:T(8,128)(2,1)S(1)} %copy-done.1, bf16[8,656,128]{2,1,0:T(8,128)(2,1)S(1)} %all_to_all.22.spread_ref), custom_call_target="tpu_custom_call" | custom-call | flops 8388608 | bytes 6291456 | tf_op jit(solution)/shard_map/pallas_call | solution.py:569
  89.7 1.5 %collective-permute-start.5 = (bf16[2048,128]{1,0:T(8,128)(2,1)S(1)}, bf16[2048,128]{1,0:T(8,128)(2,1)S(1)}, u32[]{:S(2)}, u32[]{:S(2)}) collective-permute-start(bf16[2048,128]{1,0:T(8,128)(2,1)S(1)} %get-tuple-element.39), channel_id=1, source_target_pairs={{0,8},{8,0},{16,24},{24,16},{32,40},{40,32},{48,56},{56,48},{64,72... | collective-permute-start | bytes 1572872 | tf_op jit(solution)/shard_map/ppermute | solution.py:578
  91.1 0.9 shard_map.149
  92.0 0.7 collective-permute-done.5.got_ref
  92.7 2.4 %collective-permute-done.6.far_ref = bf16[2192,128]{1,0:T(8,128)(2,1)S(1)} collective-permute-done((bf16[2192,128]{1,0:T(8,128)(2,1)S(1)}, bf16[2192,128]{1,0:T(8,128)(2,1)S(1)}, u32[]{:S(2)}, u32[]{:S(2)}) %collective-permute-start.6) | collective-permute-done | bytes 561184 | tf_op jit(solution)/shard_map/ppermute | solution.py:568
  95.0 0.2 shard_map.150
  95.3 11.9 %all_to_all.23.parts_ref = bf16[4,656,128]{2,1,0:T(8,128)(2,1)S(1)} all-to-all(bf16[4,656,128]{2,1,0:T(8,128)(2,1)S(1)} %shard_map.150), channel_id=1, replica_groups={{0,64,16,80},{32,96,48,112},{8,72,56,120},{24,88,40,104},{1,65,17,81},{..., dimensions={0} | all-to-all | bytes 1343488 | tf_op jit(solution)/shard_map/all_to_all | solution.py:595
  107.2 2.2 %collective-permute-start.7 = (f32[136,128]{1,0:T(8,128)S(1)}, f32[136,128]{1,0:T(8,128)S(1)}, u32[]{:S(2)}, u32[]{:S(2)}) collective-permute-start(f32[136,128]{1,0:T(8,128)S(1)} %shard_map.152.mine_ref), channel_id=1, source_target_pairs={{0,8},{8,0},{16,24},{24,16},{32,40},{40,32},{48,56},{56,48},{64,72... | collective-permute-start | bytes 208904 | tf_op jit(solution)/shard_map/ppermute | solution.py:604
  109.4 0.8 shard_map.151
  110.2 0.1 collective-permute-done.7.other_ref
  110.3 0.7 shard_map.153
  (24 shorter events, 0.2 us)
Async XLA Ops:
  0.6 17.2 %copy-start.5 = (s32[1,1,512]{2,1,0:T(1,128)S(1)}, s32[1,1,512]{2,1,0:T(1,128)}, u32[]{:S(2)}) copy-start(s32[1,1,512]{2,1,0:T(1,128)} %param.17) | copy-start | bytes 6148
  0.6 17.2 %copy-start.8 = (s32[1,1,512]{2,1,0:T(1,128)S(1)}, s32[1,1,512]{2,1,0:T(1,128)}, u32[]{:S(2)}) copy-start(s32[1,1,512]{2,1,0:T(1,128)} %param.20) | copy-start | bytes 6148
  0.7 17.2 %copy-start.7 = (s32[1,1,512]{2,1,0:T(1,128)S(1)}, s32[1,1,512]{2,1,0:T(1,128)}, u32[]{:S(2)}) copy-start(s32[1,1,512]{2,1,0:T(1,128)} %param.19) | copy-start | bytes 6148
  0.7 17.2 %copy-start.6 = (s32[1,1,512]{2,1,0:T(1,128)S(1)}, s32[1,1,512]{2,1,0:T(1,128)}, u32[]{:S(2)}) copy-start(s32[1,1,512]{2,1,0:T(1,128)} %param.18) | copy-start | bytes 6148
  16.7 2.1 %collective-permute-start.1 = (bf16[2048,128]{1,0:T(8,128)(2,1)S(1)}, bf16[2048,128]{1,0:T(8,128)(2,1)S(1)}, u32[]{:S(2)}, u32[]{:S(2)}) collective-permute-start(bf16[2048,128]{1,0:T(8,128)(2,1)S(1)} %bitcast.11), channel_id=1, source_target_pairs={{0,8},{8,0},{16,24},{24,16},{32,40},{40,32},{48,56},{56,48},{64,72... | collective-permute-start | bytes 1572872 | tf_op jit(solution)/shard_map/ppermute | solution.py:464
  17.2 8.3 %collective-permute-start = (bf16[2048,128]{1,0:T(8,128)(2,1)S(1)}, bf16[2048,128]{1,0:T(8,128)(2,1)S(1)}, u32[]{:S(2)}, u32[]{:S(2)}) collective-permute-start(bf16[2048,128]{1,0:T(8,128)(2,1)S(1)} %bitcast.12), channel_id=1, source_target_pairs={{0,48},{8,24},{16,32},{24,8},{32,16},{40,56},{48,0},{56,40},{64,11... | collective-permute-start | bytes 1572872 | tf_op jit(solution)/shard_map/ppermute | solution.py:465
  18.8 1.6 %copy-start = (bf16[64,128,128]{2,1,0:T(8,128)(2,1)S(1)}, bf16[64,128,128]{2,1,0:T(8,128)(2,1)}, u32[]{:S(2)}) copy-start(bf16[64,128,128]{2,1,0:T(8,128)(2,1)} %patterns_ref.9) | copy-start | bytes 6291460
  25.5 3.6 %collective-permute-start.2 = (bf16[2048,128]{1,0:T(8,128)(2,1)S(1)}, bf16[2048,128]{1,0:T(8,128)(2,1)S(1)}, u32[]{:S(2)}, u32[]{:S(2)}) collective-permute-start(bf16[2048,128]{1,0:T(8,128)(2,1)S(1)} %collective-permute-done.own_ref), channel_id=1, source_target_pairs={{0,8},{8,0},{16,24},{24,16},{32,40},{40,32},{48,56},{56,48},{64,72... | collective-permute-start | bytes 1572872 | tf_op jit(solution)/shard_map/ppermute | solution.py:499
  31.6 25.1 %copy-start.2 = (bf16[512,256]{1,0:T(8,128)(2,1)S(1)}, bf16[512,256]{1,0:T(8,128)(2,1)}, u32[]{:S(2)}) copy-start(bf16[512,256]{1,0:T(8,128)(2,1)} %cotangent_ref.1) | copy-start | bytes 786436
  31.6 25.1 %copy-start.3 = (bf16[128,256]{1,0:T(8,128)(2,1)S(1)}, bf16[128,256]{1,0:T(8,128)(2,1)}, u32[]{:S(2)}) copy-start(bf16[128,256]{1,0:T(8,128)(2,1)} %weight_ref.3) | copy-start | bytes 196612
  31.6 25.1 %copy-start.4 = (s32[512]{0:T(512)S(1)}, s32[512]{0:T(512)}, u32[]{:S(2)}) copy-start(s32[512]{0:T(512)} %param.12) | copy-start | bytes 6148
  31.6 25.1 %copy-start.9 = (f32[256]{0:T(256)S(1)}, f32[256]{0:T(256)}, u32[]{:S(2)}) copy-start(f32[256]{0:T(256)} %param.15) | copy-start | bytes 3076
  57.6 1.3 %collective-permute-start.3 = (bf16[144,128]{1,0:T(8,128)(2,1)S(1)}, bf16[144,128]{1,0:T(8,128)(2,1)S(1)}, u32[]{:S(2)}, u32[]{:S(2)}) collective-permute-start(bf16[144,128]{1,0:T(8,128)(2,1)S(1)} %get-tuple-element.32), channel_id=1, source_target_pairs={{0,8},{8,0},{16,24},{24,16},{32,40},{40,32},{48,56},{56,48},{64,72... | collective-permute-start | bytes 110600 | tf_op jit(solution)/shard_map/ppermute | solution.py:522
  58.9 22.7 %copy-start.1 = (bf16[64,128,128]{2,1,0:T(8,128)(2,1)S(1)}, bf16[64,128,128]{2,1,0:T(8,128)(2,1)}, u32[]{:S(2)}) copy-start(bf16[64,128,128]{2,1,0:T(8,128)(2,1)} %patterns_ref.9) | copy-start | bytes 6291460
  83.2 3.0 %collective-permute-start.4 = (bf16[2048,128]{1,0:T(8,128)(2,1)S(1)}, bf16[2048,128]{1,0:T(8,128)(2,1)S(1)}, u32[]{:S(2)}, u32[]{:S(2)}) collective-permute-start(bf16[2048,128]{1,0:T(8,128)(2,1)S(1)} %get-tuple-element.36), channel_id=1, source_target_pairs={{0,8},{8,0},{16,24},{24,16},{32,40},{40,32},{48,56},{56,48},{64,72... | collective-permute-start | bytes 1572872 | tf_op jit(solution)/shard_map/ppermute | solution.py:550
  86.2 8.8 %collective-permute-start.6 = (bf16[2192,128]{1,0:T(8,128)(2,1)S(1)}, bf16[2192,128]{1,0:T(8,128)(2,1)S(1)}, u32[]{:S(2)}, u32[]{:S(2)}) collective-permute-start(bf16[2192,128]{1,0:T(8,128)(2,1)S(1)} %shard_map.147), channel_id=1, source_target_pairs={{0,48},{8,24},{16,32},{24,8},{32,16},{40,56},{48,0},{56,40},{64,11... | collective-permute-start | bytes 1683464 | tf_op jit(solution)/shard_map/ppermute | solution.py:568
  89.7 3.0 %collective-permute-start.5 = (bf16[2048,128]{1,0:T(8,128)(2,1)S(1)}, bf16[2048,128]{1,0:T(8,128)(2,1)S(1)}, u32[]{:S(2)}, u32[]{:S(2)}) collective-permute-start(bf16[2048,128]{1,0:T(8,128)(2,1)S(1)} %get-tuple-element.39), channel_id=1, source_target_pairs={{0,8},{8,0},{16,24},{24,16},{32,40},{40,32},{48,56},{56,48},{64,72... | collective-permute-start | bytes 1572872 | tf_op jit(solution)/shard_map/ppermute | solution.py:578
  107.2 3.1 %collective-permute-start.7 = (f32[136,128]{1,0:T(8,128)S(1)}, f32[136,128]{1,0:T(8,128)S(1)}, u32[]{:S(2)}, u32[]{:S(2)}) collective-permute-start(f32[136,128]{1,0:T(8,128)S(1)} %shard_map.152.mine_ref), channel_id=1, source_target_pairs={{0,8},{8,0},{16,24},{24,16},{32,40},{40,32},{48,56},{56,48},{64,72... | collective-permute-start | bytes 208904 | tf_op jit(solution)/shard_map/ppermute | solution.py:604
